TPU v7x, 256 devices: a whole 4x4x8 slice. The times are simulated.
256 devices in a mesh: row: 16 (over x_hi, y, core), chan: 16 (over z, x_lo).
Axes of the slice: x: 4 (x_hi: 2, x_lo: 2; x = x_hi * 2 + x_lo), y: 4, z: 8, core: 2. Of those that a mesh axis runs over, the one named last changes fastest.
Arguments:
- frames: bfloat16 [4, 128, 256, 128], P(None, 'row', 'chan'), may hold values from -11 to 11
- cache: bfloat16 [2, 2, 128, 256, 128], P(None, None, 'row', 'chan'), may hold values from -4 to 4
- norm_gain: float32 [2, 256], P(None, 'chan'), may hold values from 0.25 to 1.75
- norm_shift: float32 [2, 256], P(None, 'chan'), may hold values from -1.5 to 1.5
- conv_weight: bfloat16 [2, 256, 27, 256], P(None, 'chan'), may hold values from -0.078125 to 0.078125
- conv_bias: float32 [2, 256], P(None, 'chan'), may hold values from -1.5 to 1.5
Outputs:
- decoded: bfloat16 [4, 128, 256, 128], P(None, 'row', 'chan')
All inputs are finite; a program needn't handle non-finite values.
Results may differ from a plain program's by a relative error of at most 0.0095.
Values may be sent and summed in bfloat16 or wider, within the bound.
No kernel may reach another device: no remote copies, remote signals or barrier semaphores. Data moves between devices by JAX's collectives and lax.ppermute only.
A program may use at most 64 MiB of HBM per device.

v0:
```python
import jax
import jax.numpy as jnp
from jax import lax
from jax.sharding import PartitionSpec as P

CH = 256
GROUPS = 32


def with_halo(x, sides, width):
    for axis, dim in sides:
        size, length = (lax.axis_size(axis), x.shape[dim])
        up = [(i, (i + 1) % size) for i in range(size - 1)]
        down = [(j, i) for i, j in up]
        last = lax.slice_in_dim(x, length - width, length, axis=dim)
        first = lax.slice_in_dim(x, 0, width, axis=dim)
        before = lax.ppermute(last, axis, up)
        after = lax.ppermute(first, axis, down)
        x = jnp.concatenate([before, x, after], axis=dim)
    return x


def taps_sum(padded, weights):
    frames_out = padded.shape[0] - 2
    rows_out = padded.shape[1] - 2
    cols_out = padded.shape[3] - 2
    summed = jnp.zeros((frames_out, rows_out, weights.shape[0], cols_out), jnp.float32)
    for time_tap in range(3):
        for row_tap in range(3):
            kernel = weights[:, 9 * time_tap + 3 * row_tap : 9 * time_tap + 3 * row_tap + 3]
            window = padded[time_tap : time_tap + frames_out, row_tap : row_tap + rows_out]
            product = jnp.einsum(
                "okc,trcw->trkow", kernel, window, preferred_element_type=jnp.float32
            )
            for col_tap in range(3):
                summed = summed + product[:, :, col_tap, :, col_tap : col_tap + cols_out]
    return summed


def normalize(values, gain, shift):
    group_size = CH // GROUPS
    extent = values.shape
    grouped = values.reshape(extent[0], extent[1], extent[2] // group_size, group_size, extent[3])
    number = extent[0] * extent[1] * lax.axis_size("row") * group_size * extent[3]
    means = lax.psum(jnp.sum(grouped, axis=(0, 1, 3, 4)), "row") / number
    centred = grouped - means[None, None, :, None, None]
    spread = lax.psum(jnp.sum(centred * centred, axis=(0, 1, 3, 4)), "row") / number
    scaled = (centred * lax.rsqrt(spread + 1e-06)[None, None, :, None, None]).reshape(extent)
    shifted = scaled * gain[None, None, :, None] + shift[None, None, :, None]
    return jax.nn.silu(shifted).astype(jnp.bfloat16)


def convolve(history, normed, weights, bias):
    joined = jnp.concatenate([history, normed], axis=0)
    haloed = with_halo(joined, (("row", 1),), 1)
    padded = jnp.pad(haloed, ((0, 0), (0, 0), (0, 0), (1, 1)))
    conved = taps_sum(lax.all_gather(padded, "chan", axis=2, tiled=True), weights)
    return conved + bias[None, None, :, None]


def local(frames, cache, norm_gain, norm_shift, conv_weight, conv_bias):
    current = frames
    first_act = normalize(current.astype(jnp.float32), norm_gain[0], norm_shift[0])
    middle = convolve(cache[0], first_act, conv_weight[0], conv_bias[0]).astype(jnp.bfloat16)
    second_act = normalize(middle.astype(jnp.float32), norm_gain[1], norm_shift[1])
    branch = convolve(cache[1], second_act, conv_weight[1], conv_bias[1])
    current = (current.astype(jnp.float32) + branch).astype(jnp.bfloat16)
    return current


def solution(mesh):
    placed = (
        P(None, "row", "chan", None),
        P(None, None, "row", "chan", None),
        P(None, "chan"),
        P(None, "chan"),
        P(None, "chan", None, None),
        P(None, "chan"),
    )
    return jax.shard_map(
        local, mesh=mesh, in_specs=placed, out_specs=P(None, "row", "chan", None), check_vma=False
    )
```

profile of v0, /device:TPU:27, one launch (start us, length us, event | category | flops | bytes accessed | tf_op | source)
XLA Modules:
  0.0 561.3 jit_solution(6861651016799678981)
XLA Ops:
  6.5 1.0 convert_reduce_fusion
  7.6 0.1 reduce_sum.47
  7.7 0.1 reduce_sum.51
  7.8 32.6 %psum.28 = f32[2]{0:T(128)S(1)} all-reduce(f32[2]{0:T(128)S(1)} %reduce_sum.51), channel_id=1, replica_groups=mesh['row'=16,'chan'=16] {'row'}, use_global_device_ids=true, to_apply=%region_2.0 | all-reduce | flops 2 | bytes 16 | tf_op jit(solution)/shard_map/psum | solution.py:45
  40.6 1.1 fusion.49
  41.8 0.1 reduce_sum.54
  41.9 33.2 %psum.29 = f32[2]{0:T(128)S(1)} all-reduce(f32[2]{0:T(128)S(1)} %reduce_sum.54), channel_id=1, replica_groups=mesh['row'=16,'chan'=16] {'row'}, use_global_device_ids=true, to_apply=%region_5.6 | all-reduce | flops 2 | bytes 16 | tf_op jit(solution)/shard_map/psum | solution.py:47
  75.2 0.9 slice_bitcast_fusion.87
  76.1 0.8 slice_bitcast_fusion.128
  76.9 1.1 fusion.57
  78.0 7.8 %collective-permute-start = (bf16[6,1,16,128]{3,2,1,0:T(8,128)(2,1)S(1)}, bf16[6,1,16,128]{3,2,1,0:T(8,128)(2,1)S(1)}, u32[]{:S(2)}, u32[]{:S(2)}) collective-permute-start(bf16[6,1,16,128]{3,2,1,0:T(8,128)(2,1)S(1)} %get-tuple-element.12), channel_id=1, source_target_pairs={{0,16},{16,32},{32,48},{48,64},{64,80},{80,96},{96,112},{112,128},... | collective-permute-start | bytes 73736 | tf_op jit(solution)/shard_map/ppermute | solution.py:17
  85.8 1.9 collective-permute-start.1
  87.7 6.8 %collective-permute-done.1 = bf16[6,1,16,128]{3,2,1,0:T(8,128)(2,1)S(1)} collective-permute-done((bf16[6,1,16,128]{3,2,1,0:T(8,128)(2,1)S(1)}, bf16[6,1,16,128]{3,2,1,0:T(8,128)(2,1)S(1)}, u32[]{:S(2)}, u32[]{:S(2)}) %collective-permute-start.1) | collective-permute-done | bytes 24608 | tf_op jit(solution)/shard_map/ppermute | solution.py:18
  94.5 1.1 fusion.44
  95.7 0.8 slice_bitcast_fusion.124
  96.4 1.8 slice_bitcast_fusion.84
  98.2 168.7 %all-gather.3.cloned.1.call-done = bf16[6,10,256,130]{3,2,1,0:T(8,128)(2,1)} async-done(((bf16[6,10,16,130]{3,2,1,0:T(8,128)(2,1)}), bf16[6,10,256,130]{3,2,1,0:T(8,128)(2,1)}) %all-gather.3.cloned.1.call-update) | async-done | bytes 3993616 | tf_op jit(solution)/shard_map/all_gather | solution.py:57
  267.0 3.2 fusion.23
  270.1 3.9 fusion.24
  274.1 0.8 fusion.25
  274.9 0.8 fusion.26
  275.8 0.8 fusion.18
  276.6 0.8 fusion.19
  277.4 0.8 fusion.20
  278.3 0.8 fusion.21
  279.1 0.8 fusion.22
  280.0 2.1 convert_reduce_fusion.1
  282.1 0.1 reduce_sum.72
  282.3 32.6 %psum.30 = f32[2]{0:T(128)S(1)} all-reduce(f32[2]{0:T(128)S(1)} %reduce_sum.72), channel_id=1, replica_groups=mesh['row'=16,'chan'=16] {'row'}, use_global_device_ids=true, to_apply=%region_8.9 | all-reduce | flops 2 | bytes 16 | tf_op jit(solution)/shard_map/psum | solution.py:45
  315.0 1.1 fusion.59
  316.2 0.1 reduce_sum.75
  316.4 33.2 %psum.31 = f32[2]{0:T(128)S(1)} all-reduce(f32[2]{0:T(128)S(1)} %reduce_sum.75), channel_id=1, replica_groups=mesh['row'=16,'chan'=16] {'row'}, use_global_device_ids=true, to_apply=%region_11.12 | all-reduce | flops 2 | bytes 16 | tf_op jit(solution)/shard_map/psum | solution.py:47
  349.7 2.0 multiply_convert_fusion
  351.7 7.8 %collective-permute-start.2 = (bf16[6,1,16,128]{3,2,1,0:T(8,128)(2,1)S(1)}, bf16[6,1,16,128]{3,2,1,0:T(8,128)(2,1)S(1)}, u32[]{:S(2)}, u32[]{:S(2)}) collective-permute-start(bf16[6,1,16,128]{3,2,1,0:T(8,128)(2,1)S(1)} %get-tuple-element.10), channel_id=1, source_target_pairs={{0,16},{16,32},{32,48},{48,64},{64,80},{80,96},{96,112},{112,128},... | collective-permute-start | bytes 73736 | tf_op jit(solution)/shard_map/ppermute | solution.py:17
  359.6 2.2 collective-permute-start.3
  361.8 6.6 %collective-permute-done.3 = bf16[6,1,16,128]{3,2,1,0:T(8,128)(2,1)S(1)} collective-permute-done((bf16[6,1,16,128]{3,2,1,0:T(8,128)(2,1)S(1)}, bf16[6,1,16,128]{3,2,1,0:T(8,128)(2,1)S(1)}, u32[]{:S(2)}, u32[]{:S(2)}) %collective-permute-start.3) | collective-permute-done | bytes 24608 | tf_op jit(solution)/shard_map/ppermute | solution.py:18
  368.4 1.1 select_maximum_fusion
  369.5 170.5 %all-gather.5.cloned.1.call-done = bf16[6,10,256,130]{3,2,1,0:T(8,128)(2,1)} async-done(((bf16[6,10,16,130]{3,2,1,0:T(8,128)(2,1)}), bf16[6,10,256,130]{3,2,1,0:T(8,128)(2,1)}) %all-gather.5.cloned.1.call-update) | async-done | bytes 3993616 | tf_op jit(solution)/shard_map/all_gather | solution.py:57
  540.0 3.2 fusion.27
  543.2 3.3 fusion.28
  546.5 0.8 fusion.29
  547.4 0.8 fusion.30
  548.2 0.8 fusion.31
  549.1 0.8 fusion.32
  549.9 0.8 fusion.33
  550.8 0.8 fusion.34
  551.6 0.8 fusion.35
  552.5 1.9 fusion.60
  (35 shorter events, 1.1 us)
Async XLA Ops:
  6.5 260.4 %all-gather.3.cloned.1.call-start = ((), (), s32[]{:S(2)}) async-start(), calls=%async_computation | async-start | bytes 8355840 | tf_op jit(solution)/shard_map/all_gather | solution.py:57
  78.0 9.7 %collective-permute-start = (bf16[6,1,16,128]{3,2,1,0:T(8,128)(2,1)S(1)}, bf16[6,1,16,128]{3,2,1,0:T(8,128)(2,1)S(1)}, u32[]{:S(2)}, u32[]{:S(2)}) collective-permute-start(bf16[6,1,16,128]{3,2,1,0:T(8,128)(2,1)S(1)} %get-tuple-element.12), channel_id=1, source_target_pairs={{0,16},{16,32},{32,48},{48,64},{64,80},{80,96},{96,112},{112,128},... | collective-permute-start | bytes 73736 | tf_op jit(solution)/shard_map/ppermute | solution.py:17
  85.8 8.8 %collective-permute-start.1 = (bf16[6,1,16,128]{3,2,1,0:T(8,128)(2,1)S(1)}, bf16[6,1,16,128]{3,2,1,0:T(8,128)(2,1)S(1)}, u32[]{:S(2)}, u32[]{:S(2)}) collective-permute-start(bf16[6,1,16,128]{3,2,1,0:T(8,128)(2,1)S(1)} %get-tuple-element.13), channel_id=1, source_target_pairs={{16,0},{32,16},{48,32},{64,48},{80,64},{96,80},{112,96},{128,112},... | collective-permute-start | bytes 73736 | tf_op jit(solution)/shard_map/ppermute | solution.py:18
  95.6 444.4 %all-gather.5.cloned.1.call-start = ((), (), s32[]{:S(2)}) async-start(), calls=%async_computation.1 | async-start | bytes 8355840 | tf_op jit(solution)/shard_map/all_gather | solution.py:57
  267.0 7.1 %copy-start = (bf16[6,10,256,130]{3,2,1,0:T(8,128)(2,1)S(1)}, bf16[6,10,256,130]{3,2,1,0:T(8,128)(2,1)}, u32[]{:S(2)}) copy-start(bf16[6,10,256,130]{3,2,1,0:T(8,128)(2,1)} %all-gather.3.cloned.1.call-done) | copy-start | bytes 11980804
  270.1 9.9 %copy-start.3 = (f32[4,8,3,16,130]{4,3,1,0,2:T(8,128)}, f32[4,8,3,16,130]{4,3,1,0,2:T(8,128)S(1)}, u32[]{:S(2)}) copy-start(f32[4,8,3,16,130]{4,3,1,0,2:T(8,128)S(1)} %fusion.23) | copy-start | bytes 2396164
  275.7 4.2 copy-start.2
  351.7 10.1 %collective-permute-start.2 = (bf16[6,1,16,128]{3,2,1,0:T(8,128)(2,1)S(1)}, bf16[6,1,16,128]{3,2,1,0:T(8,128)(2,1)S(1)}, u32[]{:S(2)}, u32[]{:S(2)}) collective-permute-start(bf16[6,1,16,128]{3,2,1,0:T(8,128)(2,1)S(1)} %get-tuple-element.10), channel_id=1, source_target_pairs={{0,16},{16,32},{32,48},{48,64},{64,80},{80,96},{96,112},{112,128},... | collective-permute-start | bytes 73736 | tf_op jit(solution)/shard_map/ppermute | solution.py:17
  359.5 183.6 %copy-start.4 = (bf16[16,27,256]{2,0,1:T(8,128)(2,1)S(1)}, bf16[16,27,256]{2,0,1:T(8,128)(2,1)}, u32[]{:S(2)}) copy-start(bf16[16,27,256]{2,0,1:T(8,128)(2,1)} %get-tuple-element.8) | copy-start | bytes 663556
  359.6 8.9 %collective-permute-start.3 = (bf16[6,1,16,128]{3,2,1,0:T(8,128)(2,1)S(1)}, bf16[6,1,16,128]{3,2,1,0:T(8,128)(2,1)S(1)}, u32[]{:S(2)}, u32[]{:S(2)}) collective-permute-start(bf16[6,1,16,128]{3,2,1,0:T(8,128)(2,1)S(1)} %get-tuple-element.11), channel_id=1, source_target_pairs={{16,0},{32,16},{48,32},{64,48},{80,64},{96,80},{112,96},{128,112},... | collective-permute-start | bytes 73736 | tf_op jit(solution)/shard_map/ppermute | solution.py:18
  540.0 6.5 %copy-start.5 = (bf16[6,10,256,130]{3,2,1,0:T(8,128)(2,1)S(1)}, bf16[6,10,256,130]{3,2,1,0:T(8,128)(2,1)}, u32[]{:S(2)}) copy-start(bf16[6,10,256,130]{3,2,1,0:T(8,128)(2,1)} %all-gather.5.cloned.1.call-done) | copy-start | bytes 11980804
  551.6 0.9 copy-start.1
Sparse Core Ops, SparseCore 0:
  95.7 171.1 all-gather.2
  369.6 170.2 all-gather.4
where the time goes:
time: 564 us; the launch traced here: 561 us
  waiting for transfers between devices  353 us (63%)
  blocking collectives  132 us (23%)
  matrix products  25.3 us (4%)
  starting transfers between devices  19.8 us (4%)
  between operations  13.7 us (2%)
  other arithmetic  13 us (2%)
    all_gather x2, waiting for transfers between devices, convolve(): lax.all_gather(padded, 'chan', axis=2, tiled=True)  339 us
    psum x2, blocking collectives, normalize(): lax.psum(jnp.sum(centred * centred, axis=(0, 1, 3, 4)), 'row') / number  66.3 us
    psum x2, blocking collectives, normalize(): means = lax.psum(jnp.sum(grouped, axis=(0, 1, 3, 4)), 'row') / number  65.2 us
    dot_general x18, matrix products, taps_sum(): jnp.einsum('okc,trcw->trkow', kernel, window, preferred_element_type=jnp....  25.3 us
    ppermute x2, starting transfers between devices, with_halo(): before = lax.ppermute(last, axis, up)  15.6 us
    ppermute x2, waiting for transfers between devices, with_halo(): after = lax.ppermute(first, axis, down)  13.5 us
  transfers between devices with their start and end apart: 6, of which 4 were waited for; matrix products, arithmetic and copies ran while one was open for 0% of the time, Pallas kernels for 0%

commit v1 on v0

v1 whole, which is shorter than its diff:
```python
import jax
import jax.numpy as jnp
from jax import lax
from jax.experimental import pallas as pl
from jax.experimental.pallas import tpu as pltpu
from jax.sharding import Mesh, PartitionSpec as P

CH = 256
GROUP = 8
EPS = 1e-06
BF16 = jnp.bfloat16
F32 = jnp.float32

ROW = ("xh", "y", "core")
LINE = ("xh", "y", "core", "z")
CHAN = ("z", "xl")


def dot(a, b):
    return lax.dot_general(a, b, (((1,), (0,)), ((), ())), preferred_element_type=F32)


def silu(u):
    return u / (1.0 + jnp.exp(-u))


def call(kernel, outs, *args, smem=(), scratch=(), flops=0):
    specs = [
        pl.BlockSpec(memory_space=pltpu.SMEM if i in smem else pltpu.VMEM) for i in range(len(args))
    ]
    moved = sum(a.size * a.dtype.itemsize for a in args)
    return pl.pallas_call(
        kernel,
        out_shape=outs,
        in_specs=specs,
        out_specs=jax.tree.map(lambda _: pl.BlockSpec(memory_space=pltpu.VMEM), outs),
        scratch_shapes=list(scratch),
        compiler_params=pltpu.CompilerParams(vmem_limit_bytes=40 * 1024 * 1024),
        cost_estimate=pl.CostEstimate(flops=flops, bytes_accessed=moved, transcendentals=0),
    )(*args)


def stats_kernel(x_ref, o_ref):
    x = x_ref[...].astype(F32).reshape(32, 2, GROUP, 128)
    mean = jnp.sum(x, axis=(0, 2), keepdims=True) / (32 * GROUP)
    off = x - mean
    square = jnp.sum(off * off, axis=(0, 2))
    both = jnp.concatenate([mean.reshape(2, 128), square], axis=0)
    o_ref[...] = jnp.broadcast_to(both[None], o_ref.shape)


def pack_kernel(cache_ref, up_ref, down_ref, first_ref, second_ref):
    for layer, out_ref in ((0, first_ref), (1, second_ref)):
        for z in range(8):
            for dr in range(3):
                row = z + dr - 1
                for t in range(2):
                    if row < 0:
                        slab = up_ref[4 + 2 * layer + t]
                    elif row > 7:
                        slab = down_ref[4 + 2 * layer + t]
                    else:
                        slab = cache_ref[layer, t, row]
                    lanes = slice(128 * t, 128 * (t + 1))
                    if layer == 0:
                        out_ref[2 * z, dr, :, lanes] = slab
                        out_ref[2 * z + 1, dr, :, lanes] = slab
                    else:
                        out_ref[z, dr, :, lanes] = slab


def norm_kernel(edge_ref, x_ref, up_ref, down_ref, stats_ref, affine_ref, o_ref):
    stats = stats_ref[...]
    means = stats[:, 0:2]
    mean = jnp.mean(means, axis=(0, 2), keepdims=True)
    off = means - mean
    total = jnp.sum(stats[:, 2:4] + (32 * GROUP) * (off * off), axis=(0, 2), keepdims=True)
    number = stats.shape[0] * 128 * 32 * GROUP
    inverse = lax.rsqrt(total / number + EPS)
    mean = jnp.broadcast_to(mean.reshape(2, 1, 1), (2, GROUP, 128)).reshape(16, 128)
    inverse = jnp.broadcast_to(inverse.reshape(2, 1, 1), (2, GROUP, 128)).reshape(16, 128)
    gain = affine_ref[0] * inverse
    shift = affine_ref[1]
    for row in range(-1, 9):
        for t in range(4):
            if row < 0:
                x = up_ref[t]
            elif row > 7:
                x = down_ref[t]
            else:
                x = x_ref[t, row]
            y = silu((x.astype(F32) - mean) * gain + shift)
            if row < 0:
                y = y * edge_ref[0]
            if row > 7:
                y = y * edge_ref[1]
            y = y.astype(BF16)
            for dr in range(3):
                z = row - dr + 1
                if 0 <= z < 8:
                    for xl in range(2):
                        o_ref[2 * z + xl, dr, :, 128 * t : 128 * (t + 1)] = y


def shift_columns(left, centre, right):
    lane = lax.broadcasted_iota(jnp.int32, left.shape, left.ndim - 1)
    axis = left.ndim - 1
    left = jnp.where(lane == 0, 0.0, pltpu.roll(left, 1, axis))
    right = jnp.where(lane == 127, 0.0, pltpu.roll(right, 127, axis))
    return left + centre + right


def first_kernel(x_ref, cache_ref, w_ref, mid_ref, stats_ref, affine_ref, slab_ref, prod_ref):
    for dr in range(3):
        for c in range(16):
            rows = slice(256 * dr + 16 * c, 256 * dr + 16 * c + 16)
            slab_ref[rows, 0:256] = cache_ref[c, dr]
            slab_ref[rows, 256:768] = x_ref[c, dr]
    w = w_ref[...].reshape(384, 2432)
    prod = dot(w[:, 0:768], slab_ref[:, 0:512])
    prod += dot(w[:, 768:1536], slab_ref[:, 128:640])
    prod += dot(w[:, 1536:2304], slab_ref[:, 256:768])
    prod_ref[...] = prod.reshape(8, 3, 16, 512)
    coded = w_ref[:, 0:16, 2304:2432].reshape(128, 128).astype(F32)
    bias = coded[:, 0:1] + coded[:, 1:2] + coded[:, 2:3]
    gain = coded[:, 3:4] + coded[:, 4:5] + coded[:, 5:6]
    shift = coded[:, 6:7] + coded[:, 7:8] + coded[:, 8:9]
    affine_ref[0] = jnp.broadcast_to(gain, (128, 128))
    affine_ref[1] = jnp.broadcast_to(shift, (128, 128))
    parts = []
    for t in range(4):
        lanes = slice(128 * t, 128 * (t + 1))
        summed = shift_columns(
            prod_ref[:, 0, :, lanes].reshape(128, 128),
            prod_ref[:, 1, :, lanes].reshape(128, 128),
            prod_ref[:, 2, :, lanes].reshape(128, 128),
        )
        part = (summed + bias).astype(BF16)
        mid_ref[:, lanes] = part
        parts.append(part.astype(F32))
    mean = jnp.sum(parts[0] + parts[1] + parts[2] + parts[3], axis=1, keepdims=True) / 512
    squares = jnp.zeros((128, 128), F32)
    for part in parts:
        off = part - mean
        squares += off * off
    square = jnp.sum(squares, axis=1, keepdims=True)
    same = lax.broadcasted_iota(jnp.int32, (128, 128), 0) == lax.broadcasted_iota(
        jnp.int32, (128, 128), 1
    )
    mean = jnp.sum(jnp.where(same, mean, 0.0), axis=0, keepdims=True)
    square = jnp.sum(jnp.where(same, square, 0.0), axis=0, keepdims=True)
    both = jnp.concatenate([mean, square], axis=0)
    stats_ref[...] = jnp.broadcast_to(both[None], stats_ref.shape)


def second_kernel(
    edge_ref, mid_ref, up_ref, down_ref, stats_ref, affine_ref, cache_ref, w_ref, o_ref, slab_ref, prod_ref
):
    stats = stats_ref[...]
    peers = stats.shape[0]
    means = stats[:, 0:1]
    mean = jnp.mean(means, axis=0, keepdims=True)
    off = means - mean
    square = jnp.sum(stats[:, 1:2] + 512.0 * (off * off), axis=0)
    mean = mean.reshape(1, 128)
    same = lax.broadcasted_iota(jnp.int32, (128, 128), 0) == lax.broadcasted_iota(
        jnp.int32, (128, 128), 1
    )
    mean = jnp.sum(jnp.where(same, mean, 0.0), axis=1, keepdims=True)
    square = jnp.sum(jnp.where(same, square, 0.0), axis=1, keepdims=True)
    mean = jnp.broadcast_to(mean, (128, 128)).reshape(16, GROUP, 128)
    square = jnp.broadcast_to(square, (128, 128)).reshape(16, GROUP, 128)
    group = jnp.mean(mean, axis=1, keepdims=True)
    off = mean - group
    total = jnp.sum(square + (512.0 * peers) * (off * off), axis=1, keepdims=True)
    inverse = lax.rsqrt(total / (512.0 * peers * GROUP) + EPS)
    group = jnp.broadcast_to(group, (16, GROUP, 128)).reshape(128, 128)
    inverse = jnp.broadcast_to(inverse, (16, GROUP, 128)).reshape(128, 128)
    gain = affine_ref[0] * inverse
    shift = affine_ref[1]
    for dr, ref in ((0, up_ref), (1, mid_ref), (2, down_ref)):
        for t in range(4):
            x = ref[:, 128 * t : 128 * (t + 1)].astype(F32)
            y = silu((x - group) * gain + shift)
            if dr == 0:
                y = y * edge_ref[2]
            if dr == 2:
                y = y * edge_ref[3]
            slab_ref[128 * dr : 128 * (dr + 1), 256 + 128 * t : 384 + 128 * t] = y.astype(BF16)
        for z in range(8):
            slab_ref[128 * dr + 16 * z : 128 * dr + 16 * z + 16, 0:256] = cache_ref[z, dr]
    w = w_ref[...].reshape(768, 1152)
    prod = dot(w[:, 0:384], slab_ref[:, 0:512])
    prod += dot(w[:, 384:768], slab_ref[:, 128:640])
    prod += dot(w[:, 768:1152], slab_ref[:, 256:768])
    prod_ref[...] = prod.reshape(16, 3, 16, 512)
    for t in range(4):
        lanes = slice(128 * t, 128 * (t + 1))
        summed = shift_columns(
            prod_ref[:, 0, :, lanes].reshape(256, 128),
            prod_ref[:, 1, :, lanes].reshape(256, 128),
            prod_ref[:, 2, :, lanes].reshape(256, 128),
        )
        o_ref[:, :, lanes] = summed.astype(BF16).reshape(16, 16, 128)


def last_kernel(x_ref, part_ref, bias_ref, o_ref):
    bias = bias_ref[...]
    for z in range(8):
        for t in range(4):
            lanes = slice(128 * t, 128 * (t + 1))
            branch = part_ref[2 * z, :, lanes].astype(F32) + part_ref[2 * z + 1, :, lanes].astype(F32)
            o_ref[t, z] = (x_ref[t, z].astype(F32) + (branch + bias)).astype(BF16)


def split(value):
    high = lax.reduce_precision(value, 8, 7)
    rest = value - high
    middle = lax.reduce_precision(rest, 8, 7)
    return [part.astype(BF16) for part in (high, middle, rest - middle)]


def first_weights(weight, bias, gain, shift):
    weight = weight.reshape(16, 9, 3, CH).transpose(2, 0, 1, 3).reshape(48, 9 * CH)
    coded = jnp.stack(split(bias) + split(gain) + split(shift), axis=1)
    coded = jnp.pad(coded, ((0, 32), (0, 119)))
    return lax.all_gather(jnp.concatenate([weight, coded], axis=1), "z")


def second_weights(weight):
    me = lax.axis_index("xl")
    weight = weight.reshape(16, 9, 3, 8, 2, 16).transpose(4, 2, 0, 1, 3, 5).reshape(2, 48, 1152)
    mine = jnp.where(me == 0, weight[0], weight[1])
    other = jnp.where(me == 0, weight[1], weight[0])
    other = lax.ppermute(other, "xl", [(0, 1), (1, 0)])
    first = jnp.where(me == 0, mine, other)
    second = jnp.where(me == 0, other, mine)
    return lax.all_gather(jnp.concatenate([first, second], axis=0), "z")


def both_ways(x_up, x_down, axes):
    size = 1
    for axis in axes:
        size *= lax.axis_size(axis)
    up = [(i, i + 1) for i in range(size - 1)]
    down = [(i + 1, i) for i in range(size - 1)]
    return lax.ppermute(x_up, axes, up), lax.ppermute(x_down, axes, down)


def exchange(x, axes):
    return lax.all_to_all(x, axes, 0, 0, tiled=True)


def struct(shape, dtype=BF16):
    return jax.ShapeDtypeStruct(shape, dtype)


def local(frames, cache, norm_gain, norm_shift, conv_weight, conv_bias):
    row = lax.axis_index(ROW)
    line = lax.axis_index(LINE)
    edge = jnp.stack([row > 0, row < 15, line > 0, line < 127]).astype(F32)

    stats = call(stats_kernel, struct((16, 4, 128), F32), frames)
    stats = exchange(stats, ROW)

    joined = [frames, cache[0], cache[1]]
    last = jnp.concatenate([x[:, 7] for x in joined], axis=0)
    first = jnp.concatenate([x[:, 0] for x in joined], axis=0)
    above, below = both_ways(last, first, ROW)

    w0 = first_weights(conv_weight[0], conv_bias[0], norm_gain[1], norm_shift[1])
    w1 = second_weights(conv_weight[1])

    c0, c1 = call(
        pack_kernel, (struct((16, 3, 16, 256)), struct((8, 3, 16, 256))), cache, above, below
    )
    c0 = exchange(c0, CHAN)
    c1 = exchange(c1, "z")

    affine = jnp.broadcast_to(jnp.stack([norm_gain[0], norm_shift[0]])[:, :, None], (2, 16, 128))
    normed = call(
        norm_kernel, struct((16, 3, 16, 512)), edge, frames, above, below, stats, affine, smem=(0,)
    )
    normed = exchange(normed, CHAN)

    middle, stats, affine = call(
        first_kernel,
        (struct((128, 512)), struct((128, 2, 128), F32), struct((2, 128, 128), F32)),
        normed,
        c0,
        w0,
        scratch=(pltpu.VMEM((768, 768), BF16), pltpu.VMEM((8, 3, 16, 512), F32)),
        flops=2 * 384 * 2304 * 512,
    )
    stats = exchange(stats, LINE)
    above, below = both_ways(middle, middle, LINE)

    partial = call(
        second_kernel,
        struct((16, 16, 512)),
        edge,
        middle,
        above,
        below,
        stats,
        affine,
        c1,
        w1,
        smem=(0,),
        scratch=(pltpu.VMEM((384, 768), BF16), pltpu.VMEM((16, 3, 16, 512), F32)),
        flops=2 * 768 * 1152 * 512,
    )
    partial = exchange(partial, CHAN)
    bias = jnp.broadcast_to(conv_bias[1][:, None], (16, 128))
    return call(last_kernel, struct((4, 8, 16, 128)), frames, partial, bias)


def solution(mesh):
    fine = Mesh(mesh.devices.reshape(2, 4, 2, 8, 2), ("xh", "y", "core", "z", "xl"))
    placed = (
        P(None, ROW, CHAN, None),
        P(None, None, ROW, CHAN, None),
        P(None, CHAN),
        P(None, CHAN),
        P(None, CHAN, None, None),
        P(None, CHAN),
    )
    return jax.shard_map(
        local, mesh=fine, in_specs=placed, out_specs=P(None, ROW, CHAN, None), check_vma=False
    )
```

time: 564 us -> 167 us (0.30)
  waiting for transfers between devices: 353 us -> 34.8 us
  blocking collectives: 132 us -> 32.1 us
  starting transfers between devices: 19.8 us -> 57.7 us
  matrix products: 25.3 us -> 0 us
  Pallas kernels: 0 us -> 8.62 us
  local copies, waits for them, and re-layouts: 5.22 us -> 11.4 us
  other arithmetic: 13 us -> 7.12 us
    all_gather x2, waiting for transfers between devices: 339 us -> 0.03 us  [the longest x1 0.02 us: second_weights(): return lax.all_gather(jnp.concatenate([first, second], axis=0), 'z')]
    psum x4 -> x0, blocking collectives: 132 us -> none  [the longest x2 66.3 us: normalize(): lax.psum(jnp.sum(centred * centred, axis=(0, 1, 3, 4)), 'row') / number]
    all_to_all x0 -> x5, starting transfers between devices: none -> 43.8 us  [exchange(): return lax.all_to_all(x, axes, 0, 0, tiled=True)]
    all_to_all x0 -> x1, blocking collectives: none -> 32.1 us  [exchange(): return lax.all_to_all(x, axes, 0, 0, tiled=True)]
    all_to_all x0 -> x5, waiting for transfers between devices: none -> 31.4 us  [exchange(): return lax.all_to_all(x, axes, 0, 0, tiled=True)]
    dot_general x18 -> x0, matrix products: 25.3 us -> none  [taps_sum(): jnp.einsum('okc,trcw->trkow', kernel, window, preferred_element_type=jnp....]
    ppermute x4 -> x5, waiting for transfers between devices: 13.5 us -> 3.37 us  [the longest x4 2.61 us: both_ways(): return (lax.ppermute(x_up, axes, up), lax.ppermute(x_down, axes, down))]
    pallas_call x0 -> x6, Pallas kernels: none -> 8.62 us  [call(): pl.pallas_call(kernel, out_shape=outs, in_specs=specs, out_specs=jax.tree...]
  transfers between devices with their start and end apart: 6 -> 12, of which waited for: 4 -> 8; matrix products, arithmetic and copies ran while one was open for 0% -> 7% of each run, Pallas kernels for 0% -> 3%
where the time goes in v1:
time: 167 us; the launch traced here: 165 us
  starting transfers between devices  57.7 us (35%)
  waiting for transfers between devices  34.8 us (21%)
  blocking collectives  32.1 us (19%)
  between operations  13.6 us (8%)
  local copies, waits for them, and re-layouts  11.4 us (7%)
  Pallas kernels  8.62 us (5%)
  other arithmetic  7.12 us (4%)
    all_to_all x5, starting transfers between devices, exchange(): return lax.all_to_all(x, axes, 0, 0, tiled=True)  43.8 us
    all_to_all x1, blocking collectives, exchange(): return lax.all_to_all(x, axes, 0, 0, tiled=True)  32.1 us
    all_to_all x5, waiting for transfers between devices, exchange(): return lax.all_to_all(x, axes, 0, 0, tiled=True)  31.4 us
    ppermute x4, starting transfers between devices, both_ways(): return (lax.ppermute(x_up, axes, up), lax.ppermute(x_down, axes, down))  13.5 us
    pallas_call x6, Pallas kernels, call(): pl.pallas_call(kernel, out_shape=outs, in_specs=specs, out_specs=jax.tree...  8.62 us
    select_n x1, other arithmetic, second_weights(): mine = jnp.where(me == 0, weight[0], weight[1])  4.17 us
  transfers between devices with their start and end apart: 12, of which 8 were waited for; matrix products, arithmetic and copies ran while one was open for 7% of the time, Pallas kernels for 3%

profile of v1, /device:TPU:27, one launch (start us, length us, event | category | flops | bytes accessed | tf_op | source)
XLA Modules:
  0.0 165.4 jit_solution(14673526435554184645)
XLA Ops:
  6.5 0.7 fusion.4
  7.2 0.7 fusion.2
  7.9 0.1 stack.36
  8.0 0.1 copy.40
  8.1 1.1 fusion.5
  9.2 0.1 copy.32
  9.3 0.1 copy.41
  9.3 0.7 fusion.1
  10.0 0.0 all-gather.5.cloned.1.call-update
  10.1 0.0 all-gather.7.cloned.1.call-start
  10.1 1.2 reshape_squeeze.7
  11.3 4.2 %broadcast_select_fusion.1 = (bf16[1,3,16,9,8,16]{5,0,4,2,1,3:T(2,128)(2,1)S(1)}, bf16[1,3,16,9,8,16]{5,0,4,2,1,3:T(2,128)(2,1)S(1)}) fusion(pred[]{:T(512)S(6)} %eq.2, bf16[2,3,16,9,8,16]{5,0,4,2,1,3:T(2,128)(2,1)S(1)} %bitcast.65), kind=kLoop, calls=%fused_computation.1 | loop fusion | flops 110592 | bytes 442369 | tf_op jit(solution)/shard_map/jit(_where)/select_n | solution.py:233
  15.5 1.0 copy.35
  16.5 1.8 %select_n.33 = bf16[48,1152]{1,0:T(8,128)(2,1)S(1)} reshape(bf16[1,3,16,9,8,16]{5,4,3,2,1,0:T(8,128)(2,1)} %copy.35) | data formatting | bytes 221184 | tf_op jit(solution)/shard_map/jit(_where)/select_n | solution.py:234
  18.3 0.3 collective-permute-start.4
  18.7 1.0 copy.34
  19.8 1.8 %select_n.31 = bf16[48,1152]{1,0:T(8,128)(2,1)S(1)} reshape(bf16[1,3,16,9,8,16]{5,4,3,2,1,0:T(8,128)(2,1)} %copy.34) | data formatting | bytes 221184 | tf_op jit(solution)/shard_map/jit(_where)/select_n | solution.py:233
  21.6 0.8 collective-permute-done.4
  22.4 0.7 pad_maximum_fusion
  23.1 4.8 %collective-permute-start = (bf16[8,16,128]{2,1,0:T(8,128)(2,1)S(1)}, bf16[8,16,128]{2,1,0:T(8,128)(2,1)S(1)}, u32[]{:S(2)}, u32[]{:S(2)}) collective-permute-start(bf16[8,16,128]{2,1,0:T(8,128)(2,1)S(1)} %pad_maximum_fusion.1), channel_id=1, source_target_pairs={{0,16},{16,32},{32,48},{48,64},{64,80},{80,96},{96,112},{112,128},... | collective-permute-start | bytes 98312 | tf_op jit(solution)/shard_map/ppermute | solution.py:247
  28.0 1.9 %collective-permute-start.1 = (bf16[8,16,128]{2,1,0:T(8,128)(2,1)S(1)}, bf16[8,16,128]{2,1,0:T(8,128)(2,1)S(1)}, u32[]{:S(2)}, u32[]{:S(2)}) collective-permute-start(bf16[8,16,128]{2,1,0:T(8,128)(2,1)S(1)} %pad_maximum_fusion.2), channel_id=1, source_target_pairs={{16,0},{32,16},{48,32},{64,48},{80,64},{96,80},{112,96},{128,112},... | collective-permute-start | bytes 98312 | tf_op jit(solution)/shard_map/ppermute | solution.py:247
  29.9 0.7 shard_map.64
  30.6 7.2 %all-to-all-start = ((f32[16,4,128]{2,1,0:T(4,128)}), f32[16,4,128]{2,1,0:T(4,128)S(1)}, u32[]{:S(2)}, u32[]{:S(2)}) async-start(f32[16,4,128]{2,1,0:T(4,128)} %shard_map.64), calls=%async_computation | async-start | bytes 65536 | tf_op jit(solution)/shard_map/all_to_all | solution.py:251
  37.9 0.9 shard_map.66
  38.8 4.7 %all-to-all-done.stats_ref = f32[16,4,128]{2,1,0:T(4,128)S(1)} async-done(((f32[16,4,128]{2,1,0:T(4,128)}), f32[16,4,128]{2,1,0:T(4,128)S(1)}, u32[]{:S(2)}, u32[]{:S(2)}) %all-to-all-start) | async-done | bytes 32800 | tf_op jit(solution)/shard_map/all_to_all | solution.py:251
  43.5 9.4 %all-to-all-start.2 = ((bf16[16,3,16,256]{3,2,1,0:T(8,128)(2,1)}), bf16[16,3,16,256]{3,2,1,0:T(8,128)(2,1)S(1)}, u32[]{:S(2)}, u32[]{:S(2)}) async-start(bf16[16,3,16,256]{3,2,1,0:T(8,128)(2,1)} %get-tuple-element.10), calls=%async_computation.2 | async-start | bytes 786432 | tf_op jit(solution)/shard_map/all_to_all | solution.py:251
  52.9 0.1 add_convert_fusion.edge_ref
  53.0 0.1 broadcast_in_dim.6.affine_ref
  53.1 0.9 shard_map.65
  54.0 11.1 %all-to-all-done.2.cache_ref = bf16[16,3,16,256]{3,2,1,0:T(8,128)(2,1)S(1)} async-done(((bf16[16,3,16,256]{3,2,1,0:T(8,128)(2,1)}), bf16[16,3,16,256]{3,2,1,0:T(8,128)(2,1)S(1)}, u32[]{:S(2)}, u32[]{:S(2)}) %all-to-all-start.2) | async-done | bytes 393248 | tf_op jit(solution)/shard_map/all_to_all | solution.py:251
  65.1 32.1 %all_to_all.30.x_ref = bf16[16,3,16,512]{3,2,1,0:T(8,128)(2,1)S(1)} all-to-all(bf16[16,3,16,512]{3,2,1,0:T(8,128)(2,1)S(1)} %shard_map.65), channel_id=1, replica_groups=mesh['xh'=2,'y'=4,'core'=2,'z'=8,'xl'=2] {'z','xl'}, dimensions={0} | all-to-all | bytes 1572864 | tf_op jit(solution)/shard_map/all_to_all | solution.py:251
  97.1 5.6 %all-to-all-start.4 = ((bf16[8,3,16,256]{3,2,1,0:T(8,128)(2,1)}), bf16[8,3,16,256]{3,2,1,0:T(8,128)(2,1)S(1)}, u32[]{:S(2)}, u32[]{:S(2)}) async-start(bf16[8,3,16,256]{3,2,1,0:T(8,128)(2,1)} %get-tuple-element.14), calls=%async_computation.4 | async-start | bytes 393216 | tf_op jit(solution)/shard_map/all_to_all | solution.py:251
  102.8 1.5 copy-done.2
  104.3 2.1 %shard_map.67 = (bf16[128,512]{1,0:T(8,128)(2,1)S(1)}, f32[128,2,128]{2,1,0:T(2,128)}, f32[2,128,128]{2,1,0:T(8,128)S(1)}) custom-call(bf16[16,3,16,512]{3,2,1,0:T(8,128)(2,1)S(1)} %all_to_all.30.x_ref, bf16[16,3,16,256]{3,2,1,0:T(8,128)(2,1)S(1)} %all-to-all-done.2.cache_ref, bf16[8,48,2432]{2,1,0:T(8,128)(2,1)S(1)} %bitcast.63), custom_call_target="tpu_custom_call" | custom-call | flops 905969664 | bytes 3047424 | tf_op jit(solution)/shard_map/pallas_call | solution.py:32
  106.3 4.7 %all-to-all-done.4.cache_ref = bf16[8,3,16,256]{3,2,1,0:T(8,128)(2,1)S(1)} async-done(((bf16[8,3,16,256]{3,2,1,0:T(8,128)(2,1)}), bf16[8,3,16,256]{3,2,1,0:T(8,128)(2,1)S(1)}, u32[]{:S(2)}, u32[]{:S(2)}) %all-to-all-start.4) | async-done | bytes 196640 | tf_op jit(solution)/shard_map/all_to_all | solution.py:251
  111.0 10.6 %all-to-all-start.3 = ((f32[128,2,128]{2,1,0:T(2,128)}), f32[128,2,128]{2,1,0:T(2,128)S(1)}, u32[]{:S(2)}, u32[]{:S(2)}) async-start(f32[128,2,128]{2,1,0:T(2,128)} %get-tuple-element.12), calls=%async_computation.3 | async-start | bytes 262144 | tf_op jit(solution)/shard_map/all_to_all | solution.py:251
  121.7 3.1 %collective-permute-start.2 = (bf16[128,512]{1,0:T(8,128)(2,1)S(1)}, bf16[128,512]{1,0:T(8,128)(2,1)S(1)}, u32[]{:S(2)}, u32[]{:S(2)}) collective-permute-start(bf16[128,512]{1,0:T(8,128)(2,1)S(1)} %get-tuple-element.11.mid_ref), channel_id=1, source_target_pairs={{0,2},{2,4},{4,6},{6,8},{8,10},{10,12},{12,14},{14,16},{16,18},{18... | collective-permute-start | bytes 393224 | tf_op jit(solution)/shard_map/ppermute | solution.py:247
  124.8 3.7 %collective-permute-start.3 = (bf16[128,512]{1,0:T(8,128)(2,1)S(1)}, bf16[128,512]{1,0:T(8,128)(2,1)S(1)}, u32[]{:S(2)}, u32[]{:S(2)}) collective-permute-start(bf16[128,512]{1,0:T(8,128)(2,1)S(1)} %get-tuple-element.11.mid_ref), channel_id=1, source_target_pairs={{2,0},{4,2},{6,4},{8,6},{10,8},{12,10},{14,12},{16,14},{18,16},{20... | collective-permute-start | bytes 393224 | tf_op jit(solution)/shard_map/ppermute | solution.py:247
  128.5 0.0 all-gather.7.cloned.1.call-done
  128.5 1.2 collective-permute-done.2.up_ref
  129.7 1.4 collective-permute-done.3.down_ref
  131.1 1.4 all-to-all-done.3.stats_ref
  132.5 1.5 copy-done.3
  134.0 3.4 %shard_map.68 = bf16[16,16,512]{2,1,0:T(8,128)(2,1)} custom-call(f32[4]{0:T(128)S(1)} %add_convert_fusion.edge_ref, bf16[128,512]{1,0:T(8,128)(2,1)S(1)} %get-tuple-element.11.mid_ref, bf16[128,512]{1,0:T(8,128)(2,1)S(1)} %collective-permute-done.2.up_ref, bf16[128,512]{1,0:T(8,128)(2,1)S(1)} %collective-permute-done.3.down_ref, ...), custom_call_target="tpu_custom_call" | custom-call | flops 905969664 | bytes 2621456 | tf_op jit(solution)/shard_map/pallas_call | solution.py:32
  137.4 11.0 %all-to-all-start.5 = ((bf16[16,16,512]{2,1,0:T(8,128)(2,1)}), bf16[16,16,512]{2,1,0:T(8,128)(2,1)S(1)}, u32[]{:S(2)}, u32[]{:S(2)}) async-start(bf16[16,16,512]{2,1,0:T(8,128)(2,1)} %shard_map.68), calls=%async_computation.5 | async-start | bytes 524288 | tf_op jit(solution)/shard_map/all_to_all | solution.py:251
  148.3 9.4 %all-to-all-done.5.part_ref = bf16[16,16,512]{2,1,0:T(8,128)(2,1)S(1)} async-done(((bf16[16,16,512]{2,1,0:T(8,128)(2,1)}), bf16[16,16,512]{2,1,0:T(8,128)(2,1)S(1)}, u32[]{:S(2)}, u32[]{:S(2)}) %all-to-all-start.5) | async-done | bytes 262176 | tf_op jit(solution)/shard_map/all_to_all | solution.py:251
  157.8 0.1 broadcast_in_dim.15.bias_ref
  157.8 0.7 shard_map.69
  (27 shorter events, 0.1 us)
Async XLA Ops:
  6.5 96.2 %all-gather.5.cloned.1.call-start = ((), (), s32[]{:S(2)}) async-start(), calls=%async_computation.6 | async-start | bytes 2101248 | tf_op jit(solution)/shard_map/all_gather | solution.py:227
  10.1 118.4 %all-gather.7.cloned.1.call-start = ((), (), s32[]{:S(2)}) async-start(), calls=%async_computation.7 | async-start | bytes 1990656 | tf_op jit(solution)/shard_map/all_gather | solution.py:238
  15.5 3.2 %copy-start = (bf16[4,8,16,128]{3,2,1,0:T(8,128)(2,1)S(1)}, bf16[4,8,16,128]{3,2,1,0:T(8,128)(2,1)}, u32[]{:S(2)}) copy-start(bf16[4,8,16,128]{3,2,1,0:T(8,128)(2,1)} %x_ref.5) | copy-start | bytes 393220
  15.5 3.2 %copy-start.1 = (bf16[2,2,8,16,128]{4,3,2,1,0:T(8,128)(2,1)S(1)}, bf16[2,2,8,16,128]{4,3,2,1,0:T(8,128)(2,1)}, u32[]{:S(2)}) copy-start(bf16[2,2,8,16,128]{4,3,2,1,0:T(8,128)(2,1)} %cache_ref.1) | copy-start | bytes 393220
  18.3 4.0 %collective-permute-start.4 = (bf16[48,1152]{1,0:T(8,128)(2,1)S(1)}, bf16[48,1152]{1,0:T(8,128)(2,1)S(1)}, u32[]{:S(2)}, u32[]{:S(2)}) collective-permute-start(bf16[48,1152]{1,0:T(8,128)(2,1)S(1)} %select_n.33), channel_id=1, source_target_pairs={{0,1},{1,0},{2,3},{3,2},{4,5},{5,4},{6,7},{7,6},{8,9},{9,8},{10,11... | collective-permute-start | bytes 331784 | tf_op jit(solution)/shard_map/ppermute | solution.py:235
  19.7 33.2 %slice-start = ((f32[2,16]{1,0:T(2,128)}), f32[1,16]{1,0:T(1,128)S(1)}, s32[]{:S(2)}) async-start(f32[2,16]{1,0:T(2,128)} %param.9), calls=%async_computation.8 | async-start | bytes 1024 | tf_op jit(solution)/shard_map/slice | solution.py:280
  19.8 33.2 %slice-start.1 = ((f32[2,16]{1,0:T(2,128)}), f32[1,16]{1,0:T(1,128)S(1)}, s32[]{:S(2)}) async-start(f32[2,16]{1,0:T(2,128)} %param.8), calls=%async_computation.9 | async-start | bytes 1024 | tf_op jit(solution)/shard_map/slice | solution.py:280
  23.1 14.7 %collective-permute-start = (bf16[8,16,128]{2,1,0:T(8,128)(2,1)S(1)}, bf16[8,16,128]{2,1,0:T(8,128)(2,1)S(1)}, u32[]{:S(2)}, u32[]{:S(2)}) collective-permute-start(bf16[8,16,128]{2,1,0:T(8,128)(2,1)S(1)} %pad_maximum_fusion.1), channel_id=1, source_target_pairs={{0,16},{16,32},{32,48},{48,64},{64,80},{80,96},{96,112},{112,128},... | collective-permute-start | bytes 98312 | tf_op jit(solution)/shard_map/ppermute | solution.py:247
  28.0 9.9 %collective-permute-start.1 = (bf16[8,16,128]{2,1,0:T(8,128)(2,1)S(1)}, bf16[8,16,128]{2,1,0:T(8,128)(2,1)S(1)}, u32[]{:S(2)}, u32[]{:S(2)}) collective-permute-start(bf16[8,16,128]{2,1,0:T(8,128)(2,1)S(1)} %pad_maximum_fusion.2), channel_id=1, source_target_pairs={{16,0},{32,16},{48,32},{64,48},{80,64},{96,80},{112,96},{128,112},... | collective-permute-start | bytes 98312 | tf_op jit(solution)/shard_map/ppermute | solution.py:247
  30.6 12.9 %all-to-all-start = ((f32[16,4,128]{2,1,0:T(4,128)}), f32[16,4,128]{2,1,0:T(4,128)S(1)}, u32[]{:S(2)}, u32[]{:S(2)}) async-start(f32[16,4,128]{2,1,0:T(4,128)} %shard_map.64), calls=%async_computation | async-start | bytes 65536 | tf_op jit(solution)/shard_map/all_to_all | solution.py:251
  43.5 21.5 %all-to-all-start.2 = ((bf16[16,3,16,256]{3,2,1,0:T(8,128)(2,1)}), bf16[16,3,16,256]{3,2,1,0:T(8,128)(2,1)S(1)}, u32[]{:S(2)}, u32[]{:S(2)}) async-start(bf16[16,3,16,256]{3,2,1,0:T(8,128)(2,1)} %get-tuple-element.10), calls=%async_computation.2 | async-start | bytes 786432 | tf_op jit(solution)/shard_map/all_to_all | solution.py:251
  97.1 13.9 %all-to-all-start.4 = ((bf16[8,3,16,256]{3,2,1,0:T(8,128)(2,1)}), bf16[8,3,16,256]{3,2,1,0:T(8,128)(2,1)S(1)}, u32[]{:S(2)}, u32[]{:S(2)}) async-start(bf16[8,3,16,256]{3,2,1,0:T(8,128)(2,1)} %get-tuple-element.14), calls=%async_computation.4 | async-start | bytes 393216 | tf_op jit(solution)/shard_map/all_to_all | solution.py:251
  102.7 1.5 copy-start.2
  111.0 21.5 %all-to-all-start.3 = ((f32[128,2,128]{2,1,0:T(2,128)}), f32[128,2,128]{2,1,0:T(2,128)S(1)}, u32[]{:S(2)}, u32[]{:S(2)}) async-start(f32[128,2,128]{2,1,0:T(2,128)} %get-tuple-element.12), calls=%async_computation.3 | async-start | bytes 262144 | tf_op jit(solution)/shard_map/all_to_all | solution.py:251
  121.7 8.1 %collective-permute-start.2 = (bf16[128,512]{1,0:T(8,128)(2,1)S(1)}, bf16[128,512]{1,0:T(8,128)(2,1)S(1)}, u32[]{:S(2)}, u32[]{:S(2)}) collective-permute-start(bf16[128,512]{1,0:T(8,128)(2,1)S(1)} %get-tuple-element.11.mid_ref), channel_id=1, source_target_pairs={{0,2},{2,4},{4,6},{6,8},{8,10},{10,12},{12,14},{14,16},{16,18},{18... | collective-permute-start | bytes 393224 | tf_op jit(solution)/shard_map/ppermute | solution.py:247
  124.8 6.3 %collective-permute-start.3 = (bf16[128,512]{1,0:T(8,128)(2,1)S(1)}, bf16[128,512]{1,0:T(8,128)(2,1)S(1)}, u32[]{:S(2)}, u32[]{:S(2)}) collective-permute-start(bf16[128,512]{1,0:T(8,128)(2,1)S(1)} %get-tuple-element.11.mid_ref), channel_id=1, source_target_pairs={{2,0},{4,2},{6,4},{8,6},{10,8},{12,10},{14,12},{16,14},{18,16},{20... | collective-permute-start | bytes 393224 | tf_op jit(solution)/shard_map/ppermute | solution.py:247
  132.5 1.5 copy-start.3
  134.0 14.3 %copy-start.4 = (f32[2,16]{1,0:T(2,128)S(1)}, f32[2,16]{1,0:T(2,128)}, u32[]{:S(2)}) copy-start(f32[2,16]{1,0:T(2,128)} %param.11) | copy-start | bytes 388
  137.4 20.4 %all-to-all-start.5 = ((bf16[16,16,512]{2,1,0:T(8,128)(2,1)}), bf16[16,16,512]{2,1,0:T(8,128)(2,1)S(1)}, u32[]{:S(2)}, u32[]{:S(2)}) async-start(bf16[16,16,512]{2,1,0:T(8,128)(2,1)} %shard_map.68), calls=%async_computation.5 | async-start | bytes 524288 | tf_op jit(solution)/shard_map/all_to_all | solution.py:251
Sparse Core Ops, SparseCore 0:
  10.2 39.6 all-gather.4
  51.6 53.2 all-gather.6

commit v2 on v0

v2 whole, which is shorter than its diff:
```python
import jax
import jax.numpy as jnp
from jax import lax
from jax.experimental import pallas as pl
from jax.experimental.pallas import tpu as pltpu
from jax.sharding import Mesh, PartitionSpec as P

GROUP = 8
EPS = 1e-06
BF16 = jnp.bfloat16
F32 = jnp.float32

ROW = ("xh", "y", "core")
CHAN = ("zh", "zl", "xl")
NEAR = ("zl", "xl")


def dot(a, b):
    return lax.dot_general(a, b, (((1,), (0,)), ((), ())), preferred_element_type=F32)


def silu(u):
    return u / (1.0 + jnp.exp(-u))


def call(kernel, outs, *args, smem=(), scratch=(), flops=0):
    specs = [
        pl.BlockSpec(memory_space=pltpu.SMEM if i in smem else pltpu.VMEM) for i in range(len(args))
    ]
    moved = sum(a.size * a.dtype.itemsize for a in args)
    return pl.pallas_call(
        kernel,
        out_shape=outs,
        in_specs=specs,
        out_specs=jax.tree.map(lambda _: pl.BlockSpec(memory_space=pltpu.VMEM), outs),
        scratch_shapes=list(scratch),
        compiler_params=pltpu.CompilerParams(vmem_limit_bytes=40 * 1024 * 1024),
        cost_estimate=pl.CostEstimate(flops=flops, bytes_accessed=moved, transcendentals=0),
    )(*args)


def put_stats(x, gain_ref, shift_ref, layer, note_ref, stats_ref):
    number = x.shape[0] * GROUP
    mean = jnp.sum(x, axis=(0, 2), keepdims=True) / number
    off = x - mean
    square = jnp.sum(off * off, axis=(0, 2))
    note_ref[...] = jnp.zeros((8, 128), F32)
    note_ref[0:2] = mean.reshape(2, 128)
    note_ref[2:4] = square
    note_ref[4:5, 0:16] = gain_ref[layer : layer + 1, :]
    note_ref[5:6, 0:16] = shift_ref[layer : layer + 1, :]
    stats_ref[...] = jnp.broadcast_to(note_ref[...][None], stats_ref.shape)


def begin_kernel(x_ref, cache_ref, gain_ref, shift_ref, raw_ref, later_ref, stats_ref, note_ref):
    for r in range(8):
        for t in range(2):
            lanes = slice(128 * t, 128 * (t + 1))
            raw_ref[r, :, lanes] = cache_ref[0, t, r]
            later_ref[r, :, lanes] = cache_ref[1, t, r]
        for t in range(4):
            raw_ref[r, :, 256 + 128 * t : 384 + 128 * t] = x_ref[t, r]
    x = x_ref[...].astype(F32).reshape(32, 2, GROUP, 128)
    put_stats(x, gain_ref, shift_ref, 0, note_ref, stats_ref)


def shift_columns(left, centre, right):
    lane = lax.broadcasted_iota(jnp.int32, left.shape, left.ndim - 1)
    axis = left.ndim - 1
    left = jnp.where(lane == 0, 0.0, pltpu.roll(left, 1, axis))
    right = jnp.where(lane == 127, 0.0, pltpu.roll(right, 127, axis))
    return left + centre + right


def get_affine(stats_ref, affine_ref):
    stats = stats_ref[...].reshape(16, 4, 8, 128)
    number = 32 * GROUP
    means = stats[:, :, 0:2]
    mean = jnp.mean(means, axis=(0, 3), keepdims=True)
    off = means - mean
    total = jnp.sum(stats[:, :, 2:4] + number * (off * off), axis=(0, 3), keepdims=True)
    inverse = lax.rsqrt(total / (number * 16 * 128) + EPS)
    mean = jnp.broadcast_to(mean.reshape(4, 2, 1, 1), (4, 2, GROUP, 128)).reshape(4, 16, 128)
    inverse = jnp.broadcast_to(inverse.reshape(4, 2, 1, 1), (4, 2, GROUP, 128)).reshape(4, 16, 128)
    shape = (4, 16, 128)
    same = lax.broadcasted_iota(jnp.int32, shape, 1) == lax.broadcasted_iota(jnp.int32, shape, 2)
    gain = jnp.sum(jnp.where(same, stats[0, :, 4:5], 0.0), axis=2, keepdims=True)
    shift = jnp.sum(jnp.where(same, stats[0, :, 5:6], 0.0), axis=2, keepdims=True)
    affine_ref[0] = mean
    affine_ref[1] = inverse * gain
    affine_ref[2] = jnp.broadcast_to(shift, shape)


def convolve(layer, place_ref, w_refs, o_ref, slab_ref, held_ref):
    for q, w_ref in enumerate(w_refs):
        for dt in range(3):
            held_ref[dt, q] = w_ref[layer, dt]
    for r in range(8):
        rows = slab_ref[r : r + 3].reshape(192, 768)
        prod = dot(held_ref[0].reshape(192, 192), rows[:, 0:512])
        prod += dot(held_ref[1].reshape(192, 192), rows[:, 128:640])
        prod += dot(held_ref[2].reshape(192, 192), rows[:, 256:768])
        prod = prod.reshape(4, 3, 16, 512)
        for t in range(4):
            lanes = slice(128 * t, 128 * (t + 1))
            part = prod[:, :, :, lanes]
            summed = shift_columns(part[:, 0], part[:, 1], part[:, 2]).astype(BF16)
            for q in range(4):
                o_ref[lax.rem(place_ref[1] + (4 - q), 4), r, :, lanes] = summed[q]


def norm_rows(x_of, place_ref, edge_ref, affine_ref, slab_ref):
    for k in range(4):
        b = place_ref[2 + k]
        mean = affine_ref[0, b]
        gain = affine_ref[1, b]
        shift = affine_ref[2, b]
        for r in range(10):
            for t in range(4):
                y = silu((x_of(k, r, t).astype(F32) - mean) * gain + shift)
                if r == 0:
                    y = y * edge_ref[0]
                if r == 9:
                    y = y * edge_ref[1]
                slab_ref[r, b, :, 256 + 128 * t : 384 + 128 * t] = y.astype(BF16)


def first_kernel(
    place_ref, edge_ref, a_ref, b_ref, c_ref, d_ref, stats_ref, w0, w1, w2, w3, o_ref, affine_ref, slab_ref, held_ref
):
    get_affine(stats_ref, affine_ref)
    refs = (a_ref, b_ref, c_ref, d_ref)
    for k in range(4):
        b = place_ref[2 + k]
        for r in range(10):
            slab_ref[r, b, :, 0:256] = refs[k][r, :, 0:256]

    def x_of(k, r, t):
        return refs[k][r, :, 256 + 128 * t : 384 + 128 * t]

    norm_rows(x_of, place_ref, edge_ref, affine_ref, slab_ref)
    convolve(0, place_ref, (w0, w1, w2, w3), o_ref, slab_ref, held_ref)


def second_kernel(
    place_ref, edge_ref, a_ref, b_ref, c_ref, d_ref, ca_ref, cb_ref, cc_ref, cd_ref,
    stats_ref, w0, w1, w2, w3, o_ref, affine_ref, slab_ref, held_ref,
):
    get_affine(stats_ref, affine_ref)
    refs = (a_ref, b_ref, c_ref, d_ref)
    caches = (ca_ref, cb_ref, cc_ref, cd_ref)
    for k in range(4):
        b = place_ref[2 + k]
        for r in range(10):
            slab_ref[r, b, :, 0:256] = caches[k][r]

    def x_of(k, r, t):
        return refs[k][r, :, 128 * t : 128 * (t + 1)]

    norm_rows(x_of, place_ref, edge_ref, affine_ref, slab_ref)
    convolve(1, place_ref, (w0, w1, w2, w3), o_ref, slab_ref, held_ref)


def merge_kernel(part_ref, bias_ref, gain_ref, shift_ref, mid_ref, stats_ref, note_ref):
    bias = jnp.concatenate([bias_ref[...]] * 4, axis=1)
    for r in range(8):
        summed = part_ref[0, r].astype(F32) + part_ref[1, r].astype(F32)
        summed += part_ref[2, r].astype(F32) + part_ref[3, r].astype(F32)
        mid_ref[r] = (summed + bias).astype(BF16)
    slabs = [mid_ref[:, :, 128 * t : 128 * (t + 1)].astype(F32) for t in range(4)]
    x = jnp.concatenate(slabs, axis=0).reshape(32, 2, GROUP, 128)
    put_stats(x, gain_ref, shift_ref, 1, note_ref, stats_ref)


def last_kernel(x_ref, part_ref, bias_ref, o_ref):
    bias = bias_ref[...]
    for r in range(8):
        for t in range(4):
            lanes = slice(128 * t, 128 * (t + 1))
            branch = part_ref[0, r, :, lanes].astype(F32) + part_ref[1, r, :, lanes].astype(F32)
            branch += part_ref[2, r, :, lanes].astype(F32) + part_ref[3, r, :, lanes].astype(F32)
            o_ref[t, r] = (x_ref[t, r].astype(F32) + (branch + bias)).astype(BF16)


def struct(shape, dtype=BF16):
    return jax.ShapeDtypeStruct(shape, dtype)


def with_rows(x):
    up = [(i, i + 1) for i in range(15)]
    down = [(i + 1, i) for i in range(15)]
    above = lax.ppermute(x[7:8], ROW, up)
    below = lax.ppermute(x[0:1], ROW, down)
    return jnp.concatenate([above, x, below], axis=0)


def near(x):
    return [x] + [lax.ppermute(x, NEAR, [(i, i ^ k) for i in range(4)]) for k in (1, 2, 3)]


def exchange(x, axes):
    return lax.all_to_all(x, axes, 0, 0, tiled=True)


def weights_of(weight):
    me = lax.axis_index("zh")
    weight = weight.reshape(2, 16, 3, 3, 3, 4, 64).transpose(5, 0, 2, 4, 1, 3, 6)
    weight = weight.reshape(4, 2, 3, 3, 16, 192)
    held = [lax.dynamic_index_in_dim(weight, lax.rem(me + d, 4), 0, keepdims=False) for d in range(4)]
    moved = [
        lax.ppermute(held[d], "zh", [(i, (i + d) % 4) for i in range(4)]) for d in range(1, 4)
    ]
    return [held[0]] + moved


def local(frames, cache, norm_gain, norm_shift, conv_weight, conv_bias):
    row = lax.axis_index(ROW)
    here = lax.axis_index(NEAR)
    edge = jnp.stack([row > 0, row < 15]).astype(F32)
    place = jnp.stack([row, lax.axis_index("zh"), here, here ^ 1, here ^ 2, here ^ 3]).astype(jnp.int32)
    note = pltpu.VMEM((8, 128), F32)

    raw, later, stats = call(
        begin_kernel,
        (struct((8, 16, 768)), struct((8, 16, 256)), struct((64, 8, 128), F32)),
        frames, cache, norm_gain, norm_shift,
        scratch=(note,),
    )
    stats = exchange(stats, ROW + NEAR)
    raw = near(with_rows(raw))
    weights = weights_of(conv_weight)
    later = near(with_rows(later))
    bias = jnp.broadcast_to(conv_bias[:, :, None], (2, 16, 128))
    scratch = (
        pltpu.VMEM((3, 4, 16, 128), F32),
        pltpu.VMEM((10, 4, 16, 768), BF16),
        pltpu.VMEM((3, 4, 3, 16, 192), BF16),
    )
    flops = 2 * 192 * 576 * 4096

    partial = call(
        first_kernel, struct((4, 8, 16, 512)), place, edge, *raw, stats, *weights,
        smem=(0, 1), scratch=scratch, flops=flops,
    )
    partial = exchange(partial, "zh")
    middle, stats = call(
        merge_kernel,
        (struct((8, 16, 512)), struct((64, 8, 128), F32)),
        partial, bias[0], norm_gain, norm_shift,
        scratch=(note,),
    )
    stats = exchange(stats, ROW + NEAR)
    middle = near(with_rows(middle))
    partial = call(
        second_kernel, struct((4, 8, 16, 512)), place, edge, *middle, *later, stats, *weights,
        smem=(0, 1), scratch=scratch, flops=flops,
    )
    partial = exchange(partial, "zh")
    return call(last_kernel, struct((4, 8, 16, 128)), frames, partial, bias[1])


def solution(mesh):
    fine = Mesh(mesh.devices.reshape(2, 4, 2, 4, 2, 2), ROW + CHAN)
    placed = (
        P(None, ROW, CHAN, None),
        P(None, None, ROW, CHAN, None),
        P(None, CHAN),
        P(None, CHAN),
        P(None, CHAN, None, None),
        P(None, CHAN),
    )
    return jax.shard_map(
        local, mesh=fine, in_specs=placed, out_specs=P(None, ROW, CHAN, None), check_vma=False
    )
```

time: 564 us -> 132 us (0.23)
  the two profiles are of different devices: /device:TPU:27 before, /device:TPU:8 now
where the time goes in v2:
time: 132 us
  starting transfers between devices  57.7 us (44%)
  waiting for transfers between devices  38.4 us (29%)
  blocking collectives  21.2 us (16%)
  Pallas kernels  8.8 us (7%)
  local copies, waits for them, and re-layouts  5.34 us (4%)
    all_to_all x3, starting transfers between devices, exchange(): return lax.all_to_all(x, axes, 0, 0, tiled=True)  23.8 us
    ppermute x3, waiting for transfers between devices, weights_of(): lax.ppermute(held[d], 'zh', [(i, (i + d) % 4) for i in range(4)])  21.9 us
    all_to_all x1, blocking collectives, exchange(): return lax.all_to_all(x, axes, 0, 0, tiled=True)  21.2 us
    ppermute x9, starting transfers between devices, near(): lax.ppermute(x, NEAR, [(i, i ^ k) for i in range(4)])  10.6 us
    ppermute x9, waiting for transfers between devices, near(): lax.ppermute(x, NEAR, [(i, i ^ k) for i in range(4)])  9.36 us
    ppermute x3, starting transfers between devices, with_rows(): below = lax.ppermute(x[0:1], ROW, down)  9.21 us
    pallas_call x5, Pallas kernels, call(): pl.pallas_call(kernel, out_shape=outs, in_specs=specs, out_specs=jax.tree...  8.8 us
    ppermute x3, starting transfers between devices, weights_of(): lax.ppermute(held[d], 'zh', [(i, (i + d) % 4) for i in range(4)])  8.33 us
  transfers between devices with their start and end apart: 21, of which 7 were waited for; matrix products, arithmetic and copies ran while one was open for 2% of the time, Pallas kernels for 1%

profile of v2, /device:TPU:8, one launch (start us, length us, event | category | flops | bytes accessed | tf_op | source)
XLA Modules:
  0.0 131.8 jit_solution(13947168509868581467)
XLA Ops:
  0.0 0.9 copy-done
  0.9 0.9 copy-done.2
  1.8 0.7 copy-done.3
  2.5 0.7 copy-done.5
  3.2 0.8 shard_map.64
  4.0 1.9 %collective-permute-start = (bf16[1,16,768]{2,1,0:T(8,128)(2,1)S(1)}, bf16[1,16,768]{2,1,0:T(8,128)(2,1)S(1)}, u32[]{:S(2)}, u32[]{:S(2)}) collective-permute-start(bf16[1,16,768]{2,1,0:T(8,128)(2,1)S(1)} %get-tuple-element.20), channel_id=1, source_target_pairs={{0,16},{16,32},{32,48},{48,64},{64,80},{80,96},{96,112},{112,128},... | collective-permute-start | bytes 73736 | tf_op jit(solution)/shard_map/ppermute | solution.py:192
  5.9 3.6 %collective-permute-start.1 = (bf16[1,16,768]{2,1,0:T(8,128)(2,1)S(1)}, bf16[1,16,768]{2,1,0:T(8,128)(2,1)S(1)}, u32[]{:S(2)}, u32[]{:S(2)}) collective-permute-start(bf16[1,16,768]{2,1,0:T(8,128)(2,1)S(1)} %get-tuple-element.19), channel_id=1, source_target_pairs={{16,0},{32,16},{48,32},{64,48},{80,64},{96,80},{112,96},{128,112},... | collective-permute-start | bytes 73736 | tf_op jit(solution)/shard_map/ppermute | solution.py:193
  9.6 10.3 %all-to-all-start = ((f32[64,8,128]{2,1,0:T(8,128)}), f32[64,8,128]{2,1,0:T(8,128)S(1)}, u32[]{:S(2)}, u32[]{:S(2)}) async-start(f32[64,8,128]{2,1,0:T(8,128)} %get-tuple-element.11), calls=%async_computation | async-start | bytes 524288 | tf_op jit(solution)/shard_map/all_to_all | solution.py:202
  19.9 0.3 reshape.11
  20.3 0.8 copy.10
  21.0 0.7 reshape.12
  21.8 0.0 collective-permute-done
  21.8 0.0 collective-permute-done.1
  21.9 1.6 %collective-permute-start.2 = (bf16[10,16,768]{2,1,0:T(8,128)(2,1)S(1)}, bf16[10,16,768]{2,1,0:T(8,128)(2,1)S(1)}, u32[]{:S(2)}, u32[]{:S(2)}) collective-permute-start(bf16[10,16,768]{2,1,0:T(8,128)(2,1)S(1)} %constant_dynamic-update-slice_fusion.a_ref), channel_id=1, source_target_pairs={{0,1},{1,0},{2,3},{3,2},{4,5},{5,4},{6,7},{7,6},{8,9},{9,8},{10,11... | collective-permute-start | bytes 737288 | tf_op jit(solution)/shard_map/ppermute | solution.py:198
  23.4 1.5 %collective-permute-start.3 = (bf16[10,16,768]{2,1,0:T(8,128)(2,1)S(1)}, bf16[10,16,768]{2,1,0:T(8,128)(2,1)S(1)}, u32[]{:S(2)}, u32[]{:S(2)}) collective-permute-start(bf16[10,16,768]{2,1,0:T(8,128)(2,1)S(1)} %constant_dynamic-update-slice_fusion.a_ref), channel_id=1, source_target_pairs={{0,2},{1,3},{2,0},{3,1},{4,6},{5,7},{6,4},{7,5},{8,10},{9,11},{10,... | collective-permute-start | bytes 737288 | tf_op jit(solution)/shard_map/ppermute | solution.py:198
  24.9 0.6 collective-permute-start.4
  25.5 3.3 %collective-permute-start.5 = (bf16[2,3,3,16,192]{4,3,2,1,0:T(8,128)(2,1)S(1)}, bf16[2,3,3,16,192]{4,3,2,1,0:T(8,128)(2,1)S(1)}, u32[]{:S(2)}, u32[]{:S(2)}) collective-permute-start(bf16[2,3,3,16,192]{4,3,2,1,0:T(8,128)(2,1)S(1)} %get-tuple-element.17), channel_id=1, source_target_pairs={{0,4},{4,8},{8,12},{12,0},{1,5},{5,9},{9,13},{13,1},{2,6},{6,10},{... | collective-permute-start | bytes 331784 | tf_op jit(solution)/shard_map/ppermute | solution.py:211
  28.8 4.5 %collective-permute-start.6 = (bf16[2,3,3,16,192]{4,3,2,1,0:T(8,128)(2,1)S(1)}, bf16[2,3,3,16,192]{4,3,2,1,0:T(8,128)(2,1)S(1)}, u32[]{:S(2)}, u32[]{:S(2)}) collective-permute-start(bf16[2,3,3,16,192]{4,3,2,1,0:T(8,128)(2,1)S(1)} %get-tuple-element.16), channel_id=1, source_target_pairs={{0,8},{4,12},{8,0},{12,4},{1,9},{5,13},{9,1},{13,5},{2,10},{6,14},... | collective-permute-start | bytes 331784 | tf_op jit(solution)/shard_map/ppermute | solution.py:211
  33.3 0.1 stack.36.place_ref
  33.4 16.4 %collective-permute-done.5.w1 = bf16[2,3,3,16,192]{4,3,2,1,0:T(8,128)(2,1)S(1)} collective-permute-done((bf16[2,3,3,16,192]{4,3,2,1,0:T(8,128)(2,1)S(1)}, bf16[2,3,3,16,192]{4,3,2,1,0:T(8,128)(2,1)S(1)}, u32[]{:S(2)}, u32[]{:S(2)}) %collective-permute-start.5) | collective-permute-done | bytes 110624 | tf_op jit(solution)/shard_map/ppermute | solution.py:211
  49.8 0.5 collective-permute-start.7
  50.3 0.1 add_convert_fusion.edge_ref
  50.4 2.4 %collective-permute-done.6.w2 = bf16[2,3,3,16,192]{4,3,2,1,0:T(8,128)(2,1)S(1)} collective-permute-done((bf16[2,3,3,16,192]{4,3,2,1,0:T(8,128)(2,1)S(1)}, bf16[2,3,3,16,192]{4,3,2,1,0:T(8,128)(2,1)S(1)}, u32[]{:S(2)}, u32[]{:S(2)}) %collective-permute-start.6) | collective-permute-done | bytes 110624 | tf_op jit(solution)/shard_map/ppermute | solution.py:211
  52.8 3.0 %collective-permute-done.7.w3 = bf16[2,3,3,16,192]{4,3,2,1,0:T(8,128)(2,1)S(1)} collective-permute-done((bf16[2,3,3,16,192]{4,3,2,1,0:T(8,128)(2,1)S(1)}, bf16[2,3,3,16,192]{4,3,2,1,0:T(8,128)(2,1)S(1)}, u32[]{:S(2)}, u32[]{:S(2)}) %collective-permute-start.7) | collective-permute-done | bytes 110624 | tf_op jit(solution)/shard_map/ppermute | solution.py:211
  55.9 0.0 copy-start.8
  55.9 3.6 %shard_map.65 = bf16[4,8,16,512]{3,2,1,0:T(8,128)(2,1)} custom-call(s32[6]{0:T(128)S(1)} %stack.36.place_ref, f32[2]{0:T(128)S(1)} %add_convert_fusion.edge_ref, bf16[10,16,768]{2,1,0:T(8,128)(2,1)S(1)} %constant_dynamic-update-slice_fusion.a_ref, bf16[10,16,768]{2,1,0:T(8,128)(2,1)S(1)} %collective-permute-done.2.b_ref, ...), custom_call_target="tpu_custom_call" | custom-call | flops 905969664 | bytes 1687584 | tf_op jit(solution)/shard_map/pallas_call | solution.py:31
  59.4 4.9 %all-to-all-start.1 = ((bf16[4,8,16,512]{3,2,1,0:T(8,128)(2,1)}), bf16[4,8,16,512]{3,2,1,0:T(8,128)(2,1)S(1)}, u32[]{:S(2)}, u32[]{:S(2)}) async-start(bf16[4,8,16,512]{3,2,1,0:T(8,128)(2,1)} %shard_map.65), calls=%async_computation.1 | async-start | bytes 1048576 | tf_op jit(solution)/shard_map/all_to_all | solution.py:202
  64.3 1.9 %collective-permute-start.13 = (bf16[1,16,256]{2,1,0:T(8,128)(2,1)S(1)}, bf16[1,16,256]{2,1,0:T(8,128)(2,1)S(1)}, u32[]{:S(2)}, u32[]{:S(2)}) collective-permute-start(bf16[1,16,256]{2,1,0:T(8,128)(2,1)S(1)} %get-tuple-element.24), channel_id=1, source_target_pairs={{0,16},{16,32},{32,48},{48,64},{64,80},{80,96},{96,112},{112,128},... | collective-permute-start | bytes 24584 | tf_op jit(solution)/shard_map/ppermute | solution.py:192
  66.2 3.6 %collective-permute-start.14 = (bf16[1,16,256]{2,1,0:T(8,128)(2,1)S(1)}, bf16[1,16,256]{2,1,0:T(8,128)(2,1)S(1)}, u32[]{:S(2)}, u32[]{:S(2)}) collective-permute-start(bf16[1,16,256]{2,1,0:T(8,128)(2,1)S(1)} %get-tuple-element.23), channel_id=1, source_target_pairs={{16,0},{32,16},{48,32},{64,48},{80,64},{96,80},{112,96},{128,112},... | collective-permute-start | bytes 24584 | tf_op jit(solution)/shard_map/ppermute | solution.py:193
  69.9 5.8 %all-to-all-done.1.part_ref = bf16[4,8,16,512]{3,2,1,0:T(8,128)(2,1)S(1)} async-done(((bf16[4,8,16,512]{3,2,1,0:T(8,128)(2,1)}), bf16[4,8,16,512]{3,2,1,0:T(8,128)(2,1)S(1)}, u32[]{:S(2)}, u32[]{:S(2)}) %all-to-all-start.1) | async-done | bytes 524320 | tf_op jit(solution)/shard_map/all_to_all | solution.py:202
  75.7 0.1 broadcast_in_dim.13.bias_ref
  75.8 0.9 shard_map.66
  76.7 1.9 %collective-permute-start.8 = (bf16[1,16,512]{2,1,0:T(8,128)(2,1)S(1)}, bf16[1,16,512]{2,1,0:T(8,128)(2,1)S(1)}, u32[]{:S(2)}, u32[]{:S(2)}) collective-permute-start(bf16[1,16,512]{2,1,0:T(8,128)(2,1)S(1)} %get-tuple-element.22), channel_id=1, source_target_pairs={{0,16},{16,32},{32,48},{48,64},{64,80},{80,96},{96,112},{112,128},... | collective-permute-start | bytes 49160 | tf_op jit(solution)/shard_map/ppermute | solution.py:192
  78.6 8.6 %all-to-all-start.2 = ((f32[64,8,128]{2,1,0:T(8,128)}), f32[64,8,128]{2,1,0:T(8,128)S(1)}, u32[]{:S(2)}, u32[]{:S(2)}) async-start(f32[64,8,128]{2,1,0:T(8,128)} %get-tuple-element.14), calls=%async_computation.2 | async-start | bytes 524288 | tf_op jit(solution)/shard_map/all_to_all | solution.py:202
  87.3 1.6 %collective-permute-start.15 = (bf16[10,16,256]{2,1,0:T(8,128)(2,1)S(1)}, bf16[10,16,256]{2,1,0:T(8,128)(2,1)S(1)}, u32[]{:S(2)}, u32[]{:S(2)}) collective-permute-start(bf16[10,16,256]{2,1,0:T(8,128)(2,1)S(1)} %constant_dynamic-update-slice_fusion.6.ca_ref), channel_id=1, source_target_pairs={{0,1},{1,0},{2,3},{3,2},{4,5},{5,4},{6,7},{7,6},{8,9},{9,8},{10,11... | collective-permute-start | bytes 245768 | tf_op jit(solution)/shard_map/ppermute | solution.py:198
  88.8 1.9 %collective-permute-start.9 = (bf16[1,16,512]{2,1,0:T(8,128)(2,1)S(1)}, bf16[1,16,512]{2,1,0:T(8,128)(2,1)S(1)}, u32[]{:S(2)}, u32[]{:S(2)}) collective-permute-start(bf16[1,16,512]{2,1,0:T(8,128)(2,1)S(1)} %get-tuple-element.21), channel_id=1, source_target_pairs={{16,0},{32,16},{48,32},{64,48},{80,64},{96,80},{112,96},{128,112},... | collective-permute-start | bytes 49160 | tf_op jit(solution)/shard_map/ppermute | solution.py:193
  90.8 1.4 %collective-permute-done.9 = bf16[1,16,512]{2,1,0:T(8,128)(2,1)S(1)} collective-permute-done((bf16[1,16,512]{2,1,0:T(8,128)(2,1)S(1)}, bf16[1,16,512]{2,1,0:T(8,128)(2,1)S(1)}, u32[]{:S(2)}, u32[]{:S(2)}) %collective-permute-start.9) | collective-permute-done | bytes 16416 | tf_op jit(solution)/shard_map/ppermute | solution.py:193
  92.2 0.5 collective-permute-start.10
  92.8 1.5 %collective-permute-start.11 = (bf16[10,16,512]{2,1,0:T(8,128)(2,1)S(1)}, bf16[10,16,512]{2,1,0:T(8,128)(2,1)S(1)}, u32[]{:S(2)}, u32[]{:S(2)}) collective-permute-start(bf16[10,16,512]{2,1,0:T(8,128)(2,1)S(1)} %constant_dynamic-update-slice_fusion.3.a_ref), channel_id=1, source_target_pairs={{0,2},{1,3},{2,0},{3,1},{4,6},{5,7},{6,4},{7,5},{8,10},{9,11},{10,... | collective-permute-start | bytes 491528 | tf_op jit(solution)/shard_map/ppermute | solution.py:198
  94.2 1.5 %collective-permute-start.12 = (bf16[10,16,512]{2,1,0:T(8,128)(2,1)S(1)}, bf16[10,16,512]{2,1,0:T(8,128)(2,1)S(1)}, u32[]{:S(2)}, u32[]{:S(2)}) collective-permute-start(bf16[10,16,512]{2,1,0:T(8,128)(2,1)S(1)} %constant_dynamic-update-slice_fusion.3.a_ref), channel_id=1, source_target_pairs={{0,3},{1,2},{2,1},{3,0},{4,7},{5,6},{6,5},{7,4},{8,11},{9,10},{10,... | collective-permute-start | bytes 491528 | tf_op jit(solution)/shard_map/ppermute | solution.py:198
  95.7 1.5 %collective-permute-start.16 = (bf16[10,16,256]{2,1,0:T(8,128)(2,1)S(1)}, bf16[10,16,256]{2,1,0:T(8,128)(2,1)S(1)}, u32[]{:S(2)}, u32[]{:S(2)}) collective-permute-start(bf16[10,16,256]{2,1,0:T(8,128)(2,1)S(1)} %constant_dynamic-update-slice_fusion.6.ca_ref), channel_id=1, source_target_pairs={{0,2},{1,3},{2,0},{3,1},{4,6},{5,7},{6,4},{7,5},{8,10},{9,11},{10,... | collective-permute-start | bytes 245768 | tf_op jit(solution)/shard_map/ppermute | solution.py:198
  97.2 0.5 collective-permute-start.17
  97.7 6.4 %collective-permute-done.16.cc_ref = bf16[10,16,256]{2,1,0:T(8,128)(2,1)S(1)} collective-permute-done((bf16[10,16,256]{2,1,0:T(8,128)(2,1)S(1)}, bf16[10,16,256]{2,1,0:T(8,128)(2,1)S(1)}, u32[]{:S(2)}, u32[]{:S(2)}) %collective-permute-start.16) | collective-permute-done | bytes 81952 | tf_op jit(solution)/shard_map/ppermute | solution.py:198
  104.1 3.0 %collective-permute-done.17.cd_ref = bf16[10,16,256]{2,1,0:T(8,128)(2,1)S(1)} collective-permute-done((bf16[10,16,256]{2,1,0:T(8,128)(2,1)S(1)}, bf16[10,16,256]{2,1,0:T(8,128)(2,1)S(1)}, u32[]{:S(2)}, u32[]{:S(2)}) %collective-permute-start.17) | collective-permute-done | bytes 81952 | tf_op jit(solution)/shard_map/ppermute | solution.py:198
  107.1 2.8 %shard_map.67 = bf16[4,8,16,512]{3,2,1,0:T(8,128)(2,1)S(1)} custom-call(s32[6]{0:T(128)S(1)} %stack.36.place_ref, f32[2]{0:T(128)S(1)} %add_convert_fusion.edge_ref, bf16[10,16,512]{2,1,0:T(8,128)(2,1)S(1)} %constant_dynamic-update-slice_fusion.3.a_ref, bf16[10,16,512]{2,1,0:T(8,128)(2,1)S(1)} %collective-permute-done.10.b_ref, ...), custom_call_target="tpu_custom_call" | custom-call | flops 905969664 | bytes 1687584 | tf_op jit(solution)/shard_map/pallas_call | solution.py:31
  109.8 21.2 %all_to_all.20.part_ref = bf16[4,8,16,512]{3,2,1,0:T(8,128)(2,1)S(1)} all-to-all(bf16[4,8,16,512]{3,2,1,0:T(8,128)(2,1)S(1)} %shard_map.67), channel_id=1, replica_groups=mesh['xh'=2,'y'=4,'core'=2,'zh'=4,'zl'=2,'xl'=2] {'zh'}, dimensions={0} | all-to-all | bytes 1048576 | tf_op jit(solution)/shard_map/all_to_all | solution.py:202
  131.0 0.1 broadcast_in_dim.15.bias_ref
  131.1 0.8 shard_map.68
  (39 shorter events, 0.2 us)
Async XLA Ops:
  0.0 0.9 copy-start
  0.9 0.9 copy-start.2
  1.8 0.7 copy-start.3
  2.5 0.7 copy-start.5
  3.2 16.7 %copy-start.7 = (bf16[2,16,27,256]{3,1,2,0:T(8,128)(2,1)S(1)}, bf16[2,16,27,256]{3,1,2,0:T(8,128)(2,1)}, u32[]{:S(2)}) copy-start(bf16[2,16,27,256]{3,1,2,0:T(8,128)(2,1)} %param.10) | copy-start | bytes 1327108
  4.0 17.8 %collective-permute-start = (bf16[1,16,768]{2,1,0:T(8,128)(2,1)S(1)}, bf16[1,16,768]{2,1,0:T(8,128)(2,1)S(1)}, u32[]{:S(2)}, u32[]{:S(2)}) collective-permute-start(bf16[1,16,768]{2,1,0:T(8,128)(2,1)S(1)} %get-tuple-element.20), channel_id=1, source_target_pairs={{0,16},{16,32},{32,48},{48,64},{64,80},{80,96},{96,112},{112,128},... | collective-permute-start | bytes 73736 | tf_op jit(solution)/shard_map/ppermute | solution.py:192
  5.9 15.9 %collective-permute-start.1 = (bf16[1,16,768]{2,1,0:T(8,128)(2,1)S(1)}, bf16[1,16,768]{2,1,0:T(8,128)(2,1)S(1)}, u32[]{:S(2)}, u32[]{:S(2)}) collective-permute-start(bf16[1,16,768]{2,1,0:T(8,128)(2,1)S(1)} %get-tuple-element.19), channel_id=1, source_target_pairs={{16,0},{32,16},{48,32},{64,48},{80,64},{96,80},{112,96},{128,112},... | collective-permute-start | bytes 73736 | tf_op jit(solution)/shard_map/ppermute | solution.py:193
  9.6 46.3 %all-to-all-start = ((f32[64,8,128]{2,1,0:T(8,128)}), f32[64,8,128]{2,1,0:T(8,128)S(1)}, u32[]{:S(2)}, u32[]{:S(2)}) async-start(f32[64,8,128]{2,1,0:T(8,128)} %get-tuple-element.11), calls=%async_computation | async-start | bytes 524288 | tf_op jit(solution)/shard_map/all_to_all | solution.py:202
  21.9 34.0 %collective-permute-start.2 = (bf16[10,16,768]{2,1,0:T(8,128)(2,1)S(1)}, bf16[10,16,768]{2,1,0:T(8,128)(2,1)S(1)}, u32[]{:S(2)}, u32[]{:S(2)}) collective-permute-start(bf16[10,16,768]{2,1,0:T(8,128)(2,1)S(1)} %constant_dynamic-update-slice_fusion.a_ref), channel_id=1, source_target_pairs={{0,1},{1,0},{2,3},{3,2},{4,5},{5,4},{6,7},{7,6},{8,9},{9,8},{10,11... | collective-permute-start | bytes 737288 | tf_op jit(solution)/shard_map/ppermute | solution.py:198
  23.4 32.4 %collective-permute-start.3 = (bf16[10,16,768]{2,1,0:T(8,128)(2,1)S(1)}, bf16[10,16,768]{2,1,0:T(8,128)(2,1)S(1)}, u32[]{:S(2)}, u32[]{:S(2)}) collective-permute-start(bf16[10,16,768]{2,1,0:T(8,128)(2,1)S(1)} %constant_dynamic-update-slice_fusion.a_ref), channel_id=1, source_target_pairs={{0,2},{1,3},{2,0},{3,1},{4,6},{5,7},{6,4},{7,5},{8,10},{9,11},{10,... | collective-permute-start | bytes 737288 | tf_op jit(solution)/shard_map/ppermute | solution.py:198
  24.9 31.0 %collective-permute-start.4 = (bf16[10,16,768]{2,1,0:T(8,128)(2,1)S(1)}, bf16[10,16,768]{2,1,0:T(8,128)(2,1)S(1)}, u32[]{:S(2)}, u32[]{:S(2)}) collective-permute-start(bf16[10,16,768]{2,1,0:T(8,128)(2,1)S(1)} %constant_dynamic-update-slice_fusion.a_ref), channel_id=1, source_target_pairs={{0,3},{1,2},{2,1},{3,0},{4,7},{5,6},{6,5},{7,4},{8,11},{9,10},{10,... | collective-permute-start | bytes 737288 | tf_op jit(solution)/shard_map/ppermute | solution.py:198
  25.5 24.3 %collective-permute-start.5 = (bf16[2,3,3,16,192]{4,3,2,1,0:T(8,128)(2,1)S(1)}, bf16[2,3,3,16,192]{4,3,2,1,0:T(8,128)(2,1)S(1)}, u32[]{:S(2)}, u32[]{:S(2)}) collective-permute-start(bf16[2,3,3,16,192]{4,3,2,1,0:T(8,128)(2,1)S(1)} %get-tuple-element.17), channel_id=1, source_target_pairs={{0,4},{4,8},{8,12},{12,0},{1,5},{5,9},{9,13},{13,1},{2,6},{6,10},{... | collective-permute-start | bytes 331784 | tf_op jit(solution)/shard_map/ppermute | solution.py:211
  28.8 24.0 %collective-permute-start.6 = (bf16[2,3,3,16,192]{4,3,2,1,0:T(8,128)(2,1)S(1)}, bf16[2,3,3,16,192]{4,3,2,1,0:T(8,128)(2,1)S(1)}, u32[]{:S(2)}, u32[]{:S(2)}) collective-permute-start(bf16[2,3,3,16,192]{4,3,2,1,0:T(8,128)(2,1)S(1)} %get-tuple-element.16), channel_id=1, source_target_pairs={{0,8},{4,12},{8,0},{12,4},{1,9},{5,13},{9,1},{13,5},{2,10},{6,14},... | collective-permute-start | bytes 331784 | tf_op jit(solution)/shard_map/ppermute | solution.py:211
  49.8 6.0 %collective-permute-start.7 = (bf16[2,3,3,16,192]{4,3,2,1,0:T(8,128)(2,1)S(1)}, bf16[2,3,3,16,192]{4,3,2,1,0:T(8,128)(2,1)S(1)}, u32[]{:S(2)}, u32[]{:S(2)}) collective-permute-start(bf16[2,3,3,16,192]{4,3,2,1,0:T(8,128)(2,1)S(1)} %get-tuple-element.15), channel_id=1, source_target_pairs={{0,12},{4,0},{8,4},{12,8},{1,13},{5,1},{9,5},{13,9},{2,14},{6,2},{... | collective-permute-start | bytes 331784 | tf_op jit(solution)/shard_map/ppermute | solution.py:211
  55.9 14.0 %copy-start.8 = (f32[2,16]{1,0:T(2,128)S(1)}, f32[2,16]{1,0:T(2,128)}, u32[]{:S(2)}) copy-start(f32[2,16]{1,0:T(2,128)} %param.11) | copy-start | bytes 388
  59.4 16.4 %copy-start.4 = (f32[2,16]{1,0:T(2,128)S(1)}, f32[2,16]{1,0:T(2,128)}, u32[]{:S(2)}) copy-start(f32[2,16]{1,0:T(2,128)} %gain_ref.3) | copy-start | bytes 388
  59.4 16.4 %copy-start.6 = (f32[2,16]{1,0:T(2,128)S(1)}, f32[2,16]{1,0:T(2,128)}, u32[]{:S(2)}) copy-start(f32[2,16]{1,0:T(2,128)} %shift_ref.3) | copy-start | bytes 388
  59.4 16.3 %all-to-all-start.1 = ((bf16[4,8,16,512]{3,2,1,0:T(8,128)(2,1)}), bf16[4,8,16,512]{3,2,1,0:T(8,128)(2,1)S(1)}, u32[]{:S(2)}, u32[]{:S(2)}) async-start(bf16[4,8,16,512]{3,2,1,0:T(8,128)(2,1)} %shard_map.65), calls=%async_computation.1 | async-start | bytes 1048576 | tf_op jit(solution)/shard_map/all_to_all | solution.py:202
  64.3 5.6 %collective-permute-start.13 = (bf16[1,16,256]{2,1,0:T(8,128)(2,1)S(1)}, bf16[1,16,256]{2,1,0:T(8,128)(2,1)S(1)}, u32[]{:S(2)}, u32[]{:S(2)}) collective-permute-start(bf16[1,16,256]{2,1,0:T(8,128)(2,1)S(1)} %get-tuple-element.24), channel_id=1, source_target_pairs={{0,16},{16,32},{32,48},{48,64},{64,80},{80,96},{96,112},{112,128},... | collective-permute-start | bytes 24584 | tf_op jit(solution)/shard_map/ppermute | solution.py:192
  66.2 21.0 %collective-permute-start.14 = (bf16[1,16,256]{2,1,0:T(8,128)(2,1)S(1)}, bf16[1,16,256]{2,1,0:T(8,128)(2,1)S(1)}, u32[]{:S(2)}, u32[]{:S(2)}) collective-permute-start(bf16[1,16,256]{2,1,0:T(8,128)(2,1)S(1)} %get-tuple-element.23), channel_id=1, source_target_pairs={{16,0},{32,16},{48,32},{64,48},{80,64},{96,80},{112,96},{128,112},... | collective-permute-start | bytes 24584 | tf_op jit(solution)/shard_map/ppermute | solution.py:193
  76.7 14.1 %collective-permute-start.8 = (bf16[1,16,512]{2,1,0:T(8,128)(2,1)S(1)}, bf16[1,16,512]{2,1,0:T(8,128)(2,1)S(1)}, u32[]{:S(2)}, u32[]{:S(2)}) collective-permute-start(bf16[1,16,512]{2,1,0:T(8,128)(2,1)S(1)} %get-tuple-element.22), channel_id=1, source_target_pairs={{0,16},{16,32},{32,48},{48,64},{64,80},{80,96},{96,112},{112,128},... | collective-permute-start | bytes 49160 | tf_op jit(solution)/shard_map/ppermute | solution.py:192
  78.6 28.4 %all-to-all-start.2 = ((f32[64,8,128]{2,1,0:T(8,128)}), f32[64,8,128]{2,1,0:T(8,128)S(1)}, u32[]{:S(2)}, u32[]{:S(2)}) async-start(f32[64,8,128]{2,1,0:T(8,128)} %get-tuple-element.14), calls=%async_computation.2 | async-start | bytes 524288 | tf_op jit(solution)/shard_map/all_to_all | solution.py:202
  87.3 9.9 %collective-permute-start.15 = (bf16[10,16,256]{2,1,0:T(8,128)(2,1)S(1)}, bf16[10,16,256]{2,1,0:T(8,128)(2,1)S(1)}, u32[]{:S(2)}, u32[]{:S(2)}) collective-permute-start(bf16[10,16,256]{2,1,0:T(8,128)(2,1)S(1)} %constant_dynamic-update-slice_fusion.6.ca_ref), channel_id=1, source_target_pairs={{0,1},{1,0},{2,3},{3,2},{4,5},{5,4},{6,7},{7,6},{8,9},{9,8},{10,11... | collective-permute-start | bytes 245768 | tf_op jit(solution)/shard_map/ppermute | solution.py:198
  88.8 3.4 %collective-permute-start.9 = (bf16[1,16,512]{2,1,0:T(8,128)(2,1)S(1)}, bf16[1,16,512]{2,1,0:T(8,128)(2,1)S(1)}, u32[]{:S(2)}, u32[]{:S(2)}) collective-permute-start(bf16[1,16,512]{2,1,0:T(8,128)(2,1)S(1)} %get-tuple-element.21), channel_id=1, source_target_pairs={{16,0},{32,16},{48,32},{64,48},{80,64},{96,80},{112,96},{128,112},... | collective-permute-start | bytes 49160 | tf_op jit(solution)/shard_map/ppermute | solution.py:193
  92.2 38.9 %copy-start.1 = (bf16[4,8,16,128]{3,2,1,0:T(8,128)(2,1)S(1)}, bf16[4,8,16,128]{3,2,1,0:T(8,128)(2,1)}, u32[]{:S(2)}) copy-start(bf16[4,8,16,128]{3,2,1,0:T(8,128)(2,1)} %x_ref.3) | copy-start | bytes 393220
  92.2 14.8 %collective-permute-start.10 = (bf16[10,16,512]{2,1,0:T(8,128)(2,1)S(1)}, bf16[10,16,512]{2,1,0:T(8,128)(2,1)S(1)}, u32[]{:S(2)}, u32[]{:S(2)}) collective-permute-start(bf16[10,16,512]{2,1,0:T(8,128)(2,1)S(1)} %constant_dynamic-update-slice_fusion.3.a_ref), channel_id=1, source_target_pairs={{0,1},{1,0},{2,3},{3,2},{4,5},{5,4},{6,7},{7,6},{8,9},{9,8},{10,11... | collective-permute-start | bytes 491528 | tf_op jit(solution)/shard_map/ppermute | solution.py:198
  92.8 14.3 %collective-permute-start.11 = (bf16[10,16,512]{2,1,0:T(8,128)(2,1)S(1)}, bf16[10,16,512]{2,1,0:T(8,128)(2,1)S(1)}, u32[]{:S(2)}, u32[]{:S(2)}) collective-permute-start(bf16[10,16,512]{2,1,0:T(8,128)(2,1)S(1)} %constant_dynamic-update-slice_fusion.3.a_ref), channel_id=1, source_target_pairs={{0,2},{1,3},{2,0},{3,1},{4,6},{5,7},{6,4},{7,5},{8,10},{9,11},{10,... | collective-permute-start | bytes 491528 | tf_op jit(solution)/shard_map/ppermute | solution.py:198
  94.2 12.8 %collective-permute-start.12 = (bf16[10,16,512]{2,1,0:T(8,128)(2,1)S(1)}, bf16[10,16,512]{2,1,0:T(8,128)(2,1)S(1)}, u32[]{:S(2)}, u32[]{:S(2)}) collective-permute-start(bf16[10,16,512]{2,1,0:T(8,128)(2,1)S(1)} %constant_dynamic-update-slice_fusion.3.a_ref), channel_id=1, source_target_pairs={{0,3},{1,2},{2,1},{3,0},{4,7},{5,6},{6,5},{7,4},{8,11},{9,10},{10,... | collective-permute-start | bytes 491528 | tf_op jit(solution)/shard_map/ppermute | solution.py:198
  95.7 8.4 %collective-permute-start.16 = (bf16[10,16,256]{2,1,0:T(8,128)(2,1)S(1)}, bf16[10,16,256]{2,1,0:T(8,128)(2,1)S(1)}, u32[]{:S(2)}, u32[]{:S(2)}) collective-permute-start(bf16[10,16,256]{2,1,0:T(8,128)(2,1)S(1)} %constant_dynamic-update-slice_fusion.6.ca_ref), channel_id=1, source_target_pairs={{0,2},{1,3},{2,0},{3,1},{4,6},{5,7},{6,4},{7,5},{8,10},{9,11},{10,... | collective-permute-start | bytes 245768 | tf_op jit(solution)/shard_map/ppermute | solution.py:198
  97.2 9.9 %collective-permute-start.17 = (bf16[10,16,256]{2,1,0:T(8,128)(2,1)S(1)}, bf16[10,16,256]{2,1,0:T(8,128)(2,1)S(1)}, u32[]{:S(2)}, u32[]{:S(2)}) collective-permute-start(bf16[10,16,256]{2,1,0:T(8,128)(2,1)S(1)} %constant_dynamic-update-slice_fusion.6.ca_ref), channel_id=1, source_target_pairs={{0,3},{1,2},{2,1},{3,0},{4,7},{5,6},{6,5},{7,4},{8,11},{9,10},{10,... | collective-permute-start | bytes 245768 | tf_op jit(solution)/shard_map/ppermute | solution.py:198

commit v3 on v2

--- a/solution.py
+++ b/solution.py
@@ -23,10 +23,8 @@
     return u / (1.0 + jnp.exp(-u))
 
 
-def call(kernel, outs, *args, smem=(), scratch=(), flops=0):
-    specs = [
-        pl.BlockSpec(memory_space=pltpu.SMEM if i in smem else pltpu.VMEM) for i in range(len(args))
-    ]
+def call(kernel, outs, *args, smem=(), scratch=(), flops=0, space=pltpu.VMEM):
+    specs = [pl.BlockSpec(memory_space=pltpu.SMEM if i in smem else space) for i in range(len(args))]
     moved = sum(a.size * a.dtype.itemsize for a in args)
     return pl.pallas_call(
         kernel,
@@ -34,7 +32,7 @@
         in_specs=specs,
         out_specs=jax.tree.map(lambda _: pl.BlockSpec(memory_space=pltpu.VMEM), outs),
         scratch_shapes=list(scratch),
-        compiler_params=pltpu.CompilerParams(vmem_limit_bytes=40 * 1024 * 1024),
+        compiler_params=pltpu.CompilerParams(vmem_limit_bytes=(40 if space is pltpu.VMEM else 60) * 1024 * 1024),
         cost_estimate=pl.CostEstimate(flops=flops, bytes_accessed=moved, transcendentals=0),
     )(*args)
 
@@ -52,7 +50,18 @@
     stats_ref[...] = jnp.broadcast_to(note_ref[...][None], stats_ref.shape)
 
 
-def begin_kernel(x_ref, cache_ref, gain_ref, shift_ref, raw_ref, later_ref, stats_ref, note_ref):
+def begin_kernel(
+    place_ref, x_hbm, cache_hbm, gain_hbm, shift_hbm, w_hbm,
+    raw_ref, later_ref, stats_ref, o_ref, x_ref, cache_ref, gain_ref, shift_ref, w_ref, note_ref, sems,
+):
+    pairs = (
+        (x_hbm, x_ref), (cache_hbm, cache_ref), (gain_hbm, gain_ref), (shift_hbm, shift_ref), (w_hbm, w_ref)
+    )
+    copies = [pltpu.make_async_copy(src, dst, sems.at[i]) for i, (src, dst) in enumerate(pairs)]
+    for copy in copies:
+        copy.start()
+    for copy in copies:
+        copy.wait()
     for r in range(8):
         for t in range(2):
             lanes = slice(128 * t, 128 * (t + 1))
@@ -60,6 +69,15 @@
             later_ref[r, :, lanes] = cache_ref[1, t, r]
         for t in range(4):
             raw_ref[r, :, 256 + 128 * t : 384 + 128 * t] = x_ref[t, r]
+    for q in range(4):
+        place = lax.rem(q + 4 - place_ref[1], 4)
+        for layer in range(2):
+            for dt in range(3):
+                for dc in range(3):
+                    taps = [
+                        w_ref[layer, 9 * dt + 3 * dr + dc, :, 64 * q : 64 * (q + 1)] for dr in range(3)
+                    ]
+                    o_ref[place, layer, dt, dc] = jnp.concatenate(taps, axis=1)
     x = x_ref[...].astype(F32).reshape(32, 2, GROUP, 128)
     put_stats(x, gain_ref, shift_ref, 0, note_ref, stats_ref)
 
@@ -125,25 +143,33 @@
                 slab_ref[r, b, :, 256 + 128 * t : 384 + 128 * t] = y.astype(BF16)
 
 
+def row_of(refs, above_ref, below_ref, k, r):
+    if r == 0:
+        return above_ref.at[k]
+    return below_ref.at[k] if r == 9 else refs[k].at[r - 1]
+
+
 def first_kernel(
-    place_ref, edge_ref, a_ref, b_ref, c_ref, d_ref, stats_ref, w0, w1, w2, w3, o_ref, affine_ref, slab_ref, held_ref
+    place_ref, edge_ref, a_ref, b_ref, c_ref, d_ref, above_ref, below_ref, stats_ref,
+    w0, w1, w2, w3, o_ref, affine_ref, slab_ref, held_ref,
 ):
     get_affine(stats_ref, affine_ref)
     refs = (a_ref, b_ref, c_ref, d_ref)
     for k in range(4):
         b = place_ref[2 + k]
         for r in range(10):
-            slab_ref[r, b, :, 0:256] = refs[k][r, :, 0:256]
+            slab_ref[r, b, :, 0:256] = row_of(refs, above_ref, below_ref, k, r)[:, 0:256]
 
     def x_of(k, r, t):
-        return refs[k][r, :, 256 + 128 * t : 384 + 128 * t]
+        return row_of(refs, above_ref, below_ref, k, r)[:, 256 + 128 * t : 384 + 128 * t]
 
     norm_rows(x_of, place_ref, edge_ref, affine_ref, slab_ref)
     convolve(0, place_ref, (w0, w1, w2, w3), o_ref, slab_ref, held_ref)
 
 
 def second_kernel(
-    place_ref, edge_ref, a_ref, b_ref, c_ref, d_ref, ca_ref, cb_ref, cc_ref, cd_ref,
+    place_ref, edge_ref, a_ref, b_ref, c_ref, d_ref, above_ref, below_ref,
+    ca_ref, cb_ref, cc_ref, cd_ref, cabove_ref, cbelow_ref,
     stats_ref, w0, w1, w2, w3, o_ref, affine_ref, slab_ref, held_ref,
 ):
     get_affine(stats_ref, affine_ref)
@@ -152,10 +178,10 @@
     for k in range(4):
         b = place_ref[2 + k]
         for r in range(10):
-            slab_ref[r, b, :, 0:256] = caches[k][r]
+            slab_ref[r, b, :, 0:256] = row_of(caches, cabove_ref, cbelow_ref, k, r)[...]
 
     def x_of(k, r, t):
-        return refs[k][r, :, 128 * t : 128 * (t + 1)]
+        return row_of(refs, above_ref, below_ref, k, r)[:, 128 * t : 128 * (t + 1)]
 
     norm_rows(x_of, place_ref, edge_ref, affine_ref, slab_ref)
     convolve(1, place_ref, (w0, w1, w2, w3), o_ref, slab_ref, held_ref)
@@ -186,12 +212,12 @@
     return jax.ShapeDtypeStruct(shape, dtype)
 
 
-def with_rows(x):
+def rows_beside(blocks):
     up = [(i, i + 1) for i in range(15)]
     down = [(i + 1, i) for i in range(15)]
-    above = lax.ppermute(x[7:8], ROW, up)
-    below = lax.ppermute(x[0:1], ROW, down)
-    return jnp.concatenate([above, x, below], axis=0)
+    above = lax.ppermute(jnp.stack([x[7] for x in blocks]), ROW, up)
+    below = lax.ppermute(jnp.stack([x[0] for x in blocks]), ROW, down)
+    return [above, below]
 
 
 def near(x):
@@ -200,17 +226,6 @@
 
 def exchange(x, axes):
     return lax.all_to_all(x, axes, 0, 0, tiled=True)
-
-
-def weights_of(weight):
-    me = lax.axis_index("zh")
-    weight = weight.reshape(2, 16, 3, 3, 3, 4, 64).transpose(5, 0, 2, 4, 1, 3, 6)
-    weight = weight.reshape(4, 2, 3, 3, 16, 192)
-    held = [lax.dynamic_index_in_dim(weight, lax.rem(me + d, 4), 0, keepdims=False) for d in range(4)]
-    moved = [
-        lax.ppermute(held[d], "zh", [(i, (i + d) % 4) for i in range(4)]) for d in range(1, 4)
-    ]
-    return [held[0]] + moved
 
 
 def local(frames, cache, norm_gain, norm_shift, conv_weight, conv_bias):
@@ -220,16 +235,30 @@
     place = jnp.stack([row, lax.axis_index("zh"), here, here ^ 1, here ^ 2, here ^ 3]).astype(jnp.int32)
     note = pltpu.VMEM((8, 128), F32)
 
-    raw, later, stats = call(
+    raw, later, stats, held = call(
         begin_kernel,
-        (struct((8, 16, 768)), struct((8, 16, 256)), struct((64, 8, 128), F32)),
-        frames, cache, norm_gain, norm_shift,
-        scratch=(note,),
-    )
+        (
+            struct((8, 16, 768)), struct((8, 16, 256)), struct((64, 8, 128), F32),
+            struct((4, 2, 3, 3, 16, 192)),
+        ),
+        place, frames, cache, norm_gain, norm_shift, conv_weight.transpose(0, 2, 1, 3),
+        smem=(0,),
+        scratch=(
+            pltpu.VMEM((4, 8, 16, 128), BF16), pltpu.VMEM((2, 2, 8, 16, 128), BF16),
+            pltpu.VMEM((2, 16), F32), pltpu.VMEM((2, 16), F32), pltpu.VMEM((2, 27, 16, 256), BF16),
+            note, pltpu.SemaphoreType.DMA((5,)),
+        ),
+        space=pl.ANY,
+    )
+    raw = near(raw)
+    weights = [held[0]] + [
+        lax.ppermute(held[d], "zh", [(i, (i + d) % 4) for i in range(4)]) for d in range(1, 4)
+    ]
     stats = exchange(stats, ROW + NEAR)
-    raw = near(with_rows(raw))
-    weights = weights_of(conv_weight)
-    later = near(with_rows(later))
+    raw = raw + rows_beside(raw)
+    raw, later = lax.optimization_barrier((raw, later))
+    later = near(later)
+    later = later + rows_beside(later)
     bias = jnp.broadcast_to(conv_bias[:, :, None], (2, 16, 128))
     scratch = (
         pltpu.VMEM((3, 4, 16, 128), F32),
@@ -243,14 +272,16 @@
         smem=(0, 1), scratch=scratch, flops=flops,
     )
     partial = exchange(partial, "zh")
+    partial, later = lax.optimization_barrier((partial, later))
     middle, stats = call(
         merge_kernel,
         (struct((8, 16, 512)), struct((64, 8, 128), F32)),
         partial, bias[0], norm_gain, norm_shift,
         scratch=(note,),
     )
+    middle = near(middle)
     stats = exchange(stats, ROW + NEAR)
-    middle = near(with_rows(middle))
+    middle = middle + rows_beside(middle)
     partial = call(
         second_kernel, struct((4, 8, 16, 512)), place, edge, *middle, *later, stats, *weights,
         smem=(0, 1), scratch=scratch, flops=flops,

time: 132 us -> 119 us (0.902)
  the two profiles are of different devices: /device:TPU:8 before, /device:TPU:27 now
where the time goes in v3:
time: 119 us; the launch traced here: 117 us
  starting transfers between devices  58.3 us (49%)
  waiting for transfers between devices  24.8 us (21%)
  blocking collectives  19.6 us (16%)
  Pallas kernels  11 us (9%)
  local copies, waits for them, and re-layouts  3.22 us (3%)
    ppermute x3, waiting for transfers between devices, rows_beside(): below = lax.ppermute(jnp.stack([x[0] for x in blocks]), ROW, down)  22.3 us
    all_to_all x1, blocking collectives, exchange(): return lax.all_to_all(x, axes, 0, 0, tiled=True)  19.6 us
    all_to_all x3, starting transfers between devices, exchange(): return lax.all_to_all(x, axes, 0, 0, tiled=True)  19.6 us
    ppermute x3, starting transfers between devices, rows_beside(): above = lax.ppermute(jnp.stack([x[7] for x in blocks]), ROW, up)  12.1 us
    ppermute x9, starting transfers between devices, near(): lax.ppermute(x, NEAR, [(i, i ^ k) for i in range(4)])  11.1 us
    pallas_call x5, Pallas kernels, call(): pl.pallas_call(kernel, out_shape=outs, in_specs=specs, out_specs=jax.tree...  11 us
    ppermute x3, starting transfers between devices, local(): lax.ppermute(held[d], 'zh', [(i, (i + d) % 4) for i in range(4)])  9.74 us
    ppermute x3, starting transfers between devices, rows_beside(): below = lax.ppermute(jnp.stack([x[0] for x in blocks]), ROW, down)  5.76 us
  transfers between devices with their start and end apart: 21, of which 4 were waited for; matrix products, arithmetic and copies ran while one was open for 1% of the time, Pallas kernels for 3%

profile of v3, /device:TPU:27, one launch (start us, length us, event | category | flops | bytes accessed | tf_op | source)
XLA Modules:
  0.0 117.5 jit_solution(5297783596075924104)
XLA Ops:
  0.0 0.6 stack.54.place_ref
  0.6 3.0 %shard_map.64 = (bf16[8,16,768]{2,1,0:T(8,128)(2,1)}, bf16[8,16,256]{2,1,0:T(8,128)(2,1)}, f32[64,8,128]{2,1,0:T(8,128)}, bf16[4,2,3,3,16,192]{5,4,3,2,1,0:T(8,128)(2,1)}) custom-call(s32[6]{0:T(128)} %stack.54.place_ref, bf16[4,8,16,128]{3,2,1,0:T(8,128)(2,1)} %x_ref.1, bf16[2,2,8,16,128]{4,3,2,1,0:T(8,128)(2,1)} %cache_hbm.1, f32[2,16]{1,0:T(2,128)} %gain_ref.1, ...), custom_call_target="tpu_custom_call" | custom-call | bytes 704792 | tf_op jit(solution)/shard_map/pallas_call | solution.py:29
  3.6 0.3 collective-permute-start
  4.0 1.6 %collective-permute-start.1 = (bf16[8,16,768]{2,1,0:T(8,128)(2,1)}, bf16[8,16,768]{2,1,0:T(8,128)(2,1)S(1)}, u32[]{:S(2)}, u32[]{:S(2)}) collective-permute-start(bf16[8,16,768]{2,1,0:T(8,128)(2,1)} %get-tuple-element.27.a_ref), channel_id=1, source_target_pairs={{0,2},{1,3},{2,0},{3,1},{4,6},{5,7},{6,4},{7,5},{8,10},{9,11},{10,... | collective-permute-start | bytes 589832 | tf_op jit(solution)/shard_map/ppermute | solution.py:224
  5.6 0.9 collective-permute-start.2
  6.5 10.1 %all-to-all-start = ((f32[64,8,128]{2,1,0:T(8,128)}), f32[64,8,128]{2,1,0:T(8,128)S(1)}, u32[]{:S(2)}, u32[]{:S(2)}) async-start(f32[64,8,128]{2,1,0:T(8,128)} %get-tuple-element.33), calls=%async_computation | async-start | bytes 524288 | tf_op jit(solution)/shard_map/all_to_all | solution.py:228
  16.6 1.2 %slice_bitcast_fusion = (bf16[2,3,3,16,192]{4,3,2,1,0:T(8,128)(2,1)S(1)}, bf16[2,3,3,16,192]{4,3,2,1,0:T(8,128)(2,1)S(1)}, bf16[2,3,3,16,192]{4,3,2,1,0:T(8,128)(2,1)S(1)}, bf16[2,3,3,16,192]{4,3,2,1,0:T(8,128)(2,1)S(1)}) fusion(bf16[4,2,3,3,16,192]{5,4,3,2,1,0:T(8,128)(2,1)} %get-tuple-element.34), kind=kLoop, calls=%fused_computation | loop fusion | bytes 884736 | tf_op jit(solution)/shard_map/squeeze | solution.py:255
  17.8 3.1 %collective-permute-start.5 = (bf16[2,3,3,16,192]{4,3,2,1,0:T(8,128)(2,1)S(1)}, bf16[2,3,3,16,192]{4,3,2,1,0:T(8,128)(2,1)S(1)}, u32[]{:S(2)}, u32[]{:S(2)}) collective-permute-start(bf16[2,3,3,16,192]{4,3,2,1,0:T(8,128)(2,1)S(1)} %get-tuple-element.47), channel_id=1, source_target_pairs={{0,4},{4,8},{8,12},{12,0},{1,5},{5,9},{9,13},{13,1},{2,6},{6,10},{... | collective-permute-start | bytes 331784 | tf_op jit(solution)/shard_map/ppermute | solution.py:255
  20.9 4.2 %collective-permute-start.6 = (bf16[2,3,3,16,192]{4,3,2,1,0:T(8,128)(2,1)S(1)}, bf16[2,3,3,16,192]{4,3,2,1,0:T(8,128)(2,1)S(1)}, u32[]{:S(2)}, u32[]{:S(2)}) collective-permute-start(bf16[2,3,3,16,192]{4,3,2,1,0:T(8,128)(2,1)S(1)} %get-tuple-element.46), channel_id=1, source_target_pairs={{0,8},{4,12},{8,0},{12,4},{1,9},{5,13},{9,1},{13,5},{2,10},{6,14},... | collective-permute-start | bytes 331784 | tf_op jit(solution)/shard_map/ppermute | solution.py:255
  25.1 2.5 %collective-permute-start.7 = (bf16[2,3,3,16,192]{4,3,2,1,0:T(8,128)(2,1)S(1)}, bf16[2,3,3,16,192]{4,3,2,1,0:T(8,128)(2,1)S(1)}, u32[]{:S(2)}, u32[]{:S(2)}) collective-permute-start(bf16[2,3,3,16,192]{4,3,2,1,0:T(8,128)(2,1)S(1)} %get-tuple-element.45), channel_id=1, source_target_pairs={{0,12},{4,0},{8,4},{12,8},{1,13},{5,1},{9,5},{13,9},{2,14},{6,2},{... | collective-permute-start | bytes 331784 | tf_op jit(solution)/shard_map/ppermute | solution.py:255
  27.7 4.8 %collective-permute-start.3 = (bf16[4,16,768]{2,1,0:T(8,128)(2,1)S(1)}, bf16[4,16,768]{2,1,0:T(8,128)(2,1)S(1)}, u32[]{:S(2)}, u32[]{:S(2)}) collective-permute-start(bf16[4,16,768]{2,1,0:T(8,128)(2,1)S(1)} %pad_maximum_fusion), channel_id=1, source_target_pairs={{0,16},{16,32},{32,48},{48,64},{64,80},{80,96},{96,112},{112,128},... | collective-permute-start | bytes 294920 | tf_op jit(solution)/shard_map/ppermute | solution.py:218
  32.5 0.0 copy-start.4
  32.5 1.9 %collective-permute-start.4 = (bf16[4,16,768]{2,1,0:T(8,128)(2,1)S(1)}, bf16[4,16,768]{2,1,0:T(8,128)(2,1)S(1)}, u32[]{:S(2)}, u32[]{:S(2)}) collective-permute-start(bf16[4,16,768]{2,1,0:T(8,128)(2,1)S(1)} %pad_maximum_fusion.1), channel_id=1, source_target_pairs={{16,0},{32,16},{48,32},{64,48},{80,64},{96,80},{112,96},{128,112},... | collective-permute-start | bytes 294920 | tf_op jit(solution)/shard_map/ppermute | solution.py:219
  34.5 0.1 add_convert_fusion.edge_ref
  34.5 0.0 collective-permute-done.3.above_ref
  34.5 8.2 %collective-permute-done.4.below_ref = bf16[4,16,768]{2,1,0:T(8,128)(2,1)S(1)} collective-permute-done((bf16[4,16,768]{2,1,0:T(8,128)(2,1)S(1)}, bf16[4,16,768]{2,1,0:T(8,128)(2,1)S(1)}, u32[]{:S(2)}, u32[]{:S(2)}) %collective-permute-start.4) | collective-permute-done | bytes 98336 | tf_op jit(solution)/shard_map/ppermute | solution.py:219
  42.7 0.8 collective-permute-start.8
  43.5 1.6 %collective-permute-start.10 = (bf16[8,16,256]{2,1,0:T(8,128)(2,1)S(1)}, bf16[8,16,256]{2,1,0:T(8,128)(2,1)S(1)}, u32[]{:S(2)}, u32[]{:S(2)}) collective-permute-start(bf16[8,16,256]{2,1,0:T(8,128)(2,1)S(1)} %copy-done.4), channel_id=1, source_target_pairs={{0,3},{1,2},{2,1},{3,0},{4,7},{5,6},{6,5},{7,4},{8,11},{9,10},{10,... | collective-permute-start | bytes 196616 | tf_op jit(solution)/shard_map/ppermute | solution.py:224
  45.2 2.4 %collective-permute-done.10.cd_ref = bf16[8,16,256]{2,1,0:T(8,128)(2,1)S(1)} collective-permute-done((bf16[8,16,256]{2,1,0:T(8,128)(2,1)S(1)}, bf16[8,16,256]{2,1,0:T(8,128)(2,1)S(1)}, u32[]{:S(2)}, u32[]{:S(2)}) %collective-permute-start.10) | collective-permute-done | bytes 65568 | tf_op jit(solution)/shard_map/ppermute | solution.py:224
  47.6 1.3 %collective-permute-start.9 = (bf16[8,16,256]{2,1,0:T(8,128)(2,1)S(1)}, bf16[8,16,256]{2,1,0:T(8,128)(2,1)S(1)}, u32[]{:S(2)}, u32[]{:S(2)}) collective-permute-start(bf16[8,16,256]{2,1,0:T(8,128)(2,1)S(1)} %copy-done.4), channel_id=1, source_target_pairs={{0,2},{1,3},{2,0},{3,1},{4,6},{5,7},{6,4},{7,5},{8,10},{9,11},{10,... | collective-permute-start | bytes 196616 | tf_op jit(solution)/shard_map/ppermute | solution.py:224
  48.9 0.0 collective-permute-done.5.w1
  48.9 0.0 collective-permute-done.6.w2
  48.9 0.0 all-to-all-done.stats_ref
  48.9 0.6 copy-done.5
  49.5 3.6 %shard_map.65 = bf16[4,8,16,512]{3,2,1,0:T(8,128)(2,1)} custom-call(s32[6]{0:T(128)S(1)} %copy-done.5, f32[2]{0:T(128)S(1)} %add_convert_fusion.edge_ref, bf16[8,16,768]{2,1,0:T(8,128)(2,1)S(1)} %copy-done.1, bf16[8,16,768]{2,1,0:T(8,128)(2,1)S(1)} %collective-permute-done.b_ref, bf16[8,16,768]{2,1,0:T(8,128)(2,1)S(1)} %collective-permute-done.1.c_ref, ...), custom_call_target="tpu_custom_call" | custom-call | flops 905969664 | bytes 1687584 | tf_op jit(solution)/shard_map/pallas_call | solution.py:29
  53.1 3.5 %all-to-all-start.1 = ((bf16[4,8,16,512]{3,2,1,0:T(8,128)(2,1)}), bf16[4,8,16,512]{3,2,1,0:T(8,128)(2,1)S(1)}, u32[]{:S(2)}, u32[]{:S(2)}) async-start(bf16[4,8,16,512]{3,2,1,0:T(8,128)(2,1)} %shard_map.65), calls=%async_computation.1 | async-start | bytes 1048576 | tf_op jit(solution)/shard_map/all_to_all | solution.py:228
  56.6 0.0 collective-permute-done.8.cb_ref
  56.6 3.3 %collective-permute-start.11 = (bf16[4,16,256]{2,1,0:T(8,128)(2,1)S(1)}, bf16[4,16,256]{2,1,0:T(8,128)(2,1)S(1)}, u32[]{:S(2)}, u32[]{:S(2)}) collective-permute-start(bf16[4,16,256]{2,1,0:T(8,128)(2,1)S(1)} %pad_maximum_fusion.4), channel_id=1, source_target_pairs={{0,16},{16,32},{32,48},{48,64},{64,80},{80,96},{96,112},{112,128},... | collective-permute-start | bytes 98312 | tf_op jit(solution)/shard_map/ppermute | solution.py:218
  59.9 0.0 copy-start.6
  59.9 1.9 %collective-permute-start.12 = (bf16[4,16,256]{2,1,0:T(8,128)(2,1)S(1)}, bf16[4,16,256]{2,1,0:T(8,128)(2,1)S(1)}, u32[]{:S(2)}, u32[]{:S(2)}) collective-permute-start(bf16[4,16,256]{2,1,0:T(8,128)(2,1)S(1)} %pad_maximum_fusion.5), channel_id=1, source_target_pairs={{16,0},{32,16},{48,32},{64,48},{80,64},{96,80},{112,96},{128,112},... | collective-permute-start | bytes 98312 | tf_op jit(solution)/shard_map/ppermute | solution.py:219
  61.9 6.9 %collective-permute-done.12.cbelow_ref = bf16[4,16,256]{2,1,0:T(8,128)(2,1)S(1)} collective-permute-done((bf16[4,16,256]{2,1,0:T(8,128)(2,1)S(1)}, bf16[4,16,256]{2,1,0:T(8,128)(2,1)S(1)}, u32[]{:S(2)}, u32[]{:S(2)}) %collective-permute-start.12) | collective-permute-done | bytes 32800 | tf_op jit(solution)/shard_map/ppermute | solution.py:219
  68.8 0.0 all-to-all-done.1.part_ref
  68.8 0.1 broadcast_in_dim.13.bias_ref
  68.8 0.6 copy-done.2
  69.5 0.0 copy-done.3
  69.5 0.9 shard_map.66
  70.4 3.2 %collective-permute-start.13 = (bf16[8,16,512]{2,1,0:T(8,128)(2,1)S(1)}, bf16[8,16,512]{2,1,0:T(8,128)(2,1)S(1)}, u32[]{:S(2)}, u32[]{:S(2)}) collective-permute-start(bf16[8,16,512]{2,1,0:T(8,128)(2,1)S(1)} %get-tuple-element.37.a_ref), channel_id=1, source_target_pairs={{0,1},{1,0},{2,3},{3,2},{4,5},{5,4},{6,7},{7,6},{8,9},{9,8},{10,11... | collective-permute-start | bytes 393224 | tf_op jit(solution)/shard_map/ppermute | solution.py:224
  73.6 0.0 collective-permute-start.14
  73.6 1.2 %collective-permute-start.15 = (bf16[8,16,512]{2,1,0:T(8,128)(2,1)S(1)}, bf16[8,16,512]{2,1,0:T(8,128)(2,1)S(1)}, u32[]{:S(2)}, u32[]{:S(2)}) collective-permute-start(bf16[8,16,512]{2,1,0:T(8,128)(2,1)S(1)} %get-tuple-element.37.a_ref), channel_id=1, source_target_pairs={{0,3},{1,2},{2,1},{3,0},{4,7},{5,6},{6,5},{7,4},{8,11},{9,10},{10,... | collective-permute-start | bytes 393224 | tf_op jit(solution)/shard_map/ppermute | solution.py:224
  74.8 6.1 %all-to-all-start.2 = ((f32[64,8,128]{2,1,0:T(8,128)}), f32[64,8,128]{2,1,0:T(8,128)S(1)}, u32[]{:S(2)}, u32[]{:S(2)}) async-start(f32[64,8,128]{2,1,0:T(8,128)} %get-tuple-element.44), calls=%async_computation.2 | async-start | bytes 524288 | tf_op jit(solution)/shard_map/all_to_all | solution.py:228
  81.0 4.0 %collective-permute-start.16 = (bf16[4,16,512]{2,1,0:T(8,128)(2,1)S(1)}, bf16[4,16,512]{2,1,0:T(8,128)(2,1)S(1)}, u32[]{:S(2)}, u32[]{:S(2)}) collective-permute-start(bf16[4,16,512]{2,1,0:T(8,128)(2,1)S(1)} %pad_maximum_fusion.2), channel_id=1, source_target_pairs={{0,16},{16,32},{32,48},{48,64},{64,80},{80,96},{96,112},{112,128},... | collective-permute-start | bytes 196616 | tf_op jit(solution)/shard_map/ppermute | solution.py:218
  85.0 1.9 %collective-permute-start.17 = (bf16[4,16,512]{2,1,0:T(8,128)(2,1)S(1)}, bf16[4,16,512]{2,1,0:T(8,128)(2,1)S(1)}, u32[]{:S(2)}, u32[]{:S(2)}) collective-permute-start(bf16[4,16,512]{2,1,0:T(8,128)(2,1)S(1)} %pad_maximum_fusion.3), channel_id=1, source_target_pairs={{16,0},{32,16},{48,32},{64,48},{80,64},{96,80},{112,96},{128,112},... | collective-permute-start | bytes 196616 | tf_op jit(solution)/shard_map/ppermute | solution.py:219
  87.0 7.3 %collective-permute-done.17.below_ref = bf16[4,16,512]{2,1,0:T(8,128)(2,1)S(1)} collective-permute-done((bf16[4,16,512]{2,1,0:T(8,128)(2,1)S(1)}, bf16[4,16,512]{2,1,0:T(8,128)(2,1)S(1)}, u32[]{:S(2)}, u32[]{:S(2)}) %collective-permute-start.17) | collective-permute-done | bytes 65568 | tf_op jit(solution)/shard_map/ppermute | solution.py:219
  94.2 2.8 %shard_map.67 = bf16[4,8,16,512]{3,2,1,0:T(8,128)(2,1)S(1)} custom-call(s32[6]{0:T(128)S(1)} %copy-done.5, f32[2]{0:T(128)S(1)} %add_convert_fusion.edge_ref, bf16[8,16,512]{2,1,0:T(8,128)(2,1)S(1)} %get-tuple-element.37.a_ref, bf16[8,16,512]{2,1,0:T(8,128)(2,1)S(1)} %collective-permute-done.13.b_ref, bf16[8,16,512]{2,1,0:T(8,128)(2,1)S(1)} %collective-permute-done.14.c_ref, ...), custom_call_target="tpu_custom_call" | custom-call | flops 905969664 | bytes 1687584 | tf_op jit(solution)/shard_map/pallas_call | solution.py:29
  97.0 0.0 copy-start
  97.0 19.6 %all_to_all.20.part_ref = bf16[4,8,16,512]{3,2,1,0:T(8,128)(2,1)S(1)} all-to-all(bf16[4,8,16,512]{3,2,1,0:T(8,128)(2,1)S(1)} %shard_map.67), channel_id=1, replica_groups=mesh['xh'=2,'y'=4,'core'=2,'zh'=4,'zl'=2,'xl'=2] {'zh'}, dimensions={0} | all-to-all | bytes 1048576 | tf_op jit(solution)/shard_map/all_to_all | solution.py:228
  116.6 0.1 broadcast_in_dim.15.bias_ref
  116.7 0.8 shard_map.68
  (38 shorter events, 0.2 us)
Async XLA Ops:
  3.6 24.0 %collective-permute-start = (bf16[8,16,768]{2,1,0:T(8,128)(2,1)}, bf16[8,16,768]{2,1,0:T(8,128)(2,1)S(1)}, u32[]{:S(2)}, u32[]{:S(2)}) collective-permute-start(bf16[8,16,768]{2,1,0:T(8,128)(2,1)} %get-tuple-element.27.a_ref), channel_id=1, source_target_pairs={{0,1},{1,0},{2,3},{3,2},{4,5},{5,4},{6,7},{7,6},{8,9},{9,8},{10,11... | collective-permute-start | bytes 589832 | tf_op jit(solution)/shard_map/ppermute | solution.py:224
  4.0 23.6 %collective-permute-start.1 = (bf16[8,16,768]{2,1,0:T(8,128)(2,1)}, bf16[8,16,768]{2,1,0:T(8,128)(2,1)S(1)}, u32[]{:S(2)}, u32[]{:S(2)}) collective-permute-start(bf16[8,16,768]{2,1,0:T(8,128)(2,1)} %get-tuple-element.27.a_ref), channel_id=1, source_target_pairs={{0,2},{1,3},{2,0},{3,1},{4,6},{5,7},{6,4},{7,5},{8,10},{9,11},{10,... | collective-permute-start | bytes 589832 | tf_op jit(solution)/shard_map/ppermute | solution.py:224
  5.6 19.5 %collective-permute-start.2 = (bf16[8,16,768]{2,1,0:T(8,128)(2,1)}, bf16[8,16,768]{2,1,0:T(8,128)(2,1)S(1)}, u32[]{:S(2)}, u32[]{:S(2)}) collective-permute-start(bf16[8,16,768]{2,1,0:T(8,128)(2,1)} %get-tuple-element.27.a_ref), channel_id=1, source_target_pairs={{0,3},{1,2},{2,1},{3,0},{4,7},{5,6},{6,5},{7,4},{8,11},{9,10},{10,... | collective-permute-start | bytes 589832 | tf_op jit(solution)/shard_map/ppermute | solution.py:224
  6.5 42.4 %all-to-all-start = ((f32[64,8,128]{2,1,0:T(8,128)}), f32[64,8,128]{2,1,0:T(8,128)S(1)}, u32[]{:S(2)}, u32[]{:S(2)}) async-start(f32[64,8,128]{2,1,0:T(8,128)} %get-tuple-element.33), calls=%async_computation | async-start | bytes 524288 | tf_op jit(solution)/shard_map/all_to_all | solution.py:228
  16.6 8.5 %copy-start.1 = (bf16[8,16,768]{2,1,0:T(8,128)(2,1)S(1)}, bf16[8,16,768]{2,1,0:T(8,128)(2,1)}, u32[]{:S(2)}) copy-start(bf16[8,16,768]{2,1,0:T(8,128)(2,1)} %get-tuple-element.27.a_ref) | copy-start | bytes 589828
  17.8 31.1 %collective-permute-start.5 = (bf16[2,3,3,16,192]{4,3,2,1,0:T(8,128)(2,1)S(1)}, bf16[2,3,3,16,192]{4,3,2,1,0:T(8,128)(2,1)S(1)}, u32[]{:S(2)}, u32[]{:S(2)}) collective-permute-start(bf16[2,3,3,16,192]{4,3,2,1,0:T(8,128)(2,1)S(1)} %get-tuple-element.47), channel_id=1, source_target_pairs={{0,4},{4,8},{8,12},{12,0},{1,5},{5,9},{9,13},{13,1},{2,6},{6,10},{... | collective-permute-start | bytes 331784 | tf_op jit(solution)/shard_map/ppermute | solution.py:255
  20.9 28.0 %collective-permute-start.6 = (bf16[2,3,3,16,192]{4,3,2,1,0:T(8,128)(2,1)S(1)}, bf16[2,3,3,16,192]{4,3,2,1,0:T(8,128)(2,1)S(1)}, u32[]{:S(2)}, u32[]{:S(2)}) collective-permute-start(bf16[2,3,3,16,192]{4,3,2,1,0:T(8,128)(2,1)S(1)} %get-tuple-element.46), channel_id=1, source_target_pairs={{0,8},{4,12},{8,0},{12,4},{1,9},{5,13},{9,1},{13,5},{2,10},{6,14},... | collective-permute-start | bytes 331784 | tf_op jit(solution)/shard_map/ppermute | solution.py:255
  25.1 23.8 %collective-permute-start.7 = (bf16[2,3,3,16,192]{4,3,2,1,0:T(8,128)(2,1)S(1)}, bf16[2,3,3,16,192]{4,3,2,1,0:T(8,128)(2,1)S(1)}, u32[]{:S(2)}, u32[]{:S(2)}) collective-permute-start(bf16[2,3,3,16,192]{4,3,2,1,0:T(8,128)(2,1)S(1)} %get-tuple-element.45), channel_id=1, source_target_pairs={{0,12},{4,0},{8,4},{12,8},{1,13},{5,1},{9,5},{13,9},{2,14},{6,2},{... | collective-permute-start | bytes 331784 | tf_op jit(solution)/shard_map/ppermute | solution.py:255
  27.7 6.9 %collective-permute-start.3 = (bf16[4,16,768]{2,1,0:T(8,128)(2,1)S(1)}, bf16[4,16,768]{2,1,0:T(8,128)(2,1)S(1)}, u32[]{:S(2)}, u32[]{:S(2)}) collective-permute-start(bf16[4,16,768]{2,1,0:T(8,128)(2,1)S(1)} %pad_maximum_fusion), channel_id=1, source_target_pairs={{0,16},{16,32},{32,48},{48,64},{64,80},{80,96},{96,112},{112,128},... | collective-permute-start | bytes 294920 | tf_op jit(solution)/shard_map/ppermute | solution.py:218
  32.5 10.2 %copy-start.4 = (bf16[8,16,256]{2,1,0:T(8,128)(2,1)S(1)}, bf16[8,16,256]{2,1,0:T(8,128)(2,1)}, u32[]{:S(2)}) copy-start(bf16[8,16,256]{2,1,0:T(8,128)(2,1)} %get-tuple-element.38.ca_ref) | copy-start | bytes 196612
  32.5 10.2 %collective-permute-start.4 = (bf16[4,16,768]{2,1,0:T(8,128)(2,1)S(1)}, bf16[4,16,768]{2,1,0:T(8,128)(2,1)S(1)}, u32[]{:S(2)}, u32[]{:S(2)}) collective-permute-start(bf16[4,16,768]{2,1,0:T(8,128)(2,1)S(1)} %pad_maximum_fusion.1), channel_id=1, source_target_pairs={{16,0},{32,16},{48,32},{64,48},{80,64},{96,80},{112,96},{128,112},... | collective-permute-start | bytes 294920 | tf_op jit(solution)/shard_map/ppermute | solution.py:219
  42.7 13.9 %collective-permute-start.8 = (bf16[8,16,256]{2,1,0:T(8,128)(2,1)S(1)}, bf16[8,16,256]{2,1,0:T(8,128)(2,1)S(1)}, u32[]{:S(2)}, u32[]{:S(2)}) collective-permute-start(bf16[8,16,256]{2,1,0:T(8,128)(2,1)S(1)} %copy-done.4), channel_id=1, source_target_pairs={{0,1},{1,0},{2,3},{3,2},{4,5},{5,4},{6,7},{7,6},{8,9},{9,8},{10,11... | collective-permute-start | bytes 196616 | tf_op jit(solution)/shard_map/ppermute | solution.py:224
  43.5 4.0 %collective-permute-start.10 = (bf16[8,16,256]{2,1,0:T(8,128)(2,1)S(1)}, bf16[8,16,256]{2,1,0:T(8,128)(2,1)S(1)}, u32[]{:S(2)}, u32[]{:S(2)}) collective-permute-start(bf16[8,16,256]{2,1,0:T(8,128)(2,1)S(1)} %copy-done.4), channel_id=1, source_target_pairs={{0,3},{1,2},{2,1},{3,0},{4,7},{5,6},{6,5},{7,4},{8,11},{9,10},{10,... | collective-permute-start | bytes 196616 | tf_op jit(solution)/shard_map/ppermute | solution.py:224
  47.6 9.0 %collective-permute-start.9 = (bf16[8,16,256]{2,1,0:T(8,128)(2,1)S(1)}, bf16[8,16,256]{2,1,0:T(8,128)(2,1)S(1)}, u32[]{:S(2)}, u32[]{:S(2)}) collective-permute-start(bf16[8,16,256]{2,1,0:T(8,128)(2,1)S(1)} %copy-done.4), channel_id=1, source_target_pairs={{0,2},{1,3},{2,0},{3,1},{4,6},{5,7},{6,4},{7,5},{8,10},{9,11},{10,... | collective-permute-start | bytes 196616 | tf_op jit(solution)/shard_map/ppermute | solution.py:224
  48.9 0.6 copy-start.5
  53.1 15.7 %all-to-all-start.1 = ((bf16[4,8,16,512]{3,2,1,0:T(8,128)(2,1)}), bf16[4,8,16,512]{3,2,1,0:T(8,128)(2,1)S(1)}, u32[]{:S(2)}, u32[]{:S(2)}) async-start(bf16[4,8,16,512]{3,2,1,0:T(8,128)(2,1)} %shard_map.65), calls=%async_computation.1 | async-start | bytes 1048576 | tf_op jit(solution)/shard_map/all_to_all | solution.py:228
  56.6 5.3 %collective-permute-start.11 = (bf16[4,16,256]{2,1,0:T(8,128)(2,1)S(1)}, bf16[4,16,256]{2,1,0:T(8,128)(2,1)S(1)}, u32[]{:S(2)}, u32[]{:S(2)}) collective-permute-start(bf16[4,16,256]{2,1,0:T(8,128)(2,1)S(1)} %pad_maximum_fusion.4), channel_id=1, source_target_pairs={{0,16},{16,32},{32,48},{48,64},{64,80},{80,96},{96,112},{112,128},... | collective-permute-start | bytes 98312 | tf_op jit(solution)/shard_map/ppermute | solution.py:218
  59.9 2.0 %copy-start.6 = (f32[2,16]{1,0:T(2,128)S(1)}, f32[2,16]{1,0:T(2,128)}, u32[]{:S(2)}) copy-start(f32[2,16]{1,0:T(2,128)} %param.11) | copy-start | bytes 388
  59.9 8.8 %collective-permute-start.12 = (bf16[4,16,256]{2,1,0:T(8,128)(2,1)S(1)}, bf16[4,16,256]{2,1,0:T(8,128)(2,1)S(1)}, u32[]{:S(2)}, u32[]{:S(2)}) collective-permute-start(bf16[4,16,256]{2,1,0:T(8,128)(2,1)S(1)} %pad_maximum_fusion.5), channel_id=1, source_target_pairs={{16,0},{32,16},{48,32},{64,48},{80,64},{96,80},{112,96},{128,112},... | collective-permute-start | bytes 98312 | tf_op jit(solution)/shard_map/ppermute | solution.py:219
  68.8 0.7 copy-start.2
  68.8 0.7 copy-start.3
  70.4 10.6 %collective-permute-start.13 = (bf16[8,16,512]{2,1,0:T(8,128)(2,1)S(1)}, bf16[8,16,512]{2,1,0:T(8,128)(2,1)S(1)}, u32[]{:S(2)}, u32[]{:S(2)}) collective-permute-start(bf16[8,16,512]{2,1,0:T(8,128)(2,1)S(1)} %get-tuple-element.37.a_ref), channel_id=1, source_target_pairs={{0,1},{1,0},{2,3},{3,2},{4,5},{5,4},{6,7},{7,6},{8,9},{9,8},{10,11... | collective-permute-start | bytes 393224 | tf_op jit(solution)/shard_map/ppermute | solution.py:224
  73.6 7.3 %collective-permute-start.14 = (bf16[8,16,512]{2,1,0:T(8,128)(2,1)S(1)}, bf16[8,16,512]{2,1,0:T(8,128)(2,1)S(1)}, u32[]{:S(2)}, u32[]{:S(2)}) collective-permute-start(bf16[8,16,512]{2,1,0:T(8,128)(2,1)S(1)} %get-tuple-element.37.a_ref), channel_id=1, source_target_pairs={{0,2},{1,3},{2,0},{3,1},{4,6},{5,7},{6,4},{7,5},{8,10},{9,11},{10,... | collective-permute-start | bytes 393224 | tf_op jit(solution)/shard_map/ppermute | solution.py:224
  73.6 7.3 %collective-permute-start.15 = (bf16[8,16,512]{2,1,0:T(8,128)(2,1)S(1)}, bf16[8,16,512]{2,1,0:T(8,128)(2,1)S(1)}, u32[]{:S(2)}, u32[]{:S(2)}) collective-permute-start(bf16[8,16,512]{2,1,0:T(8,128)(2,1)S(1)} %get-tuple-element.37.a_ref), channel_id=1, source_target_pairs={{0,3},{1,2},{2,1},{3,0},{4,7},{5,6},{6,5},{7,4},{8,11},{9,10},{10,... | collective-permute-start | bytes 393224 | tf_op jit(solution)/shard_map/ppermute | solution.py:224
  74.8 19.4 %all-to-all-start.2 = ((f32[64,8,128]{2,1,0:T(8,128)}), f32[64,8,128]{2,1,0:T(8,128)S(1)}, u32[]{:S(2)}, u32[]{:S(2)}) async-start(f32[64,8,128]{2,1,0:T(8,128)} %get-tuple-element.44), calls=%async_computation.2 | async-start | bytes 524288 | tf_op jit(solution)/shard_map/all_to_all | solution.py:228
  81.0 5.9 %collective-permute-start.16 = (bf16[4,16,512]{2,1,0:T(8,128)(2,1)S(1)}, bf16[4,16,512]{2,1,0:T(8,128)(2,1)S(1)}, u32[]{:S(2)}, u32[]{:S(2)}) collective-permute-start(bf16[4,16,512]{2,1,0:T(8,128)(2,1)S(1)} %pad_maximum_fusion.2), channel_id=1, source_target_pairs={{0,16},{16,32},{32,48},{48,64},{64,80},{80,96},{96,112},{112,128},... | collective-permute-start | bytes 196616 | tf_op jit(solution)/shard_map/ppermute | solution.py:218
  85.0 9.2 %collective-permute-start.17 = (bf16[4,16,512]{2,1,0:T(8,128)(2,1)S(1)}, bf16[4,16,512]{2,1,0:T(8,128)(2,1)S(1)}, u32[]{:S(2)}, u32[]{:S(2)}) collective-permute-start(bf16[4,16,512]{2,1,0:T(8,128)(2,1)S(1)} %pad_maximum_fusion.3), channel_id=1, source_target_pairs={{16,0},{32,16},{48,32},{64,48},{80,64},{96,80},{112,96},{128,112},... | collective-permute-start | bytes 196616 | tf_op jit(solution)/shard_map/ppermute | solution.py:219
  97.0 19.7 %copy-start = (bf16[4,8,16,128]{3,2,1,0:T(8,128)(2,1)S(1)}, bf16[4,8,16,128]{3,2,1,0:T(8,128)(2,1)}, u32[]{:S(2)}) copy-start(bf16[4,8,16,128]{3,2,1,0:T(8,128)(2,1)} %x_ref.1) | copy-start | bytes 393220

commit v4 on v3

v4 whole, which is shorter than its diff:
```python
import functools

import jax
import jax.numpy as jnp
from jax import lax
from jax.experimental import pallas as pl
from jax.experimental.pallas import tpu as pltpu
from jax.sharding import Mesh, PartitionSpec as P

GROUP = 8
EPS = 1e-06
BF16 = jnp.bfloat16
F32 = jnp.float32

ROW = ("xh", "y", "core")
CHAN = ("zh", "zl", "xl")
NEAR = ("zl", "xl")


def dot(a, b):
    return lax.dot_general(a, b, (((1,), (0,)), ((), ())), preferred_element_type=F32)


def silu(u):
    return u / (1.0 + jnp.exp(-u))


def call(kernel, outs, *args, far=(), scratch=(), flops=0):
    specs = [pl.BlockSpec(memory_space=pl.ANY if i in far else pltpu.VMEM) for i in range(len(args))]
    moved = sum(a.size * a.dtype.itemsize for a in args)
    return pl.pallas_call(
        kernel,
        out_shape=outs,
        in_specs=specs,
        out_specs=jax.tree.map(lambda _: pl.BlockSpec(memory_space=pltpu.VMEM), outs),
        scratch_shapes=list(scratch),
        compiler_params=pltpu.CompilerParams(vmem_limit_bytes=(60 if far else 40) * 1024 * 1024),
        cost_estimate=pl.CostEstimate(flops=flops, bytes_accessed=moved, transcendentals=0),
    )(*args)


def place():
    return lax.axis_index(ROW), lax.axis_index("zh"), lax.axis_index(NEAR)


def put_stats(rows_ref, note_ref, stats_ref):
    slabs = [rows_ref[:, :, 256 + 128 * t : 384 + 128 * t].astype(F32) for t in range(4)]
    x = jnp.concatenate(slabs, axis=0).reshape(32, 2, GROUP, 128)
    number = x.shape[0] * GROUP
    mean = jnp.sum(x, axis=(0, 2), keepdims=True) / number
    off = x - mean
    square = jnp.sum(off * off, axis=(0, 2))
    note_ref[0:2] = mean.reshape(2, 128)
    note_ref[2:4] = square
    stats_ref[...] = jnp.broadcast_to(note_ref[...][None], stats_ref.shape)


def fetch(pairs, sems):
    copies = [pltpu.make_async_copy(src, dst, sems.at[i]) for i, (src, dst) in enumerate(pairs)]
    for copy in copies:
        copy.start()
    for copy in copies:
        copy.wait()


def rows_kernel(x_hbm, cache_hbm, raw_ref, later_ref, x_ref, cache_ref, sems):
    fetch(((x_hbm, x_ref), (cache_hbm, cache_ref)), sems)
    for r in range(8):
        for t in range(2):
            lanes = slice(128 * t, 128 * (t + 1))
            raw_ref[r, :, lanes] = cache_ref[0, t, r]
            later_ref[r, :, lanes] = cache_ref[1, t, r]
        for t in range(4):
            raw_ref[r, :, 256 + 128 * t : 384 + 128 * t] = x_ref[t, r]


def stats_kernel(
    raw_ref, gain_hbm, shift_hbm, w_hbm, stats_ref, next_ref, w0_ref, w1_ref,
    gain_ref, shift_ref, w_ref, note_ref, sems,
):
    fetch(((gain_hbm, gain_ref), (shift_hbm, shift_ref), (w_hbm, w_ref)), sems)
    _, me, _ = place()
    for q in range(4):
        for dt in range(3):
            for dc in range(3):
                taps = [
                    [
                        w_ref[layer, 9 * dt + 3 * dr + dc, :, 64 * q : 64 * (q + 1)]
                        for dr in range(3)
                    ]
                    for layer in range(2)
                ]
                w0_ref[q, dt, dc] = jnp.concatenate(taps[0], axis=1)
                w1_ref[lax.rem(q + 4 - me, 4), dt, dc] = jnp.concatenate(taps[1], axis=1)
    for layer, ref in ((0, note_ref), (1, next_ref)):
        ref[...] = jnp.zeros((8, 128), F32)
        ref[4:5, 0:16] = gain_ref[layer : layer + 1, :]
        ref[5:6, 0:16] = shift_ref[layer : layer + 1, :]
    put_stats(raw_ref, note_ref, stats_ref)


def second_stats_kernel(mid_ref, next_ref, stats_ref, note_ref):
    note_ref[...] = next_ref[...]
    put_stats(mid_ref, note_ref, stats_ref)


def shift_columns(left, centre, right):
    lane = lax.broadcasted_iota(jnp.int32, left.shape, left.ndim - 1)
    axis = left.ndim - 1
    left = jnp.where(lane == 0, 0.0, pltpu.roll(left, 1, axis))
    right = jnp.where(lane == 127, 0.0, pltpu.roll(right, 127, axis))
    return left + centre + right


def get_affine(stats_ref, affine_ref):
    stats = stats_ref[...].reshape(16, 4, 8, 128)
    number = 32 * GROUP
    means = stats[:, :, 0:2]
    mean = jnp.mean(means, axis=(0, 3), keepdims=True)
    off = means - mean
    total = jnp.sum(stats[:, :, 2:4] + number * (off * off), axis=(0, 3), keepdims=True)
    inverse = lax.rsqrt(total / (number * 16 * 128) + EPS)
    mean = jnp.broadcast_to(mean.reshape(4, 2, 1, 1), (4, 2, GROUP, 128)).reshape(4, 16, 128)
    inverse = jnp.broadcast_to(inverse.reshape(4, 2, 1, 1), (4, 2, GROUP, 128)).reshape(4, 16, 128)
    shape = (4, 16, 128)
    same = lax.broadcasted_iota(jnp.int32, shape, 1) == lax.broadcasted_iota(jnp.int32, shape, 2)
    gain = jnp.sum(jnp.where(same, stats[0, :, 4:5], 0.0), axis=2, keepdims=True)
    shift = jnp.sum(jnp.where(same, stats[0, :, 5:6], 0.0), axis=2, keepdims=True)
    affine_ref[0] = mean
    affine_ref[1] = inverse * gain
    affine_ref[2] = jnp.broadcast_to(shift, shape)


def conv_kernel(
    first, a_ref, b_ref, c_ref, d_ref, chip_ref, next_ref, stats_ref, *refs
):
    *w_refs, o_ref, affine_ref, slab_ref, held_ref = refs
    row, me, here = place()
    get_affine(stats_ref, affine_ref)
    upper = lax.rem(row, 2) == 0
    not_top = (row > 0).astype(F32)
    not_bottom = (row < 15).astype(F32)
    for k, ref in enumerate((a_ref, b_ref, c_ref, d_ref)):
        b = lax.bitwise_xor(here, k)
        mean = affine_ref[0, b]
        gain = affine_ref[1, b]
        shift = affine_ref[2, b]
        for r in range(10):
            for t in range(6):
                lanes = slice(128 * t, 128 * (t + 1))
                if r == 0:
                    x = jnp.where(upper, next_ref[k, :, lanes].astype(F32), chip_ref[k, :, lanes].astype(F32))
                elif r == 9:
                    x = jnp.where(upper, chip_ref[k, :, lanes].astype(F32), next_ref[k, :, lanes].astype(F32))
                elif t < 2:
                    x = ref[r - 1, :, lanes]
                else:
                    x = ref[r - 1, :, lanes].astype(F32)
                if t >= 2:
                    x = silu((x - mean) * gain + shift)
                if r == 0:
                    x = x * not_top
                if r == 9:
                    x = x * not_bottom
                slab_ref[r, b, :, lanes] = x.astype(BF16)
    for q in range(4):
        for dt in range(3):
            held_ref[dt, q] = w_refs[0][q, dt] if first else w_refs[q][dt]
    for r in range(8):
        rows = slab_ref[r : r + 3].reshape(192, 768)
        prod = dot(held_ref[0].reshape(192, 192), rows[:, 0:512])
        prod += dot(held_ref[1].reshape(192, 192), rows[:, 128:640])
        prod += dot(held_ref[2].reshape(192, 192), rows[:, 256:768])
        prod = prod.reshape(4, 3, 16, 512)
        for t in range(4):
            lanes = slice(128 * t, 128 * (t + 1))
            part = prod[:, :, :, lanes]
            summed = shift_columns(part[:, 0], part[:, 1], part[:, 2]).astype(BF16)
            for q in range(4):
                target = q if first else lax.rem(me + (4 - q), 4)
                o_ref[target, r, :, lanes] = summed[q]


def merge_kernel(part_ref, bias_ref, later_ref, mid_ref):
    bias = jnp.concatenate([bias_ref[...]] * 4, axis=1)
    for r in range(8):
        summed = part_ref[0, r].astype(F32) + part_ref[1, r].astype(F32)
        summed += part_ref[2, r].astype(F32) + part_ref[3, r].astype(F32)
        mid_ref[r, :, 0:256] = later_ref[r]
        mid_ref[r, :, 256:768] = (summed + bias).astype(BF16)


def last_kernel(x_ref, part_ref, bias_ref, o_ref):
    bias = bias_ref[...]
    for r in range(8):
        for t in range(4):
            lanes = slice(128 * t, 128 * (t + 1))
            branch = part_ref[0, r, :, lanes].astype(F32) + part_ref[1, r, :, lanes].astype(F32)
            branch += part_ref[2, r, :, lanes].astype(F32) + part_ref[3, r, :, lanes].astype(F32)
            o_ref[t, r] = (x_ref[t, r].astype(F32) + (branch + bias)).astype(BF16)


def struct(shape, dtype=BF16):
    return jax.ShapeDtypeStruct(shape, dtype)


def edge_kernel(a_ref, b_ref, c_ref, d_ref, chip_ref, next_ref):
    upper = lax.rem(lax.axis_index(ROW), 2) == 0
    towards = jnp.where(upper, 7, 0)
    for k, ref in enumerate((a_ref, b_ref, c_ref, d_ref)):
        chip_ref[k] = ref[towards]
        next_ref[k] = ref[7 - towards]


def rows_beside(blocks):
    chip, beyond = call(edge_kernel, (struct((4, 16, 768)), struct((4, 16, 768))), *blocks, flops=2 * 10**10)
    chip = lax.ppermute(chip, ROW, [(i, i ^ 1) for i in range(16)])
    pairs = [(i, i + 1) for i in range(1, 15, 2)] + [(i + 1, i) for i in range(1, 15, 2)]
    beyond = lax.ppermute(beyond, ROW, pairs)
    return [chip, beyond]


def near(x):
    return [x] + [lax.ppermute(x, NEAR, [(i, i ^ k) for i in range(4)]) for k in (1, 2, 3)]


def exchange(x, axes):
    return lax.all_to_all(x, axes, 0, 0, tiled=True)


def local(frames, cache, norm_gain, norm_shift, conv_weight, conv_bias):
    note = pltpu.VMEM((8, 128), F32)
    raw, later = call(
        rows_kernel, (struct((8, 16, 768)), struct((8, 16, 256))), frames, cache,
        scratch=(
            pltpu.VMEM((4, 8, 16, 128), BF16), pltpu.VMEM((2, 2, 8, 16, 128), BF16),
            pltpu.SemaphoreType.DMA((2,)),
        ),
        far=(0, 1),
    )
    stats, note1, w0, w1 = call(
        stats_kernel,
        (
            struct((64, 8, 128), F32), struct((8, 128), F32),
            struct((4, 3, 3, 16, 192)), struct((4, 3, 3, 16, 192)),
        ),
        raw, norm_gain, norm_shift, conv_weight.transpose(0, 2, 1, 3),
        scratch=(
            pltpu.VMEM((2, 16), F32), pltpu.VMEM((2, 16), F32), pltpu.VMEM((2, 27, 16, 256), BF16),
            note, pltpu.SemaphoreType.DMA((3,)),
        ),
        far=(1, 2, 3),
    )
    raw = near(raw)
    w0 = exchange(w0, "zh")
    stats, w0 = lax.optimization_barrier((stats, w0))
    stats = exchange(stats, ROW + NEAR)
    raw = raw + rows_beside(raw)
    bias = jnp.broadcast_to(conv_bias[:, :, None], (2, 16, 128))
    scratch = (
        pltpu.VMEM((3, 4, 16, 128), F32),
        pltpu.VMEM((10, 4, 16, 768), BF16),
        pltpu.VMEM((3, 4, 3, 16, 192), BF16),
    )
    flops = 2 * 192 * 576 * 4096

    partial = call(
        functools.partial(conv_kernel, True), struct((4, 8, 16, 512)), *raw, stats, w0,
        scratch=scratch, flops=flops,
    )
    partial, w1 = lax.optimization_barrier((partial, w1))
    w1 = [w1[0]] + [
        lax.ppermute(w1[d], "zh", [(i, (i + d) % 4) for i in range(4)]) for d in range(1, 4)
    ]
    partial = exchange(partial, "zh")
    partial, w1 = lax.optimization_barrier((partial, w1))
    middle = call(merge_kernel, struct((8, 16, 768)), partial, bias[0], later)
    stats = call(second_stats_kernel, struct((64, 8, 128), F32), middle, note1, scratch=(note,))
    middle = near(middle)
    stats = exchange(stats, ROW + NEAR)
    middle = middle + rows_beside(middle)
    partial = call(
        functools.partial(conv_kernel, False), struct((4, 8, 16, 512)), *middle, stats, *w1,
        scratch=scratch, flops=flops,
    )
    partial = exchange(partial, "zh")
    return call(last_kernel, struct((4, 8, 16, 128)), frames, partial, bias[1])


def solution(mesh):
    fine = Mesh(mesh.devices.reshape(2, 4, 2, 4, 2, 2), ROW + CHAN)
    placed = (
        P(None, ROW, CHAN, None),
        P(None, None, ROW, CHAN, None),
        P(None, CHAN),
        P(None, CHAN),
        P(None, CHAN, None, None),
        P(None, CHAN),
    )
    return jax.shard_map(
        local, mesh=fine, in_specs=placed, out_specs=P(None, ROW, CHAN, None), check_vma=False
    )
```

time: 119 us -> 117 us (0.983)
  waiting for transfers between devices: 24.8 us -> 28 us
  local copies, waits for them, and re-layouts: 3.22 us -> 0.19 us
    all_to_all x3 -> x4, starting transfers between devices: 19.6 us -> 34.4 us  [exchange(): return lax.all_to_all(x, axes, 0, 0, tiled=True)]
    ppermute x9 -> x7, starting transfers between devices: 27.6 us -> 17.4 us  [the longest x3 8.97 us: local(): lax.ppermute(w1[d], 'zh', [(i, (i + d) % 4) for i in range(4)])]
    all_to_all x3 -> x4, waiting for transfers between devices: 0.01 us -> 6 us  [exchange(): return lax.all_to_all(x, axes, 0, 0, tiled=True)]
    ppermute x9 -> x6, starting transfers between devices: 11.1 us -> 5.72 us  [near(): lax.ppermute(x, NEAR, [(i, i ^ k) for i in range(4)])]
    ppermute x9 -> x6, waiting for transfers between devices: 2.42 us -> 0.02 us  [near(): lax.ppermute(x, NEAR, [(i, i ^ k) for i in range(4)])]
    unnamed x14 -> x12, local copies, waits for them, and re-layouts: 1.22 us -> 0.03 us
    pallas_call x5 -> x9, Pallas kernels: 11 us -> 11.8 us  [call(): pl.pallas_call(kernel, out_shape=outs, in_specs=specs, out_specs=jax.tree...]
    ppermute x9 -> x7, waiting for transfers between devices: 22.3 us -> 22 us  [the longest x2 11.5 us: rows_beside(): beyond = lax.ppermute(beyond, ROW, pairs)]
  transfers between devices with their start and end apart: 21 -> 17, of which waited for: 4 -> 5; matrix products, arithmetic and copies ran while one was open for 1% -> 0% of each run, Pallas kernels for 3% -> 1%
where the time goes in v4:
time: 117 us; the launch traced here: 116 us
  starting transfers between devices  57.5 us (49%)
  waiting for transfers between devices  28 us (24%)
  blocking collectives  18.6 us (16%)
  Pallas kernels  11.8 us (10%)
    all_to_all x4, starting transfers between devices, exchange(): return lax.all_to_all(x, axes, 0, 0, tiled=True)  34.4 us
    all_to_all x1, blocking collectives, exchange(): return lax.all_to_all(x, axes, 0, 0, tiled=True)  18.6 us
    pallas_call x9, Pallas kernels, call(): pl.pallas_call(kernel, out_shape=outs, in_specs=specs, out_specs=jax.tree...  11.8 us
    ppermute x2, waiting for transfers between devices, rows_beside(): beyond = lax.ppermute(beyond, ROW, pairs)  11.5 us
    ppermute x3, waiting for transfers between devices, local(): lax.ppermute(w1[d], 'zh', [(i, (i + d) % 4) for i in range(4)])  10.5 us
    ppermute x3, starting transfers between devices, local(): lax.ppermute(w1[d], 'zh', [(i, (i + d) % 4) for i in range(4)])  8.97 us
    ppermute x2, starting transfers between devices, rows_beside(): beyond = lax.ppermute(beyond, ROW, pairs)  7.56 us
    all_to_all x4, waiting for transfers between devices, exchange(): return lax.all_to_all(x, axes, 0, 0, tiled=True)  6 us
  transfers between devices with their start and end apart: 17, of which 5 were waited for; matrix products, arithmetic and copies ran while one was open for 0% of the time, Pallas kernels for 1%

profile of v4, /device:TPU:27, one launch (start us, length us, event | category | flops | bytes accessed | tf_op | source)
XLA Modules:
  0.0 116.4 jit_solution(1637147288733789881)
XLA Ops:
  0.0 1.7 %shard_map.64 = (bf16[8,16,768]{2,1,0:T(8,128)(2,1)}, bf16[8,16,256]{2,1,0:T(8,128)(2,1)}) custom-call(bf16[4,8,16,128]{3,2,1,0:T(8,128)(2,1)} %x_ref.1, bf16[2,2,8,16,128]{4,3,2,1,0:T(8,128)(2,1)} %cache_hbm.1), custom_call_target="tpu_custom_call" | custom-call | bytes 262144 | tf_op jit(solution)/shard_map/pallas_call | solution.py:31
  1.7 3.1 %shard_map.66 = (f32[64,8,128]{2,1,0:T(8,128)}, f32[8,128]{1,0:T(8,128)}, bf16[4,3,3,16,192]{4,3,2,1,0:T(8,128)(2,1)}, bf16[4,3,3,16,192]{4,3,2,1,0:T(8,128)(2,1)}) custom-call(bf16[8,16,768]{2,1,0:T(8,128)(2,1)} %get-tuple-element.24.a_ref.raw_ref, f32[2,16]{1,0:T(2,128)} %gain_hbm.1, f32[2,16]{1,0:T(2,128)} %shift_hbm.1, bf16[2,27,16,256]{3,2,1,0:T(8,128)(2,1)} %bitcast.13), custom_call_target="tpu_custom_call" | custom-call | bytes 639232 | tf_op jit(solution)/shard_map/pallas_call | solution.py:31
  4.9 0.0 copy-start.1
  4.9 8.3 %all-to-all-start = ((bf16[4,3,3,16,192]{4,3,2,1,0:T(8,128)(2,1)}), bf16[4,3,3,16,192]{4,3,2,1,0:T(8,128)(2,1)S(1)}, u32[]{:S(2)}, u32[]{:S(2)}) async-start(bf16[4,3,3,16,192]{4,3,2,1,0:T(8,128)(2,1)} %get-tuple-element.28), calls=%async_computation | async-start | bytes 589824 | tf_op jit(solution)/shard_map/all_to_all | solution.py:228
  13.2 0.0 copy-done.1
  13.2 0.3 collective-permute-start
  13.5 0.7 collective-permute-start.1
  14.2 1.7 %collective-permute-start.2 = (bf16[8,16,768]{2,1,0:T(8,128)(2,1)S(1)}, bf16[8,16,768]{2,1,0:T(8,128)(2,1)S(1)}, u32[]{:S(2)}, u32[]{:S(2)}) collective-permute-start(bf16[8,16,768]{2,1,0:T(8,128)(2,1)S(1)} %copy-done.1), channel_id=1, source_target_pairs={{0,3},{1,2},{2,1},{3,0},{4,7},{5,6},{6,5},{7,4},{8,11},{9,10},{10,... | collective-permute-start | bytes 589832 | tf_op jit(solution)/shard_map/ppermute | solution.py:224
  15.9 6.0 %all-to-all-done.refs_0_ = bf16[4,3,3,16,192]{4,3,2,1,0:T(8,128)(2,1)S(1)} async-done(((bf16[4,3,3,16,192]{4,3,2,1,0:T(8,128)(2,1)}), bf16[4,3,3,16,192]{4,3,2,1,0:T(8,128)(2,1)S(1)}, u32[]{:S(2)}, u32[]{:S(2)}) %all-to-all-start) | async-done | bytes 221216 | tf_op jit(solution)/shard_map/all_to_all | solution.py:228
  21.8 13.6 %all-to-all-start.1 = ((f32[64,8,128]{2,1,0:T(8,128)}), f32[64,8,128]{2,1,0:T(8,128)S(1)}, u32[]{:S(2)}, u32[]{:S(2)}) async-start(f32[64,8,128]{2,1,0:T(8,128)} %get-tuple-element.29), calls=%async_computation.1 | async-start | bytes 524288 | tf_op jit(solution)/shard_map/all_to_all | solution.py:228
  35.5 0.0 collective-permute-done.b_ref
  35.5 0.0 collective-permute-done.1.c_ref
  35.5 0.0 collective-permute-done.2.d_ref
  35.6 0.4 collective-permute-start.3
  36.0 3.8 %collective-permute-start.4 = (bf16[4,16,768]{2,1,0:T(8,128)(2,1)S(1)}, bf16[4,16,768]{2,1,0:T(8,128)(2,1)S(1)}, u32[]{:S(2)}, u32[]{:S(2)}) collective-permute-start(bf16[4,16,768]{2,1,0:T(8,128)(2,1)S(1)} %get-tuple-element.26), channel_id=1, source_target_pairs={{16,32},{48,64},{80,96},{112,128},{144,160},{176,192},{208,224},{3... | collective-permute-start | bytes 294920 | tf_op jit(solution)/shard_map/ppermute | solution.py:219
  39.8 0.0 collective-permute-done.3.chip_ref
  39.8 5.7 %collective-permute-done.4.next_ref = bf16[4,16,768]{2,1,0:T(8,128)(2,1)S(1)} collective-permute-done((bf16[4,16,768]{2,1,0:T(8,128)(2,1)S(1)}, bf16[4,16,768]{2,1,0:T(8,128)(2,1)S(1)}, u32[]{:S(2)}, u32[]{:S(2)}) %collective-permute-start.4) | collective-permute-done | bytes 98336 | tf_op jit(solution)/shard_map/ppermute | solution.py:219
  45.6 0.0 all-to-all-done.1.stats_ref
  45.6 3.0 %shard_map.67 = bf16[4,8,16,512]{3,2,1,0:T(8,128)(2,1)} custom-call(bf16[8,16,768]{2,1,0:T(8,128)(2,1)S(1)} %copy-done.1, bf16[8,16,768]{2,1,0:T(8,128)(2,1)S(1)} %collective-permute-done.b_ref, bf16[8,16,768]{2,1,0:T(8,128)(2,1)S(1)} %collective-permute-done.1.c_ref, bf16[8,16,768]{2,1,0:T(8,128)(2,1)S(1)} %collective-permute-done.2.d_ref, ...), custom_call_target="tpu_custom_call" | custom-call | flops 905969664 | bytes 1466368 | tf_op jit(solution)/shard_map/pallas_call | solution.py:31
  48.6 3.6 %all-to-all-start.2 = ((bf16[4,8,16,512]{3,2,1,0:T(8,128)(2,1)}), bf16[4,8,16,512]{3,2,1,0:T(8,128)(2,1)S(1)}, u32[]{:S(2)}, u32[]{:S(2)}) async-start(bf16[4,8,16,512]{3,2,1,0:T(8,128)(2,1)} %shard_map.67), calls=%async_computation.2 | async-start | bytes 1048576 | tf_op jit(solution)/shard_map/all_to_all | solution.py:228
  52.2 2.4 %collective-permute-start.5 = (bf16[3,3,16,192]{3,2,1,0:T(8,128)(2,1)S(1)}, bf16[3,3,16,192]{3,2,1,0:T(8,128)(2,1)S(1)}, u32[]{:S(2)}, u32[]{:S(2)}) collective-permute-start(bf16[3,3,16,192]{3,2,1,0:T(8,128)(2,1)S(1)} %get-tuple-element.45), channel_id=1, source_target_pairs={{0,4},{4,8},{8,12},{12,0},{1,5},{5,9},{9,13},{13,1},{2,6},{6,10},{... | collective-permute-start | bytes 165896 | tf_op jit(solution)/shard_map/ppermute | solution.py:273
  54.6 3.3 %collective-permute-start.6 = (bf16[3,3,16,192]{3,2,1,0:T(8,128)(2,1)S(1)}, bf16[3,3,16,192]{3,2,1,0:T(8,128)(2,1)S(1)}, u32[]{:S(2)}, u32[]{:S(2)}) collective-permute-start(bf16[3,3,16,192]{3,2,1,0:T(8,128)(2,1)S(1)} %get-tuple-element.44), channel_id=1, source_target_pairs={{0,8},{4,12},{8,0},{12,4},{1,9},{5,13},{9,1},{13,5},{2,10},{6,14},... | collective-permute-start | bytes 165896 | tf_op jit(solution)/shard_map/ppermute | solution.py:273
  57.9 3.3 %collective-permute-start.7 = (bf16[3,3,16,192]{3,2,1,0:T(8,128)(2,1)S(1)}, bf16[3,3,16,192]{3,2,1,0:T(8,128)(2,1)S(1)}, u32[]{:S(2)}, u32[]{:S(2)}) collective-permute-start(bf16[3,3,16,192]{3,2,1,0:T(8,128)(2,1)S(1)} %get-tuple-element.43), channel_id=1, source_target_pairs={{0,12},{4,0},{8,4},{12,8},{1,13},{5,1},{9,5},{13,9},{2,14},{6,2},{... | collective-permute-start | bytes 165896 | tf_op jit(solution)/shard_map/ppermute | solution.py:273
  61.2 0.0 copy-done.5
  61.2 5.1 %collective-permute-done.5.refs_1_ = bf16[3,3,16,192]{3,2,1,0:T(8,128)(2,1)S(1)} collective-permute-done((bf16[3,3,16,192]{3,2,1,0:T(8,128)(2,1)S(1)}, bf16[3,3,16,192]{3,2,1,0:T(8,128)(2,1)S(1)}, u32[]{:S(2)}, u32[]{:S(2)}) %collective-permute-start.5) | collective-permute-done | bytes 55328 | tf_op jit(solution)/shard_map/ppermute | solution.py:273
  66.4 5.4 %collective-permute-done.6.refs_2_ = bf16[3,3,16,192]{3,2,1,0:T(8,128)(2,1)S(1)} collective-permute-done((bf16[3,3,16,192]{3,2,1,0:T(8,128)(2,1)S(1)}, bf16[3,3,16,192]{3,2,1,0:T(8,128)(2,1)S(1)}, u32[]{:S(2)}, u32[]{:S(2)}) %collective-permute-start.6) | collective-permute-done | bytes 55328 | tf_op jit(solution)/shard_map/ppermute | solution.py:273
  71.8 0.0 collective-permute-done.7.refs_3_
  71.8 0.0 all-to-all-done.2.part_ref
  71.8 0.1 broadcast_in_dim.13.bias_ref
  71.8 0.1 shard_map.68.a_ref.mid_ref
  71.9 2.0 %collective-permute-start.10 = (bf16[8,16,768]{2,1,0:T(8,128)(2,1)S(1)}, bf16[8,16,768]{2,1,0:T(8,128)(2,1)S(1)}, u32[]{:S(2)}, u32[]{:S(2)}) collective-permute-start(bf16[8,16,768]{2,1,0:T(8,128)(2,1)S(1)} %shard_map.68.a_ref.mid_ref), channel_id=1, source_target_pairs={{0,3},{1,2},{2,1},{3,0},{4,7},{5,6},{6,5},{7,4},{8,11},{9,10},{10,... | collective-permute-start | bytes 589832 | tf_op jit(solution)/shard_map/ppermute | solution.py:224
  73.9 0.7 collective-permute-start.8
  74.6 0.4 collective-permute-start.9
  75.0 0.8 shard_map.70
  75.8 8.8 %all-to-all-start.3 = ((f32[64,8,128]{2,1,0:T(8,128)}), f32[64,8,128]{2,1,0:T(8,128)S(1)}, u32[]{:S(2)}, u32[]{:S(2)}) async-start(f32[64,8,128]{2,1,0:T(8,128)} %shard_map.70), calls=%async_computation.3 | async-start | bytes 524288 | tf_op jit(solution)/shard_map/all_to_all | solution.py:228
  84.6 0.0 collective-permute-done.10.d_ref
  84.6 0.0 collective-permute-done.8.b_ref
  84.6 0.0 collective-permute-done.9.c_ref
  84.7 0.4 collective-permute-start.11
  85.1 3.8 %collective-permute-start.12 = (bf16[4,16,768]{2,1,0:T(8,128)(2,1)S(1)}, bf16[4,16,768]{2,1,0:T(8,128)(2,1)S(1)}, u32[]{:S(2)}, u32[]{:S(2)}) collective-permute-start(bf16[4,16,768]{2,1,0:T(8,128)(2,1)S(1)} %get-tuple-element.37), channel_id=1, source_target_pairs={{16,32},{48,64},{80,96},{112,128},{144,160},{176,192},{208,224},{3... | collective-permute-start | bytes 294920 | tf_op jit(solution)/shard_map/ppermute | solution.py:219
  88.9 0.0 collective-permute-done.11.chip_ref
  88.9 5.7 %collective-permute-done.12.next_ref = bf16[4,16,768]{2,1,0:T(8,128)(2,1)S(1)} collective-permute-done((bf16[4,16,768]{2,1,0:T(8,128)(2,1)S(1)}, bf16[4,16,768]{2,1,0:T(8,128)(2,1)S(1)}, u32[]{:S(2)}, u32[]{:S(2)}) %collective-permute-start.12) | collective-permute-done | bytes 98336 | tf_op jit(solution)/shard_map/ppermute | solution.py:219
  94.7 0.0 all-to-all-done.3.stats_ref
  94.7 2.2 %shard_map.71 = bf16[4,8,16,512]{3,2,1,0:T(8,128)(2,1)S(1)} custom-call(bf16[8,16,768]{2,1,0:T(8,128)(2,1)S(1)} %shard_map.68.a_ref.mid_ref, bf16[8,16,768]{2,1,0:T(8,128)(2,1)S(1)} %collective-permute-done.8.b_ref, bf16[8,16,768]{2,1,0:T(8,128)(2,1)S(1)} %collective-permute-done.9.c_ref, bf16[8,16,768]{2,1,0:T(8,128)(2,1)S(1)} %collective-permute-done.10.d_ref, ...), custom_call_target="tpu_custom_call" | custom-call | flops 905969664 | bytes 1466368 | tf_op jit(solution)/shard_map/pallas_call | solution.py:31
  96.9 0.0 copy-start
  96.9 18.6 %all_to_all.25.part_ref = bf16[4,8,16,512]{3,2,1,0:T(8,128)(2,1)S(1)} all-to-all(bf16[4,8,16,512]{3,2,1,0:T(8,128)(2,1)S(1)} %shard_map.71), channel_id=1, replica_groups=mesh['xh'=2,'y'=4,'core'=2,'zh'=4,'zl'=2,'xl'=2] {'zh'}, dimensions={0} | all-to-all | bytes 1048576 | tf_op jit(solution)/shard_map/all_to_all | solution.py:228
  115.5 0.1 broadcast_in_dim.15.bias_ref
  115.6 0.8 shard_map.72
  (12 shorter events, 0.1 us)
Async XLA Ops:
  4.9 8.3 %copy-start.1 = (bf16[8,16,768]{2,1,0:T(8,128)(2,1)S(1)}, bf16[8,16,768]{2,1,0:T(8,128)(2,1)}, u32[]{:S(2)}) copy-start(bf16[8,16,768]{2,1,0:T(8,128)(2,1)} %get-tuple-element.24.a_ref.raw_ref) | copy-start | bytes 589828
  4.9 17.0 %all-to-all-start = ((bf16[4,3,3,16,192]{4,3,2,1,0:T(8,128)(2,1)}), bf16[4,3,3,16,192]{4,3,2,1,0:T(8,128)(2,1)S(1)}, u32[]{:S(2)}, u32[]{:S(2)}) async-start(bf16[4,3,3,16,192]{4,3,2,1,0:T(8,128)(2,1)} %get-tuple-element.28), calls=%async_computation | async-start | bytes 589824 | tf_op jit(solution)/shard_map/all_to_all | solution.py:228
  13.2 22.3 %collective-permute-start = (bf16[8,16,768]{2,1,0:T(8,128)(2,1)S(1)}, bf16[8,16,768]{2,1,0:T(8,128)(2,1)S(1)}, u32[]{:S(2)}, u32[]{:S(2)}) collective-permute-start(bf16[8,16,768]{2,1,0:T(8,128)(2,1)S(1)} %copy-done.1), channel_id=1, source_target_pairs={{0,1},{1,0},{2,3},{3,2},{4,5},{5,4},{6,7},{7,6},{8,9},{9,8},{10,11... | collective-permute-start | bytes 589832 | tf_op jit(solution)/shard_map/ppermute | solution.py:224
  13.5 22.0 %collective-permute-start.1 = (bf16[8,16,768]{2,1,0:T(8,128)(2,1)S(1)}, bf16[8,16,768]{2,1,0:T(8,128)(2,1)S(1)}, u32[]{:S(2)}, u32[]{:S(2)}) collective-permute-start(bf16[8,16,768]{2,1,0:T(8,128)(2,1)S(1)} %copy-done.1), channel_id=1, source_target_pairs={{0,2},{1,3},{2,0},{3,1},{4,6},{5,7},{6,4},{7,5},{8,10},{9,11},{10,... | collective-permute-start | bytes 589832 | tf_op jit(solution)/shard_map/ppermute | solution.py:224
  14.2 21.3 %collective-permute-start.2 = (bf16[8,16,768]{2,1,0:T(8,128)(2,1)S(1)}, bf16[8,16,768]{2,1,0:T(8,128)(2,1)S(1)}, u32[]{:S(2)}, u32[]{:S(2)}) collective-permute-start(bf16[8,16,768]{2,1,0:T(8,128)(2,1)S(1)} %copy-done.1), channel_id=1, source_target_pairs={{0,3},{1,2},{2,1},{3,0},{4,7},{5,6},{6,5},{7,4},{8,11},{9,10},{10,... | collective-permute-start | bytes 589832 | tf_op jit(solution)/shard_map/ppermute | solution.py:224
  21.8 23.7 %all-to-all-start.1 = ((f32[64,8,128]{2,1,0:T(8,128)}), f32[64,8,128]{2,1,0:T(8,128)S(1)}, u32[]{:S(2)}, u32[]{:S(2)}) async-start(f32[64,8,128]{2,1,0:T(8,128)} %get-tuple-element.29), calls=%async_computation.1 | async-start | bytes 524288 | tf_op jit(solution)/shard_map/all_to_all | solution.py:228
  35.6 4.2 %collective-permute-start.3 = (bf16[4,16,768]{2,1,0:T(8,128)(2,1)S(1)}, bf16[4,16,768]{2,1,0:T(8,128)(2,1)S(1)}, u32[]{:S(2)}, u32[]{:S(2)}) collective-permute-start(bf16[4,16,768]{2,1,0:T(8,128)(2,1)S(1)} %get-tuple-element.25), channel_id=1, source_target_pairs={{0,16},{16,0},{32,48},{48,32},{64,80},{80,64},{96,112},{112,96},{1... | collective-permute-start | bytes 294920 | tf_op jit(solution)/shard_map/ppermute | solution.py:217
  36.0 9.5 %collective-permute-start.4 = (bf16[4,16,768]{2,1,0:T(8,128)(2,1)S(1)}, bf16[4,16,768]{2,1,0:T(8,128)(2,1)S(1)}, u32[]{:S(2)}, u32[]{:S(2)}) collective-permute-start(bf16[4,16,768]{2,1,0:T(8,128)(2,1)S(1)} %get-tuple-element.26), channel_id=1, source_target_pairs={{16,32},{48,64},{80,96},{112,128},{144,160},{176,192},{208,224},{3... | collective-permute-start | bytes 294920 | tf_op jit(solution)/shard_map/ppermute | solution.py:219
  48.6 3.6 %copy-start.4 = (bf16[4,3,3,16,192]{4,3,2,1,0:T(8,128)(2,1)S(1)}, bf16[4,3,3,16,192]{4,3,2,1,0:T(8,128)(2,1)}, u32[]{:S(2)}) copy-start(bf16[4,3,3,16,192]{4,3,2,1,0:T(8,128)(2,1)} %get-tuple-element.33) | copy-start | bytes 663556
  48.6 23.3 %copy-start.2 = (bf16[8,16,256]{2,1,0:T(8,128)(2,1)S(1)}, bf16[8,16,256]{2,1,0:T(8,128)(2,1)}, u32[]{:S(2)}) copy-start(bf16[8,16,256]{2,1,0:T(8,128)(2,1)} %get-tuple-element.35.later_ref) | copy-start | bytes 196612
  48.6 23.2 %all-to-all-start.2 = ((bf16[4,8,16,512]{3,2,1,0:T(8,128)(2,1)}), bf16[4,8,16,512]{3,2,1,0:T(8,128)(2,1)S(1)}, u32[]{:S(2)}, u32[]{:S(2)}) async-start(bf16[4,8,16,512]{3,2,1,0:T(8,128)(2,1)} %shard_map.67), calls=%async_computation.2 | async-start | bytes 1048576 | tf_op jit(solution)/shard_map/all_to_all | solution.py:228
  52.2 14.1 %collective-permute-start.5 = (bf16[3,3,16,192]{3,2,1,0:T(8,128)(2,1)S(1)}, bf16[3,3,16,192]{3,2,1,0:T(8,128)(2,1)S(1)}, u32[]{:S(2)}, u32[]{:S(2)}) collective-permute-start(bf16[3,3,16,192]{3,2,1,0:T(8,128)(2,1)S(1)} %get-tuple-element.45), channel_id=1, source_target_pairs={{0,4},{4,8},{8,12},{12,0},{1,5},{5,9},{9,13},{13,1},{2,6},{6,10},{... | collective-permute-start | bytes 165896 | tf_op jit(solution)/shard_map/ppermute | solution.py:273
  54.6 6.6 %copy-start.5 = (f32[2,16]{1,0:T(2,128)S(1)}, f32[2,16]{1,0:T(2,128)}, u32[]{:S(2)}) copy-start(f32[2,16]{1,0:T(2,128)} %param.11) | copy-start | bytes 388
  54.6 17.1 %collective-permute-start.6 = (bf16[3,3,16,192]{3,2,1,0:T(8,128)(2,1)S(1)}, bf16[3,3,16,192]{3,2,1,0:T(8,128)(2,1)S(1)}, u32[]{:S(2)}, u32[]{:S(2)}) collective-permute-start(bf16[3,3,16,192]{3,2,1,0:T(8,128)(2,1)S(1)} %get-tuple-element.44), channel_id=1, source_target_pairs={{0,8},{4,12},{8,0},{12,4},{1,9},{5,13},{9,1},{13,5},{2,10},{6,14},... | collective-permute-start | bytes 165896 | tf_op jit(solution)/shard_map/ppermute | solution.py:273
  57.9 13.8 %collective-permute-start.7 = (bf16[3,3,16,192]{3,2,1,0:T(8,128)(2,1)S(1)}, bf16[3,3,16,192]{3,2,1,0:T(8,128)(2,1)S(1)}, u32[]{:S(2)}, u32[]{:S(2)}) collective-permute-start(bf16[3,3,16,192]{3,2,1,0:T(8,128)(2,1)S(1)} %get-tuple-element.43), channel_id=1, source_target_pairs={{0,12},{4,0},{8,4},{12,8},{1,13},{5,1},{9,5},{13,9},{2,14},{6,2},{... | collective-permute-start | bytes 165896 | tf_op jit(solution)/shard_map/ppermute | solution.py:273
  71.8 3.2 %copy-start.3 = (f32[8,128]{1,0:T(8,128)S(1)}, f32[8,128]{1,0:T(8,128)}, u32[]{:S(2)}) copy-start(f32[8,128]{1,0:T(8,128)} %get-tuple-element.38.next_ref) | copy-start | bytes 12292
  71.9 12.7 %collective-permute-start.10 = (bf16[8,16,768]{2,1,0:T(8,128)(2,1)S(1)}, bf16[8,16,768]{2,1,0:T(8,128)(2,1)S(1)}, u32[]{:S(2)}, u32[]{:S(2)}) collective-permute-start(bf16[8,16,768]{2,1,0:T(8,128)(2,1)S(1)} %shard_map.68.a_ref.mid_ref), channel_id=1, source_target_pairs={{0,3},{1,2},{2,1},{3,0},{4,7},{5,6},{6,5},{7,4},{8,11},{9,10},{10,... | collective-permute-start | bytes 589832 | tf_op jit(solution)/shard_map/ppermute | solution.py:224
  73.9 10.7 %collective-permute-start.8 = (bf16[8,16,768]{2,1,0:T(8,128)(2,1)S(1)}, bf16[8,16,768]{2,1,0:T(8,128)(2,1)S(1)}, u32[]{:S(2)}, u32[]{:S(2)}) collective-permute-start(bf16[8,16,768]{2,1,0:T(8,128)(2,1)S(1)} %shard_map.68.a_ref.mid_ref), channel_id=1, source_target_pairs={{0,1},{1,0},{2,3},{3,2},{4,5},{5,4},{6,7},{7,6},{8,9},{9,8},{10,11... | collective-permute-start | bytes 589832 | tf_op jit(solution)/shard_map/ppermute | solution.py:224
  74.6 10.0 %collective-permute-start.9 = (bf16[8,16,768]{2,1,0:T(8,128)(2,1)S(1)}, bf16[8,16,768]{2,1,0:T(8,128)(2,1)S(1)}, u32[]{:S(2)}, u32[]{:S(2)}) collective-permute-start(bf16[8,16,768]{2,1,0:T(8,128)(2,1)S(1)} %shard_map.68.a_ref.mid_ref), channel_id=1, source_target_pairs={{0,2},{1,3},{2,0},{3,1},{4,6},{5,7},{6,4},{7,5},{8,10},{9,11},{10,... | collective-permute-start | bytes 589832 | tf_op jit(solution)/shard_map/ppermute | solution.py:224
  75.8 18.9 %all-to-all-start.3 = ((f32[64,8,128]{2,1,0:T(8,128)}), f32[64,8,128]{2,1,0:T(8,128)S(1)}, u32[]{:S(2)}, u32[]{:S(2)}) async-start(f32[64,8,128]{2,1,0:T(8,128)} %shard_map.70), calls=%async_computation.3 | async-start | bytes 524288 | tf_op jit(solution)/shard_map/all_to_all | solution.py:228
  84.7 4.2 %collective-permute-start.11 = (bf16[4,16,768]{2,1,0:T(8,128)(2,1)S(1)}, bf16[4,16,768]{2,1,0:T(8,128)(2,1)S(1)}, u32[]{:S(2)}, u32[]{:S(2)}) collective-permute-start(bf16[4,16,768]{2,1,0:T(8,128)(2,1)S(1)} %get-tuple-element.36), channel_id=1, source_target_pairs={{0,16},{16,0},{32,48},{48,32},{64,80},{80,64},{96,112},{112,96},{1... | collective-permute-start | bytes 294920 | tf_op jit(solution)/shard_map/ppermute | solution.py:217
  85.1 9.5 %collective-permute-start.12 = (bf16[4,16,768]{2,1,0:T(8,128)(2,1)S(1)}, bf16[4,16,768]{2,1,0:T(8,128)(2,1)S(1)}, u32[]{:S(2)}, u32[]{:S(2)}) collective-permute-start(bf16[4,16,768]{2,1,0:T(8,128)(2,1)S(1)} %get-tuple-element.37), channel_id=1, source_target_pairs={{16,32},{48,64},{80,96},{112,128},{144,160},{176,192},{208,224},{3... | collective-permute-start | bytes 294920 | tf_op jit(solution)/shard_map/ppermute | solution.py:219
  96.9 18.7 %copy-start = (bf16[4,8,16,128]{3,2,1,0:T(8,128)(2,1)S(1)}, bf16[4,8,16,128]{3,2,1,0:T(8,128)(2,1)}, u32[]{:S(2)}) copy-start(bf16[4,8,16,128]{3,2,1,0:T(8,128)(2,1)} %x_ref.1) | copy-start | bytes 393220

commit v5 on v4

--- a/solution.py
+++ b/solution.py
@@ -63,8 +63,18 @@
         copy.wait()
 
 
-def rows_kernel(x_hbm, cache_hbm, raw_ref, later_ref, x_ref, cache_ref, sems):
-    fetch(((x_hbm, x_ref), (cache_hbm, cache_ref)), sems)
+def begin_kernel(
+    x_hbm, cache_hbm, gain_hbm, shift_hbm, w_hbm,
+    raw_ref, later_ref, stats_ref, note1_ref, own_ref, side_ref, far_ref,
+    x_ref, cache_ref, gain_ref, shift_ref, w_ref, note_ref, pieces_ref, sems,
+):
+    fetch(
+        (
+            (x_hbm, x_ref), (cache_hbm, cache_ref), (gain_hbm, gain_ref), (shift_hbm, shift_ref),
+            (w_hbm, w_ref),
+        ),
+        sems,
+    )
     for r in range(8):
         for t in range(2):
             lanes = slice(128 * t, 128 * (t + 1))
@@ -72,36 +82,25 @@
             later_ref[r, :, lanes] = cache_ref[1, t, r]
         for t in range(4):
             raw_ref[r, :, 256 + 128 * t : 384 + 128 * t] = x_ref[t, r]
-
-
-def stats_kernel(
-    raw_ref, gain_hbm, shift_hbm, w_hbm, stats_ref, next_ref, w0_ref, w1_ref,
-    gain_ref, shift_ref, w_ref, note_ref, sems,
-):
-    fetch(((gain_hbm, gain_ref), (shift_hbm, shift_ref), (w_hbm, w_ref)), sems)
-    _, me, _ = place()
+    row, me, _ = place()
+    core = lax.rem(row, 2)
     for q in range(4):
-        for dt in range(3):
-            for dc in range(3):
-                taps = [
-                    [
-                        w_ref[layer, 9 * dt + 3 * dr + dc, :, 64 * q : 64 * (q + 1)]
-                        for dr in range(3)
+        ahead = lax.rem(q + 4 - me, 4)
+        for layer in range(2):
+            for dt in range(3):
+                for dc in range(3):
+                    taps = [
+                        w_ref[layer, 9 * dt + 3 * dr + dc, :, 64 * q : 64 * (q + 1)] for dr in range(3)
                     ]
-                    for layer in range(2)
-                ]
-                w0_ref[q, dt, dc] = jnp.concatenate(taps[0], axis=1)
-                w1_ref[lax.rem(q + 4 - me, 4), dt, dc] = jnp.concatenate(taps[1], axis=1)
-    for layer, ref in ((0, note_ref), (1, next_ref)):
+                    pieces_ref[ahead, layer, dt, dc] = jnp.concatenate(taps, axis=1)
+    own_ref[...] = pieces_ref[0]
+    side_ref[...] = pieces_ref[1 + 2 * core]
+    far_ref[...] = pieces_ref[2, core]
+    for layer, ref in ((0, note_ref), (1, note1_ref)):
         ref[...] = jnp.zeros((8, 128), F32)
         ref[4:5, 0:16] = gain_ref[layer : layer + 1, :]
         ref[5:6, 0:16] = shift_ref[layer : layer + 1, :]
     put_stats(raw_ref, note_ref, stats_ref)
-
-
-def second_stats_kernel(mid_ref, next_ref, stats_ref, note_ref):
-    note_ref[...] = next_ref[...]
-    put_stats(mid_ref, note_ref, stats_ref)
 
 
 def shift_columns(left, centre, right):
@@ -132,9 +131,9 @@
 
 
 def conv_kernel(
-    first, a_ref, b_ref, c_ref, d_ref, chip_ref, next_ref, stats_ref, *refs
+    layer, a_ref, b_ref, c_ref, d_ref, chip_ref, next_ref, stats_ref,
+    own_ref, side_ref, far_ref, side2_ref, far2_ref, o_ref, affine_ref, slab_ref, held_ref,
 ):
-    *w_refs, o_ref, affine_ref, slab_ref, held_ref = refs
     row, me, here = place()
     get_affine(stats_ref, affine_ref)
     upper = lax.rem(row, 2) == 0
@@ -163,9 +162,23 @@
                 if r == 9:
                     x = x * not_bottom
                 slab_ref[r, b, :, lanes] = x.astype(BF16)
-    for q in range(4):
+    core = lax.rem(row, 2)
+    sources = (me, lax.rem(me + 3 - 2 * core, 4), lax.rem(me + 1 + 2 * core, 4), lax.rem(me + 2, 4))
+    for dt in range(3):
+        held_ref[dt, 0] = own_ref[layer, dt]
+        held_ref[dt, 1] = side_ref[layer, dt]
+        held_ref[dt, 2] = side2_ref[layer, dt]
+
+    @pl.when(core == layer)
+    def _():
         for dt in range(3):
-            held_ref[dt, q] = w_refs[0][q, dt] if first else w_refs[q][dt]
+            held_ref[dt, 3] = far_ref[dt]
+
+    @pl.when(core != layer)
+    def _():
+        for dt in range(3):
+            held_ref[dt, 3] = far2_ref[dt]
+
     for r in range(8):
         rows = slab_ref[r : r + 3].reshape(192, 768)
         prod = dot(held_ref[0].reshape(192, 192), rows[:, 0:512])
@@ -177,17 +190,18 @@
             part = prod[:, :, :, lanes]
             summed = shift_columns(part[:, 0], part[:, 1], part[:, 2]).astype(BF16)
             for q in range(4):
-                target = q if first else lax.rem(me + (4 - q), 4)
-                o_ref[target, r, :, lanes] = summed[q]
-
-
-def merge_kernel(part_ref, bias_ref, later_ref, mid_ref):
+                o_ref[sources[q], r, :, lanes] = summed[q]
+
+
+def merge_kernel(part_ref, bias_ref, later_ref, note1_ref, mid_ref, stats_ref, note_ref):
     bias = jnp.concatenate([bias_ref[...]] * 4, axis=1)
     for r in range(8):
         summed = part_ref[0, r].astype(F32) + part_ref[1, r].astype(F32)
         summed += part_ref[2, r].astype(F32) + part_ref[3, r].astype(F32)
         mid_ref[r, :, 0:256] = later_ref[r]
         mid_ref[r, :, 256:768] = (summed + bias).astype(BF16)
+    note_ref[...] = note1_ref[...]
+    put_stats(mid_ref, note_ref, stats_ref)
 
 
 def last_kernel(x_ref, part_ref, bias_ref, o_ref):
@@ -230,32 +244,29 @@
 
 def local(frames, cache, norm_gain, norm_shift, conv_weight, conv_bias):
     note = pltpu.VMEM((8, 128), F32)
-    raw, later = call(
-        rows_kernel, (struct((8, 16, 768)), struct((8, 16, 256))), frames, cache,
+    piece = (2, 3, 3, 16, 192)
+    raw, later, stats, note1, own, side, far = call(
+        begin_kernel,
+        (
+            struct((8, 16, 768)), struct((8, 16, 256)), struct((64, 8, 128), F32), struct((8, 128), F32),
+            struct(piece), struct(piece), struct(piece[1:]),
+        ),
+        frames, cache, norm_gain, norm_shift, conv_weight.transpose(0, 2, 1, 3),
         scratch=(
             pltpu.VMEM((4, 8, 16, 128), BF16), pltpu.VMEM((2, 2, 8, 16, 128), BF16),
-            pltpu.SemaphoreType.DMA((2,)),
+            pltpu.VMEM((2, 16), F32), pltpu.VMEM((2, 16), F32), pltpu.VMEM((2, 27, 16, 256), BF16),
+            note, pltpu.VMEM((4,) + piece, BF16), pltpu.SemaphoreType.DMA((5,)),
         ),
-        far=(0, 1),
-    )
-    stats, note1, w0, w1 = call(
-        stats_kernel,
-        (
-            struct((64, 8, 128), F32), struct((8, 128), F32),
-            struct((4, 3, 3, 16, 192)), struct((4, 3, 3, 16, 192)),
-        ),
-        raw, norm_gain, norm_shift, conv_weight.transpose(0, 2, 1, 3),
-        scratch=(
-            pltpu.VMEM((2, 16), F32), pltpu.VMEM((2, 16), F32), pltpu.VMEM((2, 27, 16, 256), BF16),
-            note, pltpu.SemaphoreType.DMA((3,)),
-        ),
-        far=(1, 2, 3),
-    )
+        far=(0, 1, 2, 3, 4),
+    )
+    around = [(i, (i + 1) % 4) for i in range(4)] + [(4 + i, 4 + (i + 3) % 4) for i in range(4)]
+    side = lax.ppermute(side, ("core", "zh"), around)
+    far = lax.ppermute(far, "zh", [(i, (i + 2) % 4) for i in range(4)])
     raw = near(raw)
-    w0 = exchange(w0, "zh")
-    stats, w0 = lax.optimization_barrier((stats, w0))
     stats = exchange(stats, ROW + NEAR)
     raw = raw + rows_beside(raw)
+    swap = [(0, 1), (1, 0)]
+    weights = [own, side, far, lax.ppermute(side, "core", swap), lax.ppermute(far, "core", swap)]
     bias = jnp.broadcast_to(conv_bias[:, :, None], (2, 16, 128))
     scratch = (
         pltpu.VMEM((3, 4, 16, 128), F32),
@@ -265,22 +276,19 @@
     flops = 2 * 192 * 576 * 4096
 
     partial = call(
-        functools.partial(conv_kernel, True), struct((4, 8, 16, 512)), *raw, stats, w0,
+        functools.partial(conv_kernel, 0), struct((4, 8, 16, 512)), *raw, stats, *weights,
         scratch=scratch, flops=flops,
     )
-    partial, w1 = lax.optimization_barrier((partial, w1))
-    w1 = [w1[0]] + [
-        lax.ppermute(w1[d], "zh", [(i, (i + d) % 4) for i in range(4)]) for d in range(1, 4)
-    ]
     partial = exchange(partial, "zh")
-    partial, w1 = lax.optimization_barrier((partial, w1))
-    middle = call(merge_kernel, struct((8, 16, 768)), partial, bias[0], later)
-    stats = call(second_stats_kernel, struct((64, 8, 128), F32), middle, note1, scratch=(note,))
+    middle, stats = call(
+        merge_kernel, (struct((8, 16, 768)), struct((64, 8, 128), F32)), partial, bias[0], later, note1,
+        scratch=(note,),
+    )
     middle = near(middle)
     stats = exchange(stats, ROW + NEAR)
     middle = middle + rows_beside(middle)
     partial = call(
-        functools.partial(conv_kernel, False), struct((4, 8, 16, 512)), *middle, stats, *w1,
+        functools.partial(conv_kernel, 1), struct((4, 8, 16, 512)), *middle, stats, *weights,
         scratch=scratch, flops=flops,
     )
     partial = exchange(partial, "zh")

time: 117 us -> 101 us (0.86)
  starting transfers between devices: 57.5 us -> 47.1 us
  waiting for transfers between devices: 28 us -> 24.6 us
  Pallas kernels: 11.8 us -> 9.31 us
    ppermute x3 -> x4, waiting for transfers between devices: 10.5 us -> 1.26 us  [the longest x1 1.25 us: local(): lax.ppermute(far, 'core', swap)]
    all_to_all x4 -> x3, starting transfers between devices: 34.4 us -> 25.1 us  [exchange(): return lax.all_to_all(x, axes, 0, 0, tiled=True)]
    all_to_all x4 -> x3, waiting for transfers between devices: 6 us -> 13.3 us  [exchange(): return lax.all_to_all(x, axes, 0, 0, tiled=True)]
    pallas_call x9 -> x7, Pallas kernels: 11.8 us -> 9.31 us  [call(): pl.pallas_call(kernel, out_shape=outs, in_specs=specs, out_specs=jax.tree...]
    ppermute x2, waiting for transfers between devices: 11.5 us -> 10 us  [rows_beside(): beyond = lax.ppermute(beyond, ROW, pairs)]
    ppermute x3 -> x4, starting transfers between devices: 8.97 us -> 8.04 us  [the longest x1 5.85 us: local(): side = lax.ppermute(side, ('core', 'zh'), around)]
  transfers between devices with their start and end apart: 17 -> 17, of which waited for: 5 -> 4; matrix products, arithmetic and copies ran while one was open for 0% -> 0% of each run, Pallas kernels for 1% -> 0%
where the time goes in v5:
time: 101 us
  starting transfers between devices  47.1 us (47%)
  waiting for transfers between devices  24.6 us (24%)
  blocking collectives  18.9 us (19%)
  Pallas kernels  9.31 us (9%)
    all_to_all x3, starting transfers between devices, exchange(): return lax.all_to_all(x, axes, 0, 0, tiled=True)  25.1 us
    all_to_all x1, blocking collectives, exchange(): return lax.all_to_all(x, axes, 0, 0, tiled=True)  18.9 us
    all_to_all x3, waiting for transfers between devices, exchange(): return lax.all_to_all(x, axes, 0, 0, tiled=True)  13.3 us
    ppermute x2, waiting for transfers between devices, rows_beside(): beyond = lax.ppermute(beyond, ROW, pairs)  10 us
    pallas_call x7, Pallas kernels, call(): pl.pallas_call(kernel, out_shape=outs, in_specs=specs, out_specs=jax.tree...  9.31 us
    ppermute x2, starting transfers between devices, rows_beside(): beyond = lax.ppermute(beyond, ROW, pairs)  7.69 us
    ppermute x1, starting transfers between devices, local(): side = lax.ppermute(side, ('core', 'zh'), around)  5.85 us
    ppermute x6, starting transfers between devices, near(): lax.ppermute(x, NEAR, [(i, i ^ k) for i in range(4)])  5.56 us
  transfers between devices with their start and end apart: 17, of which 4 were waited for; matrix products, arithmetic and copies ran while one was open for 0% of the time, Pallas kernels for 0%

profile of v5, /device:TPU:27, one launch (start us, length us, event | category | flops | bytes accessed | tf_op | source)
XLA Modules:
  0.0 100.8 jit_solution(1774481820070915576)
XLA Ops:
  0.0 2.3 %shard_map.64 = (bf16[8,16,768]{2,1,0:T(8,128)(2,1)}, bf16[8,16,256]{2,1,0:T(8,128)(2,1)}, f32[64,8,128]{2,1,0:T(8,128)}, f32[8,128]{1,0:T(8,128)}, bf16[2,3,3,1...) custom-call(bf16[4,8,16,128]{3,2,1,0:T(8,128)(2,1)} %x_ref.1, ...), custom_call_target="tpu_custom_call" | custom-call | bytes 704768 | tf_op jit(solution)/shard_map/pallas_call | solution.py:31
  2.3 0.3 collective-permute-start
  2.7 1.6 %collective-permute-start.1 = (bf16[8,16,768]{2,1,0:T(8,128)(2,1)}, bf16[8,16,768]{2,1,0:T(8,128)(2,1)S(1)}, u32[]{:S(2)}, u32[]{:S(2)}) collective-permute-start(bf16[8,16,768]{2,1,0:T(8,128)(2,1)} %get-tuple-element.18.a_ref), channel_id=1, source_target_pairs={{0,2},{1,3},{2,0},{3,1},{4,6},{5,7},{6,4},{7,5},{8,10},{9,11},{10,... | collective-permute-start | bytes 589832 | tf_op jit(solution)/shard_map/ppermute | solution.py:238
  4.3 0.9 collective-permute-start.2
  5.2 5.8 %collective-permute-start.5 = (bf16[2,3,3,16,192]{4,3,2,1,0:T(8,128)(2,1)}, bf16[2,3,3,16,192]{4,3,2,1,0:T(8,128)(2,1)S(1)}, u32[]{:S(2)}, u32[]{:S(2)}) collective-permute-start(bf16[2,3,3,16,192]{4,3,2,1,0:T(8,128)(2,1)} %get-tuple-element.23), channel_id=1, source_target_pairs={{0,4},{4,8},{8,12},{12,0},{16,28},{20,16},{24,20},{28,24},{1,5},{5... | collective-permute-start | bytes 331784 | tf_op jit(solution)/shard_map/ppermute | solution.py:263
  11.1 0.9 collective-permute-start.6
  12.0 11.2 %all-to-all-start = ((f32[64,8,128]{2,1,0:T(8,128)}), f32[64,8,128]{2,1,0:T(8,128)S(1)}, u32[]{:S(2)}, u32[]{:S(2)}) async-start(f32[64,8,128]{2,1,0:T(8,128)} %get-tuple-element.21), calls=%async_computation | async-start | bytes 524288 | tf_op jit(solution)/shard_map/all_to_all | solution.py:242
  23.2 0.0 copy-start.4
  23.2 0.0 collective-permute-done.5.side_ref
  23.2 1.2 %collective-permute-start.7 = (bf16[2,3,3,16,192]{4,3,2,1,0:T(8,128)(2,1)S(1)}, bf16[2,3,3,16,192]{4,3,2,1,0:T(8,128)(2,1)S(1)}, u32[]{:S(2)}, u32[]{:S(2)}) collective-permute-start(bf16[2,3,3,16,192]{4,3,2,1,0:T(8,128)(2,1)S(1)} %collective-permute-done.5.side_ref), channel_id=1, source_target_pairs={{0,16},{16,0},{1,17},{17,1},{2,18},{18,2},{3,19},{19,3},{4,20},{20... | collective-permute-start | bytes 331784 | tf_op jit(solution)/shard_map/ppermute | solution.py:269
  24.4 0.0 collective-permute-done.b_ref
  24.4 0.0 collective-permute-done.1.c_ref
  24.4 0.0 collective-permute-done.2.d_ref
  24.5 0.1 collective-permute-start.3
  24.6 4.1 %collective-permute-start.4 = (bf16[4,16,768]{2,1,0:T(8,128)(2,1)S(1)}, bf16[4,16,768]{2,1,0:T(8,128)(2,1)S(1)}, u32[]{:S(2)}, u32[]{:S(2)}) collective-permute-start(bf16[4,16,768]{2,1,0:T(8,128)(2,1)S(1)} %get-tuple-element.20), channel_id=1, source_target_pairs={{16,32},{48,64},{80,96},{112,128},{144,160},{176,192},{208,224},{3... | collective-permute-start | bytes 294920 | tf_op jit(solution)/shard_map/ppermute | solution.py:233
  28.7 0.0 collective-permute-done.6.far_ref
  28.7 0.1 collective-permute-start.8
  28.8 1.3 %collective-permute-done.8.far2_ref = bf16[3,3,16,192]{3,2,1,0:T(8,128)(2,1)S(1)} collective-permute-done((bf16[3,3,16,192]{3,2,1,0:T(8,128)(2,1)S(1)}, bf16[3,3,16,192]{3,2,1,0:T(8,128)(2,1)S(1)}, u32[]{:S(2)}, u32[]{:S(2)}) %collective-permute-start.8) | collective-permute-done | bytes 55328 | tf_op jit(solution)/shard_map/ppermute | solution.py:269
  30.0 0.0 collective-permute-done.7.side2_ref
  30.0 0.0 collective-permute-done.3.chip_ref
  30.1 4.1 %collective-permute-done.4.next_ref = bf16[4,16,768]{2,1,0:T(8,128)(2,1)S(1)} collective-permute-done((bf16[4,16,768]{2,1,0:T(8,128)(2,1)S(1)}, bf16[4,16,768]{2,1,0:T(8,128)(2,1)S(1)}, u32[]{:S(2)}, u32[]{:S(2)}) %collective-permute-start.4) | collective-permute-done | bytes 98336 | tf_op jit(solution)/shard_map/ppermute | solution.py:233
  34.1 0.0 all-to-all-done.stats_ref
  34.2 0.0 copy-done.4
  34.2 3.1 %shard_map.66 = bf16[4,8,16,512]{3,2,1,0:T(8,128)(2,1)} custom-call(bf16[8,16,768]{2,1,0:T(8,128)(2,1)S(1)} %copy-done.3, bf16[8,16,768]{2,1,0:T(8,128)(2,1)S(1)} %collective-permute-done.b_ref, bf16[8,16,768]{2,1,0:T(8,128)(2,1)S(1)} %collective-permute-done.1.c_ref, bf16[8,16,768]{2,1,0:T(8,128)(2,1)S(1)} %collective-permute-done.2.d_ref, ...), custom_call_target="tpu_custom_call" | custom-call | flops 905969664 | bytes 1687552 | tf_op jit(solution)/shard_map/pallas_call | solution.py:31
  37.2 3.6 %all-to-all-start.1 = ((bf16[4,8,16,512]{3,2,1,0:T(8,128)(2,1)}), bf16[4,8,16,512]{3,2,1,0:T(8,128)(2,1)S(1)}, u32[]{:S(2)}, u32[]{:S(2)}) async-start(bf16[4,8,16,512]{3,2,1,0:T(8,128)(2,1)} %shard_map.66), calls=%async_computation.1 | async-start | bytes 1048576 | tf_op jit(solution)/shard_map/all_to_all | solution.py:242
  40.8 0.0 copy-done.5
  40.9 13.3 %all-to-all-done.1.part_ref = bf16[4,8,16,512]{3,2,1,0:T(8,128)(2,1)S(1)} async-done(((bf16[4,8,16,512]{3,2,1,0:T(8,128)(2,1)}), bf16[4,8,16,512]{3,2,1,0:T(8,128)(2,1)S(1)}, u32[]{:S(2)}, u32[]{:S(2)}) %all-to-all-start.1) | async-done | bytes 524320 | tf_op jit(solution)/shard_map/all_to_all | solution.py:242
  54.2 0.1 broadcast_in_dim.13.bias_ref
  54.2 0.6 copy-done.2
  54.8 0.9 shard_map.67
  55.7 0.1 collective-permute-start.10
  55.8 1.9 %collective-permute-start.11 = (bf16[8,16,768]{2,1,0:T(8,128)(2,1)S(1)}, bf16[8,16,768]{2,1,0:T(8,128)(2,1)S(1)}, u32[]{:S(2)}, u32[]{:S(2)}) collective-permute-start(bf16[8,16,768]{2,1,0:T(8,128)(2,1)S(1)} %get-tuple-element.27.a_ref), channel_id=1, source_target_pairs={{0,3},{1,2},{2,1},{3,0},{4,7},{5,6},{6,5},{7,4},{8,11},{9,10},{10,... | collective-permute-start | bytes 589832 | tf_op jit(solution)/shard_map/ppermute | solution.py:238
  57.7 0.6 collective-permute-start.9
  58.4 10.3 %all-to-all-start.2 = ((f32[64,8,128]{2,1,0:T(8,128)}), f32[64,8,128]{2,1,0:T(8,128)S(1)}, u32[]{:S(2)}, u32[]{:S(2)}) async-start(f32[64,8,128]{2,1,0:T(8,128)} %get-tuple-element.30), calls=%async_computation.2 | async-start | bytes 524288 | tf_op jit(solution)/shard_map/all_to_all | solution.py:242
  68.7 0.0 collective-permute-done.10.c_ref
  68.7 0.0 collective-permute-done.11.d_ref
  68.7 0.0 collective-permute-done.9.b_ref
  68.7 0.6 collective-permute-start.12
  69.4 3.6 %collective-permute-start.13 = (bf16[4,16,768]{2,1,0:T(8,128)(2,1)S(1)}, bf16[4,16,768]{2,1,0:T(8,128)(2,1)S(1)}, u32[]{:S(2)}, u32[]{:S(2)}) collective-permute-start(bf16[4,16,768]{2,1,0:T(8,128)(2,1)S(1)} %get-tuple-element.29), channel_id=1, source_target_pairs={{16,32},{48,64},{80,96},{112,128},{144,160},{176,192},{208,224},{3... | collective-permute-start | bytes 294920 | tf_op jit(solution)/shard_map/ppermute | solution.py:233
  73.0 0.0 collective-permute-done.12.chip_ref
  73.0 5.9 %collective-permute-done.13.next_ref = bf16[4,16,768]{2,1,0:T(8,128)(2,1)S(1)} collective-permute-done((bf16[4,16,768]{2,1,0:T(8,128)(2,1)S(1)}, bf16[4,16,768]{2,1,0:T(8,128)(2,1)S(1)}, u32[]{:S(2)}, u32[]{:S(2)}) %collective-permute-start.13) | collective-permute-done | bytes 98336 | tf_op jit(solution)/shard_map/ppermute | solution.py:233
  78.9 0.0 all-to-all-done.2.stats_ref
  78.9 2.2 %shard_map.69 = bf16[4,8,16,512]{3,2,1,0:T(8,128)(2,1)S(1)} custom-call(bf16[8,16,768]{2,1,0:T(8,128)(2,1)S(1)} %get-tuple-element.27.a_ref, bf16[8,16,768]{2,1,0:T(8,128)(2,1)S(1)} %collective-permute-done.9.b_ref, bf16[8,16,768]{2,1,0:T(8,128)(2,1)S(1)} %collective-permute-done.10.c_ref, bf16[8,16,768]{2,1,0:T(8,128)(2,1)S(1)} %collective-permute-done.11.d_ref, ...), custom_call_target="tpu_custom_call" | custom-call | flops 905969664 | bytes 1687552 | tf_op jit(solution)/shard_map/pallas_call | solution.py:31
  81.1 0.0 copy-start
  81.1 18.9 %all_to_all.20.part_ref = bf16[4,8,16,512]{3,2,1,0:T(8,128)(2,1)S(1)} all-to-all(bf16[4,8,16,512]{3,2,1,0:T(8,128)(2,1)S(1)} %shard_map.69), channel_id=1, replica_groups=mesh['xh'=2,'y'=4,'core'=2,'zh'=4,'zl'=2,'xl'=2] {'zh'}, dimensions={0} | all-to-all | bytes 1048576 | tf_op jit(solution)/shard_map/all_to_all | solution.py:242
  100.0 0.1 broadcast_in_dim.15.bias_ref
  100.1 0.0 copy-done
  100.1 0.8 shard_map.70
  (9 shorter events, 0.1 us)
Async XLA Ops:
  2.3 22.1 %collective-permute-start = (bf16[8,16,768]{2,1,0:T(8,128)(2,1)}, bf16[8,16,768]{2,1,0:T(8,128)(2,1)S(1)}, u32[]{:S(2)}, u32[]{:S(2)}) collective-permute-start(bf16[8,16,768]{2,1,0:T(8,128)(2,1)} %get-tuple-element.18.a_ref), channel_id=1, source_target_pairs={{0,1},{1,0},{2,3},{3,2},{4,5},{5,4},{6,7},{7,6},{8,9},{9,8},{10,11... | collective-permute-start | bytes 589832 | tf_op jit(solution)/shard_map/ppermute | solution.py:238
  2.7 21.8 %collective-permute-start.1 = (bf16[8,16,768]{2,1,0:T(8,128)(2,1)}, bf16[8,16,768]{2,1,0:T(8,128)(2,1)S(1)}, u32[]{:S(2)}, u32[]{:S(2)}) collective-permute-start(bf16[8,16,768]{2,1,0:T(8,128)(2,1)} %get-tuple-element.18.a_ref), channel_id=1, source_target_pairs={{0,2},{1,3},{2,0},{3,1},{4,6},{5,7},{6,4},{7,5},{8,10},{9,11},{10,... | collective-permute-start | bytes 589832 | tf_op jit(solution)/shard_map/ppermute | solution.py:238
  4.3 20.1 %collective-permute-start.2 = (bf16[8,16,768]{2,1,0:T(8,128)(2,1)}, bf16[8,16,768]{2,1,0:T(8,128)(2,1)S(1)}, u32[]{:S(2)}, u32[]{:S(2)}) collective-permute-start(bf16[8,16,768]{2,1,0:T(8,128)(2,1)} %get-tuple-element.18.a_ref), channel_id=1, source_target_pairs={{0,3},{1,2},{2,1},{3,0},{4,7},{5,6},{6,5},{7,4},{8,11},{9,10},{10,... | collective-permute-start | bytes 589832 | tf_op jit(solution)/shard_map/ppermute | solution.py:238
  5.2 18.0 %collective-permute-start.5 = (bf16[2,3,3,16,192]{4,3,2,1,0:T(8,128)(2,1)}, bf16[2,3,3,16,192]{4,3,2,1,0:T(8,128)(2,1)S(1)}, u32[]{:S(2)}, u32[]{:S(2)}) collective-permute-start(bf16[2,3,3,16,192]{4,3,2,1,0:T(8,128)(2,1)} %get-tuple-element.23), channel_id=1, source_target_pairs={{0,4},{4,8},{8,12},{12,0},{16,28},{20,16},{24,20},{28,24},{1,5},{5... | collective-permute-start | bytes 331784 | tf_op jit(solution)/shard_map/ppermute | solution.py:263
  11.1 17.6 %collective-permute-start.6 = (bf16[3,3,16,192]{3,2,1,0:T(8,128)(2,1)}, bf16[3,3,16,192]{3,2,1,0:T(8,128)(2,1)S(1)}, u32[]{:S(2)}, u32[]{:S(2)}) collective-permute-start(bf16[3,3,16,192]{3,2,1,0:T(8,128)(2,1)} %get-tuple-element.24), channel_id=1, source_target_pairs={{0,8},{4,12},{8,0},{12,4},{1,9},{5,13},{9,1},{13,5},{2,10},{6,14},... | collective-permute-start | bytes 165896 | tf_op jit(solution)/shard_map/ppermute | solution.py:264
  12.0 12.5 %copy-start.3 = (bf16[8,16,768]{2,1,0:T(8,128)(2,1)S(1)}, bf16[8,16,768]{2,1,0:T(8,128)(2,1)}, u32[]{:S(2)}) copy-start(bf16[8,16,768]{2,1,0:T(8,128)(2,1)} %get-tuple-element.18.a_ref) | copy-start | bytes 589828
  12.0 22.2 %all-to-all-start = ((f32[64,8,128]{2,1,0:T(8,128)}), f32[64,8,128]{2,1,0:T(8,128)S(1)}, u32[]{:S(2)}, u32[]{:S(2)}) async-start(f32[64,8,128]{2,1,0:T(8,128)} %get-tuple-element.21), calls=%async_computation | async-start | bytes 524288 | tf_op jit(solution)/shard_map/all_to_all | solution.py:242
  23.2 10.9 %copy-start.4 = (bf16[2,3,3,16,192]{4,3,2,1,0:T(8,128)(2,1)S(1)}, bf16[2,3,3,16,192]{4,3,2,1,0:T(8,128)(2,1)}, u32[]{:S(2)}) copy-start(bf16[2,3,3,16,192]{4,3,2,1,0:T(8,128)(2,1)} %get-tuple-element.22.own_ref) | copy-start | bytes 331780
  23.2 6.8 %collective-permute-start.7 = (bf16[2,3,3,16,192]{4,3,2,1,0:T(8,128)(2,1)S(1)}, bf16[2,3,3,16,192]{4,3,2,1,0:T(8,128)(2,1)S(1)}, u32[]{:S(2)}, u32[]{:S(2)}) collective-permute-start(bf16[2,3,3,16,192]{4,3,2,1,0:T(8,128)(2,1)S(1)} %collective-permute-done.5.side_ref), channel_id=1, source_target_pairs={{0,16},{16,0},{1,17},{17,1},{2,18},{18,2},{3,19},{19,3},{4,20},{20... | collective-permute-start | bytes 331784 | tf_op jit(solution)/shard_map/ppermute | solution.py:269
  24.5 5.6 %collective-permute-start.3 = (bf16[4,16,768]{2,1,0:T(8,128)(2,1)S(1)}, bf16[4,16,768]{2,1,0:T(8,128)(2,1)S(1)}, u32[]{:S(2)}, u32[]{:S(2)}) collective-permute-start(bf16[4,16,768]{2,1,0:T(8,128)(2,1)S(1)} %get-tuple-element.19), channel_id=1, source_target_pairs={{0,16},{16,0},{32,48},{48,32},{64,80},{80,64},{96,112},{112,96},{1... | collective-permute-start | bytes 294920 | tf_op jit(solution)/shard_map/ppermute | solution.py:231
  24.6 9.5 %collective-permute-start.4 = (bf16[4,16,768]{2,1,0:T(8,128)(2,1)S(1)}, bf16[4,16,768]{2,1,0:T(8,128)(2,1)S(1)}, u32[]{:S(2)}, u32[]{:S(2)}) collective-permute-start(bf16[4,16,768]{2,1,0:T(8,128)(2,1)S(1)} %get-tuple-element.20), channel_id=1, source_target_pairs={{16,32},{48,64},{80,96},{112,128},{144,160},{176,192},{208,224},{3... | collective-permute-start | bytes 294920 | tf_op jit(solution)/shard_map/ppermute | solution.py:233
  28.7 1.4 %collective-permute-start.8 = (bf16[3,3,16,192]{3,2,1,0:T(8,128)(2,1)S(1)}, bf16[3,3,16,192]{3,2,1,0:T(8,128)(2,1)S(1)}, u32[]{:S(2)}, u32[]{:S(2)}) collective-permute-start(bf16[3,3,16,192]{3,2,1,0:T(8,128)(2,1)S(1)} %collective-permute-done.6.far_ref), channel_id=1, source_target_pairs={{0,16},{16,0},{1,17},{17,1},{2,18},{18,2},{3,19},{19,3},{4,20},{20... | collective-permute-start | bytes 165896 | tf_op jit(solution)/shard_map/ppermute | solution.py:269
  37.2 3.6 %copy-start.5 = (f32[2,16]{1,0:T(2,128)S(1)}, f32[2,16]{1,0:T(2,128)}, u32[]{:S(2)}) copy-start(f32[2,16]{1,0:T(2,128)} %param.11) | copy-start | bytes 388
  37.2 17.0 %copy-start.1 = (bf16[8,16,256]{2,1,0:T(8,128)(2,1)S(1)}, bf16[8,16,256]{2,1,0:T(8,128)(2,1)}, u32[]{:S(2)}) copy-start(bf16[8,16,256]{2,1,0:T(8,128)(2,1)} %get-tuple-element.25.later_ref) | copy-start | bytes 196612
  37.2 16.9 %all-to-all-start.1 = ((bf16[4,8,16,512]{3,2,1,0:T(8,128)(2,1)}), bf16[4,8,16,512]{3,2,1,0:T(8,128)(2,1)S(1)}, u32[]{:S(2)}, u32[]{:S(2)}) async-start(bf16[4,8,16,512]{3,2,1,0:T(8,128)(2,1)} %shard_map.66), calls=%async_computation.1 | async-start | bytes 1048576 | tf_op jit(solution)/shard_map/all_to_all | solution.py:242
  54.2 0.7 copy-start.2
  55.7 13.0 %collective-permute-start.10 = (bf16[8,16,768]{2,1,0:T(8,128)(2,1)S(1)}, bf16[8,16,768]{2,1,0:T(8,128)(2,1)S(1)}, u32[]{:S(2)}, u32[]{:S(2)}) collective-permute-start(bf16[8,16,768]{2,1,0:T(8,128)(2,1)S(1)} %get-tuple-element.27.a_ref), channel_id=1, source_target_pairs={{0,2},{1,3},{2,0},{3,1},{4,6},{5,7},{6,4},{7,5},{8,10},{9,11},{10,... | collective-permute-start | bytes 589832 | tf_op jit(solution)/shard_map/ppermute | solution.py:238
  55.8 12.9 %collective-permute-start.11 = (bf16[8,16,768]{2,1,0:T(8,128)(2,1)S(1)}, bf16[8,16,768]{2,1,0:T(8,128)(2,1)S(1)}, u32[]{:S(2)}, u32[]{:S(2)}) collective-permute-start(bf16[8,16,768]{2,1,0:T(8,128)(2,1)S(1)} %get-tuple-element.27.a_ref), channel_id=1, source_target_pairs={{0,3},{1,2},{2,1},{3,0},{4,7},{5,6},{6,5},{7,4},{8,11},{9,10},{10,... | collective-permute-start | bytes 589832 | tf_op jit(solution)/shard_map/ppermute | solution.py:238
  57.7 11.0 %collective-permute-start.9 = (bf16[8,16,768]{2,1,0:T(8,128)(2,1)S(1)}, bf16[8,16,768]{2,1,0:T(8,128)(2,1)S(1)}, u32[]{:S(2)}, u32[]{:S(2)}) collective-permute-start(bf16[8,16,768]{2,1,0:T(8,128)(2,1)S(1)} %get-tuple-element.27.a_ref), channel_id=1, source_target_pairs={{0,1},{1,0},{2,3},{3,2},{4,5},{5,4},{6,7},{7,6},{8,9},{9,8},{10,11... | collective-permute-start | bytes 589832 | tf_op jit(solution)/shard_map/ppermute | solution.py:238
  58.4 20.5 %all-to-all-start.2 = ((f32[64,8,128]{2,1,0:T(8,128)}), f32[64,8,128]{2,1,0:T(8,128)S(1)}, u32[]{:S(2)}, u32[]{:S(2)}) async-start(f32[64,8,128]{2,1,0:T(8,128)} %get-tuple-element.30), calls=%async_computation.2 | async-start | bytes 524288 | tf_op jit(solution)/shard_map/all_to_all | solution.py:242
  68.7 4.2 %collective-permute-start.12 = (bf16[4,16,768]{2,1,0:T(8,128)(2,1)S(1)}, bf16[4,16,768]{2,1,0:T(8,128)(2,1)S(1)}, u32[]{:S(2)}, u32[]{:S(2)}) collective-permute-start(bf16[4,16,768]{2,1,0:T(8,128)(2,1)S(1)} %get-tuple-element.28), channel_id=1, source_target_pairs={{0,16},{16,0},{32,48},{48,32},{64,80},{80,64},{96,112},{112,96},{1... | collective-permute-start | bytes 294920 | tf_op jit(solution)/shard_map/ppermute | solution.py:231
  69.4 9.5 %collective-permute-start.13 = (bf16[4,16,768]{2,1,0:T(8,128)(2,1)S(1)}, bf16[4,16,768]{2,1,0:T(8,128)(2,1)S(1)}, u32[]{:S(2)}, u32[]{:S(2)}) collective-permute-start(bf16[4,16,768]{2,1,0:T(8,128)(2,1)S(1)} %get-tuple-element.29), channel_id=1, source_target_pairs={{16,32},{48,64},{80,96},{112,128},{144,160},{176,192},{208,224},{3... | collective-permute-start | bytes 294920 | tf_op jit(solution)/shard_map/ppermute | solution.py:233
  81.1 19.0 %copy-start = (bf16[4,8,16,128]{3,2,1,0:T(8,128)(2,1)S(1)}, bf16[4,8,16,128]{3,2,1,0:T(8,128)(2,1)}, u32[]{:S(2)}) copy-start(bf16[4,8,16,128]{3,2,1,0:T(8,128)(2,1)} %x_ref.1) | copy-start | bytes 393220

commit v6 on v5

--- a/solution.py
+++ b/solution.py
@@ -65,7 +65,7 @@
 
 def begin_kernel(
     x_hbm, cache_hbm, gain_hbm, shift_hbm, w_hbm,
-    raw_ref, later_ref, stats_ref, note1_ref, own_ref, side_ref, far_ref,
+    raw_ref, later_ref, stats_ref, own_ref, side_ref, far_ref,
     x_ref, cache_ref, gain_ref, shift_ref, w_ref, note_ref, pieces_ref, sems,
 ):
     fetch(
@@ -96,10 +96,9 @@
     own_ref[...] = pieces_ref[0]
     side_ref[...] = pieces_ref[1 + 2 * core]
     far_ref[...] = pieces_ref[2, core]
-    for layer, ref in ((0, note_ref), (1, note1_ref)):
-        ref[...] = jnp.zeros((8, 128), F32)
-        ref[4:5, 0:16] = gain_ref[layer : layer + 1, :]
-        ref[5:6, 0:16] = shift_ref[layer : layer + 1, :]
+    note_ref[...] = jnp.zeros((8, 128), F32)
+    note_ref[4:5, 0:16] = gain_ref[0:1, :]
+    note_ref[5:6, 0:16] = shift_ref[0:1, :]
     put_stats(raw_ref, note_ref, stats_ref)
 
 
@@ -132,9 +131,10 @@
 
 def conv_kernel(
     layer, a_ref, b_ref, c_ref, d_ref, chip_ref, next_ref, stats_ref,
-    own_ref, side_ref, far_ref, side2_ref, far2_ref, o_ref, affine_ref, slab_ref, held_ref,
+    own_ref, side_ref, far_ref, side2_ref, far2_ref, o0_ref, o1_ref, o2_ref, o3_ref,
+    affine_ref, slab_ref, held_ref,
 ):
-    row, me, here = place()
+    row, _, here = place()
     get_affine(stats_ref, affine_ref)
     upper = lax.rem(row, 2) == 0
     not_top = (row > 0).astype(F32)
@@ -163,7 +163,6 @@
                     x = x * not_bottom
                 slab_ref[r, b, :, lanes] = x.astype(BF16)
     core = lax.rem(row, 2)
-    sources = (me, lax.rem(me + 3 - 2 * core, 4), lax.rem(me + 1 + 2 * core, 4), lax.rem(me + 2, 4))
     for dt in range(3):
         held_ref[dt, 0] = own_ref[layer, dt]
         held_ref[dt, 1] = side_ref[layer, dt]
@@ -189,29 +188,40 @@
             lanes = slice(128 * t, 128 * (t + 1))
             part = prod[:, :, :, lanes]
             summed = shift_columns(part[:, 0], part[:, 1], part[:, 2]).astype(BF16)
-            for q in range(4):
-                o_ref[sources[q], r, :, lanes] = summed[q]
-
-
-def merge_kernel(part_ref, bias_ref, later_ref, note1_ref, mid_ref, stats_ref, note_ref):
+            for q, o_ref in enumerate((o0_ref, o1_ref, o2_ref, o3_ref)):
+                o_ref[r, :, lanes] = summed[q]
+
+
+def merge_kernel(a_ref, b_ref, c_ref, d_ref, bias_ref, later_ref, note1_ref, mid_ref, stats_ref, note_ref):
     bias = jnp.concatenate([bias_ref[...]] * 4, axis=1)
     for r in range(8):
-        summed = part_ref[0, r].astype(F32) + part_ref[1, r].astype(F32)
-        summed += part_ref[2, r].astype(F32) + part_ref[3, r].astype(F32)
+        summed = a_ref[r].astype(F32) + b_ref[r].astype(F32)
+        summed += c_ref[r].astype(F32) + d_ref[r].astype(F32)
         mid_ref[r, :, 0:256] = later_ref[r]
         mid_ref[r, :, 256:768] = (summed + bias).astype(BF16)
     note_ref[...] = note1_ref[...]
     put_stats(mid_ref, note_ref, stats_ref)
 
 
-def last_kernel(x_ref, part_ref, bias_ref, o_ref):
+def last_kernel(x_ref, a_ref, b_ref, c_ref, d_ref, bias_ref, o_ref):
     bias = bias_ref[...]
     for r in range(8):
         for t in range(4):
             lanes = slice(128 * t, 128 * (t + 1))
-            branch = part_ref[0, r, :, lanes].astype(F32) + part_ref[1, r, :, lanes].astype(F32)
-            branch += part_ref[2, r, :, lanes].astype(F32) + part_ref[3, r, :, lanes].astype(F32)
+            branch = a_ref[r, :, lanes].astype(F32) + b_ref[r, :, lanes].astype(F32)
+            branch += c_ref[r, :, lanes].astype(F32) + d_ref[r, :, lanes].astype(F32)
             o_ref[t, r] = (x_ref[t, r].astype(F32) + (branch + bias)).astype(BF16)
+
+
+def sides(step):
+    return [(i, (i + step) % 4) for i in range(4)] + [(4 + i, 4 + (i - step) % 4) for i in range(4)]
+
+
+def bring(own, side, other, far):
+    far = lax.ppermute(far, "zh", [(i, (i + 2) % 4) for i in range(4)])
+    side = lax.ppermute(side, ("core", "zh"), sides(-1))
+    other = lax.ppermute(other, ("core", "zh"), sides(1))
+    return [own, side, other, far]
 
 
 def struct(shape, dtype=BF16):
@@ -245,11 +255,11 @@
 def local(frames, cache, norm_gain, norm_shift, conv_weight, conv_bias):
     note = pltpu.VMEM((8, 128), F32)
     piece = (2, 3, 3, 16, 192)
-    raw, later, stats, note1, own, side, far = call(
+    raw, later, stats, own, side, far = call(
         begin_kernel,
         (
-            struct((8, 16, 768)), struct((8, 16, 256)), struct((64, 8, 128), F32), struct((8, 128), F32),
-            struct(piece), struct(piece), struct(piece[1:]),
+            struct((8, 16, 768)), struct((8, 16, 256)), struct((64, 8, 128), F32), struct(piece),
+            struct(piece), struct(piece[1:]),
         ),
         frames, cache, norm_gain, norm_shift, conv_weight.transpose(0, 2, 1, 3),
         scratch=(
@@ -259,8 +269,7 @@
         ),
         far=(0, 1, 2, 3, 4),
     )
-    around = [(i, (i + 1) % 4) for i in range(4)] + [(4 + i, 4 + (i + 3) % 4) for i in range(4)]
-    side = lax.ppermute(side, ("core", "zh"), around)
+    side = lax.ppermute(side, ("core", "zh"), sides(1))
     far = lax.ppermute(far, "zh", [(i, (i + 2) % 4) for i in range(4)])
     raw = near(raw)
     stats = exchange(stats, ROW + NEAR)
@@ -268,31 +277,33 @@
     swap = [(0, 1), (1, 0)]
     weights = [own, side, far, lax.ppermute(side, "core", swap), lax.ppermute(far, "core", swap)]
     bias = jnp.broadcast_to(conv_bias[:, :, None], (2, 16, 128))
+    note1 = jnp.pad(jnp.stack([norm_gain[1], norm_shift[1]]), ((4, 2), (0, 112)))
     scratch = (
         pltpu.VMEM((3, 4, 16, 128), F32),
         pltpu.VMEM((10, 4, 16, 768), BF16),
         pltpu.VMEM((3, 4, 3, 16, 192), BF16),
     )
     flops = 2 * 192 * 576 * 4096
+    parts = (struct((8, 16, 512)),) * 4
 
     partial = call(
-        functools.partial(conv_kernel, 0), struct((4, 8, 16, 512)), *raw, stats, *weights,
+        functools.partial(conv_kernel, 0), parts, *raw, stats, *weights,
         scratch=scratch, flops=flops,
     )
-    partial = exchange(partial, "zh")
+    partial = bring(*partial)
     middle, stats = call(
-        merge_kernel, (struct((8, 16, 768)), struct((64, 8, 128), F32)), partial, bias[0], later, note1,
+        merge_kernel, (struct((8, 16, 768)), struct((64, 8, 128), F32)), *partial, bias[0], later, note1,
         scratch=(note,),
     )
     middle = near(middle)
     stats = exchange(stats, ROW + NEAR)
     middle = middle + rows_beside(middle)
     partial = call(
-        functools.partial(conv_kernel, 1), struct((4, 8, 16, 512)), *middle, stats, *weights,
+        functools.partial(conv_kernel, 1), parts, *middle, stats, *weights,
         scratch=scratch, flops=flops,
     )
-    partial = exchange(partial, "zh")
-    return call(last_kernel, struct((4, 8, 16, 128)), frames, partial, bias[1])
+    partial = bring(*partial)
+    return call(last_kernel, struct((4, 8, 16, 128)), frames, *partial, bias[1])
 
 
 def solution(mesh):

time: 101 us -> 93.3 us (0.924)
  the two profiles are of different devices: /device:TPU:27 before, /device:TPU:1 now
where the time goes in v6:
time: 93.3 us; the launch traced here: 93 us
  starting transfers between devices  51.7 us (55%)
  waiting for transfers between devices  31.9 us (34%)
  Pallas kernels  8.43 us (9%)
    all_to_all x2, starting transfers between devices, exchange(): return lax.all_to_all(x, axes, 0, 0, tiled=True)  18.1 us
    ppermute x2, waiting for transfers between devices, bring(): far = lax.ppermute(far, 'zh', [(i, (i + 2) % 4) for i in range(4)])  8.53 us
    ppermute x2, waiting for transfers between devices, bring(): other = lax.ppermute(other, ('core', 'zh'), sides(1))  8.47 us
    pallas_call x7, Pallas kernels, call(): pl.pallas_call(kernel, out_shape=outs, in_specs=specs, out_specs=jax.tree...  8.43 us
    ppermute x6, starting transfers between devices, near(): lax.ppermute(x, NEAR, [(i, i ^ k) for i in range(4)])  6.42 us
    ppermute x1, starting transfers between devices, local(): side = lax.ppermute(side, ('core', 'zh'), sides(1))  5.82 us
    ppermute x2, waiting for transfers between devices, rows_beside(): beyond = lax.ppermute(beyond, ROW, pairs)  5.72 us
    ppermute x2, starting transfers between devices, rows_beside(): beyond = lax.ppermute(beyond, ROW, pairs)  5.7 us
  transfers between devices with their start and end apart: 22, of which 12 were waited for; matrix products, arithmetic and copies ran while one was open for 0% of the time, Pallas kernels for 0%

profile of v6, /device:TPU:1, one launch (start us, length us, event | category | flops | bytes accessed | tf_op | source)
XLA Modules:
  0.0 93.0 jit_solution(640832287251815340)
XLA Ops:
  0.0 2.3 %shard_map.64 = (bf16[8,16,768]{2,1,0:T(8,128)(2,1)}, bf16[8,16,256]{2,1,0:T(8,128)(2,1)}, f32[64,8,128]{2,1,0:T(8,128)}, bf16[2,3,3,16,192]{4,3,2,1,0:T(8,128)(...) custom-call(bf16[4,8,16,128]{3,2,1,0:T(8,128)(2,1)} %x_ref.1, ...), custom_call_target="tpu_custom_call" | custom-call | bytes 704768 | tf_op jit(solution)/shard_map/pallas_call | solution.py:31
  2.3 2.1 %collective-permute-start = (bf16[8,16,768]{2,1,0:T(8,128)(2,1)}, bf16[8,16,768]{2,1,0:T(8,128)(2,1)S(1)}, u32[]{:S(2)}, u32[]{:S(2)}) collective-permute-start(bf16[8,16,768]{2,1,0:T(8,128)(2,1)} %get-tuple-element.25.a_ref), channel_id=1, source_target_pairs={{0,1},{1,0},{2,3},{3,2},{4,5},{5,4},{6,7},{7,6},{8,9},{9,8},{10,11... | collective-permute-start | bytes 589832 | tf_op jit(solution)/shard_map/ppermute | solution.py:248
  4.4 1.6 %collective-permute-start.1 = (bf16[8,16,768]{2,1,0:T(8,128)(2,1)}, bf16[8,16,768]{2,1,0:T(8,128)(2,1)S(1)}, u32[]{:S(2)}, u32[]{:S(2)}) collective-permute-start(bf16[8,16,768]{2,1,0:T(8,128)(2,1)} %get-tuple-element.25.a_ref), channel_id=1, source_target_pairs={{0,2},{1,3},{2,0},{3,1},{4,6},{5,7},{6,4},{7,5},{8,10},{9,11},{10,... | collective-permute-start | bytes 589832 | tf_op jit(solution)/shard_map/ppermute | solution.py:248
  6.1 0.0 collective-permute-start.2
  6.1 5.8 %collective-permute-start.5 = (bf16[2,3,3,16,192]{4,3,2,1,0:T(8,128)(2,1)}, bf16[2,3,3,16,192]{4,3,2,1,0:T(8,128)(2,1)S(1)}, u32[]{:S(2)}, u32[]{:S(2)}) collective-permute-start(bf16[2,3,3,16,192]{4,3,2,1,0:T(8,128)(2,1)} %get-tuple-element.30), channel_id=1, source_target_pairs={{0,4},{4,8},{8,12},{12,0},{16,28},{20,16},{24,20},{28,24},{1,5},{5... | collective-permute-start | bytes 331784 | tf_op jit(solution)/shard_map/ppermute | solution.py:272
  11.9 0.9 collective-permute-start.6
  12.8 11.3 %all-to-all-start = ((f32[64,8,128]{2,1,0:T(8,128)}), f32[64,8,128]{2,1,0:T(8,128)S(1)}, u32[]{:S(2)}, u32[]{:S(2)}) async-start(f32[64,8,128]{2,1,0:T(8,128)} %get-tuple-element.28), calls=%async_computation | async-start | bytes 524288 | tf_op jit(solution)/shard_map/all_to_all | solution.py:252
  24.1 0.0 collective-permute-done.5.side_ref
  24.1 2.1 %collective-permute-start.7 = (bf16[2,3,3,16,192]{4,3,2,1,0:T(8,128)(2,1)S(1)}, bf16[2,3,3,16,192]{4,3,2,1,0:T(8,128)(2,1)S(1)}, u32[]{:S(2)}, u32[]{:S(2)}) collective-permute-start(bf16[2,3,3,16,192]{4,3,2,1,0:T(8,128)(2,1)S(1)} %collective-permute-done.5.side_ref), channel_id=1, source_target_pairs={{0,16},{16,0},{1,17},{17,1},{2,18},{18,2},{3,19},{19,3},{4,20},{20... | collective-permute-start | bytes 331784 | tf_op jit(solution)/shard_map/ppermute | solution.py:278
  26.2 0.0 collective-permute-done.b_ref
  26.3 0.1 collective-permute-start.3
  26.4 3.6 %collective-permute-start.4 = (bf16[4,16,768]{2,1,0:T(8,128)(2,1)S(1)}, bf16[4,16,768]{2,1,0:T(8,128)(2,1)S(1)}, u32[]{:S(2)}, u32[]{:S(2)}) collective-permute-start(bf16[4,16,768]{2,1,0:T(8,128)(2,1)S(1)} %get-tuple-element.27), channel_id=1, source_target_pairs={{16,32},{48,64},{80,96},{112,128},{144,160},{176,192},{208,224},{3... | collective-permute-start | bytes 294920 | tf_op jit(solution)/shard_map/ppermute | solution.py:243
  29.9 0.0 collective-permute-done.6.far_ref
  30.0 0.1 collective-permute-start.8
  30.1 1.3 %collective-permute-done.8.far2_ref = bf16[3,3,16,192]{3,2,1,0:T(8,128)(2,1)S(1)} collective-permute-done((bf16[3,3,16,192]{3,2,1,0:T(8,128)(2,1)S(1)}, bf16[3,3,16,192]{3,2,1,0:T(8,128)(2,1)S(1)}, u32[]{:S(2)}, u32[]{:S(2)}) %collective-permute-start.8) | collective-permute-done | bytes 55328 | tf_op jit(solution)/shard_map/ppermute | solution.py:278
  31.3 1.5 %collective-permute-done.4.next_ref = bf16[4,16,768]{2,1,0:T(8,128)(2,1)S(1)} collective-permute-done((bf16[4,16,768]{2,1,0:T(8,128)(2,1)S(1)}, bf16[4,16,768]{2,1,0:T(8,128)(2,1)S(1)}, u32[]{:S(2)}, u32[]{:S(2)}) %collective-permute-start.4) | collective-permute-done | bytes 98336 | tf_op jit(solution)/shard_map/ppermute | solution.py:243
  32.8 1.2 %all-to-all-done.stats_ref = f32[64,8,128]{2,1,0:T(8,128)S(1)} async-done(((f32[64,8,128]{2,1,0:T(8,128)}), f32[64,8,128]{2,1,0:T(8,128)S(1)}, u32[]{:S(2)}, u32[]{:S(2)}) %all-to-all-start) | async-done | bytes 262176 | tf_op jit(solution)/shard_map/all_to_all | solution.py:252
  34.0 2.2 %shard_map.66 = (bf16[8,16,512]{2,1,0:T(8,128)(2,1)S(1)}, bf16[8,16,512]{2,1,0:T(8,128)(2,1)S(1)}, bf16[8,16,512]{2,1,0:T(8,128)(2,1)S(1)}, bf16[8,16,512]{2,1,0:T(8,128)(2,1)S(1)}) custom-call(bf16[8,16,768]{2,1,0:T(8,128)(2,1)S(1)} %copy-done.2, bf16[8,16,768]{2,1,0:T(8,128)(2,1)S(1)} %collective-permute-done.b_ref, ...), custom_call_target="tpu_custom_call" | custom-call | flops 905969664 | bytes 1687552 | tf_op jit(solution)/shard_map/pallas_call | solution.py:31
  36.3 2.5 %collective-permute-start.10 = (bf16[8,16,512]{2,1,0:T(8,128)(2,1)S(1)}, bf16[8,16,512]{2,1,0:T(8,128)(2,1)S(1)}, u32[]{:S(2)}, u32[]{:S(2)}) collective-permute-start(bf16[8,16,512]{2,1,0:T(8,128)(2,1)S(1)} %get-tuple-element.34), channel_id=1, source_target_pairs={{0,4},{4,8},{8,12},{12,0},{16,28},{20,16},{24,20},{28,24},{1,5},{5... | collective-permute-start | bytes 393224 | tf_op jit(solution)/shard_map/ppermute | solution.py:223
  38.7 1.4 %collective-permute-start.11 = (bf16[8,16,512]{2,1,0:T(8,128)(2,1)S(1)}, bf16[8,16,512]{2,1,0:T(8,128)(2,1)S(1)}, u32[]{:S(2)}, u32[]{:S(2)}) collective-permute-start(bf16[8,16,512]{2,1,0:T(8,128)(2,1)S(1)} %get-tuple-element.35), channel_id=1, source_target_pairs={{0,8},{4,12},{8,0},{12,4},{1,9},{5,13},{9,1},{13,5},{2,10},{6,14},... | collective-permute-start | bytes 393224 | tf_op jit(solution)/shard_map/ppermute | solution.py:221
  40.1 1.5 %collective-permute-start.9 = (bf16[8,16,512]{2,1,0:T(8,128)(2,1)S(1)}, bf16[8,16,512]{2,1,0:T(8,128)(2,1)S(1)}, u32[]{:S(2)}, u32[]{:S(2)}) collective-permute-start(bf16[8,16,512]{2,1,0:T(8,128)(2,1)S(1)} %get-tuple-element.33), channel_id=1, source_target_pairs={{0,12},{4,0},{8,4},{12,8},{16,20},{20,24},{24,28},{28,16},{1,13},{... | collective-permute-start | bytes 393224 | tf_op jit(solution)/shard_map/ppermute | solution.py:222
  41.6 0.0 copy-start.5
  41.7 0.7 copy-done.5
  42.3 3.5 %collective-permute-done.10.c_ref = bf16[8,16,512]{2,1,0:T(8,128)(2,1)S(1)} collective-permute-done((bf16[8,16,512]{2,1,0:T(8,128)(2,1)S(1)}, bf16[8,16,512]{2,1,0:T(8,128)(2,1)S(1)}, u32[]{:S(2)}, u32[]{:S(2)}) %collective-permute-start.10) | collective-permute-done | bytes 131104 | tf_op jit(solution)/shard_map/ppermute | solution.py:223
  45.8 4.8 %collective-permute-done.11.d_ref = bf16[8,16,512]{2,1,0:T(8,128)(2,1)S(1)} collective-permute-done((bf16[8,16,512]{2,1,0:T(8,128)(2,1)S(1)}, bf16[8,16,512]{2,1,0:T(8,128)(2,1)S(1)}, u32[]{:S(2)}, u32[]{:S(2)}) %collective-permute-start.11) | collective-permute-done | bytes 131104 | tf_op jit(solution)/shard_map/ppermute | solution.py:221
  50.6 2.4 %collective-permute-done.9.b_ref = bf16[8,16,512]{2,1,0:T(8,128)(2,1)S(1)} collective-permute-done((bf16[8,16,512]{2,1,0:T(8,128)(2,1)S(1)}, bf16[8,16,512]{2,1,0:T(8,128)(2,1)S(1)}, u32[]{:S(2)}, u32[]{:S(2)}) %collective-permute-start.9) | collective-permute-done | bytes 131104 | tf_op jit(solution)/shard_map/ppermute | solution.py:222
  53.1 0.1 broadcast_in_dim.13.bias_ref
  53.1 0.9 shard_map.67
  54.0 0.0 collective-permute-start.12
  54.0 1.1 %collective-permute-start.13 = (bf16[8,16,768]{2,1,0:T(8,128)(2,1)S(1)}, bf16[8,16,768]{2,1,0:T(8,128)(2,1)S(1)}, u32[]{:S(2)}, u32[]{:S(2)}) collective-permute-start(bf16[8,16,768]{2,1,0:T(8,128)(2,1)S(1)} %get-tuple-element.37.a_ref), channel_id=1, source_target_pairs={{0,2},{1,3},{2,0},{3,1},{4,6},{5,7},{6,4},{7,5},{8,10},{9,11},{10,... | collective-permute-start | bytes 589832 | tf_op jit(solution)/shard_map/ppermute | solution.py:248
  55.1 1.5 %collective-permute-start.14 = (bf16[8,16,768]{2,1,0:T(8,128)(2,1)S(1)}, bf16[8,16,768]{2,1,0:T(8,128)(2,1)S(1)}, u32[]{:S(2)}, u32[]{:S(2)}) collective-permute-start(bf16[8,16,768]{2,1,0:T(8,128)(2,1)S(1)} %get-tuple-element.37.a_ref), channel_id=1, source_target_pairs={{0,3},{1,2},{2,1},{3,0},{4,7},{5,6},{6,5},{7,4},{8,11},{9,10},{10,... | collective-permute-start | bytes 589832 | tf_op jit(solution)/shard_map/ppermute | solution.py:248
  56.7 6.8 %all-to-all-start.1 = ((f32[64,8,128]{2,1,0:T(8,128)}), f32[64,8,128]{2,1,0:T(8,128)S(1)}, u32[]{:S(2)}, u32[]{:S(2)}) async-start(f32[64,8,128]{2,1,0:T(8,128)} %get-tuple-element.40), calls=%async_computation.1 | async-start | bytes 524288 | tf_op jit(solution)/shard_map/all_to_all | solution.py:252
  63.5 0.0 collective-permute-done.13.c_ref
  63.5 2.7 %collective-permute-done.14.d_ref = bf16[8,16,768]{2,1,0:T(8,128)(2,1)S(1)} collective-permute-done((bf16[8,16,768]{2,1,0:T(8,128)(2,1)S(1)}, bf16[8,16,768]{2,1,0:T(8,128)(2,1)S(1)}, u32[]{:S(2)}, u32[]{:S(2)}) %collective-permute-start.14) | collective-permute-done | bytes 196640 | tf_op jit(solution)/shard_map/ppermute | solution.py:248
  66.2 0.5 collective-permute-start.15
  66.7 2.1 %collective-permute-start.16 = (bf16[4,16,768]{2,1,0:T(8,128)(2,1)S(1)}, bf16[4,16,768]{2,1,0:T(8,128)(2,1)S(1)}, u32[]{:S(2)}, u32[]{:S(2)}) collective-permute-start(bf16[4,16,768]{2,1,0:T(8,128)(2,1)S(1)} %get-tuple-element.39), channel_id=1, source_target_pairs={{16,32},{48,64},{80,96},{112,128},{144,160},{176,192},{208,224},{3... | collective-permute-start | bytes 294920 | tf_op jit(solution)/shard_map/ppermute | solution.py:243
  68.8 0.0 collective-permute-done.15.chip_ref
  68.8 4.2 %collective-permute-done.16.next_ref = bf16[4,16,768]{2,1,0:T(8,128)(2,1)S(1)} collective-permute-done((bf16[4,16,768]{2,1,0:T(8,128)(2,1)S(1)}, bf16[4,16,768]{2,1,0:T(8,128)(2,1)S(1)}, u32[]{:S(2)}, u32[]{:S(2)}) %collective-permute-start.16) | collective-permute-done | bytes 98336 | tf_op jit(solution)/shard_map/ppermute | solution.py:243
  73.1 0.3 all-to-all-done.1.stats_ref
  73.4 2.2 %shard_map.69 = (bf16[8,16,512]{2,1,0:T(8,128)(2,1)S(1)}, bf16[8,16,512]{2,1,0:T(8,128)(2,1)S(1)}, bf16[8,16,512]{2,1,0:T(8,128)(2,1)S(1)}, bf16[8,16,512]{2,1,0:T(8,128)(2,1)S(1)}) custom-call(bf16[8,16,768]{2,1,0:T(8,128)(2,1)S(1)} %get-tuple-element.37.a_ref, bf16[8,16,768]{2,1,0:T(8,128)(2,1)S(1)} %collective-permute-done.12.b_ref, ...), custom_call_target="tpu_custom_call" | custom-call | flops 905969664 | bytes 1687552 | tf_op jit(solution)/shard_map/pallas_call | solution.py:31
  75.6 1.5 %collective-permute-start.17 = (bf16[8,16,512]{2,1,0:T(8,128)(2,1)S(1)}, bf16[8,16,512]{2,1,0:T(8,128)(2,1)S(1)}, u32[]{:S(2)}, u32[]{:S(2)}) collective-permute-start(bf16[8,16,512]{2,1,0:T(8,128)(2,1)S(1)} %get-tuple-element.42), channel_id=1, source_target_pairs={{0,12},{4,0},{8,4},{12,8},{16,20},{20,24},{24,28},{28,16},{1,13},{... | collective-permute-start | bytes 393224 | tf_op jit(solution)/shard_map/ppermute | solution.py:222
  77.1 2.2 %collective-permute-start.18 = (bf16[8,16,512]{2,1,0:T(8,128)(2,1)S(1)}, bf16[8,16,512]{2,1,0:T(8,128)(2,1)S(1)}, u32[]{:S(2)}, u32[]{:S(2)}) collective-permute-start(bf16[8,16,512]{2,1,0:T(8,128)(2,1)S(1)} %get-tuple-element.43), channel_id=1, source_target_pairs={{0,4},{4,8},{8,12},{12,0},{16,28},{20,16},{24,20},{28,24},{1,5},{5... | collective-permute-start | bytes 393224 | tf_op jit(solution)/shard_map/ppermute | solution.py:223
  79.3 3.0 %collective-permute-start.19 = (bf16[8,16,512]{2,1,0:T(8,128)(2,1)S(1)}, bf16[8,16,512]{2,1,0:T(8,128)(2,1)S(1)}, u32[]{:S(2)}, u32[]{:S(2)}) collective-permute-start(bf16[8,16,512]{2,1,0:T(8,128)(2,1)S(1)} %get-tuple-element.44), channel_id=1, source_target_pairs={{0,8},{4,12},{8,0},{12,4},{1,9},{5,13},{9,1},{13,5},{2,10},{6,14},... | collective-permute-start | bytes 393224 | tf_op jit(solution)/shard_map/ppermute | solution.py:221
  82.2 1.2 %collective-permute-done.17.b_ref = bf16[8,16,512]{2,1,0:T(8,128)(2,1)S(1)} collective-permute-done((bf16[8,16,512]{2,1,0:T(8,128)(2,1)S(1)}, bf16[8,16,512]{2,1,0:T(8,128)(2,1)S(1)}, u32[]{:S(2)}, u32[]{:S(2)}) %collective-permute-start.17) | collective-permute-done | bytes 131104 | tf_op jit(solution)/shard_map/ppermute | solution.py:222
  83.5 5.0 %collective-permute-done.18.c_ref = bf16[8,16,512]{2,1,0:T(8,128)(2,1)S(1)} collective-permute-done((bf16[8,16,512]{2,1,0:T(8,128)(2,1)S(1)}, bf16[8,16,512]{2,1,0:T(8,128)(2,1)S(1)}, u32[]{:S(2)}, u32[]{:S(2)}) %collective-permute-start.18) | collective-permute-done | bytes 131104 | tf_op jit(solution)/shard_map/ppermute | solution.py:223
  88.4 3.7 %collective-permute-done.19.d_ref = bf16[8,16,512]{2,1,0:T(8,128)(2,1)S(1)} collective-permute-done((bf16[8,16,512]{2,1,0:T(8,128)(2,1)S(1)}, bf16[8,16,512]{2,1,0:T(8,128)(2,1)S(1)}, u32[]{:S(2)}, u32[]{:S(2)}) %collective-permute-start.19) | collective-permute-done | bytes 131104 | tf_op jit(solution)/shard_map/ppermute | solution.py:221
  92.2 0.1 broadcast_in_dim.15.bias_ref
  92.2 0.8 shard_map.70
  (23 shorter events, 0.1 us)
Async XLA Ops:
  2.3 23.9 %collective-permute-start = (bf16[8,16,768]{2,1,0:T(8,128)(2,1)}, bf16[8,16,768]{2,1,0:T(8,128)(2,1)S(1)}, u32[]{:S(2)}, u32[]{:S(2)}) collective-permute-start(bf16[8,16,768]{2,1,0:T(8,128)(2,1)} %get-tuple-element.25.a_ref), channel_id=1, source_target_pairs={{0,1},{1,0},{2,3},{3,2},{4,5},{5,4},{6,7},{7,6},{8,9},{9,8},{10,11... | collective-permute-start | bytes 589832 | tf_op jit(solution)/shard_map/ppermute | solution.py:248
  4.4 21.8 %collective-permute-start.1 = (bf16[8,16,768]{2,1,0:T(8,128)(2,1)}, bf16[8,16,768]{2,1,0:T(8,128)(2,1)S(1)}, u32[]{:S(2)}, u32[]{:S(2)}) collective-permute-start(bf16[8,16,768]{2,1,0:T(8,128)(2,1)} %get-tuple-element.25.a_ref), channel_id=1, source_target_pairs={{0,2},{1,3},{2,0},{3,1},{4,6},{5,7},{6,4},{7,5},{8,10},{9,11},{10,... | collective-permute-start | bytes 589832 | tf_op jit(solution)/shard_map/ppermute | solution.py:248
  6.1 20.1 %collective-permute-start.2 = (bf16[8,16,768]{2,1,0:T(8,128)(2,1)}, bf16[8,16,768]{2,1,0:T(8,128)(2,1)S(1)}, u32[]{:S(2)}, u32[]{:S(2)}) collective-permute-start(bf16[8,16,768]{2,1,0:T(8,128)(2,1)} %get-tuple-element.25.a_ref), channel_id=1, source_target_pairs={{0,3},{1,2},{2,1},{3,0},{4,7},{5,6},{6,5},{7,4},{8,11},{9,10},{10,... | collective-permute-start | bytes 589832 | tf_op jit(solution)/shard_map/ppermute | solution.py:248
  6.1 18.1 %collective-permute-start.5 = (bf16[2,3,3,16,192]{4,3,2,1,0:T(8,128)(2,1)}, bf16[2,3,3,16,192]{4,3,2,1,0:T(8,128)(2,1)S(1)}, u32[]{:S(2)}, u32[]{:S(2)}) collective-permute-start(bf16[2,3,3,16,192]{4,3,2,1,0:T(8,128)(2,1)} %get-tuple-element.30), channel_id=1, source_target_pairs={{0,4},{4,8},{8,12},{12,0},{16,28},{20,16},{24,20},{28,24},{1,5},{5... | collective-permute-start | bytes 331784 | tf_op jit(solution)/shard_map/ppermute | solution.py:272
  11.9 18.1 %collective-permute-start.6 = (bf16[3,3,16,192]{3,2,1,0:T(8,128)(2,1)}, bf16[3,3,16,192]{3,2,1,0:T(8,128)(2,1)S(1)}, u32[]{:S(2)}, u32[]{:S(2)}) collective-permute-start(bf16[3,3,16,192]{3,2,1,0:T(8,128)(2,1)} %get-tuple-element.31), channel_id=1, source_target_pairs={{0,8},{4,12},{8,0},{12,4},{1,9},{5,13},{9,1},{13,5},{2,10},{6,14},... | collective-permute-start | bytes 165896 | tf_op jit(solution)/shard_map/ppermute | solution.py:273
  12.8 13.4 %copy-start.2 = (bf16[8,16,768]{2,1,0:T(8,128)(2,1)S(1)}, bf16[8,16,768]{2,1,0:T(8,128)(2,1)}, u32[]{:S(2)}) copy-start(bf16[8,16,768]{2,1,0:T(8,128)(2,1)} %get-tuple-element.25.a_ref) | copy-start | bytes 589828
  12.8 21.2 %all-to-all-start = ((f32[64,8,128]{2,1,0:T(8,128)}), f32[64,8,128]{2,1,0:T(8,128)S(1)}, u32[]{:S(2)}, u32[]{:S(2)}) async-start(f32[64,8,128]{2,1,0:T(8,128)} %get-tuple-element.28), calls=%async_computation | async-start | bytes 524288 | tf_op jit(solution)/shard_map/all_to_all | solution.py:252
  24.1 9.9 %copy-start.3 = (bf16[2,3,3,16,192]{4,3,2,1,0:T(8,128)(2,1)S(1)}, bf16[2,3,3,16,192]{4,3,2,1,0:T(8,128)(2,1)}, u32[]{:S(2)}) copy-start(bf16[2,3,3,16,192]{4,3,2,1,0:T(8,128)(2,1)} %get-tuple-element.29.own_ref) | copy-start | bytes 331780
  24.1 7.2 %collective-permute-start.7 = (bf16[2,3,3,16,192]{4,3,2,1,0:T(8,128)(2,1)S(1)}, bf16[2,3,3,16,192]{4,3,2,1,0:T(8,128)(2,1)S(1)}, u32[]{:S(2)}, u32[]{:S(2)}) collective-permute-start(bf16[2,3,3,16,192]{4,3,2,1,0:T(8,128)(2,1)S(1)} %collective-permute-done.5.side_ref), channel_id=1, source_target_pairs={{0,16},{16,0},{1,17},{17,1},{2,18},{18,2},{3,19},{19,3},{4,20},{20... | collective-permute-start | bytes 331784 | tf_op jit(solution)/shard_map/ppermute | solution.py:278
  26.3 5.1 %collective-permute-start.3 = (bf16[4,16,768]{2,1,0:T(8,128)(2,1)S(1)}, bf16[4,16,768]{2,1,0:T(8,128)(2,1)S(1)}, u32[]{:S(2)}, u32[]{:S(2)}) collective-permute-start(bf16[4,16,768]{2,1,0:T(8,128)(2,1)S(1)} %get-tuple-element.26), channel_id=1, source_target_pairs={{0,16},{16,0},{32,48},{48,32},{64,80},{80,64},{96,112},{112,96},{1... | collective-permute-start | bytes 294920 | tf_op jit(solution)/shard_map/ppermute | solution.py:241
  26.4 6.5 %collective-permute-start.4 = (bf16[4,16,768]{2,1,0:T(8,128)(2,1)S(1)}, bf16[4,16,768]{2,1,0:T(8,128)(2,1)S(1)}, u32[]{:S(2)}, u32[]{:S(2)}) collective-permute-start(bf16[4,16,768]{2,1,0:T(8,128)(2,1)S(1)} %get-tuple-element.27), channel_id=1, source_target_pairs={{16,32},{48,64},{80,96},{112,128},{144,160},{176,192},{208,224},{3... | collective-permute-start | bytes 294920 | tf_op jit(solution)/shard_map/ppermute | solution.py:243
  30.0 1.4 %collective-permute-start.8 = (bf16[3,3,16,192]{3,2,1,0:T(8,128)(2,1)S(1)}, bf16[3,3,16,192]{3,2,1,0:T(8,128)(2,1)S(1)}, u32[]{:S(2)}, u32[]{:S(2)}) collective-permute-start(bf16[3,3,16,192]{3,2,1,0:T(8,128)(2,1)S(1)} %collective-permute-done.6.far_ref), channel_id=1, source_target_pairs={{0,16},{16,0},{1,17},{17,1},{2,18},{18,2},{3,19},{19,3},{4,20},{20... | collective-permute-start | bytes 165896 | tf_op jit(solution)/shard_map/ppermute | solution.py:278
  34.0 19.1 %copy-start.1 = (bf16[8,16,256]{2,1,0:T(8,128)(2,1)S(1)}, bf16[8,16,256]{2,1,0:T(8,128)(2,1)}, u32[]{:S(2)}) copy-start(bf16[8,16,256]{2,1,0:T(8,128)(2,1)} %get-tuple-element.36.later_ref) | copy-start | bytes 196612
  36.3 9.6 %collective-permute-start.10 = (bf16[8,16,512]{2,1,0:T(8,128)(2,1)S(1)}, bf16[8,16,512]{2,1,0:T(8,128)(2,1)S(1)}, u32[]{:S(2)}, u32[]{:S(2)}) collective-permute-start(bf16[8,16,512]{2,1,0:T(8,128)(2,1)S(1)} %get-tuple-element.34), channel_id=1, source_target_pairs={{0,4},{4,8},{8,12},{12,0},{16,28},{20,16},{24,20},{28,24},{1,5},{5... | collective-permute-start | bytes 393224 | tf_op jit(solution)/shard_map/ppermute | solution.py:223
  38.7 2.9 %copy-start.6 = (f32[2,16]{1,0:T(2,128)S(1)}, f32[2,16]{1,0:T(2,128)}, u32[]{:S(2)}) copy-start(f32[2,16]{1,0:T(2,128)} %param.11) | copy-start | bytes 388
  38.7 11.9 %collective-permute-start.11 = (bf16[8,16,512]{2,1,0:T(8,128)(2,1)S(1)}, bf16[8,16,512]{2,1,0:T(8,128)(2,1)S(1)}, u32[]{:S(2)}, u32[]{:S(2)}) collective-permute-start(bf16[8,16,512]{2,1,0:T(8,128)(2,1)S(1)} %get-tuple-element.35), channel_id=1, source_target_pairs={{0,8},{4,12},{8,0},{12,4},{1,9},{5,13},{9,1},{13,5},{2,10},{6,14},... | collective-permute-start | bytes 393224 | tf_op jit(solution)/shard_map/ppermute | solution.py:221
  40.1 1.5 %copy-start.4 = (f32[2,16]{1,0:T(2,128)S(1)}, f32[2,16]{1,0:T(2,128)}, u32[]{:S(2)}) copy-start(f32[2,16]{1,0:T(2,128)} %gain_hbm.1) | copy-start | bytes 388
  40.1 12.9 %collective-permute-start.9 = (bf16[8,16,512]{2,1,0:T(8,128)(2,1)S(1)}, bf16[8,16,512]{2,1,0:T(8,128)(2,1)S(1)}, u32[]{:S(2)}, u32[]{:S(2)}) collective-permute-start(bf16[8,16,512]{2,1,0:T(8,128)(2,1)S(1)} %get-tuple-element.33), channel_id=1, source_target_pairs={{0,12},{4,0},{8,4},{12,8},{16,20},{20,24},{24,28},{28,16},{1,13},{... | collective-permute-start | bytes 393224 | tf_op jit(solution)/shard_map/ppermute | solution.py:222
  41.6 0.7 copy-start.5
  54.0 9.5 %collective-permute-start.12 = (bf16[8,16,768]{2,1,0:T(8,128)(2,1)S(1)}, bf16[8,16,768]{2,1,0:T(8,128)(2,1)S(1)}, u32[]{:S(2)}, u32[]{:S(2)}) collective-permute-start(bf16[8,16,768]{2,1,0:T(8,128)(2,1)S(1)} %get-tuple-element.37.a_ref), channel_id=1, source_target_pairs={{0,1},{1,0},{2,3},{3,2},{4,5},{5,4},{6,7},{7,6},{8,9},{9,8},{10,11... | collective-permute-start | bytes 589832 | tf_op jit(solution)/shard_map/ppermute | solution.py:248
  54.0 9.5 %collective-permute-start.13 = (bf16[8,16,768]{2,1,0:T(8,128)(2,1)S(1)}, bf16[8,16,768]{2,1,0:T(8,128)(2,1)S(1)}, u32[]{:S(2)}, u32[]{:S(2)}) collective-permute-start(bf16[8,16,768]{2,1,0:T(8,128)(2,1)S(1)} %get-tuple-element.37.a_ref), channel_id=1, source_target_pairs={{0,2},{1,3},{2,0},{3,1},{4,6},{5,7},{6,4},{7,5},{8,10},{9,11},{10,... | collective-permute-start | bytes 589832 | tf_op jit(solution)/shard_map/ppermute | solution.py:248
  55.1 11.1 %collective-permute-start.14 = (bf16[8,16,768]{2,1,0:T(8,128)(2,1)S(1)}, bf16[8,16,768]{2,1,0:T(8,128)(2,1)S(1)}, u32[]{:S(2)}, u32[]{:S(2)}) collective-permute-start(bf16[8,16,768]{2,1,0:T(8,128)(2,1)S(1)} %get-tuple-element.37.a_ref), channel_id=1, source_target_pairs={{0,3},{1,2},{2,1},{3,0},{4,7},{5,6},{6,5},{7,4},{8,11},{9,10},{10,... | collective-permute-start | bytes 589832 | tf_op jit(solution)/shard_map/ppermute | solution.py:248
  56.7 16.7 %all-to-all-start.1 = ((f32[64,8,128]{2,1,0:T(8,128)}), f32[64,8,128]{2,1,0:T(8,128)S(1)}, u32[]{:S(2)}, u32[]{:S(2)}) async-start(f32[64,8,128]{2,1,0:T(8,128)} %get-tuple-element.40), calls=%async_computation.1 | async-start | bytes 524288 | tf_op jit(solution)/shard_map/all_to_all | solution.py:252
  66.2 2.6 %collective-permute-start.15 = (bf16[4,16,768]{2,1,0:T(8,128)(2,1)S(1)}, bf16[4,16,768]{2,1,0:T(8,128)(2,1)S(1)}, u32[]{:S(2)}, u32[]{:S(2)}) collective-permute-start(bf16[4,16,768]{2,1,0:T(8,128)(2,1)S(1)} %get-tuple-element.38), channel_id=1, source_target_pairs={{0,16},{16,0},{32,48},{48,32},{64,80},{80,64},{96,112},{112,96},{1... | collective-permute-start | bytes 294920 | tf_op jit(solution)/shard_map/ppermute | solution.py:241
  66.7 25.5 %copy-start = (bf16[4,8,16,128]{3,2,1,0:T(8,128)(2,1)S(1)}, bf16[4,8,16,128]{3,2,1,0:T(8,128)(2,1)}, u32[]{:S(2)}) copy-start(bf16[4,8,16,128]{3,2,1,0:T(8,128)(2,1)} %x_ref.1) | copy-start | bytes 393220
  66.7 6.3 %collective-permute-start.16 = (bf16[4,16,768]{2,1,0:T(8,128)(2,1)S(1)}, bf16[4,16,768]{2,1,0:T(8,128)(2,1)S(1)}, u32[]{:S(2)}, u32[]{:S(2)}) collective-permute-start(bf16[4,16,768]{2,1,0:T(8,128)(2,1)S(1)} %get-tuple-element.39), channel_id=1, source_target_pairs={{16,32},{48,64},{80,96},{112,128},{144,160},{176,192},{208,224},{3... | collective-permute-start | bytes 294920 | tf_op jit(solution)/shard_map/ppermute | solution.py:243
  75.6 7.8 %collective-permute-start.17 = (bf16[8,16,512]{2,1,0:T(8,128)(2,1)S(1)}, bf16[8,16,512]{2,1,0:T(8,128)(2,1)S(1)}, u32[]{:S(2)}, u32[]{:S(2)}) collective-permute-start(bf16[8,16,512]{2,1,0:T(8,128)(2,1)S(1)} %get-tuple-element.42), channel_id=1, source_target_pairs={{0,12},{4,0},{8,4},{12,8},{16,20},{20,24},{24,28},{28,16},{1,13},{... | collective-permute-start | bytes 393224 | tf_op jit(solution)/shard_map/ppermute | solution.py:222
  77.1 11.4 %collective-permute-start.18 = (bf16[8,16,512]{2,1,0:T(8,128)(2,1)S(1)}, bf16[8,16,512]{2,1,0:T(8,128)(2,1)S(1)}, u32[]{:S(2)}, u32[]{:S(2)}) collective-permute-start(bf16[8,16,512]{2,1,0:T(8,128)(2,1)S(1)} %get-tuple-element.43), channel_id=1, source_target_pairs={{0,4},{4,8},{8,12},{12,0},{16,28},{20,16},{24,20},{28,24},{1,5},{5... | collective-permute-start | bytes 393224 | tf_op jit(solution)/shard_map/ppermute | solution.py:223
  79.3 12.9 %collective-permute-start.19 = (bf16[8,16,512]{2,1,0:T(8,128)(2,1)S(1)}, bf16[8,16,512]{2,1,0:T(8,128)(2,1)S(1)}, u32[]{:S(2)}, u32[]{:S(2)}) collective-permute-start(bf16[8,16,512]{2,1,0:T(8,128)(2,1)S(1)} %get-tuple-element.44), channel_id=1, source_target_pairs={{0,8},{4,12},{8,0},{12,4},{1,9},{5,13},{9,1},{13,5},{2,10},{6,14},... | collective-permute-start | bytes 393224 | tf_op jit(solution)/shard_map/ppermute | solution.py:221

commit v7 on v6

--- a/solution.py
+++ b/solution.py
@@ -22,7 +22,8 @@
 
 
 def silu(u):
-    return u / (1.0 + jnp.exp(-u))
+    half = 0.5 * u
+    return half + half * jnp.tanh(half)
 
 
 def call(kernel, outs, *args, far=(), scratch=(), flops=0):
@@ -221,7 +222,7 @@
     far = lax.ppermute(far, "zh", [(i, (i + 2) % 4) for i in range(4)])
     side = lax.ppermute(side, ("core", "zh"), sides(-1))
     other = lax.ppermute(other, ("core", "zh"), sides(1))
-    return [own, side, other, far]
+    return [far, side, other, own]
 
 
 def struct(shape, dtype=BF16):
@@ -270,7 +271,7 @@
         far=(0, 1, 2, 3, 4),
     )
     side = lax.ppermute(side, ("core", "zh"), sides(1))
-    far = lax.ppermute(far, "zh", [(i, (i + 2) % 4) for i in range(4)])
+    far = lax.ppermute(lax.ppermute(far, ("core", "zh"), sides(1)), ("core", "zh"), sides(1))
     raw = near(raw)
     stats = exchange(stats, ROW + NEAR)
     raw = raw + rows_beside(raw)

time: 93.3 us -> 94.8 us (1.016)
  the two profiles are of different devices: /device:TPU:1 before, /device:TPU:27 now
where the time goes in v7:
time: 94.8 us; the launch traced here: 93 us
  starting transfers between devices  61.6 us (65%)
  waiting for transfers between devices  22.1 us (23%)
  Pallas kernels  8.32 us (9%)
    all_to_all x2, starting transfers between devices, exchange(): return lax.all_to_all(x, axes, 0, 0, tiled=True)  19.6 us
    pallas_call x7, Pallas kernels, call(): pl.pallas_call(kernel, out_shape=outs, in_specs=specs, out_specs=jax.tree...  8.32 us
    ppermute x2, waiting for transfers between devices, rows_beside(): beyond = lax.ppermute(beyond, ROW, pairs)  8.08 us
    ppermute x2, starting transfers between devices, bring(): far = lax.ppermute(far, 'zh', [(i, (i + 2) % 4) for i in range(4)])  7.98 us
    ppermute x2, starting transfers between devices, rows_beside(): beyond = lax.ppermute(beyond, ROW, pairs)  7.93 us
    ppermute x6, starting transfers between devices, near(): lax.ppermute(x, NEAR, [(i, i ^ k) for i in range(4)])  6.68 us
    ppermute x1, starting transfers between devices, local(): side = lax.ppermute(side, ('core', 'zh'), sides(1))  5.85 us
    ppermute x2, waiting for transfers between devices, bring(): other = lax.ppermute(other, ('core', 'zh'), sides(1))  5.73 us
  transfers between devices with their start and end apart: 23, of which 9 were waited for; matrix products, arithmetic and copies ran while one was open for 0% of the time, Pallas kernels for 0%

profile of v7, /device:TPU:27, one launch (start us, length us, event | category | flops | bytes accessed | tf_op | source)
XLA Modules:
  0.0 93.0 jit_solution(5767756532761547492)
XLA Ops:
  0.0 2.3 %shard_map.64 = (bf16[8,16,768]{2,1,0:T(8,128)(2,1)}, bf16[8,16,256]{2,1,0:T(8,128)(2,1)}, f32[64,8,128]{2,1,0:T(8,128)}, bf16[2,3,3,16,192]{4,3,2,1,0:T(8,128)(...) custom-call(bf16[4,8,16,128]{3,2,1,0:T(8,128)(2,1)} %x_ref.1, ...), custom_call_target="tpu_custom_call" | custom-call | bytes 704768 | tf_op jit(solution)/shard_map/pallas_call | solution.py:32
  2.3 0.3 collective-permute-start
  2.7 1.6 %collective-permute-start.1 = (bf16[8,16,768]{2,1,0:T(8,128)(2,1)}, bf16[8,16,768]{2,1,0:T(8,128)(2,1)S(1)}, u32[]{:S(2)}, u32[]{:S(2)}) collective-permute-start(bf16[8,16,768]{2,1,0:T(8,128)(2,1)} %get-tuple-element.25.a_ref), channel_id=1, source_target_pairs={{0,2},{1,3},{2,0},{3,1},{4,6},{5,7},{6,4},{7,5},{8,10},{9,11},{10,... | collective-permute-start | bytes 589832 | tf_op jit(solution)/shard_map/ppermute | solution.py:249
  4.3 0.9 %collective-permute-start.2 = (bf16[8,16,768]{2,1,0:T(8,128)(2,1)}, bf16[8,16,768]{2,1,0:T(8,128)(2,1)S(1)}, u32[]{:S(2)}, u32[]{:S(2)}) collective-permute-start(bf16[8,16,768]{2,1,0:T(8,128)(2,1)} %get-tuple-element.25.a_ref), channel_id=1, source_target_pairs={{0,3},{1,2},{2,1},{3,0},{4,7},{5,6},{6,5},{7,4},{8,11},{9,10},{10,... | collective-permute-start | bytes 589832 | tf_op jit(solution)/shard_map/ppermute | solution.py:249
  5.2 5.8 %collective-permute-start.5 = (bf16[2,3,3,16,192]{4,3,2,1,0:T(8,128)(2,1)}, bf16[2,3,3,16,192]{4,3,2,1,0:T(8,128)(2,1)S(1)}, u32[]{:S(2)}, u32[]{:S(2)}) collective-permute-start(bf16[2,3,3,16,192]{4,3,2,1,0:T(8,128)(2,1)} %get-tuple-element.30), channel_id=1, source_target_pairs={{0,4},{4,8},{8,12},{12,0},{16,28},{20,16},{24,20},{28,24},{1,5},{5... | collective-permute-start | bytes 331784 | tf_op jit(solution)/shard_map/ppermute | solution.py:273
  11.1 1.2 %collective-permute-start.6 = (bf16[3,3,16,192]{3,2,1,0:T(8,128)(2,1)}, bf16[3,3,16,192]{3,2,1,0:T(8,128)(2,1)S(1)}, u32[]{:S(2)}, u32[]{:S(2)}) collective-permute-start(bf16[3,3,16,192]{3,2,1,0:T(8,128)(2,1)} %get-tuple-element.31), channel_id=1, source_target_pairs={{0,4},{4,8},{8,12},{12,0},{16,28},{20,16},{24,20},{28,24},{1,5},{5... | collective-permute-start | bytes 165896 | tf_op jit(solution)/shard_map/ppermute | solution.py:274
  12.2 10.0 %all-to-all-start = ((f32[64,8,128]{2,1,0:T(8,128)}), f32[64,8,128]{2,1,0:T(8,128)S(1)}, u32[]{:S(2)}, u32[]{:S(2)}) async-start(f32[64,8,128]{2,1,0:T(8,128)} %get-tuple-element.28), calls=%async_computation | async-start | bytes 524288 | tf_op jit(solution)/shard_map/all_to_all | solution.py:253
  22.3 0.3 collective-permute-start.7
  22.7 2.1 %collective-permute-start.8 = (bf16[2,3,3,16,192]{4,3,2,1,0:T(8,128)(2,1)S(1)}, bf16[2,3,3,16,192]{4,3,2,1,0:T(8,128)(2,1)S(1)}, u32[]{:S(2)}, u32[]{:S(2)}) collective-permute-start(bf16[2,3,3,16,192]{4,3,2,1,0:T(8,128)(2,1)S(1)} %collective-permute-done.5.side_ref), channel_id=1, source_target_pairs={{0,16},{16,0},{1,17},{17,1},{2,18},{18,2},{3,19},{19,3},{4,20},{20... | collective-permute-start | bytes 331784 | tf_op jit(solution)/shard_map/ppermute | solution.py:279
  24.7 0.0 collective-permute-done.b_ref
  24.8 0.0 collective-permute-done.1.c_ref
  24.8 0.0 collective-permute-done.2.d_ref
  24.8 0.1 collective-permute-start.3
  24.9 4.0 %collective-permute-start.4 = (bf16[4,16,768]{2,1,0:T(8,128)(2,1)S(1)}, bf16[4,16,768]{2,1,0:T(8,128)(2,1)S(1)}, u32[]{:S(2)}, u32[]{:S(2)}) collective-permute-start(bf16[4,16,768]{2,1,0:T(8,128)(2,1)S(1)} %get-tuple-element.27), channel_id=1, source_target_pairs={{16,32},{48,64},{80,96},{112,128},{144,160},{176,192},{208,224},{3... | collective-permute-start | bytes 294920 | tf_op jit(solution)/shard_map/ppermute | solution.py:244
  29.0 2.2 %collective-permute-start.9 = (bf16[3,3,16,192]{3,2,1,0:T(8,128)(2,1)S(1)}, bf16[3,3,16,192]{3,2,1,0:T(8,128)(2,1)S(1)}, u32[]{:S(2)}, u32[]{:S(2)}) collective-permute-start(bf16[3,3,16,192]{3,2,1,0:T(8,128)(2,1)S(1)} %collective-permute-done.7.far_ref), channel_id=1, source_target_pairs={{0,16},{16,0},{1,17},{17,1},{2,18},{18,2},{3,19},{19,3},{4,20},{20... | collective-permute-start | bytes 165896 | tf_op jit(solution)/shard_map/ppermute | solution.py:279
  31.2 0.9 collective-permute-done.9.far2_ref
  32.1 0.0 collective-permute-done.8.side2_ref
  32.1 0.0 collective-permute-done.3.chip_ref
  32.1 2.3 %collective-permute-done.4.next_ref = bf16[4,16,768]{2,1,0:T(8,128)(2,1)S(1)} collective-permute-done((bf16[4,16,768]{2,1,0:T(8,128)(2,1)S(1)}, bf16[4,16,768]{2,1,0:T(8,128)(2,1)S(1)}, u32[]{:S(2)}, u32[]{:S(2)}) %collective-permute-start.4) | collective-permute-done | bytes 98336 | tf_op jit(solution)/shard_map/ppermute | solution.py:244
  34.5 0.0 all-to-all-done.stats_ref
  34.5 2.2 %shard_map.66 = (bf16[8,16,512]{2,1,0:T(8,128)(2,1)S(1)}, bf16[8,16,512]{2,1,0:T(8,128)(2,1)S(1)}, bf16[8,16,512]{2,1,0:T(8,128)(2,1)S(1)}, bf16[8,16,512]{2,1,0:T(8,128)(2,1)S(1)}) custom-call(bf16[8,16,768]{2,1,0:T(8,128)(2,1)S(1)} %copy-done.2, bf16[8,16,768]{2,1,0:T(8,128)(2,1)S(1)} %collective-permute-done.b_ref, ...), custom_call_target="tpu_custom_call" | custom-call | flops 905969664 | bytes 1687552 | tf_op jit(solution)/shard_map/pallas_call | solution.py:32
  36.6 4.1 %collective-permute-start.10 = (bf16[8,16,512]{2,1,0:T(8,128)(2,1)S(1)}, bf16[8,16,512]{2,1,0:T(8,128)(2,1)S(1)}, u32[]{:S(2)}, u32[]{:S(2)}) collective-permute-start(bf16[8,16,512]{2,1,0:T(8,128)(2,1)S(1)} %get-tuple-element.32), channel_id=1, source_target_pairs={{0,8},{4,12},{8,0},{12,4},{1,9},{5,13},{9,1},{13,5},{2,10},{6,14},... | collective-permute-start | bytes 393224 | tf_op jit(solution)/shard_map/ppermute | solution.py:222
  40.8 1.9 %collective-permute-start.11 = (bf16[8,16,512]{2,1,0:T(8,128)(2,1)S(1)}, bf16[8,16,512]{2,1,0:T(8,128)(2,1)S(1)}, u32[]{:S(2)}, u32[]{:S(2)}) collective-permute-start(bf16[8,16,512]{2,1,0:T(8,128)(2,1)S(1)} %get-tuple-element.33), channel_id=1, source_target_pairs={{0,12},{4,0},{8,4},{12,8},{16,20},{20,24},{24,28},{28,16},{1,13},{... | collective-permute-start | bytes 393224 | tf_op jit(solution)/shard_map/ppermute | solution.py:223
  42.7 1.7 %collective-permute-start.12 = (bf16[8,16,512]{2,1,0:T(8,128)(2,1)S(1)}, bf16[8,16,512]{2,1,0:T(8,128)(2,1)S(1)}, u32[]{:S(2)}, u32[]{:S(2)}) collective-permute-start(bf16[8,16,512]{2,1,0:T(8,128)(2,1)S(1)} %get-tuple-element.34), channel_id=1, source_target_pairs={{0,4},{4,8},{8,12},{12,0},{16,28},{20,16},{24,20},{28,24},{1,5},{5... | collective-permute-start | bytes 393224 | tf_op jit(solution)/shard_map/ppermute | solution.py:224
  44.3 0.0 copy-start.5
  44.4 0.7 copy-done.5
  45.0 1.2 %collective-permute-done.10.a_ref = bf16[8,16,512]{2,1,0:T(8,128)(2,1)S(1)} collective-permute-done((bf16[8,16,512]{2,1,0:T(8,128)(2,1)S(1)}, bf16[8,16,512]{2,1,0:T(8,128)(2,1)S(1)}, u32[]{:S(2)}, u32[]{:S(2)}) %collective-permute-start.10) | collective-permute-done | bytes 131104 | tf_op jit(solution)/shard_map/ppermute | solution.py:222
  46.2 2.7 %collective-permute-done.11.b_ref = bf16[8,16,512]{2,1,0:T(8,128)(2,1)S(1)} collective-permute-done((bf16[8,16,512]{2,1,0:T(8,128)(2,1)S(1)}, bf16[8,16,512]{2,1,0:T(8,128)(2,1)S(1)}, u32[]{:S(2)}, u32[]{:S(2)}) %collective-permute-start.11) | collective-permute-done | bytes 131104 | tf_op jit(solution)/shard_map/ppermute | solution.py:223
  48.9 2.3 %collective-permute-done.12.c_ref = bf16[8,16,512]{2,1,0:T(8,128)(2,1)S(1)} collective-permute-done((bf16[8,16,512]{2,1,0:T(8,128)(2,1)S(1)}, bf16[8,16,512]{2,1,0:T(8,128)(2,1)S(1)}, u32[]{:S(2)}, u32[]{:S(2)}) %collective-permute-start.12) | collective-permute-done | bytes 131104 | tf_op jit(solution)/shard_map/ppermute | solution.py:224
  51.2 0.1 broadcast_in_dim.13.bias_ref
  51.3 0.9 shard_map.67
  52.2 0.8 collective-permute-start.13
  53.0 3.0 %collective-permute-start.14 = (bf16[8,16,768]{2,1,0:T(8,128)(2,1)S(1)}, bf16[8,16,768]{2,1,0:T(8,128)(2,1)S(1)}, u32[]{:S(2)}, u32[]{:S(2)}) collective-permute-start(bf16[8,16,768]{2,1,0:T(8,128)(2,1)S(1)} %get-tuple-element.37.a_ref), channel_id=1, source_target_pairs={{0,2},{1,3},{2,0},{3,1},{4,6},{5,7},{6,4},{7,5},{8,10},{9,11},{10,... | collective-permute-start | bytes 589832 | tf_op jit(solution)/shard_map/ppermute | solution.py:249
  56.0 9.6 %all-to-all-start.1 = ((f32[64,8,128]{2,1,0:T(8,128)}), f32[64,8,128]{2,1,0:T(8,128)S(1)}, u32[]{:S(2)}, u32[]{:S(2)}) async-start(f32[64,8,128]{2,1,0:T(8,128)} %get-tuple-element.40), calls=%async_computation.1 | async-start | bytes 524288 | tf_op jit(solution)/shard_map/all_to_all | solution.py:253
  65.6 0.0 collective-permute-done.13.b_ref
  65.6 0.0 collective-permute-done.15.d_ref
  65.6 0.4 collective-permute-start.16
  66.1 3.9 %collective-permute-start.17 = (bf16[4,16,768]{2,1,0:T(8,128)(2,1)S(1)}, bf16[4,16,768]{2,1,0:T(8,128)(2,1)S(1)}, u32[]{:S(2)}, u32[]{:S(2)}) collective-permute-start(bf16[4,16,768]{2,1,0:T(8,128)(2,1)S(1)} %get-tuple-element.39), channel_id=1, source_target_pairs={{16,32},{48,64},{80,96},{112,128},{144,160},{176,192},{208,224},{3... | collective-permute-start | bytes 294920 | tf_op jit(solution)/shard_map/ppermute | solution.py:244
  70.0 5.7 %collective-permute-done.17.next_ref = bf16[4,16,768]{2,1,0:T(8,128)(2,1)S(1)} collective-permute-done((bf16[4,16,768]{2,1,0:T(8,128)(2,1)S(1)}, bf16[4,16,768]{2,1,0:T(8,128)(2,1)S(1)}, u32[]{:S(2)}, u32[]{:S(2)}) %collective-permute-start.17) | collective-permute-done | bytes 98336 | tf_op jit(solution)/shard_map/ppermute | solution.py:244
  75.8 2.2 %shard_map.69 = (bf16[8,16,512]{2,1,0:T(8,128)(2,1)S(1)}, bf16[8,16,512]{2,1,0:T(8,128)(2,1)S(1)}, bf16[8,16,512]{2,1,0:T(8,128)(2,1)S(1)}, bf16[8,16,512]{2,1,0:T(8,128)(2,1)S(1)}) custom-call(bf16[8,16,768]{2,1,0:T(8,128)(2,1)S(1)} %get-tuple-element.37.a_ref, bf16[8,16,768]{2,1,0:T(8,128)(2,1)S(1)} %collective-permute-done.13.b_ref, ...), custom_call_target="tpu_custom_call" | custom-call | flops 905969664 | bytes 1687552 | tf_op jit(solution)/shard_map/pallas_call | solution.py:32
  77.9 3.9 %collective-permute-start.18 = (bf16[8,16,512]{2,1,0:T(8,128)(2,1)S(1)}, bf16[8,16,512]{2,1,0:T(8,128)(2,1)S(1)}, u32[]{:S(2)}, u32[]{:S(2)}) collective-permute-start(bf16[8,16,512]{2,1,0:T(8,128)(2,1)S(1)} %get-tuple-element.41), channel_id=1, source_target_pairs={{0,8},{4,12},{8,0},{12,4},{1,9},{5,13},{9,1},{13,5},{2,10},{6,14},... | collective-permute-start | bytes 393224 | tf_op jit(solution)/shard_map/ppermute | solution.py:222
  81.8 0.1 collective-permute-start.19
  81.9 3.4 %collective-permute-start.20 = (bf16[8,16,512]{2,1,0:T(8,128)(2,1)S(1)}, bf16[8,16,512]{2,1,0:T(8,128)(2,1)S(1)}, u32[]{:S(2)}, u32[]{:S(2)}) collective-permute-start(bf16[8,16,512]{2,1,0:T(8,128)(2,1)S(1)} %get-tuple-element.43), channel_id=1, source_target_pairs={{0,4},{4,8},{8,12},{12,0},{16,28},{20,16},{24,20},{28,24},{1,5},{5... | collective-permute-start | bytes 393224 | tf_op jit(solution)/shard_map/ppermute | solution.py:224
  85.4 2.7 %collective-permute-done.18.a_ref = bf16[8,16,512]{2,1,0:T(8,128)(2,1)S(1)} collective-permute-done((bf16[8,16,512]{2,1,0:T(8,128)(2,1)S(1)}, bf16[8,16,512]{2,1,0:T(8,128)(2,1)S(1)}, u32[]{:S(2)}, u32[]{:S(2)}) %collective-permute-start.18) | collective-permute-done | bytes 131104 | tf_op jit(solution)/shard_map/ppermute | solution.py:222
  88.1 0.7 collective-permute-done.19.b_ref
  88.8 3.4 %collective-permute-done.20.c_ref = bf16[8,16,512]{2,1,0:T(8,128)(2,1)S(1)} collective-permute-done((bf16[8,16,512]{2,1,0:T(8,128)(2,1)S(1)}, bf16[8,16,512]{2,1,0:T(8,128)(2,1)S(1)}, u32[]{:S(2)}, u32[]{:S(2)}) %collective-permute-start.20) | collective-permute-done | bytes 131104 | tf_op jit(solution)/shard_map/ppermute | solution.py:224
  92.2 0.1 broadcast_in_dim.15.bias_ref
  92.3 0.8 shard_map.70
  (25 shorter events, 0.1 us)
Async XLA Ops:
  2.3 22.4 %collective-permute-start = (bf16[8,16,768]{2,1,0:T(8,128)(2,1)}, bf16[8,16,768]{2,1,0:T(8,128)(2,1)S(1)}, u32[]{:S(2)}, u32[]{:S(2)}) collective-permute-start(bf16[8,16,768]{2,1,0:T(8,128)(2,1)} %get-tuple-element.25.a_ref), channel_id=1, source_target_pairs={{0,1},{1,0},{2,3},{3,2},{4,5},{5,4},{6,7},{7,6},{8,9},{9,8},{10,11... | collective-permute-start | bytes 589832 | tf_op jit(solution)/shard_map/ppermute | solution.py:249
  2.7 22.1 %collective-permute-start.1 = (bf16[8,16,768]{2,1,0:T(8,128)(2,1)}, bf16[8,16,768]{2,1,0:T(8,128)(2,1)S(1)}, u32[]{:S(2)}, u32[]{:S(2)}) collective-permute-start(bf16[8,16,768]{2,1,0:T(8,128)(2,1)} %get-tuple-element.25.a_ref), channel_id=1, source_target_pairs={{0,2},{1,3},{2,0},{3,1},{4,6},{5,7},{6,4},{7,5},{8,10},{9,11},{10,... | collective-permute-start | bytes 589832 | tf_op jit(solution)/shard_map/ppermute | solution.py:249
  4.3 20.5 %collective-permute-start.2 = (bf16[8,16,768]{2,1,0:T(8,128)(2,1)}, bf16[8,16,768]{2,1,0:T(8,128)(2,1)S(1)}, u32[]{:S(2)}, u32[]{:S(2)}) collective-permute-start(bf16[8,16,768]{2,1,0:T(8,128)(2,1)} %get-tuple-element.25.a_ref), channel_id=1, source_target_pairs={{0,3},{1,2},{2,1},{3,0},{4,7},{5,6},{6,5},{7,4},{8,11},{9,10},{10,... | collective-permute-start | bytes 589832 | tf_op jit(solution)/shard_map/ppermute | solution.py:249
  5.2 17.4 %collective-permute-start.5 = (bf16[2,3,3,16,192]{4,3,2,1,0:T(8,128)(2,1)}, bf16[2,3,3,16,192]{4,3,2,1,0:T(8,128)(2,1)S(1)}, u32[]{:S(2)}, u32[]{:S(2)}) collective-permute-start(bf16[2,3,3,16,192]{4,3,2,1,0:T(8,128)(2,1)} %get-tuple-element.30), channel_id=1, source_target_pairs={{0,4},{4,8},{8,12},{12,0},{16,28},{20,16},{24,20},{28,24},{1,5},{5... | collective-permute-start | bytes 331784 | tf_op jit(solution)/shard_map/ppermute | solution.py:273
  11.1 11.2 %collective-permute-start.6 = (bf16[3,3,16,192]{3,2,1,0:T(8,128)(2,1)}, bf16[3,3,16,192]{3,2,1,0:T(8,128)(2,1)S(1)}, u32[]{:S(2)}, u32[]{:S(2)}) collective-permute-start(bf16[3,3,16,192]{3,2,1,0:T(8,128)(2,1)} %get-tuple-element.31), channel_id=1, source_target_pairs={{0,4},{4,8},{8,12},{12,0},{16,28},{20,16},{24,20},{28,24},{1,5},{5... | collective-permute-start | bytes 165896 | tf_op jit(solution)/shard_map/ppermute | solution.py:274
  12.2 12.5 %copy-start.2 = (bf16[8,16,768]{2,1,0:T(8,128)(2,1)S(1)}, bf16[8,16,768]{2,1,0:T(8,128)(2,1)}, u32[]{:S(2)}) copy-start(bf16[8,16,768]{2,1,0:T(8,128)(2,1)} %get-tuple-element.25.a_ref) | copy-start | bytes 589828
  12.2 22.2 %all-to-all-start = ((f32[64,8,128]{2,1,0:T(8,128)}), f32[64,8,128]{2,1,0:T(8,128)S(1)}, u32[]{:S(2)}, u32[]{:S(2)}) async-start(f32[64,8,128]{2,1,0:T(8,128)} %get-tuple-element.28), calls=%async_computation | async-start | bytes 524288 | tf_op jit(solution)/shard_map/all_to_all | solution.py:253
  22.3 12.2 %copy-start.3 = (bf16[2,3,3,16,192]{4,3,2,1,0:T(8,128)(2,1)S(1)}, bf16[2,3,3,16,192]{4,3,2,1,0:T(8,128)(2,1)}, u32[]{:S(2)}) copy-start(bf16[2,3,3,16,192]{4,3,2,1,0:T(8,128)(2,1)} %get-tuple-element.29.own_ref) | copy-start | bytes 331780
  22.3 6.6 %collective-permute-start.7 = (bf16[3,3,16,192]{3,2,1,0:T(8,128)(2,1)S(1)}, bf16[3,3,16,192]{3,2,1,0:T(8,128)(2,1)S(1)}, u32[]{:S(2)}, u32[]{:S(2)}) collective-permute-start(bf16[3,3,16,192]{3,2,1,0:T(8,128)(2,1)S(1)} %collective-permute-done.6), channel_id=1, source_target_pairs={{0,4},{4,8},{8,12},{12,0},{16,28},{20,16},{24,20},{28,24},{1,5},{5... | collective-permute-start | bytes 165896 | tf_op jit(solution)/shard_map/ppermute | solution.py:274
  22.7 9.5 %collective-permute-start.8 = (bf16[2,3,3,16,192]{4,3,2,1,0:T(8,128)(2,1)S(1)}, bf16[2,3,3,16,192]{4,3,2,1,0:T(8,128)(2,1)S(1)}, u32[]{:S(2)}, u32[]{:S(2)}) collective-permute-start(bf16[2,3,3,16,192]{4,3,2,1,0:T(8,128)(2,1)S(1)} %collective-permute-done.5.side_ref), channel_id=1, source_target_pairs={{0,16},{16,0},{1,17},{17,1},{2,18},{18,2},{3,19},{19,3},{4,20},{20... | collective-permute-start | bytes 331784 | tf_op jit(solution)/shard_map/ppermute | solution.py:279
  24.8 7.3 %collective-permute-start.3 = (bf16[4,16,768]{2,1,0:T(8,128)(2,1)S(1)}, bf16[4,16,768]{2,1,0:T(8,128)(2,1)S(1)}, u32[]{:S(2)}, u32[]{:S(2)}) collective-permute-start(bf16[4,16,768]{2,1,0:T(8,128)(2,1)S(1)} %get-tuple-element.26), channel_id=1, source_target_pairs={{0,16},{16,0},{32,48},{48,32},{64,80},{80,64},{96,112},{112,96},{1... | collective-permute-start | bytes 294920 | tf_op jit(solution)/shard_map/ppermute | solution.py:242
  24.9 9.5 %collective-permute-start.4 = (bf16[4,16,768]{2,1,0:T(8,128)(2,1)S(1)}, bf16[4,16,768]{2,1,0:T(8,128)(2,1)S(1)}, u32[]{:S(2)}, u32[]{:S(2)}) collective-permute-start(bf16[4,16,768]{2,1,0:T(8,128)(2,1)S(1)} %get-tuple-element.27), channel_id=1, source_target_pairs={{16,32},{48,64},{80,96},{112,128},{144,160},{176,192},{208,224},{3... | collective-permute-start | bytes 294920 | tf_op jit(solution)/shard_map/ppermute | solution.py:244
  29.0 3.2 %collective-permute-start.9 = (bf16[3,3,16,192]{3,2,1,0:T(8,128)(2,1)S(1)}, bf16[3,3,16,192]{3,2,1,0:T(8,128)(2,1)S(1)}, u32[]{:S(2)}, u32[]{:S(2)}) collective-permute-start(bf16[3,3,16,192]{3,2,1,0:T(8,128)(2,1)S(1)} %collective-permute-done.7.far_ref), channel_id=1, source_target_pairs={{0,16},{16,0},{1,17},{17,1},{2,18},{18,2},{3,19},{19,3},{4,20},{20... | collective-permute-start | bytes 165896 | tf_op jit(solution)/shard_map/ppermute | solution.py:279
  34.5 16.8 %copy-start.1 = (bf16[8,16,256]{2,1,0:T(8,128)(2,1)S(1)}, bf16[8,16,256]{2,1,0:T(8,128)(2,1)}, u32[]{:S(2)}) copy-start(bf16[8,16,256]{2,1,0:T(8,128)(2,1)} %get-tuple-element.36.later_ref) | copy-start | bytes 196612
  36.6 9.6 %collective-permute-start.10 = (bf16[8,16,512]{2,1,0:T(8,128)(2,1)S(1)}, bf16[8,16,512]{2,1,0:T(8,128)(2,1)S(1)}, u32[]{:S(2)}, u32[]{:S(2)}) collective-permute-start(bf16[8,16,512]{2,1,0:T(8,128)(2,1)S(1)} %get-tuple-element.32), channel_id=1, source_target_pairs={{0,8},{4,12},{8,0},{12,4},{1,9},{5,13},{9,1},{13,5},{2,10},{6,14},... | collective-permute-start | bytes 393224 | tf_op jit(solution)/shard_map/ppermute | solution.py:222
  40.8 3.6 %copy-start.6 = (f32[2,16]{1,0:T(2,128)S(1)}, f32[2,16]{1,0:T(2,128)}, u32[]{:S(2)}) copy-start(f32[2,16]{1,0:T(2,128)} %param.11) | copy-start | bytes 388
  40.8 8.2 %collective-permute-start.11 = (bf16[8,16,512]{2,1,0:T(8,128)(2,1)S(1)}, bf16[8,16,512]{2,1,0:T(8,128)(2,1)S(1)}, u32[]{:S(2)}, u32[]{:S(2)}) collective-permute-start(bf16[8,16,512]{2,1,0:T(8,128)(2,1)S(1)} %get-tuple-element.33), channel_id=1, source_target_pairs={{0,12},{4,0},{8,4},{12,8},{16,20},{20,24},{24,28},{28,16},{1,13},{... | collective-permute-start | bytes 393224 | tf_op jit(solution)/shard_map/ppermute | solution.py:223
  42.7 1.7 %copy-start.4 = (f32[2,16]{1,0:T(2,128)S(1)}, f32[2,16]{1,0:T(2,128)}, u32[]{:S(2)}) copy-start(f32[2,16]{1,0:T(2,128)} %gain_hbm.1) | copy-start | bytes 388
  42.7 8.6 %collective-permute-start.12 = (bf16[8,16,512]{2,1,0:T(8,128)(2,1)S(1)}, bf16[8,16,512]{2,1,0:T(8,128)(2,1)S(1)}, u32[]{:S(2)}, u32[]{:S(2)}) collective-permute-start(bf16[8,16,512]{2,1,0:T(8,128)(2,1)S(1)} %get-tuple-element.34), channel_id=1, source_target_pairs={{0,4},{4,8},{8,12},{12,0},{16,28},{20,16},{24,20},{28,24},{1,5},{5... | collective-permute-start | bytes 393224 | tf_op jit(solution)/shard_map/ppermute | solution.py:224
  44.3 0.7 copy-start.5
  52.2 13.4 %collective-permute-start.13 = (bf16[8,16,768]{2,1,0:T(8,128)(2,1)S(1)}, bf16[8,16,768]{2,1,0:T(8,128)(2,1)S(1)}, u32[]{:S(2)}, u32[]{:S(2)}) collective-permute-start(bf16[8,16,768]{2,1,0:T(8,128)(2,1)S(1)} %get-tuple-element.37.a_ref), channel_id=1, source_target_pairs={{0,1},{1,0},{2,3},{3,2},{4,5},{5,4},{6,7},{7,6},{8,9},{9,8},{10,11... | collective-permute-start | bytes 589832 | tf_op jit(solution)/shard_map/ppermute | solution.py:249
  53.0 12.6 %collective-permute-start.14 = (bf16[8,16,768]{2,1,0:T(8,128)(2,1)S(1)}, bf16[8,16,768]{2,1,0:T(8,128)(2,1)S(1)}, u32[]{:S(2)}, u32[]{:S(2)}) collective-permute-start(bf16[8,16,768]{2,1,0:T(8,128)(2,1)S(1)} %get-tuple-element.37.a_ref), channel_id=1, source_target_pairs={{0,2},{1,3},{2,0},{3,1},{4,6},{5,7},{6,4},{7,5},{8,10},{9,11},{10,... | collective-permute-start | bytes 589832 | tf_op jit(solution)/shard_map/ppermute | solution.py:249
  56.0 9.6 %collective-permute-start.15 = (bf16[8,16,768]{2,1,0:T(8,128)(2,1)S(1)}, bf16[8,16,768]{2,1,0:T(8,128)(2,1)S(1)}, u32[]{:S(2)}, u32[]{:S(2)}) collective-permute-start(bf16[8,16,768]{2,1,0:T(8,128)(2,1)S(1)} %get-tuple-element.37.a_ref), channel_id=1, source_target_pairs={{0,3},{1,2},{2,1},{3,0},{4,7},{5,6},{6,5},{7,4},{8,11},{9,10},{10,... | collective-permute-start | bytes 589832 | tf_op jit(solution)/shard_map/ppermute | solution.py:249
  56.0 19.8 %all-to-all-start.1 = ((f32[64,8,128]{2,1,0:T(8,128)}), f32[64,8,128]{2,1,0:T(8,128)S(1)}, u32[]{:S(2)}, u32[]{:S(2)}) async-start(f32[64,8,128]{2,1,0:T(8,128)} %get-tuple-element.40), calls=%async_computation.1 | async-start | bytes 524288 | tf_op jit(solution)/shard_map/all_to_all | solution.py:253
  65.6 4.4 %collective-permute-start.16 = (bf16[4,16,768]{2,1,0:T(8,128)(2,1)S(1)}, bf16[4,16,768]{2,1,0:T(8,128)(2,1)S(1)}, u32[]{:S(2)}, u32[]{:S(2)}) collective-permute-start(bf16[4,16,768]{2,1,0:T(8,128)(2,1)S(1)} %get-tuple-element.38), channel_id=1, source_target_pairs={{0,16},{16,0},{32,48},{48,32},{64,80},{80,64},{96,112},{112,96},{1... | collective-permute-start | bytes 294920 | tf_op jit(solution)/shard_map/ppermute | solution.py:242
  66.1 26.2 %copy-start = (bf16[4,8,16,128]{3,2,1,0:T(8,128)(2,1)S(1)}, bf16[4,8,16,128]{3,2,1,0:T(8,128)(2,1)}, u32[]{:S(2)}) copy-start(bf16[4,8,16,128]{3,2,1,0:T(8,128)(2,1)} %x_ref.1) | copy-start | bytes 393220
  66.1 9.7 %collective-permute-start.17 = (bf16[4,16,768]{2,1,0:T(8,128)(2,1)S(1)}, bf16[4,16,768]{2,1,0:T(8,128)(2,1)S(1)}, u32[]{:S(2)}, u32[]{:S(2)}) collective-permute-start(bf16[4,16,768]{2,1,0:T(8,128)(2,1)S(1)} %get-tuple-element.39), channel_id=1, source_target_pairs={{16,32},{48,64},{80,96},{112,128},{144,160},{176,192},{208,224},{3... | collective-permute-start | bytes 294920 | tf_op jit(solution)/shard_map/ppermute | solution.py:244
  77.9 10.2 %collective-permute-start.18 = (bf16[8,16,512]{2,1,0:T(8,128)(2,1)S(1)}, bf16[8,16,512]{2,1,0:T(8,128)(2,1)S(1)}, u32[]{:S(2)}, u32[]{:S(2)}) collective-permute-start(bf16[8,16,512]{2,1,0:T(8,128)(2,1)S(1)} %get-tuple-element.41), channel_id=1, source_target_pairs={{0,8},{4,12},{8,0},{12,4},{1,9},{5,13},{9,1},{13,5},{2,10},{6,14},... | collective-permute-start | bytes 393224 | tf_op jit(solution)/shard_map/ppermute | solution.py:222
  81.8 7.0 %collective-permute-start.19 = (bf16[8,16,512]{2,1,0:T(8,128)(2,1)S(1)}, bf16[8,16,512]{2,1,0:T(8,128)(2,1)S(1)}, u32[]{:S(2)}, u32[]{:S(2)}) collective-permute-start(bf16[8,16,512]{2,1,0:T(8,128)(2,1)S(1)} %get-tuple-element.42), channel_id=1, source_target_pairs={{0,12},{4,0},{8,4},{12,8},{16,20},{20,24},{24,28},{28,16},{1,13},{... | collective-permute-start | bytes 393224 | tf_op jit(solution)/shard_map/ppermute | solution.py:223
  81.9 10.3 %collective-permute-start.20 = (bf16[8,16,512]{2,1,0:T(8,128)(2,1)S(1)}, bf16[8,16,512]{2,1,0:T(8,128)(2,1)S(1)}, u32[]{:S(2)}, u32[]{:S(2)}) collective-permute-start(bf16[8,16,512]{2,1,0:T(8,128)(2,1)S(1)} %get-tuple-element.43), channel_id=1, source_target_pairs={{0,4},{4,8},{8,12},{12,0},{16,28},{20,16},{24,20},{28,24},{1,5},{5... | collective-permute-start | bytes 393224 | tf_op jit(solution)/shard_map/ppermute | solution.py:224

commit v8 on v6

--- a/solution.py
+++ b/solution.py
@@ -43,6 +43,15 @@
     return lax.axis_index(ROW), lax.axis_index("zh"), lax.axis_index(NEAR)
 
 
+def gathered_lanes():
+    shape = (256, 256)
+    old = lax.broadcasted_iota(jnp.int32, shape, 0)
+    new = lax.broadcasted_iota(jnp.int32, shape, 1)
+    group, rest = lax.shift_right_logical(old, 6), lax.bitwise_and(old, 15)
+    member = lax.bitwise_and(lax.shift_right_logical(old, 4), 3)
+    return jnp.where(new == 64 * member + 16 * group + rest, 1.0, 0.0).astype(BF16)
+
+
 def put_stats(rows_ref, note_ref, stats_ref):
     slabs = [rows_ref[:, :, 256 + 128 * t : 384 + 128 * t].astype(F32) for t in range(4)]
     x = jnp.concatenate(slabs, axis=0).reshape(32, 2, GROUP, 128)
@@ -65,7 +74,7 @@
 
 def begin_kernel(
     x_hbm, cache_hbm, gain_hbm, shift_hbm, w_hbm,
-    raw_ref, later_ref, stats_ref, own_ref, side_ref, far_ref,
+    raw_ref, later_ref, stats_ref, own_ref, w1_ref, w2_ref, w3_ref,
     x_ref, cache_ref, gain_ref, shift_ref, w_ref, note_ref, pieces_ref, sems,
 ):
     fetch(
@@ -82,20 +91,18 @@
             later_ref[r, :, lanes] = cache_ref[1, t, r]
         for t in range(4):
             raw_ref[r, :, 256 + 128 * t : 384 + 128 * t] = x_ref[t, r]
-    row, me, _ = place()
-    core = lax.rem(row, 2)
-    for q in range(4):
-        ahead = lax.rem(q + 4 - me, 4)
+    _, _, here = place()
+    held = dot(w_ref[...].reshape(864, 256), gathered_lanes()).astype(BF16).reshape(2, 27, 16, 256)
+    for n in range(4):
         for layer in range(2):
             for dt in range(3):
                 for dc in range(3):
                     taps = [
-                        w_ref[layer, 9 * dt + 3 * dr + dc, :, 64 * q : 64 * (q + 1)] for dr in range(3)
+                        held[layer, 9 * dt + 3 * dr + dc, :, 64 * n : 64 * (n + 1)] for dr in range(3)
                     ]
-                    pieces_ref[ahead, layer, dt, dc] = jnp.concatenate(taps, axis=1)
-    own_ref[...] = pieces_ref[0]
-    side_ref[...] = pieces_ref[1 + 2 * core]
-    far_ref[...] = pieces_ref[2, core]
+                    pieces_ref[lax.bitwise_xor(here, n), layer, dt, dc] = jnp.concatenate(taps, axis=1)
+    for k, ref in enumerate((own_ref, w1_ref, w2_ref, w3_ref)):
+        ref[...] = pieces_ref[k]
     note_ref[...] = jnp.zeros((8, 128), F32)
     note_ref[4:5, 0:16] = gain_ref[0:1, :]
     note_ref[5:6, 0:16] = shift_ref[0:1, :]
@@ -131,10 +138,10 @@
 
 def conv_kernel(
     layer, a_ref, b_ref, c_ref, d_ref, chip_ref, next_ref, stats_ref,
-    own_ref, side_ref, far_ref, side2_ref, far2_ref, o0_ref, o1_ref, o2_ref, o3_ref,
+    w0_ref, w1_ref, w2_ref, w3_ref, o0_ref, o1_ref, o2_ref, o3_ref,
     affine_ref, slab_ref, held_ref,
 ):
-    row, _, here = place()
+    row, here, _ = place()
     get_affine(stats_ref, affine_ref)
     upper = lax.rem(row, 2) == 0
     not_top = (row > 0).astype(F32)
@@ -162,22 +169,9 @@
                 if r == 9:
                     x = x * not_bottom
                 slab_ref[r, b, :, lanes] = x.astype(BF16)
-    core = lax.rem(row, 2)
-    for dt in range(3):
-        held_ref[dt, 0] = own_ref[layer, dt]
-        held_ref[dt, 1] = side_ref[layer, dt]
-        held_ref[dt, 2] = side2_ref[layer, dt]
-
-    @pl.when(core == layer)
-    def _():
+    for k, w_ref in enumerate((w0_ref, w1_ref, w2_ref, w3_ref)):
         for dt in range(3):
-            held_ref[dt, 3] = far_ref[dt]
-
-    @pl.when(core != layer)
-    def _():
-        for dt in range(3):
-            held_ref[dt, 3] = far2_ref[dt]
-
+            held_ref[dt, k] = w_ref[layer, dt]
     for r in range(8):
         rows = slab_ref[r : r + 3].reshape(192, 768)
         prod = dot(held_ref[0].reshape(192, 192), rows[:, 0:512])
@@ -213,17 +207,6 @@
             o_ref[t, r] = (x_ref[t, r].astype(F32) + (branch + bias)).astype(BF16)
 
 
-def sides(step):
-    return [(i, (i + step) % 4) for i in range(4)] + [(4 + i, 4 + (i - step) % 4) for i in range(4)]
-
-
-def bring(own, side, other, far):
-    far = lax.ppermute(far, "zh", [(i, (i + 2) % 4) for i in range(4)])
-    side = lax.ppermute(side, ("core", "zh"), sides(-1))
-    other = lax.ppermute(other, ("core", "zh"), sides(1))
-    return [own, side, other, far]
-
-
 def struct(shape, dtype=BF16):
     return jax.ShapeDtypeStruct(shape, dtype)
 
@@ -244,8 +227,13 @@
     return [chip, beyond]
 
 
-def near(x):
-    return [x] + [lax.ppermute(x, NEAR, [(i, i ^ k) for i in range(4)]) for k in (1, 2, 3)]
+def gather(x):
+    return [x] + [lax.ppermute(x, "zh", [(i, i ^ k) for i in range(4)]) for k in (1, 2, 3)]
+
+
+def bring(blocks):
+    moved = [lax.ppermute(blocks[k], NEAR, [(i, i ^ k) for i in range(4)]) for k in (1, 2, 3)]
+    return [blocks[0]] + moved
 
 
 def exchange(x, axes):
@@ -255,11 +243,11 @@
 def local(frames, cache, norm_gain, norm_shift, conv_weight, conv_bias):
     note = pltpu.VMEM((8, 128), F32)
     piece = (2, 3, 3, 16, 192)
-    raw, later, stats, own, side, far = call(
+    raw, later, stats, *weights = call(
         begin_kernel,
         (
             struct((8, 16, 768)), struct((8, 16, 256)), struct((64, 8, 128), F32), struct(piece),
-            struct(piece), struct(piece[1:]),
+            struct(piece), struct(piece), struct(piece),
         ),
         frames, cache, norm_gain, norm_shift, conv_weight.transpose(0, 2, 1, 3),
         scratch=(
@@ -269,13 +257,10 @@
         ),
         far=(0, 1, 2, 3, 4),
     )
-    side = lax.ppermute(side, ("core", "zh"), sides(1))
-    far = lax.ppermute(far, "zh", [(i, (i + 2) % 4) for i in range(4)])
-    raw = near(raw)
-    stats = exchange(stats, ROW + NEAR)
+    raw = gather(raw)
+    weights = bring(weights)
+    stats = exchange(stats, ROW + ("zh",))
     raw = raw + rows_beside(raw)
-    swap = [(0, 1), (1, 0)]
-    weights = [own, side, far, lax.ppermute(side, "core", swap), lax.ppermute(far, "core", swap)]
     bias = jnp.broadcast_to(conv_bias[:, :, None], (2, 16, 128))
     note1 = jnp.pad(jnp.stack([norm_gain[1], norm_shift[1]]), ((4, 2), (0, 112)))
     scratch = (
@@ -290,19 +275,19 @@
         functools.partial(conv_kernel, 0), parts, *raw, stats, *weights,
         scratch=scratch, flops=flops,
     )
-    partial = bring(*partial)
+    partial = bring(partial)
     middle, stats = call(
         merge_kernel, (struct((8, 16, 768)), struct((64, 8, 128), F32)), *partial, bias[0], later, note1,
         scratch=(note,),
     )
-    middle = near(middle)
-    stats = exchange(stats, ROW + NEAR)
+    middle = gather(middle)
+    stats = exchange(stats, ROW + ("zh",))
     middle = middle + rows_beside(middle)
     partial = call(
         functools.partial(conv_kernel, 1), parts, *middle, stats, *weights,
         scratch=scratch, flops=flops,
     )
-    partial = bring(*partial)
+    partial = bring(partial)
     return call(last_kernel, struct((4, 8, 16, 128)), frames, *partial, bias[1])
 
 

time: 93.3 us -> 102 us (1.093)
  the two profiles are of different devices: /device:TPU:1 before, /device:TPU:27 now
where the time goes in v8:
time: 102 us; the launch traced here: 99.9 us
  starting transfers between devices  59.7 us (59%)
  waiting for transfers between devices  30.5 us (30%)
  Pallas kernels  8.66 us (8%)
    all_to_all x2, starting transfers between devices, exchange(): return lax.all_to_all(x, axes, 0, 0, tiled=True)  23.2 us
    ppermute x9, waiting for transfers between devices, bring(): lax.ppermute(blocks[k], NEAR, [(i, i ^ k) for i in range(4)])  14.5 us
    ppermute x6, starting transfers between devices, gather(): lax.ppermute(x, 'zh', [(i, i ^ k) for i in range(4)])  13.8 us
    ppermute x2, waiting for transfers between devices, rows_beside(): beyond = lax.ppermute(beyond, ROW, pairs)  10.1 us
    ppermute x2, starting transfers between devices, rows_beside(): chip = lax.ppermute(chip, ROW, [(i, i ^ 1) for i in range(16)])  8.8 us
    pallas_call x7, Pallas kernels, call(): pl.pallas_call(kernel, out_shape=outs, in_specs=specs, out_specs=jax.tree...  8.66 us
    ppermute x9, starting transfers between devices, bring(): lax.ppermute(blocks[k], NEAR, [(i, i ^ k) for i in range(4)])  8.51 us
    ppermute x6, waiting for transfers between devices, gather(): lax.ppermute(x, 'zh', [(i, i ^ k) for i in range(4)])  5.96 us
  transfers between devices with their start and end apart: 21, of which 10 were waited for; matrix products, arithmetic and copies ran while one was open for 0% of the time, Pallas kernels for 0%

profile of v8, /device:TPU:27, one launch (start us, length us, event | category | flops | bytes accessed | tf_op | source)
XLA Modules:
  0.0 99.9 jit_solution(7707130472621867573)
XLA Ops:
  0.0 2.5 %shard_map.64 = (bf16[8,16,768]{2,1,0:T(8,128)(2,1)}, bf16[8,16,256]{2,1,0:T(8,128)(2,1)}, f32[64,8,128]{2,1,0:T(8,128)}, bf16[2,3,3,16,192]{4,3,2,1,0:T(8,128)(...) custom-call(bf16[4,8,16,128]{3,2,1,0:T(8,128)(2,1)} %x_ref.1, ...), custom_call_target="tpu_custom_call" | custom-call | bytes 704768 | tf_op jit(solution)/shard_map/pallas_call | solution.py:31
  2.5 3.1 %collective-permute-start = (bf16[8,16,768]{2,1,0:T(8,128)(2,1)}, bf16[8,16,768]{2,1,0:T(8,128)(2,1)S(1)}, u32[]{:S(2)}, u32[]{:S(2)}) collective-permute-start(bf16[8,16,768]{2,1,0:T(8,128)(2,1)} %get-tuple-element.26.a_ref), channel_id=1, source_target_pairs={{0,4},{4,0},{8,12},{12,8},{1,5},{5,1},{9,13},{13,9},{2,6},{6,2},{1... | collective-permute-start | bytes 589832 | tf_op jit(solution)/shard_map/ppermute | solution.py:231
  5.6 5.1 %collective-permute-start.1 = (bf16[8,16,768]{2,1,0:T(8,128)(2,1)}, bf16[8,16,768]{2,1,0:T(8,128)(2,1)S(1)}, u32[]{:S(2)}, u32[]{:S(2)}) collective-permute-start(bf16[8,16,768]{2,1,0:T(8,128)(2,1)} %get-tuple-element.26.a_ref), channel_id=1, source_target_pairs={{0,8},{4,12},{8,0},{12,4},{1,9},{5,13},{9,1},{13,5},{2,10},{6,14},... | collective-permute-start | bytes 589832 | tf_op jit(solution)/shard_map/ppermute | solution.py:231
  10.7 0.0 collective-permute-start.2
  10.7 0.3 collective-permute-start.5
  11.0 0.7 collective-permute-start.6
  11.7 13.2 %all-to-all-start = ((f32[64,8,128]{2,1,0:T(8,128)}), f32[64,8,128]{2,1,0:T(8,128)S(1)}, u32[]{:S(2)}, u32[]{:S(2)}) async-start(f32[64,8,128]{2,1,0:T(8,128)} %get-tuple-element.29), calls=%async_computation | async-start | bytes 524288 | tf_op jit(solution)/shard_map/all_to_all | solution.py:240
  24.9 0.0 collective-permute-done.b_ref
  24.9 2.1 %collective-permute-start.7 = (bf16[2,3,3,16,192]{4,3,2,1,0:T(8,128)(2,1)S(1)}, bf16[2,3,3,16,192]{4,3,2,1,0:T(8,128)(2,1)S(1)}, u32[]{:S(2)}, u32[]{:S(2)}) collective-permute-start(bf16[2,3,3,16,192]{4,3,2,1,0:T(8,128)(2,1)S(1)} %copy-done.7), channel_id=1, source_target_pairs={{0,3},{1,2},{2,1},{3,0},{4,7},{5,6},{6,5},{7,4},{8,11},{9,10},{10,... | collective-permute-start | bytes 331784 | tf_op jit(solution)/shard_map/ppermute | solution.py:235
  27.0 0.0 collective-permute-done.1.c_ref
  27.0 0.0 collective-permute-done.2.d_ref
  27.0 3.6 %collective-permute-start.3 = (bf16[4,16,768]{2,1,0:T(8,128)(2,1)S(1)}, bf16[4,16,768]{2,1,0:T(8,128)(2,1)S(1)}, u32[]{:S(2)}, u32[]{:S(2)}) collective-permute-start(bf16[4,16,768]{2,1,0:T(8,128)(2,1)S(1)} %get-tuple-element.27), channel_id=1, source_target_pairs={{0,16},{16,0},{32,48},{48,32},{64,80},{80,64},{96,112},{112,96},{1... | collective-permute-start | bytes 294920 | tf_op jit(solution)/shard_map/ppermute | solution.py:224
  30.7 3.3 %collective-permute-start.4 = (bf16[4,16,768]{2,1,0:T(8,128)(2,1)S(1)}, bf16[4,16,768]{2,1,0:T(8,128)(2,1)S(1)}, u32[]{:S(2)}, u32[]{:S(2)}) collective-permute-start(bf16[4,16,768]{2,1,0:T(8,128)(2,1)S(1)} %get-tuple-element.28), channel_id=1, source_target_pairs={{16,32},{48,64},{80,96},{112,128},{144,160},{176,192},{208,224},{3... | collective-permute-start | bytes 294920 | tf_op jit(solution)/shard_map/ppermute | solution.py:226
  34.0 0.0 collective-permute-done.6.w2_ref
  34.0 5.6 %collective-permute-done.7.w3_ref = bf16[2,3,3,16,192]{4,3,2,1,0:T(8,128)(2,1)S(1)} collective-permute-done((bf16[2,3,3,16,192]{4,3,2,1,0:T(8,128)(2,1)S(1)}, bf16[2,3,3,16,192]{4,3,2,1,0:T(8,128)(2,1)S(1)}, u32[]{:S(2)}, u32[]{:S(2)}) %collective-permute-start.7) | collective-permute-done | bytes 110624 | tf_op jit(solution)/shard_map/ppermute | solution.py:235
  39.6 2.5 %collective-permute-done.4.next_ref = bf16[4,16,768]{2,1,0:T(8,128)(2,1)S(1)} collective-permute-done((bf16[4,16,768]{2,1,0:T(8,128)(2,1)S(1)}, bf16[4,16,768]{2,1,0:T(8,128)(2,1)S(1)}, u32[]{:S(2)}, u32[]{:S(2)}) %collective-permute-start.4) | collective-permute-done | bytes 98336 | tf_op jit(solution)/shard_map/ppermute | solution.py:226
  42.1 0.0 all-to-all-done.stats_ref
  42.1 2.2 %shard_map.66 = (bf16[8,16,512]{2,1,0:T(8,128)(2,1)S(1)}, bf16[8,16,512]{2,1,0:T(8,128)(2,1)S(1)}, bf16[8,16,512]{2,1,0:T(8,128)(2,1)S(1)}, bf16[8,16,512]{2,1,0:T(8,128)(2,1)S(1)}) custom-call(bf16[8,16,768]{2,1,0:T(8,128)(2,1)S(1)} %copy-done.2, bf16[8,16,768]{2,1,0:T(8,128)(2,1)S(1)} %collective-permute-done.b_ref, ...), custom_call_target="tpu_custom_call" | custom-call | flops 905969664 | bytes 1687552 | tf_op jit(solution)/shard_map/pallas_call | solution.py:31
  44.4 0.1 collective-permute-start.10
  44.5 0.0 copy-start.6
  44.5 1.1 %collective-permute-start.8 = (bf16[8,16,512]{2,1,0:T(8,128)(2,1)S(1)}, bf16[8,16,512]{2,1,0:T(8,128)(2,1)S(1)}, u32[]{:S(2)}, u32[]{:S(2)}) collective-permute-start(bf16[8,16,512]{2,1,0:T(8,128)(2,1)S(1)} %get-tuple-element.35), channel_id=1, source_target_pairs={{0,1},{1,0},{2,3},{3,2},{4,5},{5,4},{6,7},{7,6},{8,9},{9,8},{10,11... | collective-permute-start | bytes 393224 | tf_op jit(solution)/shard_map/ppermute | solution.py:235
  45.6 1.5 %collective-permute-start.9 = (bf16[8,16,512]{2,1,0:T(8,128)(2,1)S(1)}, bf16[8,16,512]{2,1,0:T(8,128)(2,1)S(1)}, u32[]{:S(2)}, u32[]{:S(2)}) collective-permute-start(bf16[8,16,512]{2,1,0:T(8,128)(2,1)S(1)} %get-tuple-element.36), channel_id=1, source_target_pairs={{0,2},{1,3},{2,0},{3,1},{4,6},{5,7},{6,4},{7,5},{8,10},{9,11},{10,... | collective-permute-start | bytes 393224 | tf_op jit(solution)/shard_map/ppermute | solution.py:235
  47.1 0.0 copy-start.5
  47.2 0.7 copy-done.5
  47.8 1.9 %collective-permute-done.10.d_ref = bf16[8,16,512]{2,1,0:T(8,128)(2,1)S(1)} collective-permute-done((bf16[8,16,512]{2,1,0:T(8,128)(2,1)S(1)}, bf16[8,16,512]{2,1,0:T(8,128)(2,1)S(1)}, u32[]{:S(2)}, u32[]{:S(2)}) %collective-permute-start.10) | collective-permute-done | bytes 131104 | tf_op jit(solution)/shard_map/ppermute | solution.py:235
  49.8 2.7 %collective-permute-done.8.b_ref = bf16[8,16,512]{2,1,0:T(8,128)(2,1)S(1)} collective-permute-done((bf16[8,16,512]{2,1,0:T(8,128)(2,1)S(1)}, bf16[8,16,512]{2,1,0:T(8,128)(2,1)S(1)}, u32[]{:S(2)}, u32[]{:S(2)}) %collective-permute-start.8) | collective-permute-done | bytes 131104 | tf_op jit(solution)/shard_map/ppermute | solution.py:235
  52.5 0.1 collective-permute-done.9.c_ref
  52.5 0.1 broadcast_in_dim.13.bias_ref
  52.6 0.9 shard_map.67
  53.5 1.6 %collective-permute-start.11 = (bf16[8,16,768]{2,1,0:T(8,128)(2,1)S(1)}, bf16[8,16,768]{2,1,0:T(8,128)(2,1)S(1)}, u32[]{:S(2)}, u32[]{:S(2)}) collective-permute-start(bf16[8,16,768]{2,1,0:T(8,128)(2,1)S(1)} %get-tuple-element.39.a_ref), channel_id=1, source_target_pairs={{0,4},{4,0},{8,12},{12,8},{1,5},{5,1},{9,13},{13,9},{2,6},{6,2},{1... | collective-permute-start | bytes 589832 | tf_op jit(solution)/shard_map/ppermute | solution.py:231
  55.0 3.4 %collective-permute-start.12 = (bf16[8,16,768]{2,1,0:T(8,128)(2,1)S(1)}, bf16[8,16,768]{2,1,0:T(8,128)(2,1)S(1)}, u32[]{:S(2)}, u32[]{:S(2)}) collective-permute-start(bf16[8,16,768]{2,1,0:T(8,128)(2,1)S(1)} %get-tuple-element.39.a_ref), channel_id=1, source_target_pairs={{0,8},{4,12},{8,0},{12,4},{1,9},{5,13},{9,1},{13,5},{2,10},{6,14},... | collective-permute-start | bytes 589832 | tf_op jit(solution)/shard_map/ppermute | solution.py:231
  58.4 0.7 collective-permute-start.13
  59.1 10.0 %all-to-all-start.1 = ((f32[64,8,128]{2,1,0:T(8,128)}), f32[64,8,128]{2,1,0:T(8,128)S(1)}, u32[]{:S(2)}, u32[]{:S(2)}) async-start(f32[64,8,128]{2,1,0:T(8,128)} %get-tuple-element.42), calls=%async_computation.1 | async-start | bytes 524288 | tf_op jit(solution)/shard_map/all_to_all | solution.py:240
  69.2 5.4 %collective-permute-done.11.b_ref = bf16[8,16,768]{2,1,0:T(8,128)(2,1)S(1)} collective-permute-done((bf16[8,16,768]{2,1,0:T(8,128)(2,1)S(1)}, bf16[8,16,768]{2,1,0:T(8,128)(2,1)S(1)}, u32[]{:S(2)}, u32[]{:S(2)}) %collective-permute-start.11) | collective-permute-done | bytes 196640 | tf_op jit(solution)/shard_map/ppermute | solution.py:231
  74.5 0.6 collective-permute-done.13.d_ref
  75.1 5.2 %collective-permute-start.14 = (bf16[4,16,768]{2,1,0:T(8,128)(2,1)S(1)}, bf16[4,16,768]{2,1,0:T(8,128)(2,1)S(1)}, u32[]{:S(2)}, u32[]{:S(2)}) collective-permute-start(bf16[4,16,768]{2,1,0:T(8,128)(2,1)S(1)} %get-tuple-element.40), channel_id=1, source_target_pairs={{0,16},{16,0},{32,48},{48,32},{64,80},{80,64},{96,112},{112,96},{1... | collective-permute-start | bytes 294920 | tf_op jit(solution)/shard_map/ppermute | solution.py:224
  80.3 2.1 %collective-permute-start.15 = (bf16[4,16,768]{2,1,0:T(8,128)(2,1)S(1)}, bf16[4,16,768]{2,1,0:T(8,128)(2,1)S(1)}, u32[]{:S(2)}, u32[]{:S(2)}) collective-permute-start(bf16[4,16,768]{2,1,0:T(8,128)(2,1)S(1)} %get-tuple-element.41), channel_id=1, source_target_pairs={{16,32},{48,64},{80,96},{112,128},{144,160},{176,192},{208,224},{3... | collective-permute-start | bytes 294920 | tf_op jit(solution)/shard_map/ppermute | solution.py:226
  82.4 0.0 collective-permute-done.14.chip_ref
  82.4 7.6 %collective-permute-done.15.next_ref = bf16[4,16,768]{2,1,0:T(8,128)(2,1)S(1)} collective-permute-done((bf16[4,16,768]{2,1,0:T(8,128)(2,1)S(1)}, bf16[4,16,768]{2,1,0:T(8,128)(2,1)S(1)}, u32[]{:S(2)}, u32[]{:S(2)}) %collective-permute-start.15) | collective-permute-done | bytes 98336 | tf_op jit(solution)/shard_map/ppermute | solution.py:226
  89.9 0.0 all-to-all-done.1.stats_ref
  90.0 2.2 %shard_map.69 = (bf16[8,16,512]{2,1,0:T(8,128)(2,1)S(1)}, bf16[8,16,512]{2,1,0:T(8,128)(2,1)S(1)}, bf16[8,16,512]{2,1,0:T(8,128)(2,1)S(1)}, bf16[8,16,512]{2,1,0:T(8,128)(2,1)S(1)}) custom-call(bf16[8,16,768]{2,1,0:T(8,128)(2,1)S(1)} %get-tuple-element.39.a_ref, bf16[8,16,768]{2,1,0:T(8,128)(2,1)S(1)} %collective-permute-done.11.b_ref, ...), custom_call_target="tpu_custom_call" | custom-call | flops 905969664 | bytes 1687552 | tf_op jit(solution)/shard_map/pallas_call | solution.py:31
  92.2 1.3 %collective-permute-start.16 = (bf16[8,16,512]{2,1,0:T(8,128)(2,1)S(1)}, bf16[8,16,512]{2,1,0:T(8,128)(2,1)S(1)}, u32[]{:S(2)}, u32[]{:S(2)}) collective-permute-start(bf16[8,16,512]{2,1,0:T(8,128)(2,1)S(1)} %get-tuple-element.44), channel_id=1, source_target_pairs={{0,1},{1,0},{2,3},{3,2},{4,5},{5,4},{6,7},{7,6},{8,9},{9,8},{10,11... | collective-permute-start | bytes 393224 | tf_op jit(solution)/shard_map/ppermute | solution.py:235
  93.5 0.0 collective-permute-start.17
  93.5 1.4 %collective-permute-start.18 = (bf16[8,16,512]{2,1,0:T(8,128)(2,1)S(1)}, bf16[8,16,512]{2,1,0:T(8,128)(2,1)S(1)}, u32[]{:S(2)}, u32[]{:S(2)}) collective-permute-start(bf16[8,16,512]{2,1,0:T(8,128)(2,1)S(1)} %get-tuple-element.46), channel_id=1, source_target_pairs={{0,3},{1,2},{2,1},{3,0},{4,7},{5,6},{6,5},{7,4},{8,11},{9,10},{10,... | collective-permute-start | bytes 393224 | tf_op jit(solution)/shard_map/ppermute | solution.py:235
  94.9 2.6 %collective-permute-done.16.b_ref = bf16[8,16,512]{2,1,0:T(8,128)(2,1)S(1)} collective-permute-done((bf16[8,16,512]{2,1,0:T(8,128)(2,1)S(1)}, bf16[8,16,512]{2,1,0:T(8,128)(2,1)S(1)}, u32[]{:S(2)}, u32[]{:S(2)}) %collective-permute-start.16) | collective-permute-done | bytes 131104 | tf_op jit(solution)/shard_map/ppermute | solution.py:235
  97.5 1.6 %collective-permute-done.18.d_ref = bf16[8,16,512]{2,1,0:T(8,128)(2,1)S(1)} collective-permute-done((bf16[8,16,512]{2,1,0:T(8,128)(2,1)S(1)}, bf16[8,16,512]{2,1,0:T(8,128)(2,1)S(1)}, u32[]{:S(2)}, u32[]{:S(2)}) %collective-permute-start.18) | collective-permute-done | bytes 131104 | tf_op jit(solution)/shard_map/ppermute | solution.py:235
  99.1 0.1 broadcast_in_dim.15.bias_ref
  99.2 0.8 shard_map.70
  (23 shorter events, 0.1 us)
Async XLA Ops:
  2.5 22.4 %collective-permute-start = (bf16[8,16,768]{2,1,0:T(8,128)(2,1)}, bf16[8,16,768]{2,1,0:T(8,128)(2,1)S(1)}, u32[]{:S(2)}, u32[]{:S(2)}) collective-permute-start(bf16[8,16,768]{2,1,0:T(8,128)(2,1)} %get-tuple-element.26.a_ref), channel_id=1, source_target_pairs={{0,4},{4,0},{8,12},{12,8},{1,5},{5,1},{9,13},{13,9},{2,6},{6,2},{1... | collective-permute-start | bytes 589832 | tf_op jit(solution)/shard_map/ppermute | solution.py:231
  5.6 21.4 %collective-permute-start.1 = (bf16[8,16,768]{2,1,0:T(8,128)(2,1)}, bf16[8,16,768]{2,1,0:T(8,128)(2,1)S(1)}, u32[]{:S(2)}, u32[]{:S(2)}) collective-permute-start(bf16[8,16,768]{2,1,0:T(8,128)(2,1)} %get-tuple-element.26.a_ref), channel_id=1, source_target_pairs={{0,8},{4,12},{8,0},{12,4},{1,9},{5,13},{9,1},{13,5},{2,10},{6,14},... | collective-permute-start | bytes 589832 | tf_op jit(solution)/shard_map/ppermute | solution.py:231
  10.7 16.3 %collective-permute-start.2 = (bf16[8,16,768]{2,1,0:T(8,128)(2,1)}, bf16[8,16,768]{2,1,0:T(8,128)(2,1)S(1)}, u32[]{:S(2)}, u32[]{:S(2)}) collective-permute-start(bf16[8,16,768]{2,1,0:T(8,128)(2,1)} %get-tuple-element.26.a_ref), channel_id=1, source_target_pairs={{0,12},{4,8},{8,4},{12,0},{1,13},{5,9},{9,5},{13,1},{2,14},{6,10},... | collective-permute-start | bytes 589832 | tf_op jit(solution)/shard_map/ppermute | solution.py:231
  10.7 23.3 %collective-permute-start.5 = (bf16[2,3,3,16,192]{4,3,2,1,0:T(8,128)(2,1)}, bf16[2,3,3,16,192]{4,3,2,1,0:T(8,128)(2,1)S(1)}, u32[]{:S(2)}, u32[]{:S(2)}) collective-permute-start(bf16[2,3,3,16,192]{4,3,2,1,0:T(8,128)(2,1)} %get-tuple-element.31), channel_id=1, source_target_pairs={{0,1},{1,0},{2,3},{3,2},{4,5},{5,4},{6,7},{7,6},{8,9},{9,8},{10,11... | collective-permute-start | bytes 331784 | tf_op jit(solution)/shard_map/ppermute | solution.py:235
  11.0 23.0 %collective-permute-start.6 = (bf16[2,3,3,16,192]{4,3,2,1,0:T(8,128)(2,1)}, bf16[2,3,3,16,192]{4,3,2,1,0:T(8,128)(2,1)S(1)}, u32[]{:S(2)}, u32[]{:S(2)}) collective-permute-start(bf16[2,3,3,16,192]{4,3,2,1,0:T(8,128)(2,1)} %get-tuple-element.32), channel_id=1, source_target_pairs={{0,2},{1,3},{2,0},{3,1},{4,6},{5,7},{6,4},{7,5},{8,10},{9,11},{10,... | collective-permute-start | bytes 331784 | tf_op jit(solution)/shard_map/ppermute | solution.py:235
  11.7 13.2 %copy-start.7 = (bf16[2,3,3,16,192]{4,3,2,1,0:T(8,128)(2,1)S(1)}, bf16[2,3,3,16,192]{4,3,2,1,0:T(8,128)(2,1)}, u32[]{:S(2)}) copy-start(bf16[2,3,3,16,192]{4,3,2,1,0:T(8,128)(2,1)} %get-tuple-element.33) | copy-start | bytes 331780
  11.7 15.3 %copy-start.2 = (bf16[8,16,768]{2,1,0:T(8,128)(2,1)S(1)}, bf16[8,16,768]{2,1,0:T(8,128)(2,1)}, u32[]{:S(2)}) copy-start(bf16[8,16,768]{2,1,0:T(8,128)(2,1)} %get-tuple-element.26.a_ref) | copy-start | bytes 589828
  11.7 30.4 %all-to-all-start = ((f32[64,8,128]{2,1,0:T(8,128)}), f32[64,8,128]{2,1,0:T(8,128)S(1)}, u32[]{:S(2)}, u32[]{:S(2)}) async-start(f32[64,8,128]{2,1,0:T(8,128)} %get-tuple-element.29), calls=%async_computation | async-start | bytes 524288 | tf_op jit(solution)/shard_map/all_to_all | solution.py:240
  24.9 17.2 %copy-start.3 = (bf16[2,3,3,16,192]{4,3,2,1,0:T(8,128)(2,1)S(1)}, bf16[2,3,3,16,192]{4,3,2,1,0:T(8,128)(2,1)}, u32[]{:S(2)}) copy-start(bf16[2,3,3,16,192]{4,3,2,1,0:T(8,128)(2,1)} %get-tuple-element.30.w0_ref) | copy-start | bytes 331780
  24.9 14.7 %collective-permute-start.7 = (bf16[2,3,3,16,192]{4,3,2,1,0:T(8,128)(2,1)S(1)}, bf16[2,3,3,16,192]{4,3,2,1,0:T(8,128)(2,1)S(1)}, u32[]{:S(2)}, u32[]{:S(2)}) collective-permute-start(bf16[2,3,3,16,192]{4,3,2,1,0:T(8,128)(2,1)S(1)} %copy-done.7), channel_id=1, source_target_pairs={{0,3},{1,2},{2,1},{3,0},{4,7},{5,6},{6,5},{7,4},{8,11},{9,10},{10,... | collective-permute-start | bytes 331784 | tf_op jit(solution)/shard_map/ppermute | solution.py:235
  27.0 12.6 %collective-permute-start.3 = (bf16[4,16,768]{2,1,0:T(8,128)(2,1)S(1)}, bf16[4,16,768]{2,1,0:T(8,128)(2,1)S(1)}, u32[]{:S(2)}, u32[]{:S(2)}) collective-permute-start(bf16[4,16,768]{2,1,0:T(8,128)(2,1)S(1)} %get-tuple-element.27), channel_id=1, source_target_pairs={{0,16},{16,0},{32,48},{48,32},{64,80},{80,64},{96,112},{112,96},{1... | collective-permute-start | bytes 294920 | tf_op jit(solution)/shard_map/ppermute | solution.py:224
  30.7 11.4 %collective-permute-start.4 = (bf16[4,16,768]{2,1,0:T(8,128)(2,1)S(1)}, bf16[4,16,768]{2,1,0:T(8,128)(2,1)S(1)}, u32[]{:S(2)}, u32[]{:S(2)}) collective-permute-start(bf16[4,16,768]{2,1,0:T(8,128)(2,1)S(1)} %get-tuple-element.28), channel_id=1, source_target_pairs={{16,32},{48,64},{80,96},{112,128},{144,160},{176,192},{208,224},{3... | collective-permute-start | bytes 294920 | tf_op jit(solution)/shard_map/ppermute | solution.py:226
  42.1 10.5 %copy-start.1 = (bf16[8,16,256]{2,1,0:T(8,128)(2,1)S(1)}, bf16[8,16,256]{2,1,0:T(8,128)(2,1)}, u32[]{:S(2)}) copy-start(bf16[8,16,256]{2,1,0:T(8,128)(2,1)} %get-tuple-element.38.later_ref) | copy-start | bytes 196612
  44.4 5.4 %collective-permute-start.10 = (bf16[8,16,512]{2,1,0:T(8,128)(2,1)S(1)}, bf16[8,16,512]{2,1,0:T(8,128)(2,1)S(1)}, u32[]{:S(2)}, u32[]{:S(2)}) collective-permute-start(bf16[8,16,512]{2,1,0:T(8,128)(2,1)S(1)} %get-tuple-element.37), channel_id=1, source_target_pairs={{0,3},{1,2},{2,1},{3,0},{4,7},{5,6},{6,5},{7,4},{8,11},{9,10},{10,... | collective-permute-start | bytes 393224 | tf_op jit(solution)/shard_map/ppermute | solution.py:235
  44.5 2.6 %copy-start.6 = (f32[2,16]{1,0:T(2,128)S(1)}, f32[2,16]{1,0:T(2,128)}, u32[]{:S(2)}) copy-start(f32[2,16]{1,0:T(2,128)} %param.11) | copy-start | bytes 388
  44.5 8.0 %collective-permute-start.8 = (bf16[8,16,512]{2,1,0:T(8,128)(2,1)S(1)}, bf16[8,16,512]{2,1,0:T(8,128)(2,1)S(1)}, u32[]{:S(2)}, u32[]{:S(2)}) collective-permute-start(bf16[8,16,512]{2,1,0:T(8,128)(2,1)S(1)} %get-tuple-element.35), channel_id=1, source_target_pairs={{0,1},{1,0},{2,3},{3,2},{4,5},{5,4},{6,7},{7,6},{8,9},{9,8},{10,11... | collective-permute-start | bytes 393224 | tf_op jit(solution)/shard_map/ppermute | solution.py:235
  45.6 1.5 %copy-start.4 = (f32[2,16]{1,0:T(2,128)S(1)}, f32[2,16]{1,0:T(2,128)}, u32[]{:S(2)}) copy-start(f32[2,16]{1,0:T(2,128)} %gain_hbm.1) | copy-start | bytes 388
  45.6 6.9 %collective-permute-start.9 = (bf16[8,16,512]{2,1,0:T(8,128)(2,1)S(1)}, bf16[8,16,512]{2,1,0:T(8,128)(2,1)S(1)}, u32[]{:S(2)}, u32[]{:S(2)}) collective-permute-start(bf16[8,16,512]{2,1,0:T(8,128)(2,1)S(1)} %get-tuple-element.36), channel_id=1, source_target_pairs={{0,2},{1,3},{2,0},{3,1},{4,6},{5,7},{6,4},{7,5},{8,10},{9,11},{10,... | collective-permute-start | bytes 393224 | tf_op jit(solution)/shard_map/ppermute | solution.py:235
  47.1 0.7 copy-start.5
  53.5 21.1 %collective-permute-start.11 = (bf16[8,16,768]{2,1,0:T(8,128)(2,1)S(1)}, bf16[8,16,768]{2,1,0:T(8,128)(2,1)S(1)}, u32[]{:S(2)}, u32[]{:S(2)}) collective-permute-start(bf16[8,16,768]{2,1,0:T(8,128)(2,1)S(1)} %get-tuple-element.39.a_ref), channel_id=1, source_target_pairs={{0,4},{4,0},{8,12},{12,8},{1,5},{5,1},{9,13},{13,9},{2,6},{6,2},{1... | collective-permute-start | bytes 589832 | tf_op jit(solution)/shard_map/ppermute | solution.py:231
  55.0 19.5 %collective-permute-start.12 = (bf16[8,16,768]{2,1,0:T(8,128)(2,1)S(1)}, bf16[8,16,768]{2,1,0:T(8,128)(2,1)S(1)}, u32[]{:S(2)}, u32[]{:S(2)}) collective-permute-start(bf16[8,16,768]{2,1,0:T(8,128)(2,1)S(1)} %get-tuple-element.39.a_ref), channel_id=1, source_target_pairs={{0,8},{4,12},{8,0},{12,4},{1,9},{5,13},{9,1},{13,5},{2,10},{6,14},... | collective-permute-start | bytes 589832 | tf_op jit(solution)/shard_map/ppermute | solution.py:231
  58.4 16.7 %collective-permute-start.13 = (bf16[8,16,768]{2,1,0:T(8,128)(2,1)S(1)}, bf16[8,16,768]{2,1,0:T(8,128)(2,1)S(1)}, u32[]{:S(2)}, u32[]{:S(2)}) collective-permute-start(bf16[8,16,768]{2,1,0:T(8,128)(2,1)S(1)} %get-tuple-element.39.a_ref), channel_id=1, source_target_pairs={{0,12},{4,8},{8,4},{12,0},{1,13},{5,9},{9,5},{13,1},{2,14},{6,10},... | collective-permute-start | bytes 589832 | tf_op jit(solution)/shard_map/ppermute | solution.py:231
  59.1 30.8 %all-to-all-start.1 = ((f32[64,8,128]{2,1,0:T(8,128)}), f32[64,8,128]{2,1,0:T(8,128)S(1)}, u32[]{:S(2)}, u32[]{:S(2)}) async-start(f32[64,8,128]{2,1,0:T(8,128)} %get-tuple-element.42), calls=%async_computation.1 | async-start | bytes 524288 | tf_op jit(solution)/shard_map/all_to_all | solution.py:240
  75.1 7.2 %collective-permute-start.14 = (bf16[4,16,768]{2,1,0:T(8,128)(2,1)S(1)}, bf16[4,16,768]{2,1,0:T(8,128)(2,1)S(1)}, u32[]{:S(2)}, u32[]{:S(2)}) collective-permute-start(bf16[4,16,768]{2,1,0:T(8,128)(2,1)S(1)} %get-tuple-element.40), channel_id=1, source_target_pairs={{0,16},{16,0},{32,48},{48,32},{64,80},{80,64},{96,112},{112,96},{1... | collective-permute-start | bytes 294920 | tf_op jit(solution)/shard_map/ppermute | solution.py:224
  80.3 18.9 %copy-start = (bf16[4,8,16,128]{3,2,1,0:T(8,128)(2,1)S(1)}, bf16[4,8,16,128]{3,2,1,0:T(8,128)(2,1)}, u32[]{:S(2)}) copy-start(bf16[4,8,16,128]{3,2,1,0:T(8,128)(2,1)} %x_ref.1) | copy-start | bytes 393220
  80.3 9.7 %collective-permute-start.15 = (bf16[4,16,768]{2,1,0:T(8,128)(2,1)S(1)}, bf16[4,16,768]{2,1,0:T(8,128)(2,1)S(1)}, u32[]{:S(2)}, u32[]{:S(2)}) collective-permute-start(bf16[4,16,768]{2,1,0:T(8,128)(2,1)S(1)} %get-tuple-element.41), channel_id=1, source_target_pairs={{16,32},{48,64},{80,96},{112,128},{144,160},{176,192},{208,224},{3... | collective-permute-start | bytes 294920 | tf_op jit(solution)/shard_map/ppermute | solution.py:226
  92.2 5.3 %collective-permute-start.16 = (bf16[8,16,512]{2,1,0:T(8,128)(2,1)S(1)}, bf16[8,16,512]{2,1,0:T(8,128)(2,1)S(1)}, u32[]{:S(2)}, u32[]{:S(2)}) collective-permute-start(bf16[8,16,512]{2,1,0:T(8,128)(2,1)S(1)} %get-tuple-element.44), channel_id=1, source_target_pairs={{0,1},{1,0},{2,3},{3,2},{4,5},{5,4},{6,7},{7,6},{8,9},{9,8},{10,11... | collective-permute-start | bytes 393224 | tf_op jit(solution)/shard_map/ppermute | solution.py:235
  93.5 4.0 %collective-permute-start.17 = (bf16[8,16,512]{2,1,0:T(8,128)(2,1)S(1)}, bf16[8,16,512]{2,1,0:T(8,128)(2,1)S(1)}, u32[]{:S(2)}, u32[]{:S(2)}) collective-permute-start(bf16[8,16,512]{2,1,0:T(8,128)(2,1)S(1)} %get-tuple-element.45), channel_id=1, source_target_pairs={{0,2},{1,3},{2,0},{3,1},{4,6},{5,7},{6,4},{7,5},{8,10},{9,11},{10,... | collective-permute-start | bytes 393224 | tf_op jit(solution)/shard_map/ppermute | solution.py:235
  93.5 5.6 %collective-permute-start.18 = (bf16[8,16,512]{2,1,0:T(8,128)(2,1)S(1)}, bf16[8,16,512]{2,1,0:T(8,128)(2,1)S(1)}, u32[]{:S(2)}, u32[]{:S(2)}) collective-permute-start(bf16[8,16,512]{2,1,0:T(8,128)(2,1)S(1)} %get-tuple-element.46), channel_id=1, source_target_pairs={{0,3},{1,2},{2,1},{3,0},{4,7},{5,6},{6,5},{7,4},{8,11},{9,10},{10,... | collective-permute-start | bytes 393224 | tf_op jit(solution)/shard_map/ppermute | solution.py:235

commit v9 on v6

--- a/solution.py
+++ b/solution.py
@@ -43,7 +43,7 @@
     return lax.axis_index(ROW), lax.axis_index("zh"), lax.axis_index(NEAR)
 
 
-def put_stats(rows_ref, note_ref, stats_ref):
+def put_stats(rows_ref, note_ref):
     slabs = [rows_ref[:, :, 256 + 128 * t : 384 + 128 * t].astype(F32) for t in range(4)]
     x = jnp.concatenate(slabs, axis=0).reshape(32, 2, GROUP, 128)
     number = x.shape[0] * GROUP
@@ -52,7 +52,11 @@
     square = jnp.sum(off * off, axis=(0, 2))
     note_ref[0:2] = mean.reshape(2, 128)
     note_ref[2:4] = square
-    stats_ref[...] = jnp.broadcast_to(note_ref[...][None], stats_ref.shape)
+
+
+def spread_kernel(a_ref, b_ref, c_ref, d_ref, stats_ref):
+    for k, ref in enumerate((a_ref, b_ref, c_ref, d_ref)):
+        stats_ref[:, k] = jnp.broadcast_to(ref[...][None], (16, 8, 128))
 
 
 def fetch(pairs, sems):
@@ -65,8 +69,8 @@
 
 def begin_kernel(
     x_hbm, cache_hbm, gain_hbm, shift_hbm, w_hbm,
-    raw_ref, later_ref, stats_ref, own_ref, side_ref, far_ref,
-    x_ref, cache_ref, gain_ref, shift_ref, w_ref, note_ref, pieces_ref, sems,
+    raw_ref, later_ref, note_ref, own_ref, side_ref, far_ref,
+    x_ref, cache_ref, gain_ref, shift_ref, w_ref, pieces_ref, sems,
 ):
     fetch(
         (
@@ -99,7 +103,7 @@
     note_ref[...] = jnp.zeros((8, 128), F32)
     note_ref[4:5, 0:16] = gain_ref[0:1, :]
     note_ref[5:6, 0:16] = shift_ref[0:1, :]
-    put_stats(raw_ref, note_ref, stats_ref)
+    put_stats(raw_ref, note_ref)
 
 
 def shift_columns(left, centre, right):
@@ -111,7 +115,7 @@
 
 
 def get_affine(stats_ref, affine_ref):
-    stats = stats_ref[...].reshape(16, 4, 8, 128)
+    stats = stats_ref[...]
     number = 32 * GROUP
     means = stats[:, :, 0:2]
     mean = jnp.mean(means, axis=(0, 3), keepdims=True)
@@ -141,9 +145,9 @@
     not_bottom = (row < 15).astype(F32)
     for k, ref in enumerate((a_ref, b_ref, c_ref, d_ref)):
         b = lax.bitwise_xor(here, k)
-        mean = affine_ref[0, b]
-        gain = affine_ref[1, b]
-        shift = affine_ref[2, b]
+        mean = affine_ref[0, k]
+        gain = affine_ref[1, k]
+        shift = affine_ref[2, k]
         for r in range(10):
             for t in range(6):
                 lanes = slice(128 * t, 128 * (t + 1))
@@ -192,7 +196,7 @@
                 o_ref[r, :, lanes] = summed[q]
 
 
-def merge_kernel(a_ref, b_ref, c_ref, d_ref, bias_ref, later_ref, note1_ref, mid_ref, stats_ref, note_ref):
+def merge_kernel(a_ref, b_ref, c_ref, d_ref, bias_ref, later_ref, note1_ref, mid_ref, note_ref):
     bias = jnp.concatenate([bias_ref[...]] * 4, axis=1)
     for r in range(8):
         summed = a_ref[r].astype(F32) + b_ref[r].astype(F32)
@@ -200,7 +204,7 @@
         mid_ref[r, :, 0:256] = later_ref[r]
         mid_ref[r, :, 256:768] = (summed + bias).astype(BF16)
     note_ref[...] = note1_ref[...]
-    put_stats(mid_ref, note_ref, stats_ref)
+    put_stats(mid_ref, note_ref)
 
 
 def last_kernel(x_ref, a_ref, b_ref, c_ref, d_ref, bias_ref, o_ref):
@@ -213,6 +217,14 @@
             o_ref[t, r] = (x_ref[t, r].astype(F32) + (branch + bias)).astype(BF16)
 
 
+def near_and_stats(rows, local_stats):
+    notes = near(local_stats)
+    rows, notes = lax.optimization_barrier((rows, notes))
+    rows = near(rows)
+    stats = call(spread_kernel, struct((16, 4, 8, 128), F32), *notes)
+    return rows, exchange(stats, ROW)
+
+
 def sides(step):
     return [(i, (i + step) % 4) for i in range(4)] + [(4 + i, 4 + (i - step) % 4) for i in range(4)]
 
@@ -253,26 +265,25 @@
 
 
 def local(frames, cache, norm_gain, norm_shift, conv_weight, conv_bias):
-    note = pltpu.VMEM((8, 128), F32)
+    note = struct((8, 128), F32)
     piece = (2, 3, 3, 16, 192)
-    raw, later, stats, own, side, far = call(
+    raw, later, local_stats, own, side, far = call(
         begin_kernel,
         (
-            struct((8, 16, 768)), struct((8, 16, 256)), struct((64, 8, 128), F32), struct(piece),
+            struct((8, 16, 768)), struct((8, 16, 256)), note, struct(piece),
             struct(piece), struct(piece[1:]),
         ),
         frames, cache, norm_gain, norm_shift, conv_weight.transpose(0, 2, 1, 3),
         scratch=(
             pltpu.VMEM((4, 8, 16, 128), BF16), pltpu.VMEM((2, 2, 8, 16, 128), BF16),
             pltpu.VMEM((2, 16), F32), pltpu.VMEM((2, 16), F32), pltpu.VMEM((2, 27, 16, 256), BF16),
-            note, pltpu.VMEM((4,) + piece, BF16), pltpu.SemaphoreType.DMA((5,)),
+            pltpu.VMEM((4,) + piece, BF16), pltpu.SemaphoreType.DMA((5,)),
         ),
         far=(0, 1, 2, 3, 4),
     )
     side = lax.ppermute(side, ("core", "zh"), sides(1))
     far = lax.ppermute(far, "zh", [(i, (i + 2) % 4) for i in range(4)])
-    raw = near(raw)
-    stats = exchange(stats, ROW + NEAR)
+    raw, stats = near_and_stats(raw, local_stats)
     raw = raw + rows_beside(raw)
     swap = [(0, 1), (1, 0)]
     weights = [own, side, far, lax.ppermute(side, "core", swap), lax.ppermute(far, "core", swap)]
@@ -291,12 +302,10 @@
         scratch=scratch, flops=flops,
     )
     partial = bring(*partial)
-    middle, stats = call(
-        merge_kernel, (struct((8, 16, 768)), struct((64, 8, 128), F32)), *partial, bias[0], later, note1,
-        scratch=(note,),
-    )
-    middle = near(middle)
-    stats = exchange(stats, ROW + NEAR)
+    middle, local_stats = call(
+        merge_kernel, (struct((8, 16, 768)), note), *partial, bias[0], later, note1
+    )
+    middle, stats = near_and_stats(middle, local_stats)
     middle = middle + rows_beside(middle)
     partial = call(
         functools.partial(conv_kernel, 1), parts, *middle, stats, *weights,

time: 93.3 us -> 103 us (1.10)
  the two profiles are of different devices: /device:TPU:1 before, /device:TPU:33 now
where the time goes in v9:
time: 103 us
  starting transfers between devices  56.6 us (55%)
  waiting for transfers between devices  36.2 us (35%)
  Pallas kernels  8.96 us (9%)
    all_to_all x2, starting transfers between devices, exchange(): return lax.all_to_all(x, axes, 0, 0, tiled=True)  19.3 us
    ppermute x2, waiting for transfers between devices, bring(): far = lax.ppermute(far, 'zh', [(i, (i + 2) % 4) for i in range(4)])  16.5 us
    ppermute x12, starting transfers between devices, near(): lax.ppermute(x, NEAR, [(i, i ^ k) for i in range(4)])  10.8 us
    pallas_call x9, Pallas kernels, call(): pl.pallas_call(kernel, out_shape=outs, in_specs=specs, out_specs=jax.tree...  8.96 us
    all_to_all x2, waiting for transfers between devices, exchange(): return lax.all_to_all(x, axes, 0, 0, tiled=True)  7.77 us
    ppermute x1, starting transfers between devices, local(): side = lax.ppermute(side, ('core', 'zh'), sides(1))  5.85 us
    ppermute x2, starting transfers between devices, rows_beside(): beyond = lax.ppermute(beyond, ROW, pairs)  5.57 us
    ppermute x2, starting transfers between devices, bring(): other = lax.ppermute(other, ('core', 'zh'), sides(1))  5.05 us
  transfers between devices with their start and end apart: 28, of which 13 were waited for; matrix products, arithmetic and copies ran while one was open for 0% of the time, Pallas kernels for 1%

profile of v9, /device:TPU:33, one launch (start us, length us, event | category | flops | bytes accessed | tf_op | source)
XLA Modules:
  0.0 102.9 jit_solution(3082168565912461111)
XLA Ops:
  0.0 2.2 %shard_map.64 = (bf16[8,16,768]{2,1,0:T(8,128)(2,1)}, bf16[8,16,256]{2,1,0:T(8,128)(2,1)}, f32[8,128]{1,0:T(8,128)}, bf16[2,3,3,16,192]{4,3,2,1,0:T(8,128)(2,1)}...) custom-call(bf16[4,8,16,128]{3,2,1,0:T(8,128)(2,1)} %x_ref.1, ...), custom_call_target="tpu_custom_call" | custom-call | bytes 704768 | tf_op jit(solution)/shard_map/pallas_call | solution.py:31
  2.2 1.3 %collective-permute-start = (f32[8,128]{1,0:T(8,128)}, f32[8,128]{1,0:T(8,128)S(1)}, u32[]{:S(2)}, u32[]{:S(2)}) collective-permute-start(f32[8,128]{1,0:T(8,128)} %get-tuple-element.40.a_ref), channel_id=1, source_target_pairs={{0,1},{1,0},{2,3},{3,2},{4,5},{5,4},{6,7},{7,6},{8,9},{9,8},{10,11... | collective-permute-start | bytes 12296 | tf_op jit(solution)/shard_map/ppermute | solution.py:260
  3.5 1.4 %collective-permute-start.2 = (f32[8,128]{1,0:T(8,128)}, f32[8,128]{1,0:T(8,128)S(1)}, u32[]{:S(2)}, u32[]{:S(2)}) collective-permute-start(f32[8,128]{1,0:T(8,128)} %get-tuple-element.40.a_ref), channel_id=1, source_target_pairs={{0,3},{1,2},{2,1},{3,0},{4,7},{5,6},{6,5},{7,4},{8,11},{9,10},{10,... | collective-permute-start | bytes 12296 | tf_op jit(solution)/shard_map/ppermute | solution.py:260
  5.0 1.4 %collective-permute-done.1.c_ref = f32[8,128]{1,0:T(8,128)S(1)} collective-permute-done((f32[8,128]{1,0:T(8,128)}, f32[8,128]{1,0:T(8,128)S(1)}, u32[]{:S(2)}, u32[]{:S(2)}) %collective-permute-start.1) | collective-permute-done | bytes 4128 | tf_op jit(solution)/shard_map/ppermute | solution.py:260
  6.4 0.7 collective-permute-done.2.d_ref
  7.1 0.3 collective-permute-start.3
  7.4 1.4 %collective-permute-start.4 = (bf16[8,16,768]{2,1,0:T(8,128)(2,1)}, bf16[8,16,768]{2,1,0:T(8,128)(2,1)S(1)}, u32[]{:S(2)}, u32[]{:S(2)}) collective-permute-start(bf16[8,16,768]{2,1,0:T(8,128)(2,1)} %get-tuple-element.37.a_ref), channel_id=1, source_target_pairs={{0,2},{1,3},{2,0},{3,1},{4,6},{5,7},{6,4},{7,5},{8,10},{9,11},{10,... | collective-permute-start | bytes 589832 | tf_op jit(solution)/shard_map/ppermute | solution.py:260
  8.8 0.9 collective-permute-start.5
  9.7 5.8 %collective-permute-start.8 = (bf16[2,3,3,16,192]{4,3,2,1,0:T(8,128)(2,1)}, bf16[2,3,3,16,192]{4,3,2,1,0:T(8,128)(2,1)S(1)}, u32[]{:S(2)}, u32[]{:S(2)}) collective-permute-start(bf16[2,3,3,16,192]{4,3,2,1,0:T(8,128)(2,1)} %get-tuple-element.45), channel_id=1, source_target_pairs={{0,4},{4,8},{8,12},{12,0},{16,28},{20,16},{24,20},{28,24},{1,5},{5... | collective-permute-start | bytes 331784 | tf_op jit(solution)/shard_map/ppermute | solution.py:284
  15.6 0.9 collective-permute-start.9
  16.5 0.7 shard_map.66
  17.2 11.8 %all-to-all-start = ((f32[16,4,8,128]{3,2,1,0:T(8,128)}), f32[16,4,8,128]{3,2,1,0:T(8,128)S(1)}, u32[]{:S(2)}, u32[]{:S(2)}) async-start(f32[16,4,8,128]{3,2,1,0:T(8,128)} %shard_map.66), calls=%async_computation | async-start | bytes 524288 | tf_op jit(solution)/shard_map/all_to_all | solution.py:264
  29.0 0.2 collective-permute-start.10
  29.2 0.5 collective-permute-start.6
  29.7 3.5 %collective-permute-start.7 = (bf16[4,16,768]{2,1,0:T(8,128)(2,1)S(1)}, bf16[4,16,768]{2,1,0:T(8,128)(2,1)S(1)}, u32[]{:S(2)}, u32[]{:S(2)}) collective-permute-start(bf16[4,16,768]{2,1,0:T(8,128)(2,1)S(1)} %get-tuple-element.39), channel_id=1, source_target_pairs={{16,32},{48,64},{80,96},{112,128},{144,160},{176,192},{208,224},{3... | collective-permute-start | bytes 294920 | tf_op jit(solution)/shard_map/ppermute | solution.py:255
  33.3 0.1 collective-permute-start.11
  33.4 1.3 %collective-permute-done.11.far2_ref = bf16[3,3,16,192]{3,2,1,0:T(8,128)(2,1)S(1)} collective-permute-done((bf16[3,3,16,192]{3,2,1,0:T(8,128)(2,1)S(1)}, bf16[3,3,16,192]{3,2,1,0:T(8,128)(2,1)S(1)}, u32[]{:S(2)}, u32[]{:S(2)}) %collective-permute-start.11) | collective-permute-done | bytes 55328 | tf_op jit(solution)/shard_map/ppermute | solution.py:289
  34.6 3.1 %all-to-all-done.stats_ref = f32[16,4,8,128]{3,2,1,0:T(8,128)S(1)} async-done(((f32[16,4,8,128]{3,2,1,0:T(8,128)}), f32[16,4,8,128]{3,2,1,0:T(8,128)S(1)}, u32[]{:S(2)}, u32[]{:S(2)}) %all-to-all-start) | async-done | bytes 262176 | tf_op jit(solution)/shard_map/all_to_all | solution.py:264
  37.8 2.2 %shard_map.67 = (bf16[8,16,512]{2,1,0:T(8,128)(2,1)S(1)}, bf16[8,16,512]{2,1,0:T(8,128)(2,1)S(1)}, bf16[8,16,512]{2,1,0:T(8,128)(2,1)S(1)}, bf16[8,16,512]{2,1,0:T(8,128)(2,1)S(1)}) custom-call(bf16[8,16,768]{2,1,0:T(8,128)(2,1)S(1)} %copy-done.3, bf16[8,16,768]{2,1,0:T(8,128)(2,1)S(1)} %collective-permute-done.3.b_ref, ...), custom_call_target="tpu_custom_call" | custom-call | flops 905969664 | bytes 1687552 | tf_op jit(solution)/shard_map/pallas_call | solution.py:31
  39.9 0.1 collective-permute-start.12
  40.0 3.6 %collective-permute-start.13 = (bf16[8,16,512]{2,1,0:T(8,128)(2,1)S(1)}, bf16[8,16,512]{2,1,0:T(8,128)(2,1)S(1)}, u32[]{:S(2)}, u32[]{:S(2)}) collective-permute-start(bf16[8,16,512]{2,1,0:T(8,128)(2,1)S(1)} %get-tuple-element.49), channel_id=1, source_target_pairs={{0,4},{4,8},{8,12},{12,0},{16,28},{20,16},{24,20},{28,24},{1,5},{5... | collective-permute-start | bytes 393224 | tf_op jit(solution)/shard_map/ppermute | solution.py:235
  43.6 0.9 collective-permute-start.14
  44.5 0.7 copy-done.6
  45.2 3.9 %collective-permute-done.12.b_ref = bf16[8,16,512]{2,1,0:T(8,128)(2,1)S(1)} collective-permute-done((bf16[8,16,512]{2,1,0:T(8,128)(2,1)S(1)}, bf16[8,16,512]{2,1,0:T(8,128)(2,1)S(1)}, u32[]{:S(2)}, u32[]{:S(2)}) %collective-permute-start.12) | collective-permute-done | bytes 131104 | tf_op jit(solution)/shard_map/ppermute | solution.py:234
  49.1 1.1 %collective-permute-done.13.c_ref = bf16[8,16,512]{2,1,0:T(8,128)(2,1)S(1)} collective-permute-done((bf16[8,16,512]{2,1,0:T(8,128)(2,1)S(1)}, bf16[8,16,512]{2,1,0:T(8,128)(2,1)S(1)}, u32[]{:S(2)}, u32[]{:S(2)}) %collective-permute-start.13) | collective-permute-done | bytes 131104 | tf_op jit(solution)/shard_map/ppermute | solution.py:235
  50.3 6.9 %collective-permute-done.14.d_ref = bf16[8,16,512]{2,1,0:T(8,128)(2,1)S(1)} collective-permute-done((bf16[8,16,512]{2,1,0:T(8,128)(2,1)S(1)}, bf16[8,16,512]{2,1,0:T(8,128)(2,1)S(1)}, u32[]{:S(2)}, u32[]{:S(2)}) %collective-permute-start.14) | collective-permute-done | bytes 131104 | tf_op jit(solution)/shard_map/ppermute | solution.py:233
  57.3 0.2 shard_map.68
  57.5 0.1 collective-permute-start.15
  57.6 0.3 collective-permute-start.16
  57.8 2.4 %collective-permute-start.17 = (f32[8,128]{1,0:T(8,128)S(1)}, f32[8,128]{1,0:T(8,128)S(1)}, u32[]{:S(2)}, u32[]{:S(2)}) collective-permute-start(f32[8,128]{1,0:T(8,128)S(1)} %get-tuple-element.57.a_ref), channel_id=1, source_target_pairs={{0,3},{1,2},{2,1},{3,0},{4,7},{5,6},{6,5},{7,4},{8,11},{9,10},{10,... | collective-permute-start | bytes 12296 | tf_op jit(solution)/shard_map/ppermute | solution.py:260
  60.2 0.1 collective-permute-done.16.c_ref
  60.3 1.0 collective-permute-done.17.d_ref
  61.3 1.1 %collective-permute-start.18 = (bf16[8,16,768]{2,1,0:T(8,128)(2,1)S(1)}, bf16[8,16,768]{2,1,0:T(8,128)(2,1)S(1)}, u32[]{:S(2)}, u32[]{:S(2)}) collective-permute-start(bf16[8,16,768]{2,1,0:T(8,128)(2,1)S(1)} %get-tuple-element.54.a_ref), channel_id=1, source_target_pairs={{0,1},{1,0},{2,3},{3,2},{4,5},{5,4},{6,7},{7,6},{8,9},{9,8},{10,11... | collective-permute-start | bytes 589832 | tf_op jit(solution)/shard_map/ppermute | solution.py:260
  62.4 1.5 %collective-permute-start.19 = (bf16[8,16,768]{2,1,0:T(8,128)(2,1)S(1)}, bf16[8,16,768]{2,1,0:T(8,128)(2,1)S(1)}, u32[]{:S(2)}, u32[]{:S(2)}) collective-permute-start(bf16[8,16,768]{2,1,0:T(8,128)(2,1)S(1)} %get-tuple-element.54.a_ref), channel_id=1, source_target_pairs={{0,2},{1,3},{2,0},{3,1},{4,6},{5,7},{6,4},{7,5},{8,10},{9,11},{10,... | collective-permute-start | bytes 589832 | tf_op jit(solution)/shard_map/ppermute | solution.py:260
  63.8 0.1 collective-permute-start.20
  63.9 0.7 shard_map.70
  64.6 7.6 %all-to-all-start.1 = ((f32[16,4,8,128]{3,2,1,0:T(8,128)}), f32[16,4,8,128]{3,2,1,0:T(8,128)S(1)}, u32[]{:S(2)}, u32[]{:S(2)}) async-start(f32[16,4,8,128]{3,2,1,0:T(8,128)} %shard_map.70), calls=%async_computation.1 | async-start | bytes 524288 | tf_op jit(solution)/shard_map/all_to_all | solution.py:264
  72.3 2.0 %collective-permute-start.21 = (bf16[4,16,768]{2,1,0:T(8,128)(2,1)S(1)}, bf16[4,16,768]{2,1,0:T(8,128)(2,1)S(1)}, u32[]{:S(2)}, u32[]{:S(2)}) collective-permute-start(bf16[4,16,768]{2,1,0:T(8,128)(2,1)S(1)} %get-tuple-element.55), channel_id=1, source_target_pairs={{0,16},{16,0},{32,48},{48,32},{64,80},{80,64},{96,112},{112,96},{1... | collective-permute-start | bytes 294920 | tf_op jit(solution)/shard_map/ppermute | solution.py:253
  74.3 2.0 %collective-permute-start.22 = (bf16[4,16,768]{2,1,0:T(8,128)(2,1)S(1)}, bf16[4,16,768]{2,1,0:T(8,128)(2,1)S(1)}, u32[]{:S(2)}, u32[]{:S(2)}) collective-permute-start(bf16[4,16,768]{2,1,0:T(8,128)(2,1)S(1)} %get-tuple-element.56), channel_id=1, source_target_pairs={{16,32},{48,64},{80,96},{112,128},{144,160},{176,192},{208,224},{3... | collective-permute-start | bytes 294920 | tf_op jit(solution)/shard_map/ppermute | solution.py:255
  76.3 4.7 %all-to-all-done.1.stats_ref = f32[16,4,8,128]{3,2,1,0:T(8,128)S(1)} async-done(((f32[16,4,8,128]{3,2,1,0:T(8,128)}), f32[16,4,8,128]{3,2,1,0:T(8,128)S(1)}, u32[]{:S(2)}, u32[]{:S(2)}) %all-to-all-start.1) | async-done | bytes 262176 | tf_op jit(solution)/shard_map/all_to_all | solution.py:264
  81.0 2.2 %shard_map.71 = (bf16[8,16,512]{2,1,0:T(8,128)(2,1)S(1)}, bf16[8,16,512]{2,1,0:T(8,128)(2,1)S(1)}, bf16[8,16,512]{2,1,0:T(8,128)(2,1)S(1)}, bf16[8,16,512]{2,1,0:T(8,128)(2,1)S(1)}) custom-call(bf16[8,16,768]{2,1,0:T(8,128)(2,1)S(1)} %get-tuple-element.54.a_ref, bf16[8,16,768]{2,1,0:T(8,128)(2,1)S(1)} %collective-permute-done.18.b_ref, ...), custom_call_target="tpu_custom_call" | custom-call | flops 905969664 | bytes 1687552 | tf_op jit(solution)/shard_map/pallas_call | solution.py:31
  83.2 2.2 %collective-permute-start.23 = (bf16[8,16,512]{2,1,0:T(8,128)(2,1)S(1)}, bf16[8,16,512]{2,1,0:T(8,128)(2,1)S(1)}, u32[]{:S(2)}, u32[]{:S(2)}) collective-permute-start(bf16[8,16,512]{2,1,0:T(8,128)(2,1)S(1)} %get-tuple-element.62), channel_id=1, source_target_pairs={{0,12},{4,0},{8,4},{12,8},{16,20},{20,24},{24,28},{28,16},{1,13},{... | collective-permute-start | bytes 393224 | tf_op jit(solution)/shard_map/ppermute | solution.py:234
  85.3 1.5 %collective-permute-start.24 = (bf16[8,16,512]{2,1,0:T(8,128)(2,1)S(1)}, bf16[8,16,512]{2,1,0:T(8,128)(2,1)S(1)}, u32[]{:S(2)}, u32[]{:S(2)}) collective-permute-start(bf16[8,16,512]{2,1,0:T(8,128)(2,1)S(1)} %get-tuple-element.63), channel_id=1, source_target_pairs={{0,4},{4,8},{8,12},{12,0},{16,28},{20,16},{24,20},{28,24},{1,5},{5... | collective-permute-start | bytes 393224 | tf_op jit(solution)/shard_map/ppermute | solution.py:235
  86.8 3.3 %collective-permute-start.25 = (bf16[8,16,512]{2,1,0:T(8,128)(2,1)S(1)}, bf16[8,16,512]{2,1,0:T(8,128)(2,1)S(1)}, u32[]{:S(2)}, u32[]{:S(2)}) collective-permute-start(bf16[8,16,512]{2,1,0:T(8,128)(2,1)S(1)} %get-tuple-element.64), channel_id=1, source_target_pairs={{0,8},{4,12},{8,0},{12,4},{1,9},{5,13},{9,1},{13,5},{2,10},{6,14},... | collective-permute-start | bytes 393224 | tf_op jit(solution)/shard_map/ppermute | solution.py:233
  90.1 0.5 collective-permute-done.23.b_ref
  90.7 1.8 %collective-permute-done.24.c_ref = bf16[8,16,512]{2,1,0:T(8,128)(2,1)S(1)} collective-permute-done((bf16[8,16,512]{2,1,0:T(8,128)(2,1)S(1)}, bf16[8,16,512]{2,1,0:T(8,128)(2,1)S(1)}, u32[]{:S(2)}, u32[]{:S(2)}) %collective-permute-start.24) | collective-permute-done | bytes 131104 | tf_op jit(solution)/shard_map/ppermute | solution.py:235
  92.5 9.6 %collective-permute-done.25.d_ref = bf16[8,16,512]{2,1,0:T(8,128)(2,1)S(1)} collective-permute-done((bf16[8,16,512]{2,1,0:T(8,128)(2,1)S(1)}, bf16[8,16,512]{2,1,0:T(8,128)(2,1)S(1)}, u32[]{:S(2)}, u32[]{:S(2)}) %collective-permute-start.25) | collective-permute-done | bytes 131104 | tf_op jit(solution)/shard_map/ppermute | solution.py:233
  102.1 0.8 shard_map.72
  (39 shorter events, 0.3 us)
Async XLA Ops:
  2.2 14.3 %copy-start.2 = (f32[8,128]{1,0:T(8,128)S(1)}, f32[8,128]{1,0:T(8,128)}, u32[]{:S(2)}) copy-start(f32[8,128]{1,0:T(8,128)} %get-tuple-element.40.a_ref) | copy-start | bytes 12292
  2.2 2.8 %collective-permute-start = (f32[8,128]{1,0:T(8,128)}, f32[8,128]{1,0:T(8,128)S(1)}, u32[]{:S(2)}, u32[]{:S(2)}) collective-permute-start(f32[8,128]{1,0:T(8,128)} %get-tuple-element.40.a_ref), channel_id=1, source_target_pairs={{0,1},{1,0},{2,3},{3,2},{4,5},{5,4},{6,7},{7,6},{8,9},{9,8},{10,11... | collective-permute-start | bytes 12296 | tf_op jit(solution)/shard_map/ppermute | solution.py:260
  3.5 2.9 %collective-permute-start.1 = (f32[8,128]{1,0:T(8,128)}, f32[8,128]{1,0:T(8,128)S(1)}, u32[]{:S(2)}, u32[]{:S(2)}) collective-permute-start(f32[8,128]{1,0:T(8,128)} %get-tuple-element.40.a_ref), channel_id=1, source_target_pairs={{0,2},{1,3},{2,0},{3,1},{4,6},{5,7},{6,4},{7,5},{8,10},{9,11},{10,... | collective-permute-start | bytes 12296 | tf_op jit(solution)/shard_map/ppermute | solution.py:260
  3.5 3.6 %collective-permute-start.2 = (f32[8,128]{1,0:T(8,128)}, f32[8,128]{1,0:T(8,128)S(1)}, u32[]{:S(2)}, u32[]{:S(2)}) collective-permute-start(f32[8,128]{1,0:T(8,128)} %get-tuple-element.40.a_ref), channel_id=1, source_target_pairs={{0,3},{1,2},{2,1},{3,0},{4,7},{5,6},{6,5},{7,4},{8,11},{9,10},{10,... | collective-permute-start | bytes 12296 | tf_op jit(solution)/shard_map/ppermute | solution.py:260
  7.1 22.1 %collective-permute-start.3 = (bf16[8,16,768]{2,1,0:T(8,128)(2,1)}, bf16[8,16,768]{2,1,0:T(8,128)(2,1)S(1)}, u32[]{:S(2)}, u32[]{:S(2)}) collective-permute-start(bf16[8,16,768]{2,1,0:T(8,128)(2,1)} %get-tuple-element.37.a_ref), channel_id=1, source_target_pairs={{0,1},{1,0},{2,3},{3,2},{4,5},{5,4},{6,7},{7,6},{8,9},{9,8},{10,11... | collective-permute-start | bytes 589832 | tf_op jit(solution)/shard_map/ppermute | solution.py:260
  7.4 21.8 %collective-permute-start.4 = (bf16[8,16,768]{2,1,0:T(8,128)(2,1)}, bf16[8,16,768]{2,1,0:T(8,128)(2,1)S(1)}, u32[]{:S(2)}, u32[]{:S(2)}) collective-permute-start(bf16[8,16,768]{2,1,0:T(8,128)(2,1)} %get-tuple-element.37.a_ref), channel_id=1, source_target_pairs={{0,2},{1,3},{2,0},{3,1},{4,6},{5,7},{6,4},{7,5},{8,10},{9,11},{10,... | collective-permute-start | bytes 589832 | tf_op jit(solution)/shard_map/ppermute | solution.py:260
  8.8 20.4 %collective-permute-start.5 = (bf16[8,16,768]{2,1,0:T(8,128)(2,1)}, bf16[8,16,768]{2,1,0:T(8,128)(2,1)S(1)}, u32[]{:S(2)}, u32[]{:S(2)}) collective-permute-start(bf16[8,16,768]{2,1,0:T(8,128)(2,1)} %get-tuple-element.37.a_ref), channel_id=1, source_target_pairs={{0,3},{1,2},{2,1},{3,0},{4,7},{5,6},{6,5},{7,4},{8,11},{9,10},{10,... | collective-permute-start | bytes 589832 | tf_op jit(solution)/shard_map/ppermute | solution.py:260
  9.7 19.2 %collective-permute-start.8 = (bf16[2,3,3,16,192]{4,3,2,1,0:T(8,128)(2,1)}, bf16[2,3,3,16,192]{4,3,2,1,0:T(8,128)(2,1)S(1)}, u32[]{:S(2)}, u32[]{:S(2)}) collective-permute-start(bf16[2,3,3,16,192]{4,3,2,1,0:T(8,128)(2,1)} %get-tuple-element.45), channel_id=1, source_target_pairs={{0,4},{4,8},{8,12},{12,0},{16,28},{20,16},{24,20},{28,24},{1,5},{5... | collective-permute-start | bytes 331784 | tf_op jit(solution)/shard_map/ppermute | solution.py:284
  15.6 17.7 %collective-permute-start.9 = (bf16[3,3,16,192]{3,2,1,0:T(8,128)(2,1)}, bf16[3,3,16,192]{3,2,1,0:T(8,128)(2,1)S(1)}, u32[]{:S(2)}, u32[]{:S(2)}) collective-permute-start(bf16[3,3,16,192]{3,2,1,0:T(8,128)(2,1)} %get-tuple-element.46), channel_id=1, source_target_pairs={{0,8},{4,12},{8,0},{12,4},{1,9},{5,13},{9,1},{13,5},{2,10},{6,14},... | collective-permute-start | bytes 165896 | tf_op jit(solution)/shard_map/ppermute | solution.py:285
  17.2 12.0 %copy-start.3 = (bf16[8,16,768]{2,1,0:T(8,128)(2,1)S(1)}, bf16[8,16,768]{2,1,0:T(8,128)(2,1)}, u32[]{:S(2)}) copy-start(bf16[8,16,768]{2,1,0:T(8,128)(2,1)} %get-tuple-element.37.a_ref) | copy-start | bytes 589828
  17.2 20.5 %all-to-all-start = ((f32[16,4,8,128]{3,2,1,0:T(8,128)}), f32[16,4,8,128]{3,2,1,0:T(8,128)S(1)}, u32[]{:S(2)}, u32[]{:S(2)}) async-start(f32[16,4,8,128]{3,2,1,0:T(8,128)} %shard_map.66), calls=%async_computation | async-start | bytes 524288 | tf_op jit(solution)/shard_map/all_to_all | solution.py:264
  29.0 8.8 %copy-start.4 = (bf16[2,3,3,16,192]{4,3,2,1,0:T(8,128)(2,1)S(1)}, bf16[2,3,3,16,192]{4,3,2,1,0:T(8,128)(2,1)}, u32[]{:S(2)}) copy-start(bf16[2,3,3,16,192]{4,3,2,1,0:T(8,128)(2,1)} %get-tuple-element.44.own_ref) | copy-start | bytes 331780
  29.0 5.7 %collective-permute-start.10 = (bf16[2,3,3,16,192]{4,3,2,1,0:T(8,128)(2,1)S(1)}, bf16[2,3,3,16,192]{4,3,2,1,0:T(8,128)(2,1)S(1)}, u32[]{:S(2)}, u32[]{:S(2)}) collective-permute-start(bf16[2,3,3,16,192]{4,3,2,1,0:T(8,128)(2,1)S(1)} %collective-permute-done.8.side_ref), channel_id=1, source_target_pairs={{0,16},{16,0},{1,17},{17,1},{2,18},{18,2},{3,19},{19,3},{4,20},{20... | collective-permute-start | bytes 331784 | tf_op jit(solution)/shard_map/ppermute | solution.py:289
  29.2 8.5 %collective-permute-start.6 = (bf16[4,16,768]{2,1,0:T(8,128)(2,1)S(1)}, bf16[4,16,768]{2,1,0:T(8,128)(2,1)S(1)}, u32[]{:S(2)}, u32[]{:S(2)}) collective-permute-start(bf16[4,16,768]{2,1,0:T(8,128)(2,1)S(1)} %get-tuple-element.38), channel_id=1, source_target_pairs={{0,16},{16,0},{32,48},{48,32},{64,80},{80,64},{96,112},{112,96},{1... | collective-permute-start | bytes 294920 | tf_op jit(solution)/shard_map/ppermute | solution.py:253
  29.7 8.0 %collective-permute-start.7 = (bf16[4,16,768]{2,1,0:T(8,128)(2,1)S(1)}, bf16[4,16,768]{2,1,0:T(8,128)(2,1)S(1)}, u32[]{:S(2)}, u32[]{:S(2)}) collective-permute-start(bf16[4,16,768]{2,1,0:T(8,128)(2,1)S(1)} %get-tuple-element.39), channel_id=1, source_target_pairs={{16,32},{48,64},{80,96},{112,128},{144,160},{176,192},{208,224},{3... | collective-permute-start | bytes 294920 | tf_op jit(solution)/shard_map/ppermute | solution.py:255
  33.3 1.4 %collective-permute-start.11 = (bf16[3,3,16,192]{3,2,1,0:T(8,128)(2,1)S(1)}, bf16[3,3,16,192]{3,2,1,0:T(8,128)(2,1)S(1)}, u32[]{:S(2)}, u32[]{:S(2)}) collective-permute-start(bf16[3,3,16,192]{3,2,1,0:T(8,128)(2,1)S(1)} %collective-permute-done.9.far_ref), channel_id=1, source_target_pairs={{0,16},{16,0},{1,17},{17,1},{2,18},{18,2},{3,19},{19,3},{4,20},{20... | collective-permute-start | bytes 165896 | tf_op jit(solution)/shard_map/ppermute | solution.py:289
  37.7 19.6 %copy-start.1 = (bf16[8,16,256]{2,1,0:T(8,128)(2,1)S(1)}, bf16[8,16,256]{2,1,0:T(8,128)(2,1)}, u32[]{:S(2)}) copy-start(bf16[8,16,256]{2,1,0:T(8,128)(2,1)} %get-tuple-element.51.later_ref) | copy-start | bytes 196612
  39.9 9.2 %collective-permute-start.12 = (bf16[8,16,512]{2,1,0:T(8,128)(2,1)S(1)}, bf16[8,16,512]{2,1,0:T(8,128)(2,1)S(1)}, u32[]{:S(2)}, u32[]{:S(2)}) collective-permute-start(bf16[8,16,512]{2,1,0:T(8,128)(2,1)S(1)} %get-tuple-element.48), channel_id=1, source_target_pairs={{0,12},{4,0},{8,4},{12,8},{16,20},{20,24},{24,28},{28,16},{1,13},{... | collective-permute-start | bytes 393224 | tf_op jit(solution)/shard_map/ppermute | solution.py:234
  40.0 4.5 %copy-start.7 = (f32[2,16]{1,0:T(2,128)S(1)}, f32[2,16]{1,0:T(2,128)}, u32[]{:S(2)}) copy-start(f32[2,16]{1,0:T(2,128)} %param.11) | copy-start | bytes 388
  40.0 10.2 %collective-permute-start.13 = (bf16[8,16,512]{2,1,0:T(8,128)(2,1)S(1)}, bf16[8,16,512]{2,1,0:T(8,128)(2,1)S(1)}, u32[]{:S(2)}, u32[]{:S(2)}) collective-permute-start(bf16[8,16,512]{2,1,0:T(8,128)(2,1)S(1)} %get-tuple-element.49), channel_id=1, source_target_pairs={{0,4},{4,8},{8,12},{12,0},{16,28},{20,16},{24,20},{28,24},{1,5},{5... | collective-permute-start | bytes 393224 | tf_op jit(solution)/shard_map/ppermute | solution.py:235
  43.6 0.9 copy-start.5
  43.6 13.6 %collective-permute-start.14 = (bf16[8,16,512]{2,1,0:T(8,128)(2,1)S(1)}, bf16[8,16,512]{2,1,0:T(8,128)(2,1)S(1)}, u32[]{:S(2)}, u32[]{:S(2)}) collective-permute-start(bf16[8,16,512]{2,1,0:T(8,128)(2,1)S(1)} %get-tuple-element.50), channel_id=1, source_target_pairs={{0,8},{4,12},{8,0},{12,4},{1,9},{5,13},{9,1},{13,5},{2,10},{6,14},... | collective-permute-start | bytes 393224 | tf_op jit(solution)/shard_map/ppermute | solution.py:233
  44.5 0.7 copy-start.6
  57.5 2.7 %collective-permute-start.15 = (f32[8,128]{1,0:T(8,128)S(1)}, f32[8,128]{1,0:T(8,128)S(1)}, u32[]{:S(2)}, u32[]{:S(2)}) collective-permute-start(f32[8,128]{1,0:T(8,128)S(1)} %get-tuple-element.57.a_ref), channel_id=1, source_target_pairs={{0,1},{1,0},{2,3},{3,2},{4,5},{5,4},{6,7},{7,6},{8,9},{9,8},{10,11... | collective-permute-start | bytes 12296 | tf_op jit(solution)/shard_map/ppermute | solution.py:260
  57.6 2.7 %collective-permute-start.16 = (f32[8,128]{1,0:T(8,128)S(1)}, f32[8,128]{1,0:T(8,128)S(1)}, u32[]{:S(2)}, u32[]{:S(2)}) collective-permute-start(f32[8,128]{1,0:T(8,128)S(1)} %get-tuple-element.57.a_ref), channel_id=1, source_target_pairs={{0,2},{1,3},{2,0},{3,1},{4,6},{5,7},{6,4},{7,5},{8,10},{9,11},{10,... | collective-permute-start | bytes 12296 | tf_op jit(solution)/shard_map/ppermute | solution.py:260
  57.8 3.4 %collective-permute-start.17 = (f32[8,128]{1,0:T(8,128)S(1)}, f32[8,128]{1,0:T(8,128)S(1)}, u32[]{:S(2)}, u32[]{:S(2)}) collective-permute-start(f32[8,128]{1,0:T(8,128)S(1)} %get-tuple-element.57.a_ref), channel_id=1, source_target_pairs={{0,3},{1,2},{2,1},{3,0},{4,7},{5,6},{6,5},{7,4},{8,11},{9,10},{10,... | collective-permute-start | bytes 12296 | tf_op jit(solution)/shard_map/ppermute | solution.py:260
  61.3 10.9 %collective-permute-start.18 = (bf16[8,16,768]{2,1,0:T(8,128)(2,1)S(1)}, bf16[8,16,768]{2,1,0:T(8,128)(2,1)S(1)}, u32[]{:S(2)}, u32[]{:S(2)}) collective-permute-start(bf16[8,16,768]{2,1,0:T(8,128)(2,1)S(1)} %get-tuple-element.54.a_ref), channel_id=1, source_target_pairs={{0,1},{1,0},{2,3},{3,2},{4,5},{5,4},{6,7},{7,6},{8,9},{9,8},{10,11... | collective-permute-start | bytes 589832 | tf_op jit(solution)/shard_map/ppermute | solution.py:260
  62.4 9.8 %collective-permute-start.19 = (bf16[8,16,768]{2,1,0:T(8,128)(2,1)S(1)}, bf16[8,16,768]{2,1,0:T(8,128)(2,1)S(1)}, u32[]{:S(2)}, u32[]{:S(2)}) collective-permute-start(bf16[8,16,768]{2,1,0:T(8,128)(2,1)S(1)} %get-tuple-element.54.a_ref), channel_id=1, source_target_pairs={{0,2},{1,3},{2,0},{3,1},{4,6},{5,7},{6,4},{7,5},{8,10},{9,11},{10,... | collective-permute-start | bytes 589832 | tf_op jit(solution)/shard_map/ppermute | solution.py:260
  63.8 8.4 %collective-permute-start.20 = (bf16[8,16,768]{2,1,0:T(8,128)(2,1)S(1)}, bf16[8,16,768]{2,1,0:T(8,128)(2,1)S(1)}, u32[]{:S(2)}, u32[]{:S(2)}) collective-permute-start(bf16[8,16,768]{2,1,0:T(8,128)(2,1)S(1)} %get-tuple-element.54.a_ref), channel_id=1, source_target_pairs={{0,3},{1,2},{2,1},{3,0},{4,7},{5,6},{6,5},{7,4},{8,11},{9,10},{10,... | collective-permute-start | bytes 589832 | tf_op jit(solution)/shard_map/ppermute | solution.py:260
  64.6 16.3 %all-to-all-start.1 = ((f32[16,4,8,128]{3,2,1,0:T(8,128)}), f32[16,4,8,128]{3,2,1,0:T(8,128)S(1)}, u32[]{:S(2)}, u32[]{:S(2)}) async-start(f32[16,4,8,128]{3,2,1,0:T(8,128)} %shard_map.70), calls=%async_computation.1 | async-start | bytes 524288 | tf_op jit(solution)/shard_map/all_to_all | solution.py:264
  72.3 8.7 %collective-permute-start.21 = (bf16[4,16,768]{2,1,0:T(8,128)(2,1)S(1)}, bf16[4,16,768]{2,1,0:T(8,128)(2,1)S(1)}, u32[]{:S(2)}, u32[]{:S(2)}) collective-permute-start(bf16[4,16,768]{2,1,0:T(8,128)(2,1)S(1)} %get-tuple-element.55), channel_id=1, source_target_pairs={{0,16},{16,0},{32,48},{48,32},{64,80},{80,64},{96,112},{112,96},{1... | collective-permute-start | bytes 294920 | tf_op jit(solution)/shard_map/ppermute | solution.py:253
  74.3 27.9 %copy-start = (bf16[4,8,16,128]{3,2,1,0:T(8,128)(2,1)S(1)}, bf16[4,8,16,128]{3,2,1,0:T(8,128)(2,1)}, u32[]{:S(2)}) copy-start(bf16[4,8,16,128]{3,2,1,0:T(8,128)(2,1)} %x_ref.1) | copy-start | bytes 393220
  74.3 6.7 %collective-permute-start.22 = (bf16[4,16,768]{2,1,0:T(8,128)(2,1)S(1)}, bf16[4,16,768]{2,1,0:T(8,128)(2,1)S(1)}, u32[]{:S(2)}, u32[]{:S(2)}) collective-permute-start(bf16[4,16,768]{2,1,0:T(8,128)(2,1)S(1)} %get-tuple-element.56), channel_id=1, source_target_pairs={{16,32},{48,64},{80,96},{112,128},{144,160},{176,192},{208,224},{3... | collective-permute-start | bytes 294920 | tf_op jit(solution)/shard_map/ppermute | solution.py:255
  83.2 7.5 %collective-permute-start.23 = (bf16[8,16,512]{2,1,0:T(8,128)(2,1)S(1)}, bf16[8,16,512]{2,1,0:T(8,128)(2,1)S(1)}, u32[]{:S(2)}, u32[]{:S(2)}) collective-permute-start(bf16[8,16,512]{2,1,0:T(8,128)(2,1)S(1)} %get-tuple-element.62), channel_id=1, source_target_pairs={{0,12},{4,0},{8,4},{12,8},{16,20},{20,24},{24,28},{28,16},{1,13},{... | collective-permute-start | bytes 393224 | tf_op jit(solution)/shard_map/ppermute | solution.py:234
  85.3 7.2 %collective-permute-start.24 = (bf16[8,16,512]{2,1,0:T(8,128)(2,1)S(1)}, bf16[8,16,512]{2,1,0:T(8,128)(2,1)S(1)}, u32[]{:S(2)}, u32[]{:S(2)}) collective-permute-start(bf16[8,16,512]{2,1,0:T(8,128)(2,1)S(1)} %get-tuple-element.63), channel_id=1, source_target_pairs={{0,4},{4,8},{8,12},{12,0},{16,28},{20,16},{24,20},{28,24},{1,5},{5... | collective-permute-start | bytes 393224 | tf_op jit(solution)/shard_map/ppermute | solution.py:235
  86.8 15.2 %collective-permute-start.25 = (bf16[8,16,512]{2,1,0:T(8,128)(2,1)S(1)}, bf16[8,16,512]{2,1,0:T(8,128)(2,1)S(1)}, u32[]{:S(2)}, u32[]{:S(2)}) collective-permute-start(bf16[8,16,512]{2,1,0:T(8,128)(2,1)S(1)} %get-tuple-element.64), channel_id=1, source_target_pairs={{0,8},{4,12},{8,0},{12,4},{1,9},{5,13},{9,1},{13,5},{2,10},{6,14},... | collective-permute-start | bytes 393224 | tf_op jit(solution)/shard_map/ppermute | solution.py:233

commit v10 on v6

--- a/solution.py
+++ b/solution.py
@@ -192,24 +192,23 @@
                 o_ref[r, :, lanes] = summed[q]
 
 
-def merge_kernel(a_ref, b_ref, c_ref, d_ref, bias_ref, later_ref, note1_ref, mid_ref, stats_ref, note_ref):
+def merge_kernel(a_ref, b_ref, c_ref, bias_ref, later_ref, note1_ref, mid_ref, stats_ref, note_ref):
     bias = jnp.concatenate([bias_ref[...]] * 4, axis=1)
     for r in range(8):
-        summed = a_ref[r].astype(F32) + b_ref[r].astype(F32)
-        summed += c_ref[r].astype(F32) + d_ref[r].astype(F32)
+        summed = a_ref[r].astype(F32) + b_ref[r].astype(F32) + c_ref[r].astype(F32)
         mid_ref[r, :, 0:256] = later_ref[r]
         mid_ref[r, :, 256:768] = (summed + bias).astype(BF16)
     note_ref[...] = note1_ref[...]
     put_stats(mid_ref, note_ref, stats_ref)
 
 
-def last_kernel(x_ref, a_ref, b_ref, c_ref, d_ref, bias_ref, o_ref):
+def last_kernel(x_ref, a_ref, b_ref, c_ref, bias_ref, o_ref):
     bias = bias_ref[...]
     for r in range(8):
         for t in range(4):
             lanes = slice(128 * t, 128 * (t + 1))
             branch = a_ref[r, :, lanes].astype(F32) + b_ref[r, :, lanes].astype(F32)
-            branch += c_ref[r, :, lanes].astype(F32) + d_ref[r, :, lanes].astype(F32)
+            branch += c_ref[r, :, lanes].astype(F32)
             o_ref[t, r] = (x_ref[t, r].astype(F32) + (branch + bias)).astype(BF16)
 
 
@@ -217,11 +216,16 @@
     return [(i, (i + step) % 4) for i in range(4)] + [(4 + i, 4 + (i - step) % 4) for i in range(4)]
 
 
+def add_kernel(a_ref, b_ref, o_ref):
+    o_ref[...] = (a_ref[...].astype(F32) + b_ref[...].astype(F32)).astype(BF16)
+
+
 def bring(own, side, other, far):
-    far = lax.ppermute(far, "zh", [(i, (i + 2) % 4) for i in range(4)])
+    far = lax.ppermute(far, ("core", "zh"), sides(-1))
+    other = lax.ppermute(other, ("core", "zh"), sides(1))
+    side = call(add_kernel, struct(side.shape), side, far)
     side = lax.ppermute(side, ("core", "zh"), sides(-1))
-    other = lax.ppermute(other, ("core", "zh"), sides(1))
-    return [own, side, other, far]
+    return [own, other, side]
 
 
 def struct(shape, dtype=BF16):

time: 93.3 us -> 94.2 us (level)
  the two profiles are of different devices: /device:TPU:1 before, /device:TPU:27 now
where the time goes in v10:
time: 94.2 us; the launch traced here: 93.9 us
  starting transfers between devices  48.7 us (52%)
  waiting for transfers between devices  35 us (37%)
  Pallas kernels  8.49 us (9%)
  local copies, waits for them, and re-layouts  1.45 us (2%)
    all_to_all x2, starting transfers between devices, exchange(): return lax.all_to_all(x, axes, 0, 0, tiled=True)  18.2 us
    ppermute x2, waiting for transfers between devices, bring(): side = lax.ppermute(side, ('core', 'zh'), sides(-1))  12 us
    ppermute x2, waiting for transfers between devices, bring(): far = lax.ppermute(far, ('core', 'zh'), sides(-1))  11.9 us
    ppermute x2, waiting for transfers between devices, rows_beside(): beyond = lax.ppermute(beyond, ROW, pairs)  9.83 us
    pallas_call x9, Pallas kernels, call(): pl.pallas_call(kernel, out_shape=outs, in_specs=specs, out_specs=jax.tree...  8.49 us
    ppermute x2, starting transfers between devices, rows_beside(): beyond = lax.ppermute(beyond, ROW, pairs)  7.86 us
    ppermute x6, starting transfers between devices, near(): lax.ppermute(x, NEAR, [(i, i ^ k) for i in range(4)])  6.58 us
    ppermute x1, starting transfers between devices, local(): side = lax.ppermute(side, ('core', 'zh'), sides(1))  5.85 us
  transfers between devices with their start and end apart: 22, of which 7 were waited for; matrix products, arithmetic and copies ran while one was open for 0% of the time, Pallas kernels for 0%

profile of v10, /device:TPU:27, one launch (start us, length us, event | category | flops | bytes accessed | tf_op | source)
XLA Modules:
  0.0 93.9 jit_solution(216319985657726202)
XLA Ops:
  0.0 2.3 %shard_map.64 = (bf16[8,16,768]{2,1,0:T(8,128)(2,1)}, bf16[8,16,256]{2,1,0:T(8,128)(2,1)}, f32[64,8,128]{2,1,0:T(8,128)}, bf16[2,3,3,16,192]{4,3,2,1,0:T(8,128)(...) custom-call(bf16[4,8,16,128]{3,2,1,0:T(8,128)(2,1)} %x_ref.1, ...), custom_call_target="tpu_custom_call" | custom-call | bytes 704768 | tf_op jit(solution)/shard_map/pallas_call | solution.py:31
  2.3 0.3 collective-permute-start
  2.6 1.6 %collective-permute-start.1 = (bf16[8,16,768]{2,1,0:T(8,128)(2,1)}, bf16[8,16,768]{2,1,0:T(8,128)(2,1)S(1)}, u32[]{:S(2)}, u32[]{:S(2)}) collective-permute-start(bf16[8,16,768]{2,1,0:T(8,128)(2,1)} %get-tuple-element.25.a_ref), channel_id=1, source_target_pairs={{0,2},{1,3},{2,0},{3,1},{4,6},{5,7},{6,4},{7,5},{8,10},{9,11},{10,... | collective-permute-start | bytes 589832 | tf_op jit(solution)/shard_map/ppermute | solution.py:252
  4.3 0.9 collective-permute-start.2
  5.2 5.8 %collective-permute-start.5 = (bf16[2,3,3,16,192]{4,3,2,1,0:T(8,128)(2,1)}, bf16[2,3,3,16,192]{4,3,2,1,0:T(8,128)(2,1)S(1)}, u32[]{:S(2)}, u32[]{:S(2)}) collective-permute-start(bf16[2,3,3,16,192]{4,3,2,1,0:T(8,128)(2,1)} %get-tuple-element.30), channel_id=1, source_target_pairs={{0,4},{4,8},{8,12},{12,0},{16,28},{20,16},{24,20},{28,24},{1,5},{5... | collective-permute-start | bytes 331784 | tf_op jit(solution)/shard_map/ppermute | solution.py:276
  11.1 0.9 collective-permute-start.6
  11.9 11.2 %all-to-all-start = ((f32[64,8,128]{2,1,0:T(8,128)}), f32[64,8,128]{2,1,0:T(8,128)S(1)}, u32[]{:S(2)}, u32[]{:S(2)}) async-start(f32[64,8,128]{2,1,0:T(8,128)} %get-tuple-element.28), calls=%async_computation | async-start | bytes 524288 | tf_op jit(solution)/shard_map/all_to_all | solution.py:256
  23.2 0.0 collective-permute-done.5.side_ref
  23.2 1.2 %collective-permute-start.7 = (bf16[2,3,3,16,192]{4,3,2,1,0:T(8,128)(2,1)S(1)}, bf16[2,3,3,16,192]{4,3,2,1,0:T(8,128)(2,1)S(1)}, u32[]{:S(2)}, u32[]{:S(2)}) collective-permute-start(bf16[2,3,3,16,192]{4,3,2,1,0:T(8,128)(2,1)S(1)} %collective-permute-done.5.side_ref), channel_id=1, source_target_pairs={{0,16},{16,0},{1,17},{17,1},{2,18},{18,2},{3,19},{19,3},{4,20},{20... | collective-permute-start | bytes 331784 | tf_op jit(solution)/shard_map/ppermute | solution.py:282
  24.4 0.0 collective-permute-done.b_ref
  24.4 0.0 collective-permute-done.1.c_ref
  24.4 0.0 collective-permute-done.2.d_ref
  24.5 0.1 collective-permute-start.3
  24.6 4.1 %collective-permute-start.4 = (bf16[4,16,768]{2,1,0:T(8,128)(2,1)S(1)}, bf16[4,16,768]{2,1,0:T(8,128)(2,1)S(1)}, u32[]{:S(2)}, u32[]{:S(2)}) collective-permute-start(bf16[4,16,768]{2,1,0:T(8,128)(2,1)S(1)} %get-tuple-element.27), channel_id=1, source_target_pairs={{16,32},{48,64},{80,96},{112,128},{144,160},{176,192},{208,224},{3... | collective-permute-start | bytes 294920 | tf_op jit(solution)/shard_map/ppermute | solution.py:247
  28.7 0.0 collective-permute-done.6.far_ref
  28.7 0.1 collective-permute-start.8
  28.8 1.3 %collective-permute-done.8.far2_ref = bf16[3,3,16,192]{3,2,1,0:T(8,128)(2,1)S(1)} collective-permute-done((bf16[3,3,16,192]{3,2,1,0:T(8,128)(2,1)S(1)}, bf16[3,3,16,192]{3,2,1,0:T(8,128)(2,1)S(1)}, u32[]{:S(2)}, u32[]{:S(2)}) %collective-permute-start.8) | collective-permute-done | bytes 55328 | tf_op jit(solution)/shard_map/ppermute | solution.py:282
  30.0 0.0 collective-permute-done.3.chip_ref
  30.0 4.1 %collective-permute-done.4.next_ref = bf16[4,16,768]{2,1,0:T(8,128)(2,1)S(1)} collective-permute-done((bf16[4,16,768]{2,1,0:T(8,128)(2,1)S(1)}, bf16[4,16,768]{2,1,0:T(8,128)(2,1)S(1)}, u32[]{:S(2)}, u32[]{:S(2)}) %collective-permute-start.4) | collective-permute-done | bytes 98336 | tf_op jit(solution)/shard_map/ppermute | solution.py:247
  34.1 0.0 all-to-all-done.stats_ref
  34.1 2.2 %shard_map.66 = (bf16[8,16,512]{2,1,0:T(8,128)(2,1)S(1)}, bf16[8,16,512]{2,1,0:T(8,128)(2,1)S(1)}, bf16[8,16,512]{2,1,0:T(8,128)(2,1)S(1)}, bf16[8,16,512]{2,1,0:T(8,128)(2,1)S(1)}) custom-call(bf16[8,16,768]{2,1,0:T(8,128)(2,1)S(1)} %copy-done.2, bf16[8,16,768]{2,1,0:T(8,128)(2,1)S(1)} %collective-permute-done.b_ref, ...), custom_call_target="tpu_custom_call" | custom-call | flops 905969664 | bytes 1687552 | tf_op jit(solution)/shard_map/pallas_call | solution.py:31
  36.4 0.1 collective-permute-start.10
  36.5 3.6 %collective-permute-start.9 = (bf16[8,16,512]{2,1,0:T(8,128)(2,1)S(1)}, bf16[8,16,512]{2,1,0:T(8,128)(2,1)S(1)}, u32[]{:S(2)}, u32[]{:S(2)}) collective-permute-start(bf16[8,16,512]{2,1,0:T(8,128)(2,1)S(1)} %get-tuple-element.33), channel_id=1, source_target_pairs={{0,4},{4,8},{8,12},{12,0},{16,28},{20,16},{24,20},{28,24},{1,5},{5... | collective-permute-start | bytes 393224 | tf_op jit(solution)/shard_map/ppermute | solution.py:225
  40.0 5.3 %collective-permute-done.10.b_ref = bf16[8,16,512]{2,1,0:T(8,128)(2,1)S(1)} collective-permute-done((bf16[8,16,512]{2,1,0:T(8,128)(2,1)S(1)}, bf16[8,16,512]{2,1,0:T(8,128)(2,1)S(1)}, u32[]{:S(2)}, u32[]{:S(2)}) %collective-permute-start.10) | collective-permute-done | bytes 131104 | tf_op jit(solution)/shard_map/ppermute | solution.py:224
  45.4 0.0 copy-start.4
  45.4 0.1 collective-permute-start.11
  45.5 0.5 copy-done.6
  46.0 0.1 copy-done.4
  46.1 0.7 copy-done.5
  46.8 5.6 %collective-permute-done.11.c_ref = bf16[8,16,512]{2,1,0:T(8,128)(2,1)S(1)} collective-permute-done((bf16[8,16,512]{2,1,0:T(8,128)(2,1)S(1)}, bf16[8,16,512]{2,1,0:T(8,128)(2,1)S(1)}, u32[]{:S(2)}, u32[]{:S(2)}) %collective-permute-start.11) | collective-permute-done | bytes 131104 | tf_op jit(solution)/shard_map/ppermute | solution.py:227
  52.4 0.1 broadcast_in_dim.13.bias_ref
  52.4 0.9 shard_map.68
  53.3 0.8 collective-permute-start.12
  54.1 1.6 %collective-permute-start.13 = (bf16[8,16,768]{2,1,0:T(8,128)(2,1)S(1)}, bf16[8,16,768]{2,1,0:T(8,128)(2,1)S(1)}, u32[]{:S(2)}, u32[]{:S(2)}) collective-permute-start(bf16[8,16,768]{2,1,0:T(8,128)(2,1)S(1)} %get-tuple-element.37.a_ref), channel_id=1, source_target_pairs={{0,2},{1,3},{2,0},{3,1},{4,6},{5,7},{6,4},{7,5},{8,10},{9,11},{10,... | collective-permute-start | bytes 589832 | tf_op jit(solution)/shard_map/ppermute | solution.py:252
  55.8 1.2 %collective-permute-start.14 = (bf16[8,16,768]{2,1,0:T(8,128)(2,1)S(1)}, bf16[8,16,768]{2,1,0:T(8,128)(2,1)S(1)}, u32[]{:S(2)}, u32[]{:S(2)}) collective-permute-start(bf16[8,16,768]{2,1,0:T(8,128)(2,1)S(1)} %get-tuple-element.37.a_ref), channel_id=1, source_target_pairs={{0,3},{1,2},{2,1},{3,0},{4,7},{5,6},{6,5},{7,4},{8,11},{9,10},{10,... | collective-permute-start | bytes 589832 | tf_op jit(solution)/shard_map/ppermute | solution.py:252
  57.0 7.0 %all-to-all-start.1 = ((f32[64,8,128]{2,1,0:T(8,128)}), f32[64,8,128]{2,1,0:T(8,128)S(1)}, u32[]{:S(2)}, u32[]{:S(2)}) async-start(f32[64,8,128]{2,1,0:T(8,128)} %get-tuple-element.40), calls=%async_computation.1 | async-start | bytes 524288 | tf_op jit(solution)/shard_map/all_to_all | solution.py:256
  63.9 0.0 collective-permute-done.13.c_ref
  64.0 0.4 collective-permute-start.15
  64.5 3.8 %collective-permute-start.16 = (bf16[4,16,768]{2,1,0:T(8,128)(2,1)S(1)}, bf16[4,16,768]{2,1,0:T(8,128)(2,1)S(1)}, u32[]{:S(2)}, u32[]{:S(2)}) collective-permute-start(bf16[4,16,768]{2,1,0:T(8,128)(2,1)S(1)} %get-tuple-element.39), channel_id=1, source_target_pairs={{16,32},{48,64},{80,96},{112,128},{144,160},{176,192},{208,224},{3... | collective-permute-start | bytes 294920 | tf_op jit(solution)/shard_map/ppermute | solution.py:247
  68.2 5.7 %collective-permute-done.16.next_ref = bf16[4,16,768]{2,1,0:T(8,128)(2,1)S(1)} collective-permute-done((bf16[4,16,768]{2,1,0:T(8,128)(2,1)S(1)}, bf16[4,16,768]{2,1,0:T(8,128)(2,1)S(1)}, u32[]{:S(2)}, u32[]{:S(2)}) %collective-permute-start.16) | collective-permute-done | bytes 98336 | tf_op jit(solution)/shard_map/ppermute | solution.py:247
  74.0 2.2 %shard_map.70 = (bf16[8,16,512]{2,1,0:T(8,128)(2,1)S(1)}, bf16[8,16,512]{2,1,0:T(8,128)(2,1)S(1)}, bf16[8,16,512]{2,1,0:T(8,128)(2,1)S(1)}, bf16[8,16,512]{2,1,0:T(8,128)(2,1)S(1)}) custom-call(bf16[8,16,768]{2,1,0:T(8,128)(2,1)S(1)} %get-tuple-element.37.a_ref, bf16[8,16,768]{2,1,0:T(8,128)(2,1)S(1)} %collective-permute-done.12.b_ref, ...), custom_call_target="tpu_custom_call" | custom-call | flops 905969664 | bytes 1687552 | tf_op jit(solution)/shard_map/pallas_call | solution.py:31
  76.2 1.4 %collective-permute-start.18 = (bf16[8,16,512]{2,1,0:T(8,128)(2,1)S(1)}, bf16[8,16,512]{2,1,0:T(8,128)(2,1)S(1)}, u32[]{:S(2)}, u32[]{:S(2)}) collective-permute-start(bf16[8,16,512]{2,1,0:T(8,128)(2,1)S(1)} %get-tuple-element.44), channel_id=1, source_target_pairs={{0,12},{4,0},{8,4},{12,8},{16,20},{20,24},{24,28},{28,16},{1,13},{... | collective-permute-start | bytes 393224 | tf_op jit(solution)/shard_map/ppermute | solution.py:224
  77.6 2.3 %collective-permute-start.17 = (bf16[8,16,512]{2,1,0:T(8,128)(2,1)S(1)}, bf16[8,16,512]{2,1,0:T(8,128)(2,1)S(1)}, u32[]{:S(2)}, u32[]{:S(2)}) collective-permute-start(bf16[8,16,512]{2,1,0:T(8,128)(2,1)S(1)} %get-tuple-element.42), channel_id=1, source_target_pairs={{0,4},{4,8},{8,12},{12,0},{16,28},{20,16},{24,20},{28,24},{1,5},{5... | collective-permute-start | bytes 393224 | tf_op jit(solution)/shard_map/ppermute | solution.py:225
  79.9 6.6 %collective-permute-done.18.b_ref = bf16[8,16,512]{2,1,0:T(8,128)(2,1)S(1)} collective-permute-done((bf16[8,16,512]{2,1,0:T(8,128)(2,1)S(1)}, bf16[8,16,512]{2,1,0:T(8,128)(2,1)S(1)}, u32[]{:S(2)}, u32[]{:S(2)}) %collective-permute-start.18) | collective-permute-done | bytes 131104 | tf_op jit(solution)/shard_map/ppermute | solution.py:224
  86.6 0.1 collective-permute-start.19
  86.7 6.4 %collective-permute-done.19.c_ref = bf16[8,16,512]{2,1,0:T(8,128)(2,1)S(1)} collective-permute-done((bf16[8,16,512]{2,1,0:T(8,128)(2,1)S(1)}, bf16[8,16,512]{2,1,0:T(8,128)(2,1)S(1)}, u32[]{:S(2)}, u32[]{:S(2)}) %collective-permute-start.19) | collective-permute-done | bytes 131104 | tf_op jit(solution)/shard_map/ppermute | solution.py:227
  93.0 0.1 broadcast_in_dim.15.bias_ref
  93.1 0.7 shard_map.72
  (25 shorter events, 0.2 us)
Async XLA Ops:
  2.3 22.1 %collective-permute-start = (bf16[8,16,768]{2,1,0:T(8,128)(2,1)}, bf16[8,16,768]{2,1,0:T(8,128)(2,1)S(1)}, u32[]{:S(2)}, u32[]{:S(2)}) collective-permute-start(bf16[8,16,768]{2,1,0:T(8,128)(2,1)} %get-tuple-element.25.a_ref), channel_id=1, source_target_pairs={{0,1},{1,0},{2,3},{3,2},{4,5},{5,4},{6,7},{7,6},{8,9},{9,8},{10,11... | collective-permute-start | bytes 589832 | tf_op jit(solution)/shard_map/ppermute | solution.py:252
  2.6 21.8 %collective-permute-start.1 = (bf16[8,16,768]{2,1,0:T(8,128)(2,1)}, bf16[8,16,768]{2,1,0:T(8,128)(2,1)S(1)}, u32[]{:S(2)}, u32[]{:S(2)}) collective-permute-start(bf16[8,16,768]{2,1,0:T(8,128)(2,1)} %get-tuple-element.25.a_ref), channel_id=1, source_target_pairs={{0,2},{1,3},{2,0},{3,1},{4,6},{5,7},{6,4},{7,5},{8,10},{9,11},{10,... | collective-permute-start | bytes 589832 | tf_op jit(solution)/shard_map/ppermute | solution.py:252
  4.3 20.1 %collective-permute-start.2 = (bf16[8,16,768]{2,1,0:T(8,128)(2,1)}, bf16[8,16,768]{2,1,0:T(8,128)(2,1)S(1)}, u32[]{:S(2)}, u32[]{:S(2)}) collective-permute-start(bf16[8,16,768]{2,1,0:T(8,128)(2,1)} %get-tuple-element.25.a_ref), channel_id=1, source_target_pairs={{0,3},{1,2},{2,1},{3,0},{4,7},{5,6},{6,5},{7,4},{8,11},{9,10},{10,... | collective-permute-start | bytes 589832 | tf_op jit(solution)/shard_map/ppermute | solution.py:252
  5.2 18.0 %collective-permute-start.5 = (bf16[2,3,3,16,192]{4,3,2,1,0:T(8,128)(2,1)}, bf16[2,3,3,16,192]{4,3,2,1,0:T(8,128)(2,1)S(1)}, u32[]{:S(2)}, u32[]{:S(2)}) collective-permute-start(bf16[2,3,3,16,192]{4,3,2,1,0:T(8,128)(2,1)} %get-tuple-element.30), channel_id=1, source_target_pairs={{0,4},{4,8},{8,12},{12,0},{16,28},{20,16},{24,20},{28,24},{1,5},{5... | collective-permute-start | bytes 331784 | tf_op jit(solution)/shard_map/ppermute | solution.py:276
  11.1 17.6 %collective-permute-start.6 = (bf16[3,3,16,192]{3,2,1,0:T(8,128)(2,1)}, bf16[3,3,16,192]{3,2,1,0:T(8,128)(2,1)S(1)}, u32[]{:S(2)}, u32[]{:S(2)}) collective-permute-start(bf16[3,3,16,192]{3,2,1,0:T(8,128)(2,1)} %get-tuple-element.31), channel_id=1, source_target_pairs={{0,8},{4,12},{8,0},{12,4},{1,9},{5,13},{9,1},{13,5},{2,10},{6,14},... | collective-permute-start | bytes 165896 | tf_op jit(solution)/shard_map/ppermute | solution.py:277
  11.9 12.5 %copy-start.2 = (bf16[8,16,768]{2,1,0:T(8,128)(2,1)S(1)}, bf16[8,16,768]{2,1,0:T(8,128)(2,1)}, u32[]{:S(2)}) copy-start(bf16[8,16,768]{2,1,0:T(8,128)(2,1)} %get-tuple-element.25.a_ref) | copy-start | bytes 589828
  11.9 22.2 %all-to-all-start = ((f32[64,8,128]{2,1,0:T(8,128)}), f32[64,8,128]{2,1,0:T(8,128)S(1)}, u32[]{:S(2)}, u32[]{:S(2)}) async-start(f32[64,8,128]{2,1,0:T(8,128)} %get-tuple-element.28), calls=%async_computation | async-start | bytes 524288 | tf_op jit(solution)/shard_map/all_to_all | solution.py:256
  23.2 10.9 %copy-start.3 = (bf16[2,3,3,16,192]{4,3,2,1,0:T(8,128)(2,1)S(1)}, bf16[2,3,3,16,192]{4,3,2,1,0:T(8,128)(2,1)}, u32[]{:S(2)}) copy-start(bf16[2,3,3,16,192]{4,3,2,1,0:T(8,128)(2,1)} %get-tuple-element.29.own_ref) | copy-start | bytes 331780
  23.2 6.8 %collective-permute-start.7 = (bf16[2,3,3,16,192]{4,3,2,1,0:T(8,128)(2,1)S(1)}, bf16[2,3,3,16,192]{4,3,2,1,0:T(8,128)(2,1)S(1)}, u32[]{:S(2)}, u32[]{:S(2)}) collective-permute-start(bf16[2,3,3,16,192]{4,3,2,1,0:T(8,128)(2,1)S(1)} %collective-permute-done.5.side_ref), channel_id=1, source_target_pairs={{0,16},{16,0},{1,17},{17,1},{2,18},{18,2},{3,19},{19,3},{4,20},{20... | collective-permute-start | bytes 331784 | tf_op jit(solution)/shard_map/ppermute | solution.py:282
  24.5 5.6 %collective-permute-start.3 = (bf16[4,16,768]{2,1,0:T(8,128)(2,1)S(1)}, bf16[4,16,768]{2,1,0:T(8,128)(2,1)S(1)}, u32[]{:S(2)}, u32[]{:S(2)}) collective-permute-start(bf16[4,16,768]{2,1,0:T(8,128)(2,1)S(1)} %get-tuple-element.26), channel_id=1, source_target_pairs={{0,16},{16,0},{32,48},{48,32},{64,80},{80,64},{96,112},{112,96},{1... | collective-permute-start | bytes 294920 | tf_op jit(solution)/shard_map/ppermute | solution.py:245
  24.6 9.5 %collective-permute-start.4 = (bf16[4,16,768]{2,1,0:T(8,128)(2,1)S(1)}, bf16[4,16,768]{2,1,0:T(8,128)(2,1)S(1)}, u32[]{:S(2)}, u32[]{:S(2)}) collective-permute-start(bf16[4,16,768]{2,1,0:T(8,128)(2,1)S(1)} %get-tuple-element.27), channel_id=1, source_target_pairs={{16,32},{48,64},{80,96},{112,128},{144,160},{176,192},{208,224},{3... | collective-permute-start | bytes 294920 | tf_op jit(solution)/shard_map/ppermute | solution.py:247
  28.7 1.4 %collective-permute-start.8 = (bf16[3,3,16,192]{3,2,1,0:T(8,128)(2,1)S(1)}, bf16[3,3,16,192]{3,2,1,0:T(8,128)(2,1)S(1)}, u32[]{:S(2)}, u32[]{:S(2)}) collective-permute-start(bf16[3,3,16,192]{3,2,1,0:T(8,128)(2,1)S(1)} %collective-permute-done.6.far_ref), channel_id=1, source_target_pairs={{0,16},{16,0},{1,17},{17,1},{2,18},{18,2},{3,19},{19,3},{4,20},{20... | collective-permute-start | bytes 165896 | tf_op jit(solution)/shard_map/ppermute | solution.py:282
  36.4 9.0 %collective-permute-start.10 = (bf16[8,16,512]{2,1,0:T(8,128)(2,1)S(1)}, bf16[8,16,512]{2,1,0:T(8,128)(2,1)S(1)}, u32[]{:S(2)}, u32[]{:S(2)}) collective-permute-start(bf16[8,16,512]{2,1,0:T(8,128)(2,1)S(1)} %get-tuple-element.35), channel_id=1, source_target_pairs={{0,12},{4,0},{8,4},{12,8},{16,20},{20,24},{24,28},{28,16},{1,13},{... | collective-permute-start | bytes 393224 | tf_op jit(solution)/shard_map/ppermute | solution.py:224
  36.5 10.3 %collective-permute-start.9 = (bf16[8,16,512]{2,1,0:T(8,128)(2,1)S(1)}, bf16[8,16,512]{2,1,0:T(8,128)(2,1)S(1)}, u32[]{:S(2)}, u32[]{:S(2)}) collective-permute-start(bf16[8,16,512]{2,1,0:T(8,128)(2,1)S(1)} %get-tuple-element.33), channel_id=1, source_target_pairs={{0,4},{4,8},{8,12},{12,0},{16,28},{20,16},{24,20},{28,24},{1,5},{5... | collective-permute-start | bytes 393224 | tf_op jit(solution)/shard_map/ppermute | solution.py:225
  45.3 0.7 copy-start.6
  45.3 7.1 %copy-start.1 = (bf16[8,16,256]{2,1,0:T(8,128)(2,1)S(1)}, bf16[8,16,256]{2,1,0:T(8,128)(2,1)}, u32[]{:S(2)}) copy-start(bf16[8,16,256]{2,1,0:T(8,128)(2,1)} %get-tuple-element.36.later_ref) | copy-start | bytes 196612
  45.4 0.7 copy-start.4
  45.4 7.0 %collective-permute-start.11 = (bf16[8,16,512]{2,1,0:T(8,128)(2,1)S(1)}, bf16[8,16,512]{2,1,0:T(8,128)(2,1)S(1)}, u32[]{:S(2)}, u32[]{:S(2)}) collective-permute-start(bf16[8,16,512]{2,1,0:T(8,128)(2,1)S(1)} %shard_map.67), channel_id=1, source_target_pairs={{0,12},{4,0},{8,4},{12,8},{16,20},{20,24},{24,28},{28,16},{1,13},{... | collective-permute-start | bytes 393224 | tf_op jit(solution)/shard_map/ppermute | solution.py:227
  46.1 0.7 copy-start.5
  53.3 10.6 %collective-permute-start.12 = (bf16[8,16,768]{2,1,0:T(8,128)(2,1)S(1)}, bf16[8,16,768]{2,1,0:T(8,128)(2,1)S(1)}, u32[]{:S(2)}, u32[]{:S(2)}) collective-permute-start(bf16[8,16,768]{2,1,0:T(8,128)(2,1)S(1)} %get-tuple-element.37.a_ref), channel_id=1, source_target_pairs={{0,1},{1,0},{2,3},{3,2},{4,5},{5,4},{6,7},{7,6},{8,9},{9,8},{10,11... | collective-permute-start | bytes 589832 | tf_op jit(solution)/shard_map/ppermute | solution.py:252
  54.1 9.8 %collective-permute-start.13 = (bf16[8,16,768]{2,1,0:T(8,128)(2,1)S(1)}, bf16[8,16,768]{2,1,0:T(8,128)(2,1)S(1)}, u32[]{:S(2)}, u32[]{:S(2)}) collective-permute-start(bf16[8,16,768]{2,1,0:T(8,128)(2,1)S(1)} %get-tuple-element.37.a_ref), channel_id=1, source_target_pairs={{0,2},{1,3},{2,0},{3,1},{4,6},{5,7},{6,4},{7,5},{8,10},{9,11},{10,... | collective-permute-start | bytes 589832 | tf_op jit(solution)/shard_map/ppermute | solution.py:252
  55.8 8.2 %collective-permute-start.14 = (bf16[8,16,768]{2,1,0:T(8,128)(2,1)S(1)}, bf16[8,16,768]{2,1,0:T(8,128)(2,1)S(1)}, u32[]{:S(2)}, u32[]{:S(2)}) collective-permute-start(bf16[8,16,768]{2,1,0:T(8,128)(2,1)S(1)} %get-tuple-element.37.a_ref), channel_id=1, source_target_pairs={{0,3},{1,2},{2,1},{3,0},{4,7},{5,6},{6,5},{7,4},{8,11},{9,10},{10,... | collective-permute-start | bytes 589832 | tf_op jit(solution)/shard_map/ppermute | solution.py:252
  57.0 17.0 %all-to-all-start.1 = ((f32[64,8,128]{2,1,0:T(8,128)}), f32[64,8,128]{2,1,0:T(8,128)S(1)}, u32[]{:S(2)}, u32[]{:S(2)}) async-start(f32[64,8,128]{2,1,0:T(8,128)} %get-tuple-element.40), calls=%async_computation.1 | async-start | bytes 524288 | tf_op jit(solution)/shard_map/all_to_all | solution.py:256
  64.0 4.2 %collective-permute-start.15 = (bf16[4,16,768]{2,1,0:T(8,128)(2,1)S(1)}, bf16[4,16,768]{2,1,0:T(8,128)(2,1)S(1)}, u32[]{:S(2)}, u32[]{:S(2)}) collective-permute-start(bf16[4,16,768]{2,1,0:T(8,128)(2,1)S(1)} %get-tuple-element.38), channel_id=1, source_target_pairs={{0,16},{16,0},{32,48},{48,32},{64,80},{80,64},{96,112},{112,96},{1... | collective-permute-start | bytes 294920 | tf_op jit(solution)/shard_map/ppermute | solution.py:245
  64.5 9.5 %collective-permute-start.16 = (bf16[4,16,768]{2,1,0:T(8,128)(2,1)S(1)}, bf16[4,16,768]{2,1,0:T(8,128)(2,1)S(1)}, u32[]{:S(2)}, u32[]{:S(2)}) collective-permute-start(bf16[4,16,768]{2,1,0:T(8,128)(2,1)S(1)} %get-tuple-element.39), channel_id=1, source_target_pairs={{16,32},{48,64},{80,96},{112,128},{144,160},{176,192},{208,224},{3... | collective-permute-start | bytes 294920 | tf_op jit(solution)/shard_map/ppermute | solution.py:247
  76.2 10.3 %collective-permute-start.18 = (bf16[8,16,512]{2,1,0:T(8,128)(2,1)S(1)}, bf16[8,16,512]{2,1,0:T(8,128)(2,1)S(1)}, u32[]{:S(2)}, u32[]{:S(2)}) collective-permute-start(bf16[8,16,512]{2,1,0:T(8,128)(2,1)S(1)} %get-tuple-element.44), channel_id=1, source_target_pairs={{0,12},{4,0},{8,4},{12,8},{16,20},{20,24},{24,28},{28,16},{1,13},{... | collective-permute-start | bytes 393224 | tf_op jit(solution)/shard_map/ppermute | solution.py:224
  77.6 9.0 %collective-permute-start.17 = (bf16[8,16,512]{2,1,0:T(8,128)(2,1)S(1)}, bf16[8,16,512]{2,1,0:T(8,128)(2,1)S(1)}, u32[]{:S(2)}, u32[]{:S(2)}) collective-permute-start(bf16[8,16,512]{2,1,0:T(8,128)(2,1)S(1)} %get-tuple-element.42), channel_id=1, source_target_pairs={{0,4},{4,8},{8,12},{12,0},{16,28},{20,16},{24,20},{28,24},{1,5},{5... | collective-permute-start | bytes 393224 | tf_op jit(solution)/shard_map/ppermute | solution.py:225
  86.5 6.6 %copy-start = (bf16[4,8,16,128]{3,2,1,0:T(8,128)(2,1)S(1)}, bf16[4,8,16,128]{3,2,1,0:T(8,128)(2,1)}, u32[]{:S(2)}) copy-start(bf16[4,8,16,128]{3,2,1,0:T(8,128)(2,1)} %x_ref.1) | copy-start | bytes 393220
  86.6 6.5 %collective-permute-start.19 = (bf16[8,16,512]{2,1,0:T(8,128)(2,1)S(1)}, bf16[8,16,512]{2,1,0:T(8,128)(2,1)S(1)}, u32[]{:S(2)}, u32[]{:S(2)}) collective-permute-start(bf16[8,16,512]{2,1,0:T(8,128)(2,1)S(1)} %shard_map.71), channel_id=1, source_target_pairs={{0,12},{4,0},{8,4},{12,8},{16,20},{20,24},{24,28},{28,16},{1,13},{... | collective-permute-start | bytes 393224 | tf_op jit(solution)/shard_map/ppermute | solution.py:227

commit v11 on v10

--- a/solution.py
+++ b/solution.py
@@ -22,7 +22,8 @@
 
 
 def silu(u):
-    return u / (1.0 + jnp.exp(-u))
+    half = 0.5 * u
+    return half + half * jnp.tanh(half)
 
 
 def call(kernel, outs, *args, far=(), scratch=(), flops=0):
@@ -129,10 +130,30 @@
     affine_ref[2] = jnp.broadcast_to(shift, shape)
 
 
+def products(layer, w_refs, o_refs, slab_ref):
+    for r in range(8):
+        rows = slab_ref[r : r + 3].reshape(192, 768)
+        prod = jnp.zeros((96, 512), F32)
+        for dt in range(3):
+            held = jnp.concatenate([ref(dt).reshape(48, 192) for ref in w_refs], axis=0)
+            prod += dot(held, rows[:, 128 * dt : 128 * dt + 512])
+        prod = prod.reshape(2, 3, 16, 512)
+        for t in range(4):
+            lanes = slice(128 * t, 128 * (t + 1))
+            part = prod[:, :, :, lanes]
+            summed = shift_columns(part[:, 0], part[:, 1], part[:, 2]).astype(BF16)
+            for q, o_ref in enumerate(o_refs):
+                o_ref[r, :, lanes] = summed[q]
+
+
+def near_kernel(layer, slab_ref, own_ref, side_ref, o0_ref, o1_ref):
+    w_refs = (lambda dt: own_ref[layer, dt], lambda dt: side_ref[layer, dt])
+    products(layer, w_refs, (o0_ref, o1_ref), slab_ref)
+
+
 def conv_kernel(
-    layer, a_ref, b_ref, c_ref, d_ref, chip_ref, next_ref, stats_ref,
-    own_ref, side_ref, far_ref, side2_ref, far2_ref, o0_ref, o1_ref, o2_ref, o3_ref,
-    affine_ref, slab_ref, held_ref,
+    layer, a_ref, b_ref, c_ref, d_ref, chip_ref, next_ref, stats_ref, other_ref, far_ref, far2_ref,
+    o2_ref, o3_ref, slab_ref, affine_ref, held_ref,
 ):
     row, _, here = place()
     get_affine(stats_ref, affine_ref)
@@ -163,33 +184,17 @@
                     x = x * not_bottom
                 slab_ref[r, b, :, lanes] = x.astype(BF16)
     core = lax.rem(row, 2)
-    for dt in range(3):
-        held_ref[dt, 0] = own_ref[layer, dt]
-        held_ref[dt, 1] = side_ref[layer, dt]
-        held_ref[dt, 2] = side2_ref[layer, dt]
 
     @pl.when(core == layer)
     def _():
-        for dt in range(3):
-            held_ref[dt, 3] = far_ref[dt]
+        held_ref[...] = far_ref[...]
 
     @pl.when(core != layer)
     def _():
-        for dt in range(3):
-            held_ref[dt, 3] = far2_ref[dt]
-
-    for r in range(8):
-        rows = slab_ref[r : r + 3].reshape(192, 768)
-        prod = dot(held_ref[0].reshape(192, 192), rows[:, 0:512])
-        prod += dot(held_ref[1].reshape(192, 192), rows[:, 128:640])
-        prod += dot(held_ref[2].reshape(192, 192), rows[:, 256:768])
-        prod = prod.reshape(4, 3, 16, 512)
-        for t in range(4):
-            lanes = slice(128 * t, 128 * (t + 1))
-            part = prod[:, :, :, lanes]
-            summed = shift_columns(part[:, 0], part[:, 1], part[:, 2]).astype(BF16)
-            for q, o_ref in enumerate((o0_ref, o1_ref, o2_ref, o3_ref)):
-                o_ref[r, :, lanes] = summed[q]
+        held_ref[...] = far2_ref[...]
+
+    w_refs = (lambda dt: other_ref[layer, dt], lambda dt: held_ref[dt])
+    products(layer, w_refs, (o2_ref, o3_ref), slab_ref)
 
 
 def merge_kernel(a_ref, b_ref, c_ref, bias_ref, later_ref, note1_ref, mid_ref, stats_ref, note_ref):
@@ -220,10 +225,20 @@
     o_ref[...] = (a_ref[...].astype(F32) + b_ref[...].astype(F32)).astype(BF16)
 
 
-def bring(own, side, other, far):
+def convolve(layer, inputs, own, side, far, other, far2):
+    part = struct((8, 16, 512))
+    flops = 2 * 96 * 576 * 4096
+    other, far, slab = call(
+        functools.partial(conv_kernel, layer), (part, part, struct((10, 4, 16, 768))),
+        *inputs, other, far, far2,
+        scratch=(pltpu.VMEM((3, 4, 16, 128), F32), pltpu.VMEM((3, 3, 16, 192), BF16)), flops=flops,
+    )
     far = lax.ppermute(far, ("core", "zh"), sides(-1))
     other = lax.ppermute(other, ("core", "zh"), sides(1))
-    side = call(add_kernel, struct(side.shape), side, far)
+    own, side = call(
+        functools.partial(near_kernel, layer), (part, part), slab, own, side, flops=flops
+    )
+    side = call(add_kernel, part, side, far)
     side = lax.ppermute(side, ("core", "zh"), sides(-1))
     return [own, other, side]
 
@@ -282,19 +297,7 @@
     weights = [own, side, far, lax.ppermute(side, "core", swap), lax.ppermute(far, "core", swap)]
     bias = jnp.broadcast_to(conv_bias[:, :, None], (2, 16, 128))
     note1 = jnp.pad(jnp.stack([norm_gain[1], norm_shift[1]]), ((4, 2), (0, 112)))
-    scratch = (
-        pltpu.VMEM((3, 4, 16, 128), F32),
-        pltpu.VMEM((10, 4, 16, 768), BF16),
-        pltpu.VMEM((3, 4, 3, 16, 192), BF16),
-    )
-    flops = 2 * 192 * 576 * 4096
-    parts = (struct((8, 16, 512)),) * 4
-
-    partial = call(
-        functools.partial(conv_kernel, 0), parts, *raw, stats, *weights,
-        scratch=scratch, flops=flops,
-    )
-    partial = bring(*partial)
+    partial = convolve(0, [*raw, stats], *weights)
     middle, stats = call(
         merge_kernel, (struct((8, 16, 768)), struct((64, 8, 128), F32)), *partial, bias[0], later, note1,
         scratch=(note,),
@@ -302,11 +305,7 @@
     middle = near(middle)
     stats = exchange(stats, ROW + NEAR)
     middle = middle + rows_beside(middle)
-    partial = call(
-        functools.partial(conv_kernel, 1), parts, *middle, stats, *weights,
-        scratch=scratch, flops=flops,
-    )
-    partial = bring(*partial)
+    partial = convolve(1, [*middle, stats], *weights)
     return call(last_kernel, struct((4, 8, 16, 128)), frames, *partial, bias[1])
 
 

time: 94.2 us -> 93.6 us (level)
  waiting for transfers between devices: 35 us -> 33.3 us
    ppermute x6, waiting for transfers between devices: 23.9 us -> 22.2 us  [the longest x2 12.2 us: convolve(): side = lax.ppermute(side, ('core', 'zh'), sides(-1))]
    pallas_call x9 -> x11, Pallas kernels: 8.49 us -> 8.81 us  [call(): pl.pallas_call(kernel, out_shape=outs, in_specs=specs, out_specs=jax.tree...]
  transfers between devices with their start and end apart: 22 -> 22, of which waited for: 7 -> 7; matrix products, arithmetic and copies ran while one was open for 0% -> 0% of each run, Pallas kernels for 0% -> 2%
where the time goes in v11:
time: 93.6 us; the launch traced here: 92.6 us
  starting transfers between devices  48.8 us (52%)
  waiting for transfers between devices  33.3 us (36%)
  Pallas kernels  8.81 us (9%)
  local copies, waits for them, and re-layouts  1.45 us (2%)
    all_to_all x2, starting transfers between devices, exchange(): return lax.all_to_all(x, axes, 0, 0, tiled=True)  18.2 us
    ppermute x2, waiting for transfers between devices, convolve(): side = lax.ppermute(side, ('core', 'zh'), sides(-1))  12.2 us
    ppermute x2, waiting for transfers between devices, convolve(): far = lax.ppermute(far, ('core', 'zh'), sides(-1))  10 us
    ppermute x2, waiting for transfers between devices, rows_beside(): beyond = lax.ppermute(beyond, ROW, pairs)  9.84 us
    pallas_call x11, Pallas kernels, call(): pl.pallas_call(kernel, out_shape=outs, in_specs=specs, out_specs=jax.tree...  8.81 us
    ppermute x2, starting transfers between devices, rows_beside(): beyond = lax.ppermute(beyond, ROW, pairs)  7.98 us
    ppermute x6, starting transfers between devices, near(): lax.ppermute(x, NEAR, [(i, i ^ k) for i in range(4)])  6.59 us
    ppermute x2, starting transfers between devices, convolve(): other = lax.ppermute(other, ('core', 'zh'), sides(1))  6.11 us
  transfers between devices with their start and end apart: 22, of which 7 were waited for; matrix products, arithmetic and copies ran while one was open for 0% of the time, Pallas kernels for 2%

profile of v11, /device:TPU:27, one launch (start us, length us, event | category | flops | bytes accessed | tf_op | source)
XLA Modules:
  0.0 92.6 jit_solution(5961695250655806121)
XLA Ops:
  0.0 2.3 %shard_map.64 = (bf16[8,16,768]{2,1,0:T(8,128)(2,1)}, bf16[8,16,256]{2,1,0:T(8,128)(2,1)}, f32[64,8,128]{2,1,0:T(8,128)}, bf16[2,3,3,16,192]{4,3,2,1,0:T(8,128)(...) custom-call(bf16[4,8,16,128]{3,2,1,0:T(8,128)(2,1)} %x_ref.1, ...), custom_call_target="tpu_custom_call" | custom-call | bytes 704768 | tf_op jit(solution)/shard_map/pallas_call | solution.py:32
  2.3 0.3 collective-permute-start
  2.6 1.6 %collective-permute-start.1 = (bf16[8,16,768]{2,1,0:T(8,128)(2,1)}, bf16[8,16,768]{2,1,0:T(8,128)(2,1)S(1)}, u32[]{:S(2)}, u32[]{:S(2)}) collective-permute-start(bf16[8,16,768]{2,1,0:T(8,128)(2,1)} %get-tuple-element.27.a_ref), channel_id=1, source_target_pairs={{0,2},{1,3},{2,0},{3,1},{4,6},{5,7},{6,4},{7,5},{8,10},{9,11},{10,... | collective-permute-start | bytes 589832 | tf_op jit(solution)/shard_map/ppermute | solution.py:267
  4.3 0.9 %collective-permute-start.2 = (bf16[8,16,768]{2,1,0:T(8,128)(2,1)}, bf16[8,16,768]{2,1,0:T(8,128)(2,1)S(1)}, u32[]{:S(2)}, u32[]{:S(2)}) collective-permute-start(bf16[8,16,768]{2,1,0:T(8,128)(2,1)} %get-tuple-element.27.a_ref), channel_id=1, source_target_pairs={{0,3},{1,2},{2,1},{3,0},{4,7},{5,6},{6,5},{7,4},{8,11},{9,10},{10,... | collective-permute-start | bytes 589832 | tf_op jit(solution)/shard_map/ppermute | solution.py:267
  5.2 5.8 %collective-permute-start.5 = (bf16[2,3,3,16,192]{4,3,2,1,0:T(8,128)(2,1)}, bf16[2,3,3,16,192]{4,3,2,1,0:T(8,128)(2,1)S(1)}, u32[]{:S(2)}, u32[]{:S(2)}) collective-permute-start(bf16[2,3,3,16,192]{4,3,2,1,0:T(8,128)(2,1)} %get-tuple-element.31), channel_id=1, source_target_pairs={{0,4},{4,8},{8,12},{12,0},{16,28},{20,16},{24,20},{28,24},{1,5},{5... | collective-permute-start | bytes 331784 | tf_op jit(solution)/shard_map/ppermute | solution.py:291
  11.1 0.9 collective-permute-start.7
  12.0 11.2 %all-to-all-start = ((f32[64,8,128]{2,1,0:T(8,128)}), f32[64,8,128]{2,1,0:T(8,128)S(1)}, u32[]{:S(2)}, u32[]{:S(2)}) async-start(f32[64,8,128]{2,1,0:T(8,128)} %get-tuple-element.30), calls=%async_computation | async-start | bytes 524288 | tf_op jit(solution)/shard_map/all_to_all | solution.py:271
  23.2 0.0 collective-permute-done.5.side_ref
  23.2 1.2 %collective-permute-start.6 = (bf16[2,3,3,16,192]{4,3,2,1,0:T(8,128)(2,1)S(1)}, bf16[2,3,3,16,192]{4,3,2,1,0:T(8,128)(2,1)S(1)}, u32[]{:S(2)}, u32[]{:S(2)}) collective-permute-start(bf16[2,3,3,16,192]{4,3,2,1,0:T(8,128)(2,1)S(1)} %collective-permute-done.5.side_ref), channel_id=1, source_target_pairs={{0,16},{16,0},{1,17},{17,1},{2,18},{18,2},{3,19},{19,3},{4,20},{20... | collective-permute-start | bytes 331784 | tf_op jit(solution)/shard_map/ppermute | solution.py:297
  24.4 0.0 collective-permute-done.b_ref
  24.4 0.0 collective-permute-done.1.c_ref
  24.4 0.0 collective-permute-done.2.d_ref
  24.5 0.1 collective-permute-start.3
  24.6 4.2 %collective-permute-start.4 = (bf16[4,16,768]{2,1,0:T(8,128)(2,1)S(1)}, bf16[4,16,768]{2,1,0:T(8,128)(2,1)S(1)}, u32[]{:S(2)}, u32[]{:S(2)}) collective-permute-start(bf16[4,16,768]{2,1,0:T(8,128)(2,1)S(1)} %get-tuple-element.29), channel_id=1, source_target_pairs={{16,32},{48,64},{80,96},{112,128},{144,160},{176,192},{208,224},{3... | collective-permute-start | bytes 294920 | tf_op jit(solution)/shard_map/ppermute | solution.py:262
  28.8 0.0 collective-permute-done.7.far_ref
  28.8 0.1 collective-permute-start.8
  28.9 1.3 %collective-permute-done.8.far2_ref = bf16[3,3,16,192]{3,2,1,0:T(8,128)(2,1)S(1)} collective-permute-done((bf16[3,3,16,192]{3,2,1,0:T(8,128)(2,1)S(1)}, bf16[3,3,16,192]{3,2,1,0:T(8,128)(2,1)S(1)}, u32[]{:S(2)}, u32[]{:S(2)}) %collective-permute-start.8) | collective-permute-done | bytes 55328 | tf_op jit(solution)/shard_map/ppermute | solution.py:297
  30.2 4.1 %collective-permute-done.4.next_ref = bf16[4,16,768]{2,1,0:T(8,128)(2,1)S(1)} collective-permute-done((bf16[4,16,768]{2,1,0:T(8,128)(2,1)S(1)}, bf16[4,16,768]{2,1,0:T(8,128)(2,1)S(1)}, u32[]{:S(2)}, u32[]{:S(2)}) %collective-permute-start.4) | collective-permute-done | bytes 98336 | tf_op jit(solution)/shard_map/ppermute | solution.py:262
  34.3 0.0 all-to-all-done.stats_ref
  34.3 1.5 %shard_map.66 = (bf16[8,16,512]{2,1,0:T(8,128)(2,1)S(1)}, bf16[8,16,512]{2,1,0:T(8,128)(2,1)S(1)}, bf16[10,4,16,768]{3,2,1,0:T(8,128)(2,1)S(1)}) custom-call(bf16[8,16,768]{2,1,0:T(8,128)(2,1)S(1)} %copy-done.2, bf16[8,16,768]{2,1,0:T(8,128)(2,1)S(1)} %collective-permute-done.b_ref, bf16[8,16,768]{2,1,0:T(8,128)(2,1)S(1)} %collective-permute-done.1.c_ref, ...), custom_call_target="tpu_custom_call" | custom-call | flops 452984832 | bytes 1466368 | tf_op jit(solution)/shard_map/pallas_call | solution.py:32
  35.8 0.1 collective-permute-start.10
  35.9 3.6 %collective-permute-start.9 = (bf16[8,16,512]{2,1,0:T(8,128)(2,1)S(1)}, bf16[8,16,512]{2,1,0:T(8,128)(2,1)S(1)}, u32[]{:S(2)}, u32[]{:S(2)}) collective-permute-start(bf16[8,16,512]{2,1,0:T(8,128)(2,1)S(1)} %get-tuple-element.36), channel_id=1, source_target_pairs={{0,4},{4,8},{8,12},{12,0},{16,28},{20,16},{24,20},{28,24},{1,5},{5... | collective-permute-start | bytes 393224 | tf_op jit(solution)/shard_map/ppermute | solution.py:237
  39.5 0.9 shard_map.67
  40.3 4.4 %collective-permute-done.10.b_ref = bf16[8,16,512]{2,1,0:T(8,128)(2,1)S(1)} collective-permute-done((bf16[8,16,512]{2,1,0:T(8,128)(2,1)S(1)}, bf16[8,16,512]{2,1,0:T(8,128)(2,1)S(1)}, u32[]{:S(2)}, u32[]{:S(2)}) %collective-permute-start.10) | collective-permute-done | bytes 131104 | tf_op jit(solution)/shard_map/ppermute | solution.py:236
  44.8 0.0 copy-start.4
  44.8 0.1 collective-permute-start.11
  44.9 0.5 copy-done.6
  45.5 0.1 copy-done.4
  45.5 0.7 copy-done.5
  46.2 5.6 %collective-permute-done.11.c_ref = bf16[8,16,512]{2,1,0:T(8,128)(2,1)S(1)} collective-permute-done((bf16[8,16,512]{2,1,0:T(8,128)(2,1)S(1)}, bf16[8,16,512]{2,1,0:T(8,128)(2,1)S(1)}, u32[]{:S(2)}, u32[]{:S(2)}) %collective-permute-start.11) | collective-permute-done | bytes 131104 | tf_op jit(solution)/shard_map/ppermute | solution.py:242
  51.8 0.1 broadcast_in_dim.13.bias_ref
  51.9 0.9 shard_map.69
  52.8 0.8 collective-permute-start.12
  53.5 1.7 %collective-permute-start.13 = (bf16[8,16,768]{2,1,0:T(8,128)(2,1)S(1)}, bf16[8,16,768]{2,1,0:T(8,128)(2,1)S(1)}, u32[]{:S(2)}, u32[]{:S(2)}) collective-permute-start(bf16[8,16,768]{2,1,0:T(8,128)(2,1)S(1)} %get-tuple-element.40.a_ref), channel_id=1, source_target_pairs={{0,2},{1,3},{2,0},{3,1},{4,6},{5,7},{6,4},{7,5},{8,10},{9,11},{10,... | collective-permute-start | bytes 589832 | tf_op jit(solution)/shard_map/ppermute | solution.py:267
  55.3 1.2 %collective-permute-start.14 = (bf16[8,16,768]{2,1,0:T(8,128)(2,1)S(1)}, bf16[8,16,768]{2,1,0:T(8,128)(2,1)S(1)}, u32[]{:S(2)}, u32[]{:S(2)}) collective-permute-start(bf16[8,16,768]{2,1,0:T(8,128)(2,1)S(1)} %get-tuple-element.40.a_ref), channel_id=1, source_target_pairs={{0,3},{1,2},{2,1},{3,0},{4,7},{5,6},{6,5},{7,4},{8,11},{9,10},{10,... | collective-permute-start | bytes 589832 | tf_op jit(solution)/shard_map/ppermute | solution.py:267
  56.4 7.0 %all-to-all-start.1 = ((f32[64,8,128]{2,1,0:T(8,128)}), f32[64,8,128]{2,1,0:T(8,128)S(1)}, u32[]{:S(2)}, u32[]{:S(2)}) async-start(f32[64,8,128]{2,1,0:T(8,128)} %get-tuple-element.43), calls=%async_computation.1 | async-start | bytes 524288 | tf_op jit(solution)/shard_map/all_to_all | solution.py:271
  63.5 0.4 collective-permute-start.15
  63.9 3.8 %collective-permute-start.16 = (bf16[4,16,768]{2,1,0:T(8,128)(2,1)S(1)}, bf16[4,16,768]{2,1,0:T(8,128)(2,1)S(1)}, u32[]{:S(2)}, u32[]{:S(2)}) collective-permute-start(bf16[4,16,768]{2,1,0:T(8,128)(2,1)S(1)} %get-tuple-element.42), channel_id=1, source_target_pairs={{16,32},{48,64},{80,96},{112,128},{144,160},{176,192},{208,224},{3... | collective-permute-start | bytes 294920 | tf_op jit(solution)/shard_map/ppermute | solution.py:262
  67.7 5.7 %collective-permute-done.16.next_ref = bf16[4,16,768]{2,1,0:T(8,128)(2,1)S(1)} collective-permute-done((bf16[4,16,768]{2,1,0:T(8,128)(2,1)S(1)}, bf16[4,16,768]{2,1,0:T(8,128)(2,1)S(1)}, u32[]{:S(2)}, u32[]{:S(2)}) %collective-permute-start.16) | collective-permute-done | bytes 98336 | tf_op jit(solution)/shard_map/ppermute | solution.py:262
  73.5 1.5 %shard_map.71 = (bf16[8,16,512]{2,1,0:T(8,128)(2,1)S(1)}, bf16[8,16,512]{2,1,0:T(8,128)(2,1)S(1)}, bf16[10,4,16,768]{3,2,1,0:T(8,128)(2,1)S(1)}) custom-call(bf16[8,16,768]{2,1,0:T(8,128)(2,1)S(1)} %get-tuple-element.40.a_ref, bf16[8,16,768]{2,1,0:T(8,128)(2,1)S(1)} %collective-permute-done.12.b_ref, bf16[8,16,768]{2,1,0:T(8,128)(2,1)S(1)} %collective-permute-done.13.c_ref, ...), custom_call_target="tpu_custom_call" | custom-call | flops 452984832 | bytes 1466368 | tf_op jit(solution)/shard_map/pallas_call | solution.py:32
  75.0 1.1 %collective-permute-start.18 = (bf16[8,16,512]{2,1,0:T(8,128)(2,1)S(1)}, bf16[8,16,512]{2,1,0:T(8,128)(2,1)S(1)}, u32[]{:S(2)}, u32[]{:S(2)}) collective-permute-start(bf16[8,16,512]{2,1,0:T(8,128)(2,1)S(1)} %get-tuple-element.48), channel_id=1, source_target_pairs={{0,12},{4,0},{8,4},{12,8},{16,20},{20,24},{24,28},{28,16},{1,13},{... | collective-permute-start | bytes 393224 | tf_op jit(solution)/shard_map/ppermute | solution.py:236
  76.1 2.5 %collective-permute-start.17 = (bf16[8,16,512]{2,1,0:T(8,128)(2,1)S(1)}, bf16[8,16,512]{2,1,0:T(8,128)(2,1)S(1)}, u32[]{:S(2)}, u32[]{:S(2)}) collective-permute-start(bf16[8,16,512]{2,1,0:T(8,128)(2,1)S(1)} %get-tuple-element.46), channel_id=1, source_target_pairs={{0,4},{4,8},{8,12},{12,0},{16,28},{20,16},{24,20},{28,24},{1,5},{5... | collective-permute-start | bytes 393224 | tf_op jit(solution)/shard_map/ppermute | solution.py:237
  78.6 0.9 shard_map.72
  79.5 5.6 %collective-permute-done.18.b_ref = bf16[8,16,512]{2,1,0:T(8,128)(2,1)S(1)} collective-permute-done((bf16[8,16,512]{2,1,0:T(8,128)(2,1)S(1)}, bf16[8,16,512]{2,1,0:T(8,128)(2,1)S(1)}, u32[]{:S(2)}, u32[]{:S(2)}) %collective-permute-start.18) | collective-permute-done | bytes 131104 | tf_op jit(solution)/shard_map/ppermute | solution.py:236
  85.1 0.1 collective-permute-start.19
  85.2 6.6 %collective-permute-done.19.c_ref = bf16[8,16,512]{2,1,0:T(8,128)(2,1)S(1)} collective-permute-done((bf16[8,16,512]{2,1,0:T(8,128)(2,1)S(1)}, bf16[8,16,512]{2,1,0:T(8,128)(2,1)S(1)}, u32[]{:S(2)}, u32[]{:S(2)}) %collective-permute-start.19) | collective-permute-done | bytes 131104 | tf_op jit(solution)/shard_map/ppermute | solution.py:242
  91.8 0.1 broadcast_in_dim.15.bias_ref
  91.9 0.7 shard_map.74
  (27 shorter events, 0.2 us)
Async XLA Ops:
  2.3 22.1 %collective-permute-start = (bf16[8,16,768]{2,1,0:T(8,128)(2,1)}, bf16[8,16,768]{2,1,0:T(8,128)(2,1)S(1)}, u32[]{:S(2)}, u32[]{:S(2)}) collective-permute-start(bf16[8,16,768]{2,1,0:T(8,128)(2,1)} %get-tuple-element.27.a_ref), channel_id=1, source_target_pairs={{0,1},{1,0},{2,3},{3,2},{4,5},{5,4},{6,7},{7,6},{8,9},{9,8},{10,11... | collective-permute-start | bytes 589832 | tf_op jit(solution)/shard_map/ppermute | solution.py:267
  2.6 21.8 %collective-permute-start.1 = (bf16[8,16,768]{2,1,0:T(8,128)(2,1)}, bf16[8,16,768]{2,1,0:T(8,128)(2,1)S(1)}, u32[]{:S(2)}, u32[]{:S(2)}) collective-permute-start(bf16[8,16,768]{2,1,0:T(8,128)(2,1)} %get-tuple-element.27.a_ref), channel_id=1, source_target_pairs={{0,2},{1,3},{2,0},{3,1},{4,6},{5,7},{6,4},{7,5},{8,10},{9,11},{10,... | collective-permute-start | bytes 589832 | tf_op jit(solution)/shard_map/ppermute | solution.py:267
  4.3 20.1 %collective-permute-start.2 = (bf16[8,16,768]{2,1,0:T(8,128)(2,1)}, bf16[8,16,768]{2,1,0:T(8,128)(2,1)S(1)}, u32[]{:S(2)}, u32[]{:S(2)}) collective-permute-start(bf16[8,16,768]{2,1,0:T(8,128)(2,1)} %get-tuple-element.27.a_ref), channel_id=1, source_target_pairs={{0,3},{1,2},{2,1},{3,0},{4,7},{5,6},{6,5},{7,4},{8,11},{9,10},{10,... | collective-permute-start | bytes 589832 | tf_op jit(solution)/shard_map/ppermute | solution.py:267
  5.2 18.0 %collective-permute-start.5 = (bf16[2,3,3,16,192]{4,3,2,1,0:T(8,128)(2,1)}, bf16[2,3,3,16,192]{4,3,2,1,0:T(8,128)(2,1)S(1)}, u32[]{:S(2)}, u32[]{:S(2)}) collective-permute-start(bf16[2,3,3,16,192]{4,3,2,1,0:T(8,128)(2,1)} %get-tuple-element.31), channel_id=1, source_target_pairs={{0,4},{4,8},{8,12},{12,0},{16,28},{20,16},{24,20},{28,24},{1,5},{5... | collective-permute-start | bytes 331784 | tf_op jit(solution)/shard_map/ppermute | solution.py:291
  11.1 17.7 %collective-permute-start.7 = (bf16[3,3,16,192]{3,2,1,0:T(8,128)(2,1)}, bf16[3,3,16,192]{3,2,1,0:T(8,128)(2,1)S(1)}, u32[]{:S(2)}, u32[]{:S(2)}) collective-permute-start(bf16[3,3,16,192]{3,2,1,0:T(8,128)(2,1)} %get-tuple-element.32), channel_id=1, source_target_pairs={{0,8},{4,12},{8,0},{12,4},{1,9},{5,13},{9,1},{13,5},{2,10},{6,14},... | collective-permute-start | bytes 165896 | tf_op jit(solution)/shard_map/ppermute | solution.py:292
  12.0 12.5 %copy-start.2 = (bf16[8,16,768]{2,1,0:T(8,128)(2,1)S(1)}, bf16[8,16,768]{2,1,0:T(8,128)(2,1)}, u32[]{:S(2)}) copy-start(bf16[8,16,768]{2,1,0:T(8,128)(2,1)} %get-tuple-element.27.a_ref) | copy-start | bytes 589828
  12.0 22.3 %all-to-all-start = ((f32[64,8,128]{2,1,0:T(8,128)}), f32[64,8,128]{2,1,0:T(8,128)S(1)}, u32[]{:S(2)}, u32[]{:S(2)}) async-start(f32[64,8,128]{2,1,0:T(8,128)} %get-tuple-element.30), calls=%async_computation | async-start | bytes 524288 | tf_op jit(solution)/shard_map/all_to_all | solution.py:271
  23.2 7.0 %collective-permute-start.6 = (bf16[2,3,3,16,192]{4,3,2,1,0:T(8,128)(2,1)S(1)}, bf16[2,3,3,16,192]{4,3,2,1,0:T(8,128)(2,1)S(1)}, u32[]{:S(2)}, u32[]{:S(2)}) collective-permute-start(bf16[2,3,3,16,192]{4,3,2,1,0:T(8,128)(2,1)S(1)} %collective-permute-done.5.side_ref), channel_id=1, source_target_pairs={{0,16},{16,0},{1,17},{17,1},{2,18},{18,2},{3,19},{19,3},{4,20},{20... | collective-permute-start | bytes 331784 | tf_op jit(solution)/shard_map/ppermute | solution.py:297
  24.5 5.7 %collective-permute-start.3 = (bf16[4,16,768]{2,1,0:T(8,128)(2,1)S(1)}, bf16[4,16,768]{2,1,0:T(8,128)(2,1)S(1)}, u32[]{:S(2)}, u32[]{:S(2)}) collective-permute-start(bf16[4,16,768]{2,1,0:T(8,128)(2,1)S(1)} %get-tuple-element.28), channel_id=1, source_target_pairs={{0,16},{16,0},{32,48},{48,32},{64,80},{80,64},{96,112},{112,96},{1... | collective-permute-start | bytes 294920 | tf_op jit(solution)/shard_map/ppermute | solution.py:260
  24.6 14.9 %copy-start.3 = (bf16[2,3,3,16,192]{4,3,2,1,0:T(8,128)(2,1)S(1)}, bf16[2,3,3,16,192]{4,3,2,1,0:T(8,128)(2,1)}, u32[]{:S(2)}) copy-start(bf16[2,3,3,16,192]{4,3,2,1,0:T(8,128)(2,1)} %get-tuple-element.34.own_ref) | copy-start | bytes 331780
  24.6 9.7 %collective-permute-start.4 = (bf16[4,16,768]{2,1,0:T(8,128)(2,1)S(1)}, bf16[4,16,768]{2,1,0:T(8,128)(2,1)S(1)}, u32[]{:S(2)}, u32[]{:S(2)}) collective-permute-start(bf16[4,16,768]{2,1,0:T(8,128)(2,1)S(1)} %get-tuple-element.29), channel_id=1, source_target_pairs={{16,32},{48,64},{80,96},{112,128},{144,160},{176,192},{208,224},{3... | collective-permute-start | bytes 294920 | tf_op jit(solution)/shard_map/ppermute | solution.py:262
  28.8 1.4 %collective-permute-start.8 = (bf16[3,3,16,192]{3,2,1,0:T(8,128)(2,1)S(1)}, bf16[3,3,16,192]{3,2,1,0:T(8,128)(2,1)S(1)}, u32[]{:S(2)}, u32[]{:S(2)}) collective-permute-start(bf16[3,3,16,192]{3,2,1,0:T(8,128)(2,1)S(1)} %collective-permute-done.7.far_ref), channel_id=1, source_target_pairs={{0,16},{16,0},{1,17},{17,1},{2,18},{18,2},{3,19},{19,3},{4,20},{20... | collective-permute-start | bytes 165896 | tf_op jit(solution)/shard_map/ppermute | solution.py:297
  35.8 9.0 %collective-permute-start.10 = (bf16[8,16,512]{2,1,0:T(8,128)(2,1)S(1)}, bf16[8,16,512]{2,1,0:T(8,128)(2,1)S(1)}, u32[]{:S(2)}, u32[]{:S(2)}) collective-permute-start(bf16[8,16,512]{2,1,0:T(8,128)(2,1)S(1)} %get-tuple-element.38), channel_id=1, source_target_pairs={{0,12},{4,0},{8,4},{12,8},{16,20},{20,24},{24,28},{28,16},{1,13},{... | collective-permute-start | bytes 393224 | tf_op jit(solution)/shard_map/ppermute | solution.py:236
  35.9 10.3 %collective-permute-start.9 = (bf16[8,16,512]{2,1,0:T(8,128)(2,1)S(1)}, bf16[8,16,512]{2,1,0:T(8,128)(2,1)S(1)}, u32[]{:S(2)}, u32[]{:S(2)}) collective-permute-start(bf16[8,16,512]{2,1,0:T(8,128)(2,1)S(1)} %get-tuple-element.36), channel_id=1, source_target_pairs={{0,4},{4,8},{8,12},{12,0},{16,28},{20,16},{24,20},{28,24},{1,5},{5... | collective-permute-start | bytes 393224 | tf_op jit(solution)/shard_map/ppermute | solution.py:237
  44.8 0.7 copy-start.6
  44.8 7.1 %copy-start.1 = (bf16[8,16,256]{2,1,0:T(8,128)(2,1)S(1)}, bf16[8,16,256]{2,1,0:T(8,128)(2,1)}, u32[]{:S(2)}) copy-start(bf16[8,16,256]{2,1,0:T(8,128)(2,1)} %get-tuple-element.39.later_ref) | copy-start | bytes 196612
  44.8 0.7 copy-start.4
  44.8 7.0 %collective-permute-start.11 = (bf16[8,16,512]{2,1,0:T(8,128)(2,1)S(1)}, bf16[8,16,512]{2,1,0:T(8,128)(2,1)S(1)}, u32[]{:S(2)}, u32[]{:S(2)}) collective-permute-start(bf16[8,16,512]{2,1,0:T(8,128)(2,1)S(1)} %shard_map.68), channel_id=1, source_target_pairs={{0,12},{4,0},{8,4},{12,8},{16,20},{20,24},{24,28},{28,16},{1,13},{... | collective-permute-start | bytes 393224 | tf_op jit(solution)/shard_map/ppermute | solution.py:242
  45.5 0.7 copy-start.5
  52.8 10.7 %collective-permute-start.12 = (bf16[8,16,768]{2,1,0:T(8,128)(2,1)S(1)}, bf16[8,16,768]{2,1,0:T(8,128)(2,1)S(1)}, u32[]{:S(2)}, u32[]{:S(2)}) collective-permute-start(bf16[8,16,768]{2,1,0:T(8,128)(2,1)S(1)} %get-tuple-element.40.a_ref), channel_id=1, source_target_pairs={{0,1},{1,0},{2,3},{3,2},{4,5},{5,4},{6,7},{7,6},{8,9},{9,8},{10,11... | collective-permute-start | bytes 589832 | tf_op jit(solution)/shard_map/ppermute | solution.py:267
  53.5 9.9 %collective-permute-start.13 = (bf16[8,16,768]{2,1,0:T(8,128)(2,1)S(1)}, bf16[8,16,768]{2,1,0:T(8,128)(2,1)S(1)}, u32[]{:S(2)}, u32[]{:S(2)}) collective-permute-start(bf16[8,16,768]{2,1,0:T(8,128)(2,1)S(1)} %get-tuple-element.40.a_ref), channel_id=1, source_target_pairs={{0,2},{1,3},{2,0},{3,1},{4,6},{5,7},{6,4},{7,5},{8,10},{9,11},{10,... | collective-permute-start | bytes 589832 | tf_op jit(solution)/shard_map/ppermute | solution.py:267
  55.3 8.2 %collective-permute-start.14 = (bf16[8,16,768]{2,1,0:T(8,128)(2,1)S(1)}, bf16[8,16,768]{2,1,0:T(8,128)(2,1)S(1)}, u32[]{:S(2)}, u32[]{:S(2)}) collective-permute-start(bf16[8,16,768]{2,1,0:T(8,128)(2,1)S(1)} %get-tuple-element.40.a_ref), channel_id=1, source_target_pairs={{0,3},{1,2},{2,1},{3,0},{4,7},{5,6},{6,5},{7,4},{8,11},{9,10},{10,... | collective-permute-start | bytes 589832 | tf_op jit(solution)/shard_map/ppermute | solution.py:267
  56.4 17.0 %all-to-all-start.1 = ((f32[64,8,128]{2,1,0:T(8,128)}), f32[64,8,128]{2,1,0:T(8,128)S(1)}, u32[]{:S(2)}, u32[]{:S(2)}) async-start(f32[64,8,128]{2,1,0:T(8,128)} %get-tuple-element.43), calls=%async_computation.1 | async-start | bytes 524288 | tf_op jit(solution)/shard_map/all_to_all | solution.py:271
  63.5 4.2 %collective-permute-start.15 = (bf16[4,16,768]{2,1,0:T(8,128)(2,1)S(1)}, bf16[4,16,768]{2,1,0:T(8,128)(2,1)S(1)}, u32[]{:S(2)}, u32[]{:S(2)}) collective-permute-start(bf16[4,16,768]{2,1,0:T(8,128)(2,1)S(1)} %get-tuple-element.41), channel_id=1, source_target_pairs={{0,16},{16,0},{32,48},{48,32},{64,80},{80,64},{96,112},{112,96},{1... | collective-permute-start | bytes 294920 | tf_op jit(solution)/shard_map/ppermute | solution.py:260
  63.9 9.5 %collective-permute-start.16 = (bf16[4,16,768]{2,1,0:T(8,128)(2,1)S(1)}, bf16[4,16,768]{2,1,0:T(8,128)(2,1)S(1)}, u32[]{:S(2)}, u32[]{:S(2)}) collective-permute-start(bf16[4,16,768]{2,1,0:T(8,128)(2,1)S(1)} %get-tuple-element.42), channel_id=1, source_target_pairs={{16,32},{48,64},{80,96},{112,128},{144,160},{176,192},{208,224},{3... | collective-permute-start | bytes 294920 | tf_op jit(solution)/shard_map/ppermute | solution.py:262
  75.0 10.1 %collective-permute-start.18 = (bf16[8,16,512]{2,1,0:T(8,128)(2,1)S(1)}, bf16[8,16,512]{2,1,0:T(8,128)(2,1)S(1)}, u32[]{:S(2)}, u32[]{:S(2)}) collective-permute-start(bf16[8,16,512]{2,1,0:T(8,128)(2,1)S(1)} %get-tuple-element.48), channel_id=1, source_target_pairs={{0,12},{4,0},{8,4},{12,8},{16,20},{20,24},{24,28},{28,16},{1,13},{... | collective-permute-start | bytes 393224 | tf_op jit(solution)/shard_map/ppermute | solution.py:236
  76.1 9.1 %collective-permute-start.17 = (bf16[8,16,512]{2,1,0:T(8,128)(2,1)S(1)}, bf16[8,16,512]{2,1,0:T(8,128)(2,1)S(1)}, u32[]{:S(2)}, u32[]{:S(2)}) collective-permute-start(bf16[8,16,512]{2,1,0:T(8,128)(2,1)S(1)} %get-tuple-element.46), channel_id=1, source_target_pairs={{0,4},{4,8},{8,12},{12,0},{16,28},{20,16},{24,20},{28,24},{1,5},{5... | collective-permute-start | bytes 393224 | tf_op jit(solution)/shard_map/ppermute | solution.py:237
  85.1 6.8 %copy-start = (bf16[4,8,16,128]{3,2,1,0:T(8,128)(2,1)S(1)}, bf16[4,8,16,128]{3,2,1,0:T(8,128)(2,1)}, u32[]{:S(2)}) copy-start(bf16[4,8,16,128]{3,2,1,0:T(8,128)(2,1)} %x_ref.1) | copy-start | bytes 393220
  85.1 6.7 %collective-permute-start.19 = (bf16[8,16,512]{2,1,0:T(8,128)(2,1)S(1)}, bf16[8,16,512]{2,1,0:T(8,128)(2,1)S(1)}, u32[]{:S(2)}, u32[]{:S(2)}) collective-permute-start(bf16[8,16,512]{2,1,0:T(8,128)(2,1)S(1)} %shard_map.73), channel_id=1, source_target_pairs={{0,12},{4,0},{8,4},{12,8},{16,20},{20,24},{24,28},{28,16},{1,13},{... | collective-permute-start | bytes 393224 | tf_op jit(solution)/shard_map/ppermute | solution.py:242

commit v12 on v11

--- a/solution.py
+++ b/solution.py
@@ -44,7 +44,7 @@
     return lax.axis_index(ROW), lax.axis_index("zh"), lax.axis_index(NEAR)
 
 
-def put_stats(rows_ref, note_ref, stats_ref):
+def put_stats(rows_ref, note_ref):
     slabs = [rows_ref[:, :, 256 + 128 * t : 384 + 128 * t].astype(F32) for t in range(4)]
     x = jnp.concatenate(slabs, axis=0).reshape(32, 2, GROUP, 128)
     number = x.shape[0] * GROUP
@@ -53,6 +53,13 @@
     square = jnp.sum(off * off, axis=(0, 2))
     note_ref[0:2] = mean.reshape(2, 128)
     note_ref[2:4] = square
+
+
+def spread_kernel(a_ref, b_ref, stats_ref, note_ref):
+    note_ref[...] = a_ref[...]
+    off = a_ref[0:2] - b_ref[0:2]
+    note_ref[0:2] = 0.5 * (a_ref[0:2] + b_ref[0:2])
+    note_ref[2:4] = a_ref[2:4] + b_ref[2:4] + (16.0 * GROUP) * (off * off)
     stats_ref[...] = jnp.broadcast_to(note_ref[...][None], stats_ref.shape)
 
 
@@ -66,8 +73,8 @@
 
 def begin_kernel(
     x_hbm, cache_hbm, gain_hbm, shift_hbm, w_hbm,
-    raw_ref, later_ref, stats_ref, own_ref, side_ref, far_ref,
-    x_ref, cache_ref, gain_ref, shift_ref, w_ref, note_ref, pieces_ref, sems,
+    raw_ref, later_ref, note_ref, own_ref, side_ref, far_ref,
+    x_ref, cache_ref, gain_ref, shift_ref, w_ref, pieces_ref, sems,
 ):
     fetch(
         (
@@ -100,7 +107,7 @@
     note_ref[...] = jnp.zeros((8, 128), F32)
     note_ref[4:5, 0:16] = gain_ref[0:1, :]
     note_ref[5:6, 0:16] = shift_ref[0:1, :]
-    put_stats(raw_ref, note_ref, stats_ref)
+    put_stats(raw_ref, note_ref)
 
 
 def shift_columns(left, centre, right):
@@ -112,13 +119,13 @@
 
 
 def get_affine(stats_ref, affine_ref):
-    stats = stats_ref[...].reshape(16, 4, 8, 128)
-    number = 32 * GROUP
+    stats = stats_ref[...].reshape(8, 4, 8, 128)
+    number = 64 * GROUP
     means = stats[:, :, 0:2]
     mean = jnp.mean(means, axis=(0, 3), keepdims=True)
     off = means - mean
     total = jnp.sum(stats[:, :, 2:4] + number * (off * off), axis=(0, 3), keepdims=True)
-    inverse = lax.rsqrt(total / (number * 16 * 128) + EPS)
+    inverse = lax.rsqrt(total / (number * 8 * 128) + EPS)
     mean = jnp.broadcast_to(mean.reshape(4, 2, 1, 1), (4, 2, GROUP, 128)).reshape(4, 16, 128)
     inverse = jnp.broadcast_to(inverse.reshape(4, 2, 1, 1), (4, 2, GROUP, 128)).reshape(4, 16, 128)
     shape = (4, 16, 128)
@@ -197,14 +204,14 @@
     products(layer, w_refs, (o2_ref, o3_ref), slab_ref)
 
 
-def merge_kernel(a_ref, b_ref, c_ref, bias_ref, later_ref, note1_ref, mid_ref, stats_ref, note_ref):
+def merge_kernel(a_ref, b_ref, c_ref, bias_ref, later_ref, note1_ref, mid_ref, note_ref):
     bias = jnp.concatenate([bias_ref[...]] * 4, axis=1)
     for r in range(8):
         summed = a_ref[r].astype(F32) + b_ref[r].astype(F32) + c_ref[r].astype(F32)
         mid_ref[r, :, 0:256] = later_ref[r]
         mid_ref[r, :, 256:768] = (summed + bias).astype(BF16)
     note_ref[...] = note1_ref[...]
-    put_stats(mid_ref, note_ref, stats_ref)
+    put_stats(mid_ref, note_ref)
 
 
 def last_kernel(x_ref, a_ref, b_ref, c_ref, bias_ref, o_ref):
@@ -217,6 +224,12 @@
             o_ref[t, r] = (x_ref[t, r].astype(F32) + (branch + bias)).astype(BF16)
 
 
+def all_stats(note):
+    other = lax.ppermute(note, "core", [(0, 1), (1, 0)])
+    return exchange(call(spread_kernel, struct((32, 8, 128), F32), note, other,
+                         scratch=(pltpu.VMEM((8, 128), F32),)), ("xh", "y") + NEAR)
+
+
 def sides(step):
     return [(i, (i + step) % 4) for i in range(4)] + [(4 + i, 4 + (i - step) % 4) for i in range(4)]
 
@@ -272,26 +285,26 @@
 
 
 def local(frames, cache, norm_gain, norm_shift, conv_weight, conv_bias):
-    note = pltpu.VMEM((8, 128), F32)
+    note = struct((8, 128), F32)
     piece = (2, 3, 3, 16, 192)
     raw, later, stats, own, side, far = call(
         begin_kernel,
         (
-            struct((8, 16, 768)), struct((8, 16, 256)), struct((64, 8, 128), F32), struct(piece),
+            struct((8, 16, 768)), struct((8, 16, 256)), note, struct(piece),
             struct(piece), struct(piece[1:]),
         ),
         frames, cache, norm_gain, norm_shift, conv_weight.transpose(0, 2, 1, 3),
         scratch=(
             pltpu.VMEM((4, 8, 16, 128), BF16), pltpu.VMEM((2, 2, 8, 16, 128), BF16),
             pltpu.VMEM((2, 16), F32), pltpu.VMEM((2, 16), F32), pltpu.VMEM((2, 27, 16, 256), BF16),
-            note, pltpu.VMEM((4,) + piece, BF16), pltpu.SemaphoreType.DMA((5,)),
+            pltpu.VMEM((4,) + piece, BF16), pltpu.SemaphoreType.DMA((5,)),
         ),
         far=(0, 1, 2, 3, 4),
     )
     side = lax.ppermute(side, ("core", "zh"), sides(1))
     far = lax.ppermute(far, "zh", [(i, (i + 2) % 4) for i in range(4)])
     raw = near(raw)
-    stats = exchange(stats, ROW + NEAR)
+    stats = all_stats(stats)
     raw = raw + rows_beside(raw)
     swap = [(0, 1), (1, 0)]
     weights = [own, side, far, lax.ppermute(side, "core", swap), lax.ppermute(far, "core", swap)]
@@ -299,11 +312,10 @@
     note1 = jnp.pad(jnp.stack([norm_gain[1], norm_shift[1]]), ((4, 2), (0, 112)))
     partial = convolve(0, [*raw, stats], *weights)
     middle, stats = call(
-        merge_kernel, (struct((8, 16, 768)), struct((64, 8, 128), F32)), *partial, bias[0], later, note1,
-        scratch=(note,),
+        merge_kernel, (struct((8, 16, 768)), note), *partial, bias[0], later, note1
     )
     middle = near(middle)
-    stats = exchange(stats, ROW + NEAR)
+    stats = all_stats(stats)
     middle = middle + rows_beside(middle)
     partial = convolve(1, [*middle, stats], *weights)
     return call(last_kernel, struct((4, 8, 16, 128)), frames, *partial, bias[1])

time: 93.6 us -> 94.9 us (1.014)
  waiting for transfers between devices: 33.3 us -> 35.9 us
  starting transfers between devices: 48.8 us -> 47.1 us
    all_to_all x2, starting transfers between devices: 18.2 us -> 13.4 us  [exchange(): return lax.all_to_all(x, axes, 0, 0, tiled=True)]
    ppermute x1, starting transfers between devices: 0.89 us -> 3.53 us  [local(): far = lax.ppermute(far, 'zh', [(i, (i + 2) % 4) for i in range(4)])]
    ppermute x0 -> x2, waiting for transfers between devices: none -> 2.33 us  [all_stats(): other = lax.ppermute(note, 'core', [(0, 1), (1, 0)])]
    ppermute x2, waiting for transfers between devices: 10 us -> 11.3 us  [convolve(): far = lax.ppermute(far, ('core', 'zh'), sides(-1))]
    ppermute x2, waiting for transfers between devices: 12.2 us -> 10.9 us  [convolve(): side = lax.ppermute(side, ('core', 'zh'), sides(-1))]
    ppermute x2, starting transfers between devices: 1.19 us -> 0.17 us  [convolve(): far = lax.ppermute(far, ('core', 'zh'), sides(-1))]
    ppermute x2, starting transfers between devices: 6.11 us -> 7.12 us  [convolve(): other = lax.ppermute(other, ('core', 'zh'), sides(1))]
    pallas_call x11 -> x13, Pallas kernels: 8.81 us -> 9.28 us  [call(): pl.pallas_call(kernel, out_shape=outs, in_specs=specs, out_specs=jax.tree...]
  transfers between devices with their start and end apart: 22 -> 24, of which waited for: 7 -> 10; matrix products, arithmetic and copies ran while one was open for 0% -> 0% of each run, Pallas kernels for 2% -> 3%
where the time goes in v12:
time: 94.9 us; the launch traced here: 93.9 us
  starting transfers between devices  47.1 us (50%)
  waiting for transfers between devices  35.9 us (38%)
  Pallas kernels  9.28 us (10%)
  local copies, waits for them, and re-layouts  1.45 us (2%)
    all_to_all x2, starting transfers between devices, exchange(): return lax.all_to_all(x, axes, 0, 0, tiled=True)  13.4 us
    ppermute x2, waiting for transfers between devices, convolve(): far = lax.ppermute(far, ('core', 'zh'), sides(-1))  11.3 us
    ppermute x2, waiting for transfers between devices, convolve(): side = lax.ppermute(side, ('core', 'zh'), sides(-1))  10.9 us
    ppermute x2, waiting for transfers between devices, rows_beside(): beyond = lax.ppermute(beyond, ROW, pairs)  9.58 us
    pallas_call x13, Pallas kernels, call(): pl.pallas_call(kernel, out_shape=outs, in_specs=specs, out_specs=jax.tree...  9.28 us
    ppermute x2, starting transfers between devices, rows_beside(): beyond = lax.ppermute(beyond, ROW, pairs)  7.78 us
    ppermute x2, starting transfers between devices, convolve(): other = lax.ppermute(other, ('core', 'zh'), sides(1))  7.12 us
    ppermute x6, starting transfers between devices, near(): lax.ppermute(x, NEAR, [(i, i ^ k) for i in range(4)])  6.78 us
  transfers between devices with their start and end apart: 24, of which 10 were waited for; matrix products, arithmetic and copies ran while one was open for 0% of the time, Pallas kernels for 3%

profile of v12, /device:TPU:27, one launch (start us, length us, event | category | flops | bytes accessed | tf_op | source)
XLA Modules:
  0.0 93.9 jit_solution(17861592081946030985)
XLA Ops:
  0.0 2.2 %shard_map.64 = (bf16[8,16,768]{2,1,0:T(8,128)(2,1)}, bf16[8,16,256]{2,1,0:T(8,128)(2,1)}, f32[8,128]{1,0:T(8,128)}, bf16[2,3,3,16,192]{4,3,2,1,0:T(8,128)(2,1)}...) custom-call(bf16[4,8,16,128]{3,2,1,0:T(8,128)(2,1)} %x_ref.1, ...), custom_call_target="tpu_custom_call" | custom-call | bytes 704768 | tf_op jit(solution)/shard_map/pallas_call | solution.py:32
  2.2 0.0 copy-start.2
  2.2 0.3 collective-permute-start
  2.6 1.6 %collective-permute-start.1 = (bf16[8,16,768]{2,1,0:T(8,128)(2,1)}, bf16[8,16,768]{2,1,0:T(8,128)(2,1)S(1)}, u32[]{:S(2)}, u32[]{:S(2)}) collective-permute-start(bf16[8,16,768]{2,1,0:T(8,128)(2,1)} %get-tuple-element.27.a_ref), channel_id=1, source_target_pairs={{0,2},{1,3},{2,0},{3,1},{4,6},{5,7},{6,4},{7,5},{8,10},{9,11},{10,... | collective-permute-start | bytes 589832 | tf_op jit(solution)/shard_map/ppermute | solution.py:280
  4.2 0.9 collective-permute-start.2
  5.1 5.8 %collective-permute-start.6 = (bf16[2,3,3,16,192]{4,3,2,1,0:T(8,128)(2,1)}, bf16[2,3,3,16,192]{4,3,2,1,0:T(8,128)(2,1)S(1)}, u32[]{:S(2)}, u32[]{:S(2)}) collective-permute-start(bf16[2,3,3,16,192]{4,3,2,1,0:T(8,128)(2,1)} %get-tuple-element.31), channel_id=1, source_target_pairs={{0,4},{4,8},{8,12},{12,0},{16,28},{20,16},{24,20},{28,24},{1,5},{5... | collective-permute-start | bytes 331784 | tf_op jit(solution)/shard_map/ppermute | solution.py:304
  11.0 1.2 %collective-permute-done.5.b_ref = f32[8,128]{1,0:T(8,128)S(1)} collective-permute-done((f32[8,128]{1,0:T(8,128)S(1)}, f32[8,128]{1,0:T(8,128)S(1)}, u32[]{:S(2)}, u32[]{:S(2)}) %collective-permute-start.5) | collective-permute-done | bytes 4128 | tf_op jit(solution)/shard_map/ppermute | solution.py:228
  12.2 3.5 %collective-permute-start.8 = (bf16[3,3,16,192]{3,2,1,0:T(8,128)(2,1)}, bf16[3,3,16,192]{3,2,1,0:T(8,128)(2,1)S(1)}, u32[]{:S(2)}, u32[]{:S(2)}) collective-permute-start(bf16[3,3,16,192]{3,2,1,0:T(8,128)(2,1)} %get-tuple-element.32), channel_id=1, source_target_pairs={{0,8},{4,12},{8,0},{12,4},{1,9},{5,13},{9,1},{13,5},{2,10},{6,14},... | collective-permute-start | bytes 165896 | tf_op jit(solution)/shard_map/ppermute | solution.py:305
  15.7 0.7 shard_map.66
  16.4 7.2 %all-to-all-start = ((f32[32,8,128]{2,1,0:T(8,128)}), f32[32,8,128]{2,1,0:T(8,128)S(1)}, u32[]{:S(2)}, u32[]{:S(2)}) async-start(f32[32,8,128]{2,1,0:T(8,128)} %shard_map.66), calls=%async_computation | async-start | bytes 262144 | tf_op jit(solution)/shard_map/all_to_all | solution.py:284
  23.6 1.3 %collective-permute-start.7 = (bf16[2,3,3,16,192]{4,3,2,1,0:T(8,128)(2,1)S(1)}, bf16[2,3,3,16,192]{4,3,2,1,0:T(8,128)(2,1)S(1)}, u32[]{:S(2)}, u32[]{:S(2)}) collective-permute-start(bf16[2,3,3,16,192]{4,3,2,1,0:T(8,128)(2,1)S(1)} %collective-permute-done.6.side_ref), channel_id=1, source_target_pairs={{0,16},{16,0},{1,17},{17,1},{2,18},{18,2},{3,19},{19,3},{4,20},{20... | collective-permute-start | bytes 331784 | tf_op jit(solution)/shard_map/ppermute | solution.py:310
  24.9 0.1 collective-permute-start.3
  25.0 4.2 %collective-permute-start.4 = (bf16[4,16,768]{2,1,0:T(8,128)(2,1)S(1)}, bf16[4,16,768]{2,1,0:T(8,128)(2,1)S(1)}, u32[]{:S(2)}, u32[]{:S(2)}) collective-permute-start(bf16[4,16,768]{2,1,0:T(8,128)(2,1)S(1)} %get-tuple-element.29), channel_id=1, source_target_pairs={{16,32},{48,64},{80,96},{112,128},{144,160},{176,192},{208,224},{3... | collective-permute-start | bytes 294920 | tf_op jit(solution)/shard_map/ppermute | solution.py:275
  29.2 0.1 collective-permute-start.9
  29.3 1.3 %collective-permute-done.9.far2_ref = bf16[3,3,16,192]{3,2,1,0:T(8,128)(2,1)S(1)} collective-permute-done((bf16[3,3,16,192]{3,2,1,0:T(8,128)(2,1)S(1)}, bf16[3,3,16,192]{3,2,1,0:T(8,128)(2,1)S(1)}, u32[]{:S(2)}, u32[]{:S(2)}) %collective-permute-start.9) | collective-permute-done | bytes 55328 | tf_op jit(solution)/shard_map/ppermute | solution.py:310
  30.6 4.1 %collective-permute-done.4.next_ref = bf16[4,16,768]{2,1,0:T(8,128)(2,1)S(1)} collective-permute-done((bf16[4,16,768]{2,1,0:T(8,128)(2,1)S(1)}, bf16[4,16,768]{2,1,0:T(8,128)(2,1)S(1)}, u32[]{:S(2)}, u32[]{:S(2)}) %collective-permute-start.4) | collective-permute-done | bytes 98336 | tf_op jit(solution)/shard_map/ppermute | solution.py:275
  34.7 1.5 %shard_map.67 = (bf16[8,16,512]{2,1,0:T(8,128)(2,1)S(1)}, bf16[8,16,512]{2,1,0:T(8,128)(2,1)S(1)}, bf16[10,4,16,768]{3,2,1,0:T(8,128)(2,1)S(1)}) custom-call(bf16[8,16,768]{2,1,0:T(8,128)(2,1)S(1)} %copy-done.3, bf16[8,16,768]{2,1,0:T(8,128)(2,1)S(1)} %collective-permute-done.b_ref, bf16[8,16,768]{2,1,0:T(8,128)(2,1)S(1)} %collective-permute-done.1.c_ref, ...), custom_call_target="tpu_custom_call" | custom-call | flops 452984832 | bytes 1335296 | tf_op jit(solution)/shard_map/pallas_call | solution.py:32
  36.2 0.1 collective-permute-start.11
  36.3 3.6 %collective-permute-start.10 = (bf16[8,16,512]{2,1,0:T(8,128)(2,1)S(1)}, bf16[8,16,512]{2,1,0:T(8,128)(2,1)S(1)}, u32[]{:S(2)}, u32[]{:S(2)}) collective-permute-start(bf16[8,16,512]{2,1,0:T(8,128)(2,1)S(1)} %get-tuple-element.36), channel_id=1, source_target_pairs={{0,4},{4,8},{8,12},{12,0},{16,28},{20,16},{24,20},{28,24},{1,5},{5... | collective-permute-start | bytes 393224 | tf_op jit(solution)/shard_map/ppermute | solution.py:250
  39.9 0.9 shard_map.68
  40.7 5.8 %collective-permute-done.11.b_ref = bf16[8,16,512]{2,1,0:T(8,128)(2,1)S(1)} collective-permute-done((bf16[8,16,512]{2,1,0:T(8,128)(2,1)S(1)}, bf16[8,16,512]{2,1,0:T(8,128)(2,1)S(1)}, u32[]{:S(2)}, u32[]{:S(2)}) %collective-permute-start.11) | collective-permute-done | bytes 131104 | tf_op jit(solution)/shard_map/ppermute | solution.py:249
  46.5 0.0 copy-start.5
  46.6 0.1 collective-permute-start.12
  46.6 0.5 copy-done.7
  47.2 0.1 copy-done.5
  47.3 0.7 copy-done.6
  48.0 4.7 %collective-permute-done.12.c_ref = bf16[8,16,512]{2,1,0:T(8,128)(2,1)S(1)} collective-permute-done((bf16[8,16,512]{2,1,0:T(8,128)(2,1)S(1)}, bf16[8,16,512]{2,1,0:T(8,128)(2,1)S(1)}, u32[]{:S(2)}, u32[]{:S(2)}) %collective-permute-start.12) | collective-permute-done | bytes 131104 | tf_op jit(solution)/shard_map/ppermute | solution.py:255
  52.7 0.1 broadcast_in_dim.13.bias_ref
  52.7 0.1 shard_map.70
  52.9 0.4 collective-permute-start.13
  53.2 2.6 %collective-permute-start.14 = (bf16[8,16,768]{2,1,0:T(8,128)(2,1)S(1)}, bf16[8,16,768]{2,1,0:T(8,128)(2,1)S(1)}, u32[]{:S(2)}, u32[]{:S(2)}) collective-permute-start(bf16[8,16,768]{2,1,0:T(8,128)(2,1)S(1)} %get-tuple-element.40.a_ref), channel_id=1, source_target_pairs={{0,2},{1,3},{2,0},{3,1},{4,6},{5,7},{6,4},{7,5},{8,10},{9,11},{10,... | collective-permute-start | bytes 589832 | tf_op jit(solution)/shard_map/ppermute | solution.py:280
  55.8 0.9 collective-permute-start.15
  56.7 1.2 %collective-permute-done.18.b_ref = f32[8,128]{1,0:T(8,128)S(1)} collective-permute-done((f32[8,128]{1,0:T(8,128)S(1)}, f32[8,128]{1,0:T(8,128)S(1)}, u32[]{:S(2)}, u32[]{:S(2)}) %collective-permute-start.18) | collective-permute-done | bytes 4128 | tf_op jit(solution)/shard_map/ppermute | solution.py:228
  57.9 0.7 shard_map.72
  58.6 6.2 %all-to-all-start.1 = ((f32[32,8,128]{2,1,0:T(8,128)}), f32[32,8,128]{2,1,0:T(8,128)S(1)}, u32[]{:S(2)}, u32[]{:S(2)}) async-start(f32[32,8,128]{2,1,0:T(8,128)} %shard_map.72), calls=%async_computation.1 | async-start | bytes 262144 | tf_op jit(solution)/shard_map/all_to_all | solution.py:284
  64.9 0.8 collective-permute-start.16
  65.7 3.6 %collective-permute-start.17 = (bf16[4,16,768]{2,1,0:T(8,128)(2,1)S(1)}, bf16[4,16,768]{2,1,0:T(8,128)(2,1)S(1)}, u32[]{:S(2)}, u32[]{:S(2)}) collective-permute-start(bf16[4,16,768]{2,1,0:T(8,128)(2,1)S(1)} %get-tuple-element.42), channel_id=1, source_target_pairs={{16,32},{48,64},{80,96},{112,128},{144,160},{176,192},{208,224},{3... | collective-permute-start | bytes 294920 | tf_op jit(solution)/shard_map/ppermute | solution.py:275
  69.3 0.5 all-to-all-done.1.stats_ref
  69.7 5.5 %collective-permute-done.17.next_ref = bf16[4,16,768]{2,1,0:T(8,128)(2,1)S(1)} collective-permute-done((bf16[4,16,768]{2,1,0:T(8,128)(2,1)S(1)}, bf16[4,16,768]{2,1,0:T(8,128)(2,1)S(1)}, u32[]{:S(2)}, u32[]{:S(2)}) %collective-permute-start.17) | collective-permute-done | bytes 98336 | tf_op jit(solution)/shard_map/ppermute | solution.py:275
  75.2 1.5 %shard_map.73 = (bf16[8,16,512]{2,1,0:T(8,128)(2,1)S(1)}, bf16[8,16,512]{2,1,0:T(8,128)(2,1)S(1)}, bf16[10,4,16,768]{3,2,1,0:T(8,128)(2,1)S(1)}) custom-call(bf16[8,16,768]{2,1,0:T(8,128)(2,1)S(1)} %get-tuple-element.40.a_ref, bf16[8,16,768]{2,1,0:T(8,128)(2,1)S(1)} %collective-permute-done.13.b_ref, bf16[8,16,768]{2,1,0:T(8,128)(2,1)S(1)} %collective-permute-done.14.c_ref, ...), custom_call_target="tpu_custom_call" | custom-call | flops 452984832 | bytes 1335296 | tf_op jit(solution)/shard_map/pallas_call | solution.py:32
  76.7 0.1 collective-permute-start.20
  76.8 3.6 %collective-permute-start.19 = (bf16[8,16,512]{2,1,0:T(8,128)(2,1)S(1)}, bf16[8,16,512]{2,1,0:T(8,128)(2,1)S(1)}, u32[]{:S(2)}, u32[]{:S(2)}) collective-permute-start(bf16[8,16,512]{2,1,0:T(8,128)(2,1)S(1)} %get-tuple-element.46), channel_id=1, source_target_pairs={{0,4},{4,8},{8,12},{12,0},{16,28},{20,16},{24,20},{28,24},{1,5},{5... | collective-permute-start | bytes 393224 | tf_op jit(solution)/shard_map/ppermute | solution.py:250
  80.4 0.9 shard_map.74
  81.2 5.5 %collective-permute-done.20.b_ref = bf16[8,16,512]{2,1,0:T(8,128)(2,1)S(1)} collective-permute-done((bf16[8,16,512]{2,1,0:T(8,128)(2,1)S(1)}, bf16[8,16,512]{2,1,0:T(8,128)(2,1)S(1)}, u32[]{:S(2)}, u32[]{:S(2)}) %collective-permute-start.20) | collective-permute-done | bytes 131104 | tf_op jit(solution)/shard_map/ppermute | solution.py:249
  86.8 0.1 collective-permute-start.21
  86.9 6.2 %collective-permute-done.21.c_ref = bf16[8,16,512]{2,1,0:T(8,128)(2,1)S(1)} collective-permute-done((bf16[8,16,512]{2,1,0:T(8,128)(2,1)S(1)}, bf16[8,16,512]{2,1,0:T(8,128)(2,1)S(1)}, u32[]{:S(2)}, u32[]{:S(2)}) %collective-permute-start.21) | collective-permute-done | bytes 131104 | tf_op jit(solution)/shard_map/ppermute | solution.py:255
  93.1 0.1 broadcast_in_dim.15.bias_ref
  93.2 0.7 shard_map.76
  (35 shorter events, 0.2 us)
Async XLA Ops:
  2.2 8.8 %copy-start.2 = (f32[8,128]{1,0:T(8,128)S(1)}, f32[8,128]{1,0:T(8,128)}, u32[]{:S(2)}) copy-start(f32[8,128]{1,0:T(8,128)} %get-tuple-element.30.a_ref) | copy-start | bytes 12292
  2.2 22.6 %collective-permute-start = (bf16[8,16,768]{2,1,0:T(8,128)(2,1)}, bf16[8,16,768]{2,1,0:T(8,128)(2,1)S(1)}, u32[]{:S(2)}, u32[]{:S(2)}) collective-permute-start(bf16[8,16,768]{2,1,0:T(8,128)(2,1)} %get-tuple-element.27.a_ref), channel_id=1, source_target_pairs={{0,1},{1,0},{2,3},{3,2},{4,5},{5,4},{6,7},{7,6},{8,9},{9,8},{10,11... | collective-permute-start | bytes 589832 | tf_op jit(solution)/shard_map/ppermute | solution.py:280
  2.6 22.3 %collective-permute-start.1 = (bf16[8,16,768]{2,1,0:T(8,128)(2,1)}, bf16[8,16,768]{2,1,0:T(8,128)(2,1)S(1)}, u32[]{:S(2)}, u32[]{:S(2)}) collective-permute-start(bf16[8,16,768]{2,1,0:T(8,128)(2,1)} %get-tuple-element.27.a_ref), channel_id=1, source_target_pairs={{0,2},{1,3},{2,0},{3,1},{4,6},{5,7},{6,4},{7,5},{8,10},{9,11},{10,... | collective-permute-start | bytes 589832 | tf_op jit(solution)/shard_map/ppermute | solution.py:280
  4.2 20.6 %collective-permute-start.2 = (bf16[8,16,768]{2,1,0:T(8,128)(2,1)}, bf16[8,16,768]{2,1,0:T(8,128)(2,1)S(1)}, u32[]{:S(2)}, u32[]{:S(2)}) collective-permute-start(bf16[8,16,768]{2,1,0:T(8,128)(2,1)} %get-tuple-element.27.a_ref), channel_id=1, source_target_pairs={{0,3},{1,2},{2,1},{3,0},{4,7},{5,6},{6,5},{7,4},{8,11},{9,10},{10,... | collective-permute-start | bytes 589832 | tf_op jit(solution)/shard_map/ppermute | solution.py:280
  5.1 18.4 %collective-permute-start.6 = (bf16[2,3,3,16,192]{4,3,2,1,0:T(8,128)(2,1)}, bf16[2,3,3,16,192]{4,3,2,1,0:T(8,128)(2,1)S(1)}, u32[]{:S(2)}, u32[]{:S(2)}) collective-permute-start(bf16[2,3,3,16,192]{4,3,2,1,0:T(8,128)(2,1)} %get-tuple-element.31), channel_id=1, source_target_pairs={{0,4},{4,8},{8,12},{12,0},{16,28},{20,16},{24,20},{28,24},{1,5},{5... | collective-permute-start | bytes 331784 | tf_op jit(solution)/shard_map/ppermute | solution.py:304
  11.0 1.2 %collective-permute-start.5 = (f32[8,128]{1,0:T(8,128)S(1)}, f32[8,128]{1,0:T(8,128)S(1)}, u32[]{:S(2)}, u32[]{:S(2)}) collective-permute-start(f32[8,128]{1,0:T(8,128)S(1)} %copy-done.2), channel_id=1, source_target_pairs={{0,16},{16,0},{1,17},{17,1},{2,18},{18,2},{3,19},{19,3},{4,20},{20... | collective-permute-start | bytes 12296 | tf_op jit(solution)/shard_map/ppermute | solution.py:228
  12.2 12.7 %copy-start.3 = (bf16[8,16,768]{2,1,0:T(8,128)(2,1)S(1)}, bf16[8,16,768]{2,1,0:T(8,128)(2,1)}, u32[]{:S(2)}) copy-start(bf16[8,16,768]{2,1,0:T(8,128)(2,1)} %get-tuple-element.27.a_ref) | copy-start | bytes 589828
  12.2 17.1 %collective-permute-start.8 = (bf16[3,3,16,192]{3,2,1,0:T(8,128)(2,1)}, bf16[3,3,16,192]{3,2,1,0:T(8,128)(2,1)S(1)}, u32[]{:S(2)}, u32[]{:S(2)}) collective-permute-start(bf16[3,3,16,192]{3,2,1,0:T(8,128)(2,1)} %get-tuple-element.32), channel_id=1, source_target_pairs={{0,8},{4,12},{8,0},{12,4},{1,9},{5,13},{9,1},{13,5},{2,10},{6,14},... | collective-permute-start | bytes 165896 | tf_op jit(solution)/shard_map/ppermute | solution.py:305
  16.4 14.2 %all-to-all-start = ((f32[32,8,128]{2,1,0:T(8,128)}), f32[32,8,128]{2,1,0:T(8,128)S(1)}, u32[]{:S(2)}, u32[]{:S(2)}) async-start(f32[32,8,128]{2,1,0:T(8,128)} %shard_map.66), calls=%async_computation | async-start | bytes 262144 | tf_op jit(solution)/shard_map/all_to_all | solution.py:284
  23.6 7.0 %collective-permute-start.7 = (bf16[2,3,3,16,192]{4,3,2,1,0:T(8,128)(2,1)S(1)}, bf16[2,3,3,16,192]{4,3,2,1,0:T(8,128)(2,1)S(1)}, u32[]{:S(2)}, u32[]{:S(2)}) collective-permute-start(bf16[2,3,3,16,192]{4,3,2,1,0:T(8,128)(2,1)S(1)} %collective-permute-done.6.side_ref), channel_id=1, source_target_pairs={{0,16},{16,0},{1,17},{17,1},{2,18},{18,2},{3,19},{19,3},{4,20},{20... | collective-permute-start | bytes 331784 | tf_op jit(solution)/shard_map/ppermute | solution.py:310
  24.9 5.7 %collective-permute-start.3 = (bf16[4,16,768]{2,1,0:T(8,128)(2,1)S(1)}, bf16[4,16,768]{2,1,0:T(8,128)(2,1)S(1)}, u32[]{:S(2)}, u32[]{:S(2)}) collective-permute-start(bf16[4,16,768]{2,1,0:T(8,128)(2,1)S(1)} %get-tuple-element.28), channel_id=1, source_target_pairs={{0,16},{16,0},{32,48},{48,32},{64,80},{80,64},{96,112},{112,96},{1... | collective-permute-start | bytes 294920 | tf_op jit(solution)/shard_map/ppermute | solution.py:273
  25.0 14.8 %copy-start.4 = (bf16[2,3,3,16,192]{4,3,2,1,0:T(8,128)(2,1)S(1)}, bf16[2,3,3,16,192]{4,3,2,1,0:T(8,128)(2,1)}, u32[]{:S(2)}) copy-start(bf16[2,3,3,16,192]{4,3,2,1,0:T(8,128)(2,1)} %get-tuple-element.34.own_ref) | copy-start | bytes 331780
  25.0 9.7 %collective-permute-start.4 = (bf16[4,16,768]{2,1,0:T(8,128)(2,1)S(1)}, bf16[4,16,768]{2,1,0:T(8,128)(2,1)S(1)}, u32[]{:S(2)}, u32[]{:S(2)}) collective-permute-start(bf16[4,16,768]{2,1,0:T(8,128)(2,1)S(1)} %get-tuple-element.29), channel_id=1, source_target_pairs={{16,32},{48,64},{80,96},{112,128},{144,160},{176,192},{208,224},{3... | collective-permute-start | bytes 294920 | tf_op jit(solution)/shard_map/ppermute | solution.py:275
  29.2 1.4 %collective-permute-start.9 = (bf16[3,3,16,192]{3,2,1,0:T(8,128)(2,1)S(1)}, bf16[3,3,16,192]{3,2,1,0:T(8,128)(2,1)S(1)}, u32[]{:S(2)}, u32[]{:S(2)}) collective-permute-start(bf16[3,3,16,192]{3,2,1,0:T(8,128)(2,1)S(1)} %collective-permute-done.8.far_ref), channel_id=1, source_target_pairs={{0,16},{16,0},{1,17},{17,1},{2,18},{18,2},{3,19},{19,3},{4,20},{20... | collective-permute-start | bytes 165896 | tf_op jit(solution)/shard_map/ppermute | solution.py:310
  36.2 10.3 %collective-permute-start.11 = (bf16[8,16,512]{2,1,0:T(8,128)(2,1)S(1)}, bf16[8,16,512]{2,1,0:T(8,128)(2,1)S(1)}, u32[]{:S(2)}, u32[]{:S(2)}) collective-permute-start(bf16[8,16,512]{2,1,0:T(8,128)(2,1)S(1)} %get-tuple-element.38), channel_id=1, source_target_pairs={{0,12},{4,0},{8,4},{12,8},{16,20},{20,24},{24,28},{28,16},{1,13},{... | collective-permute-start | bytes 393224 | tf_op jit(solution)/shard_map/ppermute | solution.py:249
  36.3 11.7 %collective-permute-start.10 = (bf16[8,16,512]{2,1,0:T(8,128)(2,1)S(1)}, bf16[8,16,512]{2,1,0:T(8,128)(2,1)S(1)}, u32[]{:S(2)}, u32[]{:S(2)}) collective-permute-start(bf16[8,16,512]{2,1,0:T(8,128)(2,1)S(1)} %get-tuple-element.36), channel_id=1, source_target_pairs={{0,4},{4,8},{8,12},{12,0},{16,28},{20,16},{24,20},{28,24},{1,5},{5... | collective-permute-start | bytes 393224 | tf_op jit(solution)/shard_map/ppermute | solution.py:250
  46.5 0.7 copy-start.7
  46.5 6.2 %copy-start.1 = (bf16[8,16,256]{2,1,0:T(8,128)(2,1)S(1)}, bf16[8,16,256]{2,1,0:T(8,128)(2,1)}, u32[]{:S(2)}) copy-start(bf16[8,16,256]{2,1,0:T(8,128)(2,1)} %get-tuple-element.39.later_ref) | copy-start | bytes 196612
  46.5 0.7 copy-start.5
  46.6 6.1 %collective-permute-start.12 = (bf16[8,16,512]{2,1,0:T(8,128)(2,1)S(1)}, bf16[8,16,512]{2,1,0:T(8,128)(2,1)S(1)}, u32[]{:S(2)}, u32[]{:S(2)}) collective-permute-start(bf16[8,16,512]{2,1,0:T(8,128)(2,1)S(1)} %shard_map.69), channel_id=1, source_target_pairs={{0,12},{4,0},{8,4},{12,8},{16,20},{20,24},{24,28},{28,16},{1,13},{... | collective-permute-start | bytes 393224 | tf_op jit(solution)/shard_map/ppermute | solution.py:255
  47.3 0.7 copy-start.6
  52.9 11.9 %collective-permute-start.13 = (bf16[8,16,768]{2,1,0:T(8,128)(2,1)S(1)}, bf16[8,16,768]{2,1,0:T(8,128)(2,1)S(1)}, u32[]{:S(2)}, u32[]{:S(2)}) collective-permute-start(bf16[8,16,768]{2,1,0:T(8,128)(2,1)S(1)} %get-tuple-element.40.a_ref), channel_id=1, source_target_pairs={{0,1},{1,0},{2,3},{3,2},{4,5},{5,4},{6,7},{7,6},{8,9},{9,8},{10,11... | collective-permute-start | bytes 589832 | tf_op jit(solution)/shard_map/ppermute | solution.py:280
  53.2 11.6 %collective-permute-start.14 = (bf16[8,16,768]{2,1,0:T(8,128)(2,1)S(1)}, bf16[8,16,768]{2,1,0:T(8,128)(2,1)S(1)}, u32[]{:S(2)}, u32[]{:S(2)}) collective-permute-start(bf16[8,16,768]{2,1,0:T(8,128)(2,1)S(1)} %get-tuple-element.40.a_ref), channel_id=1, source_target_pairs={{0,2},{1,3},{2,0},{3,1},{4,6},{5,7},{6,4},{7,5},{8,10},{9,11},{10,... | collective-permute-start | bytes 589832 | tf_op jit(solution)/shard_map/ppermute | solution.py:280
  55.8 9.0 %collective-permute-start.15 = (bf16[8,16,768]{2,1,0:T(8,128)(2,1)S(1)}, bf16[8,16,768]{2,1,0:T(8,128)(2,1)S(1)}, u32[]{:S(2)}, u32[]{:S(2)}) collective-permute-start(bf16[8,16,768]{2,1,0:T(8,128)(2,1)S(1)} %get-tuple-element.40.a_ref), channel_id=1, source_target_pairs={{0,3},{1,2},{2,1},{3,0},{4,7},{5,6},{6,5},{7,4},{8,11},{9,10},{10,... | collective-permute-start | bytes 589832 | tf_op jit(solution)/shard_map/ppermute | solution.py:280
  56.7 1.2 %collective-permute-start.18 = (f32[8,128]{1,0:T(8,128)S(1)}, f32[8,128]{1,0:T(8,128)S(1)}, u32[]{:S(2)}, u32[]{:S(2)}) collective-permute-start(f32[8,128]{1,0:T(8,128)S(1)} %get-tuple-element.43.a_ref), channel_id=1, source_target_pairs={{0,16},{16,0},{1,17},{17,1},{2,18},{18,2},{3,19},{19,3},{4,20},{20... | collective-permute-start | bytes 12296 | tf_op jit(solution)/shard_map/ppermute | solution.py:228
  58.6 11.1 %all-to-all-start.1 = ((f32[32,8,128]{2,1,0:T(8,128)}), f32[32,8,128]{2,1,0:T(8,128)S(1)}, u32[]{:S(2)}, u32[]{:S(2)}) async-start(f32[32,8,128]{2,1,0:T(8,128)} %shard_map.72), calls=%async_computation.1 | async-start | bytes 262144 | tf_op jit(solution)/shard_map/all_to_all | solution.py:284
  64.9 4.9 %collective-permute-start.16 = (bf16[4,16,768]{2,1,0:T(8,128)(2,1)S(1)}, bf16[4,16,768]{2,1,0:T(8,128)(2,1)S(1)}, u32[]{:S(2)}, u32[]{:S(2)}) collective-permute-start(bf16[4,16,768]{2,1,0:T(8,128)(2,1)S(1)} %get-tuple-element.41), channel_id=1, source_target_pairs={{0,16},{16,0},{32,48},{48,32},{64,80},{80,64},{96,112},{112,96},{1... | collective-permute-start | bytes 294920 | tf_op jit(solution)/shard_map/ppermute | solution.py:273
  65.7 9.5 %collective-permute-start.17 = (bf16[4,16,768]{2,1,0:T(8,128)(2,1)S(1)}, bf16[4,16,768]{2,1,0:T(8,128)(2,1)S(1)}, u32[]{:S(2)}, u32[]{:S(2)}) collective-permute-start(bf16[4,16,768]{2,1,0:T(8,128)(2,1)S(1)} %get-tuple-element.42), channel_id=1, source_target_pairs={{16,32},{48,64},{80,96},{112,128},{144,160},{176,192},{208,224},{3... | collective-permute-start | bytes 294920 | tf_op jit(solution)/shard_map/ppermute | solution.py:275
  76.7 10.1 %collective-permute-start.20 = (bf16[8,16,512]{2,1,0:T(8,128)(2,1)S(1)}, bf16[8,16,512]{2,1,0:T(8,128)(2,1)S(1)}, u32[]{:S(2)}, u32[]{:S(2)}) collective-permute-start(bf16[8,16,512]{2,1,0:T(8,128)(2,1)S(1)} %get-tuple-element.48), channel_id=1, source_target_pairs={{0,12},{4,0},{8,4},{12,8},{16,20},{20,24},{24,28},{28,16},{1,13},{... | collective-permute-start | bytes 393224 | tf_op jit(solution)/shard_map/ppermute | solution.py:249
  76.8 10.1 %collective-permute-start.19 = (bf16[8,16,512]{2,1,0:T(8,128)(2,1)S(1)}, bf16[8,16,512]{2,1,0:T(8,128)(2,1)S(1)}, u32[]{:S(2)}, u32[]{:S(2)}) collective-permute-start(bf16[8,16,512]{2,1,0:T(8,128)(2,1)S(1)} %get-tuple-element.46), channel_id=1, source_target_pairs={{0,4},{4,8},{8,12},{12,0},{16,28},{20,16},{24,20},{28,24},{1,5},{5... | collective-permute-start | bytes 393224 | tf_op jit(solution)/shard_map/ppermute | solution.py:250
  86.8 6.4 %copy-start = (bf16[4,8,16,128]{3,2,1,0:T(8,128)(2,1)S(1)}, bf16[4,8,16,128]{3,2,1,0:T(8,128)(2,1)}, u32[]{:S(2)}) copy-start(bf16[4,8,16,128]{3,2,1,0:T(8,128)(2,1)} %x_ref.1) | copy-start | bytes 393220
  86.8 6.3 %collective-permute-start.21 = (bf16[8,16,512]{2,1,0:T(8,128)(2,1)S(1)}, bf16[8,16,512]{2,1,0:T(8,128)(2,1)S(1)}, u32[]{:S(2)}, u32[]{:S(2)}) collective-permute-start(bf16[8,16,512]{2,1,0:T(8,128)(2,1)S(1)} %shard_map.75), channel_id=1, source_target_pairs={{0,12},{4,0},{8,4},{12,8},{16,20},{20,24},{24,28},{28,16},{1,13},{... | collective-permute-start | bytes 393224 | tf_op jit(solution)/shard_map/ppermute | solution.py:255

commit v13 on v11

--- a/solution.py
+++ b/solution.py
@@ -130,9 +130,19 @@
     affine_ref[2] = jnp.broadcast_to(shift, shape)
 
 
-def products(layer, w_refs, o_refs, slab_ref):
-    for r in range(8):
-        rows = slab_ref[r : r + 3].reshape(192, 768)
+def window(slab_ref, edge_ref, r):
+    if r == 0:
+        rows = jnp.concatenate([edge_ref[0:1], slab_ref[0:2]], axis=0)
+    elif r == 7:
+        rows = jnp.concatenate([slab_ref[6:8], edge_ref[1:2]], axis=0)
+    else:
+        rows = slab_ref[r - 1 : r + 2]
+    return rows.reshape(192, 768)
+
+
+def products(which, w_refs, o_refs, slab_ref, edge_ref):
+    for r in which:
+        rows = window(slab_ref, edge_ref, r)
         prod = jnp.zeros((96, 512), F32)
         for dt in range(3):
             held = jnp.concatenate([ref(dt).reshape(48, 192) for ref in w_refs], axis=0)
@@ -146,55 +156,73 @@
                 o_ref[r, :, lanes] = summed[q]
 
 
-def near_kernel(layer, slab_ref, own_ref, side_ref, o0_ref, o1_ref):
+def near_kernel(layer, slab_ref, edge_ref, own_ref, side_ref, o0_ref, o1_ref):
     w_refs = (lambda dt: own_ref[layer, dt], lambda dt: side_ref[layer, dt])
-    products(layer, w_refs, (o0_ref, o1_ref), slab_ref)
-
-
-def conv_kernel(
-    layer, a_ref, b_ref, c_ref, d_ref, chip_ref, next_ref, stats_ref, other_ref, far_ref, far2_ref,
+    products(range(8), w_refs, (o0_ref, o1_ref), slab_ref, edge_ref)
+
+
+def hold(layer, far_ref, far2_ref, held_ref):
+    core = lax.rem(lax.axis_index(ROW), 2)
+
+    @pl.when(core == layer)
+    def _():
+        held_ref[...] = far_ref[...]
+
+    @pl.when(core != layer)
+    def _():
+        held_ref[...] = far2_ref[...]
+
+
+def inner_kernel(
+    layer, a_ref, b_ref, c_ref, d_ref, stats_ref, other_ref, far_ref, far2_ref,
     o2_ref, o3_ref, slab_ref, affine_ref, held_ref,
 ):
-    row, _, here = place()
+    here = lax.axis_index(NEAR)
     get_affine(stats_ref, affine_ref)
-    upper = lax.rem(row, 2) == 0
-    not_top = (row > 0).astype(F32)
-    not_bottom = (row < 15).astype(F32)
     for k, ref in enumerate((a_ref, b_ref, c_ref, d_ref)):
         b = lax.bitwise_xor(here, k)
         mean = affine_ref[0, b]
         gain = affine_ref[1, b]
         shift = affine_ref[2, b]
-        for r in range(10):
-            for t in range(6):
+        for r in range(8):
+            slab_ref[r, b, :, 0:256] = ref[r, :, 0:256]
+            for t in range(2, 6):
                 lanes = slice(128 * t, 128 * (t + 1))
-                if r == 0:
-                    x = jnp.where(upper, next_ref[k, :, lanes].astype(F32), chip_ref[k, :, lanes].astype(F32))
-                elif r == 9:
-                    x = jnp.where(upper, chip_ref[k, :, lanes].astype(F32), next_ref[k, :, lanes].astype(F32))
-                elif t < 2:
-                    x = ref[r - 1, :, lanes]
-                else:
-                    x = ref[r - 1, :, lanes].astype(F32)
+                x = silu((ref[r, :, lanes].astype(F32) - mean) * gain + shift)
+                slab_ref[r, b, :, lanes] = x.astype(BF16)
+    hold(layer, far_ref, far2_ref, held_ref)
+    w_refs = (lambda dt: other_ref[layer, dt], lambda dt: held_ref[dt])
+    for o_ref in (o2_ref, o3_ref):
+        o_ref[0] = jnp.zeros((16, 512), BF16)
+        o_ref[7] = jnp.zeros((16, 512), BF16)
+    products(range(1, 7), w_refs, (o2_ref, o3_ref), slab_ref, None)
+
+
+def outer_kernel(
+    layer, chip_ref, next_ref, affine_ref, slab_ref, other_ref, far_ref, far2_ref, i2_ref, i3_ref,
+    o2_ref, o3_ref, edge_ref, held_ref,
+):
+    row, _, here = place()
+    upper = lax.rem(row, 2) == 0
+    inside = ((row > 0).astype(F32), (row < 15).astype(F32))
+    for k in range(4):
+        b = lax.bitwise_xor(here, k)
+        mean = affine_ref[0, b]
+        gain = affine_ref[1, b]
+        shift = affine_ref[2, b]
+        for t in range(6):
+            lanes = slice(128 * t, 128 * (t + 1))
+            chip = chip_ref[k, :, lanes].astype(F32)
+            beyond = next_ref[k, :, lanes].astype(F32)
+            for end, x in enumerate((jnp.where(upper, beyond, chip), jnp.where(upper, chip, beyond))):
                 if t >= 2:
                     x = silu((x - mean) * gain + shift)
-                if r == 0:
-                    x = x * not_top
-                if r == 9:
-                    x = x * not_bottom
-                slab_ref[r, b, :, lanes] = x.astype(BF16)
-    core = lax.rem(row, 2)
-
-    @pl.when(core == layer)
-    def _():
-        held_ref[...] = far_ref[...]
-
-    @pl.when(core != layer)
-    def _():
-        held_ref[...] = far2_ref[...]
-
+                edge_ref[end, b, :, lanes] = (x * inside[end]).astype(BF16)
+    hold(layer, far_ref, far2_ref, held_ref)
     w_refs = (lambda dt: other_ref[layer, dt], lambda dt: held_ref[dt])
-    products(layer, w_refs, (o2_ref, o3_ref), slab_ref)
+    for i_ref, o_ref in ((i2_ref, o2_ref), (i3_ref, o3_ref)):
+        o_ref[1:7] = i_ref[1:7]
+    products((0, 7), w_refs, (o2_ref, o3_ref), slab_ref, edge_ref)
 
 
 def merge_kernel(a_ref, b_ref, c_ref, bias_ref, later_ref, note1_ref, mid_ref, stats_ref, note_ref):
@@ -228,15 +256,23 @@
 def convolve(layer, inputs, own, side, far, other, far2):
     part = struct((8, 16, 512))
     flops = 2 * 96 * 576 * 4096
-    other, far, slab = call(
-        functools.partial(conv_kernel, layer), (part, part, struct((10, 4, 16, 768))),
-        *inputs, other, far, far2,
-        scratch=(pltpu.VMEM((3, 4, 16, 128), F32), pltpu.VMEM((3, 3, 16, 192), BF16)), flops=flops,
+    held = pltpu.VMEM((3, 3, 16, 192), BF16)
+    *blocks, chip, beyond, stats = inputs
+    other_part, far_part, slab, affine = call(
+        functools.partial(inner_kernel, layer),
+        (part, part, struct((8, 4, 16, 768)), struct((3, 4, 16, 128), F32)),
+        *blocks, stats, other, far, far2,
+        scratch=(held,), flops=flops,
+    )
+    other, far, edge = call(
+        functools.partial(outer_kernel, layer), (part, part, struct((2, 4, 16, 768))),
+        chip, beyond, affine, slab, other, far, far2, other_part, far_part,
+        scratch=(held,), flops=flops // 4,
     )
     far = lax.ppermute(far, ("core", "zh"), sides(-1))
     other = lax.ppermute(other, ("core", "zh"), sides(1))
     own, side = call(
-        functools.partial(near_kernel, layer), (part, part), slab, own, side, flops=flops
+        functools.partial(near_kernel, layer), (part, part), slab, edge, own, side, flops=flops
     )
     side = call(add_kernel, part, side, far)
     side = lax.ppermute(side, ("core", "zh"), sides(-1))

time: 93.6 us -> 94.5 us (level)
  the two profiles are of different devices: /device:TPU:27 before, /device:TPU:72 now
where the time goes in v13:
time: 94.5 us; the launch traced here: 94.2 us
  starting transfers between devices  44.4 us (47%)
  waiting for transfers between devices  38.6 us (41%)
  Pallas kernels  9.42 us (10%)
  local copies, waits for them, and re-layouts  1.45 us (2%)
    all_to_all x2, starting transfers between devices, exchange(): return lax.all_to_all(x, axes, 0, 0, tiled=True)  17.7 us
    ppermute x2, waiting for transfers between devices, convolve(): side = lax.ppermute(side, ('core', 'zh'), sides(-1))  14.3 us
    ppermute x2, waiting for transfers between devices, convolve(): far = lax.ppermute(far, ('core', 'zh'), sides(-1))  10.8 us
    pallas_call x13, Pallas kernels, call(): pl.pallas_call(kernel, out_shape=outs, in_specs=specs, out_specs=jax.tree...  9.42 us
    ppermute x2, starting transfers between devices, convolve(): other = lax.ppermute(other, ('core', 'zh'), sides(1))  8.24 us
    ppermute x6, starting transfers between devices, near(): lax.ppermute(x, NEAR, [(i, i ^ k) for i in range(4)])  7.56 us
    ppermute x1, waiting for transfers between devices, local(): far = lax.ppermute(far, 'zh', [(i, (i + 2) % 4) for i in range(4)])  6.18 us
    all_to_all x2, waiting for transfers between devices, exchange(): return lax.all_to_all(x, axes, 0, 0, tiled=True)  6 us
  transfers between devices with their start and end apart: 22, of which 7 were waited for; matrix products, arithmetic and copies ran while one was open for 0% of the time, Pallas kernels for 5%

profile of v13, /device:TPU:72, one launch (start us, length us, event | category | flops | bytes accessed | tf_op | source)
XLA Modules:
  0.0 94.2 jit_solution(17771431520662756143)
XLA Ops:
  0.0 2.3 %shard_map.64 = (bf16[8,16,768]{2,1,0:T(8,128)(2,1)}, bf16[8,16,256]{2,1,0:T(8,128)(2,1)}, f32[64,8,128]{2,1,0:T(8,128)}, bf16[2,3,3,16,192]{4,3,2,1,0:T(8,128)(...) custom-call(bf16[4,8,16,128]{3,2,1,0:T(8,128)(2,1)} %x_ref.1, ...), custom_call_target="tpu_custom_call" | custom-call | bytes 704768 | tf_op jit(solution)/shard_map/pallas_call | solution.py:32
  2.3 1.6 %collective-permute-start = (bf16[8,16,768]{2,1,0:T(8,128)(2,1)}, bf16[8,16,768]{2,1,0:T(8,128)(2,1)S(1)}, u32[]{:S(2)}, u32[]{:S(2)}) collective-permute-start(bf16[8,16,768]{2,1,0:T(8,128)(2,1)} %get-tuple-element.35.a_ref), channel_id=1, source_target_pairs={{0,1},{1,0},{2,3},{3,2},{4,5},{5,4},{6,7},{7,6},{8,9},{9,8},{10,11... | collective-permute-start | bytes 589832 | tf_op jit(solution)/shard_map/ppermute | solution.py:303
  3.9 1.9 %collective-permute-start.1 = (bf16[8,16,768]{2,1,0:T(8,128)(2,1)}, bf16[8,16,768]{2,1,0:T(8,128)(2,1)S(1)}, u32[]{:S(2)}, u32[]{:S(2)}) collective-permute-start(bf16[8,16,768]{2,1,0:T(8,128)(2,1)} %get-tuple-element.35.a_ref), channel_id=1, source_target_pairs={{0,2},{1,3},{2,0},{3,1},{4,6},{5,7},{6,4},{7,5},{8,10},{9,11},{10,... | collective-permute-start | bytes 589832 | tf_op jit(solution)/shard_map/ppermute | solution.py:303
  5.8 0.1 collective-permute-start.2
  5.9 4.5 %collective-permute-start.3 = (bf16[2,3,3,16,192]{4,3,2,1,0:T(8,128)(2,1)}, bf16[2,3,3,16,192]{4,3,2,1,0:T(8,128)(2,1)S(1)}, u32[]{:S(2)}, u32[]{:S(2)}) collective-permute-start(bf16[2,3,3,16,192]{4,3,2,1,0:T(8,128)(2,1)} %get-tuple-element.37), channel_id=1, source_target_pairs={{0,4},{4,8},{8,12},{12,0},{16,28},{20,16},{24,20},{28,24},{1,5},{5... | collective-permute-start | bytes 331784 | tf_op jit(solution)/shard_map/ppermute | solution.py:327
  10.4 8.5 %all-to-all-start = ((f32[64,8,128]{2,1,0:T(8,128)}), f32[64,8,128]{2,1,0:T(8,128)S(1)}, u32[]{:S(2)}, u32[]{:S(2)}) async-start(f32[64,8,128]{2,1,0:T(8,128)} %get-tuple-element.36), calls=%async_computation | async-start | bytes 524288 | tf_op jit(solution)/shard_map/all_to_all | solution.py:307
  18.9 1.0 %collective-permute-start.5 = (bf16[3,3,16,192]{3,2,1,0:T(8,128)(2,1)S(1)}, bf16[3,3,16,192]{3,2,1,0:T(8,128)(2,1)S(1)}, u32[]{:S(2)}, u32[]{:S(2)}) collective-permute-start(bf16[3,3,16,192]{3,2,1,0:T(8,128)(2,1)S(1)} %copy-done.7), channel_id=1, source_target_pairs={{0,8},{4,12},{8,0},{12,4},{1,9},{5,13},{9,1},{13,5},{2,10},{6,14},... | collective-permute-start | bytes 165896 | tf_op jit(solution)/shard_map/ppermute | solution.py:328
  19.9 0.0 collective-permute-done.3.side_ref
  19.9 0.0 collective-permute-start.4
  19.9 0.0 collective-permute-done.1.c_ref
  20.0 0.6 collective-permute-start.7
  20.6 2.0 %collective-permute-start.8 = (bf16[4,16,768]{2,1,0:T(8,128)(2,1)S(1)}, bf16[4,16,768]{2,1,0:T(8,128)(2,1)S(1)}, u32[]{:S(2)}, u32[]{:S(2)}) collective-permute-start(bf16[4,16,768]{2,1,0:T(8,128)(2,1)S(1)} %get-tuple-element.41), channel_id=1, source_target_pairs={{16,32},{48,64},{80,96},{112,128},{144,160},{176,192},{208,224},{3... | collective-permute-start | bytes 294920 | tf_op jit(solution)/shard_map/ppermute | solution.py:298
  22.6 6.2 %collective-permute-done.5.far_ref = bf16[3,3,16,192]{3,2,1,0:T(8,128)(2,1)S(1)} collective-permute-done((bf16[3,3,16,192]{3,2,1,0:T(8,128)(2,1)S(1)}, bf16[3,3,16,192]{3,2,1,0:T(8,128)(2,1)S(1)}, u32[]{:S(2)}, u32[]{:S(2)}) %collective-permute-start.5) | collective-permute-done | bytes 55328 | tf_op jit(solution)/shard_map/ppermute | solution.py:328
  28.7 1.3 %collective-permute-done.6.far2_ref = bf16[3,3,16,192]{3,2,1,0:T(8,128)(2,1)S(1)} collective-permute-done((bf16[3,3,16,192]{3,2,1,0:T(8,128)(2,1)S(1)}, bf16[3,3,16,192]{3,2,1,0:T(8,128)(2,1)S(1)}, u32[]{:S(2)}, u32[]{:S(2)}) %collective-permute-start.6) | collective-permute-done | bytes 55328 | tf_op jit(solution)/shard_map/ppermute | solution.py:333
  30.0 0.0 collective-permute-done.4.other_ref
  30.0 1.3 %shard_map.65 = (bf16[8,16,512]{2,1,0:T(8,128)(2,1)S(1)}, bf16[8,16,512]{2,1,0:T(8,128)(2,1)S(1)}, bf16[8,4,16,768]{3,2,1,0:T(8,128)(2,1)S(1)}, f32[3,4,16,128]{3,2,1,0:T(8,128)S(1)}) custom-call(bf16[8,16,768]{2,1,0:T(8,128)(2,1)S(1)} %copy-done.2, bf16[8,16,768]{2,1,0:T(8,128)(2,1)S(1)} %collective-permute-done.b_ref, ...), custom_call_target="tpu_custom_call" | custom-call | flops 452984832 | bytes 1269760 | tf_op jit(solution)/shard_map/pallas_call | solution.py:32
  31.3 0.0 collective-permute-done.7.chip_ref
  31.3 0.0 collective-permute-done.8.next_ref
  31.3 0.6 shard_map.67
  31.9 0.1 collective-permute-start.10
  32.0 4.1 %collective-permute-start.9 = (bf16[8,16,512]{2,1,0:T(8,128)(2,1)S(1)}, bf16[8,16,512]{2,1,0:T(8,128)(2,1)S(1)}, u32[]{:S(2)}, u32[]{:S(2)}) collective-permute-start(bf16[8,16,512]{2,1,0:T(8,128)(2,1)S(1)} %get-tuple-element.48), channel_id=1, source_target_pairs={{0,4},{4,8},{8,12},{12,0},{16,28},{20,16},{24,20},{28,24},{1,5},{5... | collective-permute-start | bytes 393224 | tf_op jit(solution)/shard_map/ppermute | solution.py:273
  36.1 0.9 shard_map.68
  37.0 5.1 %collective-permute-done.10.b_ref = bf16[8,16,512]{2,1,0:T(8,128)(2,1)S(1)} collective-permute-done((bf16[8,16,512]{2,1,0:T(8,128)(2,1)S(1)}, bf16[8,16,512]{2,1,0:T(8,128)(2,1)S(1)}, u32[]{:S(2)}, u32[]{:S(2)}) %collective-permute-start.10) | collective-permute-done | bytes 131104 | tf_op jit(solution)/shard_map/ppermute | solution.py:272
  42.1 0.0 copy-start.4
  42.1 0.1 collective-permute-start.11
  42.2 0.5 copy-done.6
  42.8 0.1 copy-done.4
  42.8 0.7 copy-done.5
  43.5 5.9 %collective-permute-done.11.c_ref = bf16[8,16,512]{2,1,0:T(8,128)(2,1)S(1)} collective-permute-done((bf16[8,16,512]{2,1,0:T(8,128)(2,1)S(1)}, bf16[8,16,512]{2,1,0:T(8,128)(2,1)S(1)}, u32[]{:S(2)}, u32[]{:S(2)}) %collective-permute-start.11) | collective-permute-done | bytes 131104 | tf_op jit(solution)/shard_map/ppermute | solution.py:278
  49.5 0.1 broadcast_in_dim.13.bias_ref
  49.5 0.9 shard_map.70
  50.4 1.4 %collective-permute-start.12 = (bf16[8,16,768]{2,1,0:T(8,128)(2,1)S(1)}, bf16[8,16,768]{2,1,0:T(8,128)(2,1)S(1)}, u32[]{:S(2)}, u32[]{:S(2)}) collective-permute-start(bf16[8,16,768]{2,1,0:T(8,128)(2,1)S(1)} %get-tuple-element.52.a_ref), channel_id=1, source_target_pairs={{0,1},{1,0},{2,3},{3,2},{4,5},{5,4},{6,7},{7,6},{8,9},{9,8},{10,11... | collective-permute-start | bytes 589832 | tf_op jit(solution)/shard_map/ppermute | solution.py:303
  51.8 2.6 %collective-permute-start.13 = (bf16[8,16,768]{2,1,0:T(8,128)(2,1)S(1)}, bf16[8,16,768]{2,1,0:T(8,128)(2,1)S(1)}, u32[]{:S(2)}, u32[]{:S(2)}) collective-permute-start(bf16[8,16,768]{2,1,0:T(8,128)(2,1)S(1)} %get-tuple-element.52.a_ref), channel_id=1, source_target_pairs={{0,2},{1,3},{2,0},{3,1},{4,6},{5,7},{6,4},{7,5},{8,10},{9,11},{10,... | collective-permute-start | bytes 589832 | tf_op jit(solution)/shard_map/ppermute | solution.py:303
  54.4 0.0 collective-permute-start.14
  54.4 9.2 %all-to-all-start.1 = ((f32[64,8,128]{2,1,0:T(8,128)}), f32[64,8,128]{2,1,0:T(8,128)S(1)}, u32[]{:S(2)}, u32[]{:S(2)}) async-start(f32[64,8,128]{2,1,0:T(8,128)} %get-tuple-element.53), calls=%async_computation.1 | async-start | bytes 524288 | tf_op jit(solution)/shard_map/all_to_all | solution.py:307
  63.6 0.2 collective-permute-start.15
  63.8 2.3 %collective-permute-start.16 = (bf16[4,16,768]{2,1,0:T(8,128)(2,1)S(1)}, bf16[4,16,768]{2,1,0:T(8,128)(2,1)S(1)}, u32[]{:S(2)}, u32[]{:S(2)}) collective-permute-start(bf16[4,16,768]{2,1,0:T(8,128)(2,1)S(1)} %get-tuple-element.56), channel_id=1, source_target_pairs={{16,32},{48,64},{80,96},{112,128},{144,160},{176,192},{208,224},{3... | collective-permute-start | bytes 294920 | tf_op jit(solution)/shard_map/ppermute | solution.py:298
  66.2 6.0 %all-to-all-done.1.stats_ref = f32[64,8,128]{2,1,0:T(8,128)S(1)} async-done(((f32[64,8,128]{2,1,0:T(8,128)}), f32[64,8,128]{2,1,0:T(8,128)S(1)}, u32[]{:S(2)}, u32[]{:S(2)}) %all-to-all-start.1) | async-done | bytes 262176 | tf_op jit(solution)/shard_map/all_to_all | solution.py:307
  72.2 1.3 %shard_map.71 = (bf16[8,16,512]{2,1,0:T(8,128)(2,1)S(1)}, bf16[8,16,512]{2,1,0:T(8,128)(2,1)S(1)}, bf16[8,4,16,768]{3,2,1,0:T(8,128)(2,1)S(1)}, f32[3,4,16,128]{3,2,1,0:T(8,128)S(1)}) custom-call(bf16[8,16,768]{2,1,0:T(8,128)(2,1)S(1)} %get-tuple-element.52.a_ref, bf16[8,16,768]{2,1,0:T(8,128)(2,1)S(1)} %collective-permute-done.12.b_ref, ...), custom_call_target="tpu_custom_call" | custom-call | flops 452984832 | bytes 1269760 | tf_op jit(solution)/shard_map/pallas_call | solution.py:32
  73.5 0.6 shard_map.73
  74.0 0.1 collective-permute-start.18
  74.1 4.1 %collective-permute-start.17 = (bf16[8,16,512]{2,1,0:T(8,128)(2,1)S(1)}, bf16[8,16,512]{2,1,0:T(8,128)(2,1)S(1)}, u32[]{:S(2)}, u32[]{:S(2)}) collective-permute-start(bf16[8,16,512]{2,1,0:T(8,128)(2,1)S(1)} %get-tuple-element.62), channel_id=1, source_target_pairs={{0,4},{4,8},{8,12},{12,0},{16,28},{20,16},{24,20},{28,24},{1,5},{5... | collective-permute-start | bytes 393224 | tf_op jit(solution)/shard_map/ppermute | solution.py:273
  78.2 0.9 shard_map.74
  79.1 5.7 %collective-permute-done.18.b_ref = bf16[8,16,512]{2,1,0:T(8,128)(2,1)S(1)} collective-permute-done((bf16[8,16,512]{2,1,0:T(8,128)(2,1)S(1)}, bf16[8,16,512]{2,1,0:T(8,128)(2,1)S(1)}, u32[]{:S(2)}, u32[]{:S(2)}) %collective-permute-start.18) | collective-permute-done | bytes 131104 | tf_op jit(solution)/shard_map/ppermute | solution.py:272
  84.8 0.1 collective-permute-start.19
  84.9 8.4 %collective-permute-done.19.c_ref = bf16[8,16,512]{2,1,0:T(8,128)(2,1)S(1)} collective-permute-done((bf16[8,16,512]{2,1,0:T(8,128)(2,1)S(1)}, bf16[8,16,512]{2,1,0:T(8,128)(2,1)S(1)}, u32[]{:S(2)}, u32[]{:S(2)}) %collective-permute-start.19) | collective-permute-done | bytes 131104 | tf_op jit(solution)/shard_map/ppermute | solution.py:278
  93.3 0.1 broadcast_in_dim.15.bias_ref
  93.4 0.7 shard_map.76
  (31 shorter events, 0.2 us)
Async XLA Ops:
  2.3 17.6 %collective-permute-start = (bf16[8,16,768]{2,1,0:T(8,128)(2,1)}, bf16[8,16,768]{2,1,0:T(8,128)(2,1)S(1)}, u32[]{:S(2)}, u32[]{:S(2)}) collective-permute-start(bf16[8,16,768]{2,1,0:T(8,128)(2,1)} %get-tuple-element.35.a_ref), channel_id=1, source_target_pairs={{0,1},{1,0},{2,3},{3,2},{4,5},{5,4},{6,7},{7,6},{8,9},{9,8},{10,11... | collective-permute-start | bytes 589832 | tf_op jit(solution)/shard_map/ppermute | solution.py:303
  3.9 16.0 %collective-permute-start.1 = (bf16[8,16,768]{2,1,0:T(8,128)(2,1)}, bf16[8,16,768]{2,1,0:T(8,128)(2,1)S(1)}, u32[]{:S(2)}, u32[]{:S(2)}) collective-permute-start(bf16[8,16,768]{2,1,0:T(8,128)(2,1)} %get-tuple-element.35.a_ref), channel_id=1, source_target_pairs={{0,2},{1,3},{2,0},{3,1},{4,6},{5,7},{6,4},{7,5},{8,10},{9,11},{10,... | collective-permute-start | bytes 589832 | tf_op jit(solution)/shard_map/ppermute | solution.py:303
  5.8 14.1 %collective-permute-start.2 = (bf16[8,16,768]{2,1,0:T(8,128)(2,1)}, bf16[8,16,768]{2,1,0:T(8,128)(2,1)S(1)}, u32[]{:S(2)}, u32[]{:S(2)}) collective-permute-start(bf16[8,16,768]{2,1,0:T(8,128)(2,1)} %get-tuple-element.35.a_ref), channel_id=1, source_target_pairs={{0,3},{1,2},{2,1},{3,0},{4,7},{5,6},{6,5},{7,4},{8,11},{9,10},{10,... | collective-permute-start | bytes 589832 | tf_op jit(solution)/shard_map/ppermute | solution.py:303
  5.9 14.0 %collective-permute-start.3 = (bf16[2,3,3,16,192]{4,3,2,1,0:T(8,128)(2,1)}, bf16[2,3,3,16,192]{4,3,2,1,0:T(8,128)(2,1)S(1)}, u32[]{:S(2)}, u32[]{:S(2)}) collective-permute-start(bf16[2,3,3,16,192]{4,3,2,1,0:T(8,128)(2,1)} %get-tuple-element.37), channel_id=1, source_target_pairs={{0,4},{4,8},{8,12},{12,0},{16,28},{20,16},{24,20},{28,24},{1,5},{5... | collective-permute-start | bytes 331784 | tf_op jit(solution)/shard_map/ppermute | solution.py:327
  10.4 8.5 %copy-start.7 = (bf16[3,3,16,192]{3,2,1,0:T(8,128)(2,1)S(1)}, bf16[3,3,16,192]{3,2,1,0:T(8,128)(2,1)}, u32[]{:S(2)}) copy-start(bf16[3,3,16,192]{3,2,1,0:T(8,128)(2,1)} %get-tuple-element.38) | copy-start | bytes 165892
  10.4 9.6 %copy-start.2 = (bf16[8,16,768]{2,1,0:T(8,128)(2,1)S(1)}, bf16[8,16,768]{2,1,0:T(8,128)(2,1)}, u32[]{:S(2)}) copy-start(bf16[8,16,768]{2,1,0:T(8,128)(2,1)} %get-tuple-element.35.a_ref) | copy-start | bytes 589828
  10.4 19.7 %all-to-all-start = ((f32[64,8,128]{2,1,0:T(8,128)}), f32[64,8,128]{2,1,0:T(8,128)S(1)}, u32[]{:S(2)}, u32[]{:S(2)}) async-start(f32[64,8,128]{2,1,0:T(8,128)} %get-tuple-element.36), calls=%async_computation | async-start | bytes 524288 | tf_op jit(solution)/shard_map/all_to_all | solution.py:307
  18.9 9.8 %collective-permute-start.5 = (bf16[3,3,16,192]{3,2,1,0:T(8,128)(2,1)S(1)}, bf16[3,3,16,192]{3,2,1,0:T(8,128)(2,1)S(1)}, u32[]{:S(2)}, u32[]{:S(2)}) collective-permute-start(bf16[3,3,16,192]{3,2,1,0:T(8,128)(2,1)S(1)} %copy-done.7), channel_id=1, source_target_pairs={{0,8},{4,12},{8,0},{12,4},{1,9},{5,13},{9,1},{13,5},{2,10},{6,14},... | collective-permute-start | bytes 165896 | tf_op jit(solution)/shard_map/ppermute | solution.py:328
  19.9 10.1 %collective-permute-start.4 = (bf16[2,3,3,16,192]{4,3,2,1,0:T(8,128)(2,1)S(1)}, bf16[2,3,3,16,192]{4,3,2,1,0:T(8,128)(2,1)S(1)}, u32[]{:S(2)}, u32[]{:S(2)}) collective-permute-start(bf16[2,3,3,16,192]{4,3,2,1,0:T(8,128)(2,1)S(1)} %collective-permute-done.3.side_ref), channel_id=1, source_target_pairs={{0,16},{16,0},{1,17},{17,1},{2,18},{18,2},{3,19},{19,3},{4,20},{20... | collective-permute-start | bytes 331784 | tf_op jit(solution)/shard_map/ppermute | solution.py:333
  20.0 11.3 %collective-permute-start.7 = (bf16[4,16,768]{2,1,0:T(8,128)(2,1)S(1)}, bf16[4,16,768]{2,1,0:T(8,128)(2,1)S(1)}, u32[]{:S(2)}, u32[]{:S(2)}) collective-permute-start(bf16[4,16,768]{2,1,0:T(8,128)(2,1)S(1)} %get-tuple-element.40), channel_id=1, source_target_pairs={{0,16},{16,0},{32,48},{48,32},{64,80},{80,64},{96,112},{112,96},{1... | collective-permute-start | bytes 294920 | tf_op jit(solution)/shard_map/ppermute | solution.py:296
  20.6 10.7 %collective-permute-start.8 = (bf16[4,16,768]{2,1,0:T(8,128)(2,1)S(1)}, bf16[4,16,768]{2,1,0:T(8,128)(2,1)S(1)}, u32[]{:S(2)}, u32[]{:S(2)}) collective-permute-start(bf16[4,16,768]{2,1,0:T(8,128)(2,1)S(1)} %get-tuple-element.41), channel_id=1, source_target_pairs={{16,32},{48,64},{80,96},{112,128},{144,160},{176,192},{208,224},{3... | collective-permute-start | bytes 294920 | tf_op jit(solution)/shard_map/ppermute | solution.py:298
  28.7 1.3 %collective-permute-start.6 = (bf16[3,3,16,192]{3,2,1,0:T(8,128)(2,1)S(1)}, bf16[3,3,16,192]{3,2,1,0:T(8,128)(2,1)S(1)}, u32[]{:S(2)}, u32[]{:S(2)}) collective-permute-start(bf16[3,3,16,192]{3,2,1,0:T(8,128)(2,1)S(1)} %collective-permute-done.5.far_ref), channel_id=1, source_target_pairs={{0,16},{16,0},{1,17},{17,1},{2,18},{18,2},{3,19},{19,3},{4,20},{20... | collective-permute-start | bytes 165896 | tf_op jit(solution)/shard_map/ppermute | solution.py:333
  31.3 4.8 %copy-start.3 = (bf16[2,3,3,16,192]{4,3,2,1,0:T(8,128)(2,1)S(1)}, bf16[2,3,3,16,192]{4,3,2,1,0:T(8,128)(2,1)}, u32[]{:S(2)}) copy-start(bf16[2,3,3,16,192]{4,3,2,1,0:T(8,128)(2,1)} %get-tuple-element.46.own_ref) | copy-start | bytes 331780
  31.9 10.2 %collective-permute-start.10 = (bf16[8,16,512]{2,1,0:T(8,128)(2,1)S(1)}, bf16[8,16,512]{2,1,0:T(8,128)(2,1)S(1)}, u32[]{:S(2)}, u32[]{:S(2)}) collective-permute-start(bf16[8,16,512]{2,1,0:T(8,128)(2,1)S(1)} %get-tuple-element.50), channel_id=1, source_target_pairs={{0,12},{4,0},{8,4},{12,8},{16,20},{20,24},{24,28},{28,16},{1,13},{... | collective-permute-start | bytes 393224 | tf_op jit(solution)/shard_map/ppermute | solution.py:272
  32.0 11.5 %collective-permute-start.9 = (bf16[8,16,512]{2,1,0:T(8,128)(2,1)S(1)}, bf16[8,16,512]{2,1,0:T(8,128)(2,1)S(1)}, u32[]{:S(2)}, u32[]{:S(2)}) collective-permute-start(bf16[8,16,512]{2,1,0:T(8,128)(2,1)S(1)} %get-tuple-element.48), channel_id=1, source_target_pairs={{0,4},{4,8},{8,12},{12,0},{16,28},{20,16},{24,20},{28,24},{1,5},{5... | collective-permute-start | bytes 393224 | tf_op jit(solution)/shard_map/ppermute | solution.py:273
  42.1 0.7 copy-start.6
  42.1 7.5 %copy-start.1 = (bf16[8,16,256]{2,1,0:T(8,128)(2,1)S(1)}, bf16[8,16,256]{2,1,0:T(8,128)(2,1)}, u32[]{:S(2)}) copy-start(bf16[8,16,256]{2,1,0:T(8,128)(2,1)} %get-tuple-element.51.later_ref) | copy-start | bytes 196612
  42.1 0.7 copy-start.4
  42.1 7.3 %collective-permute-start.11 = (bf16[8,16,512]{2,1,0:T(8,128)(2,1)S(1)}, bf16[8,16,512]{2,1,0:T(8,128)(2,1)S(1)}, u32[]{:S(2)}, u32[]{:S(2)}) collective-permute-start(bf16[8,16,512]{2,1,0:T(8,128)(2,1)S(1)} %shard_map.69), channel_id=1, source_target_pairs={{0,12},{4,0},{8,4},{12,8},{16,20},{20,24},{24,28},{28,16},{1,13},{... | collective-permute-start | bytes 393224 | tf_op jit(solution)/shard_map/ppermute | solution.py:278
  42.8 0.7 copy-start.5
  50.4 13.2 %collective-permute-start.12 = (bf16[8,16,768]{2,1,0:T(8,128)(2,1)S(1)}, bf16[8,16,768]{2,1,0:T(8,128)(2,1)S(1)}, u32[]{:S(2)}, u32[]{:S(2)}) collective-permute-start(bf16[8,16,768]{2,1,0:T(8,128)(2,1)S(1)} %get-tuple-element.52.a_ref), channel_id=1, source_target_pairs={{0,1},{1,0},{2,3},{3,2},{4,5},{5,4},{6,7},{7,6},{8,9},{9,8},{10,11... | collective-permute-start | bytes 589832 | tf_op jit(solution)/shard_map/ppermute | solution.py:303
  51.8 11.8 %collective-permute-start.13 = (bf16[8,16,768]{2,1,0:T(8,128)(2,1)S(1)}, bf16[8,16,768]{2,1,0:T(8,128)(2,1)S(1)}, u32[]{:S(2)}, u32[]{:S(2)}) collective-permute-start(bf16[8,16,768]{2,1,0:T(8,128)(2,1)S(1)} %get-tuple-element.52.a_ref), channel_id=1, source_target_pairs={{0,2},{1,3},{2,0},{3,1},{4,6},{5,7},{6,4},{7,5},{8,10},{9,11},{10,... | collective-permute-start | bytes 589832 | tf_op jit(solution)/shard_map/ppermute | solution.py:303
  54.4 9.2 %collective-permute-start.14 = (bf16[8,16,768]{2,1,0:T(8,128)(2,1)S(1)}, bf16[8,16,768]{2,1,0:T(8,128)(2,1)S(1)}, u32[]{:S(2)}, u32[]{:S(2)}) collective-permute-start(bf16[8,16,768]{2,1,0:T(8,128)(2,1)S(1)} %get-tuple-element.52.a_ref), channel_id=1, source_target_pairs={{0,3},{1,2},{2,1},{3,0},{4,7},{5,6},{6,5},{7,4},{8,11},{9,10},{10,... | collective-permute-start | bytes 589832 | tf_op jit(solution)/shard_map/ppermute | solution.py:303
  54.4 17.8 %all-to-all-start.1 = ((f32[64,8,128]{2,1,0:T(8,128)}), f32[64,8,128]{2,1,0:T(8,128)S(1)}, u32[]{:S(2)}, u32[]{:S(2)}) async-start(f32[64,8,128]{2,1,0:T(8,128)} %get-tuple-element.53), calls=%async_computation.1 | async-start | bytes 524288 | tf_op jit(solution)/shard_map/all_to_all | solution.py:307
  63.6 9.8 %collective-permute-start.15 = (bf16[4,16,768]{2,1,0:T(8,128)(2,1)S(1)}, bf16[4,16,768]{2,1,0:T(8,128)(2,1)S(1)}, u32[]{:S(2)}, u32[]{:S(2)}) collective-permute-start(bf16[4,16,768]{2,1,0:T(8,128)(2,1)S(1)} %get-tuple-element.55), channel_id=1, source_target_pairs={{0,16},{16,0},{32,48},{48,32},{64,80},{80,64},{96,112},{112,96},{1... | collective-permute-start | bytes 294920 | tf_op jit(solution)/shard_map/ppermute | solution.py:296
  63.8 9.6 %collective-permute-start.16 = (bf16[4,16,768]{2,1,0:T(8,128)(2,1)S(1)}, bf16[4,16,768]{2,1,0:T(8,128)(2,1)S(1)}, u32[]{:S(2)}, u32[]{:S(2)}) collective-permute-start(bf16[4,16,768]{2,1,0:T(8,128)(2,1)S(1)} %get-tuple-element.56), channel_id=1, source_target_pairs={{16,32},{48,64},{80,96},{112,128},{144,160},{176,192},{208,224},{3... | collective-permute-start | bytes 294920 | tf_op jit(solution)/shard_map/ppermute | solution.py:298
  74.0 10.8 %collective-permute-start.18 = (bf16[8,16,512]{2,1,0:T(8,128)(2,1)S(1)}, bf16[8,16,512]{2,1,0:T(8,128)(2,1)S(1)}, u32[]{:S(2)}, u32[]{:S(2)}) collective-permute-start(bf16[8,16,512]{2,1,0:T(8,128)(2,1)S(1)} %get-tuple-element.64), channel_id=1, source_target_pairs={{0,12},{4,0},{8,4},{12,8},{16,20},{20,24},{24,28},{28,16},{1,13},{... | collective-permute-start | bytes 393224 | tf_op jit(solution)/shard_map/ppermute | solution.py:272
  74.1 10.8 %collective-permute-start.17 = (bf16[8,16,512]{2,1,0:T(8,128)(2,1)S(1)}, bf16[8,16,512]{2,1,0:T(8,128)(2,1)S(1)}, u32[]{:S(2)}, u32[]{:S(2)}) collective-permute-start(bf16[8,16,512]{2,1,0:T(8,128)(2,1)S(1)} %get-tuple-element.62), channel_id=1, source_target_pairs={{0,4},{4,8},{8,12},{12,0},{16,28},{20,16},{24,20},{28,24},{1,5},{5... | collective-permute-start | bytes 393224 | tf_op jit(solution)/shard_map/ppermute | solution.py:273
  84.8 8.6 %copy-start = (bf16[4,8,16,128]{3,2,1,0:T(8,128)(2,1)S(1)}, bf16[4,8,16,128]{3,2,1,0:T(8,128)(2,1)}, u32[]{:S(2)}) copy-start(bf16[4,8,16,128]{3,2,1,0:T(8,128)(2,1)} %x_ref.1) | copy-start | bytes 393220
  84.8 8.5 %collective-permute-start.19 = (bf16[8,16,512]{2,1,0:T(8,128)(2,1)S(1)}, bf16[8,16,512]{2,1,0:T(8,128)(2,1)S(1)}, u32[]{:S(2)}, u32[]{:S(2)}) collective-permute-start(bf16[8,16,512]{2,1,0:T(8,128)(2,1)S(1)} %shard_map.75), channel_id=1, source_target_pairs={{0,12},{4,0},{8,4},{12,8},{16,20},{20,24},{24,28},{28,16},{1,13},{... | collective-permute-start | bytes 393224 | tf_op jit(solution)/shard_map/ppermute | solution.py:278

commit v14 on v11

--- a/solution.py
+++ b/solution.py
@@ -131,13 +131,15 @@
 
 
 def products(layer, w_refs, o_refs, slab_ref):
+    count = len(w_refs)
     for r in range(8):
         rows = slab_ref[r : r + 3].reshape(192, 768)
-        prod = jnp.zeros((96, 512), F32)
+        prod = jnp.zeros((48 * count, 512), F32)
         for dt in range(3):
-            held = jnp.concatenate([ref(dt).reshape(48, 192) for ref in w_refs], axis=0)
+            held = [ref(dt).reshape(48, 192) for ref in w_refs]
+            held = held[0] if count == 1 else jnp.concatenate(held, axis=0)
             prod += dot(held, rows[:, 128 * dt : 128 * dt + 512])
-        prod = prod.reshape(2, 3, 16, 512)
+        prod = prod.reshape(count, 3, 16, 512)
         for t in range(4):
             lanes = slice(128 * t, 128 * (t + 1))
             part = prod[:, :, :, lanes]
@@ -146,14 +148,14 @@
                 o_ref[r, :, lanes] = summed[q]
 
 
-def near_kernel(layer, slab_ref, own_ref, side_ref, o0_ref, o1_ref):
-    w_refs = (lambda dt: own_ref[layer, dt], lambda dt: side_ref[layer, dt])
-    products(layer, w_refs, (o0_ref, o1_ref), slab_ref)
+def near_kernel(layer, slab_ref, own_ref, side_ref, other_ref, o0_ref, o1_ref, o2_ref):
+    w_refs = tuple(functools.partial(lambda ref, dt: ref[layer, dt], ref) for ref in (own_ref, side_ref, other_ref))
+    products(layer, w_refs, (o0_ref, o1_ref, o2_ref), slab_ref)
 
 
 def conv_kernel(
-    layer, a_ref, b_ref, c_ref, d_ref, chip_ref, next_ref, stats_ref, other_ref, far_ref, far2_ref,
-    o2_ref, o3_ref, slab_ref, affine_ref, held_ref,
+    layer, a_ref, b_ref, c_ref, d_ref, chip_ref, next_ref, stats_ref, far_ref, far2_ref,
+    o3_ref, slab_ref, affine_ref, held_ref,
 ):
     row, _, here = place()
     get_affine(stats_ref, affine_ref)
@@ -193,8 +195,7 @@
     def _():
         held_ref[...] = far2_ref[...]
 
-    w_refs = (lambda dt: other_ref[layer, dt], lambda dt: held_ref[dt])
-    products(layer, w_refs, (o2_ref, o3_ref), slab_ref)
+    products(layer, (lambda dt: held_ref[dt],), (o3_ref,), slab_ref)
 
 
 def merge_kernel(a_ref, b_ref, c_ref, bias_ref, later_ref, note1_ref, mid_ref, stats_ref, note_ref):
@@ -227,17 +228,16 @@
 
 def convolve(layer, inputs, own, side, far, other, far2):
     part = struct((8, 16, 512))
-    flops = 2 * 96 * 576 * 4096
-    other, far, slab = call(
-        functools.partial(conv_kernel, layer), (part, part, struct((10, 4, 16, 768))),
-        *inputs, other, far, far2,
+    flops = 2 * 48 * 576 * 4096
+    far, slab = call(
+        functools.partial(conv_kernel, layer), (part, struct((10, 4, 16, 768))), *inputs, far, far2,
         scratch=(pltpu.VMEM((3, 4, 16, 128), F32), pltpu.VMEM((3, 3, 16, 192), BF16)), flops=flops,
     )
     far = lax.ppermute(far, ("core", "zh"), sides(-1))
+    own, side, other = call(
+        functools.partial(near_kernel, layer), (part,) * 3, slab, own, side, other, flops=3 * flops
+    )
     other = lax.ppermute(other, ("core", "zh"), sides(1))
-    own, side = call(
-        functools.partial(near_kernel, layer), (part, part), slab, own, side, flops=flops
-    )
     side = call(add_kernel, part, side, far)
     side = lax.ppermute(side, ("core", "zh"), sides(-1))
     return [own, other, side]

time: 93.6 us -> 94 us (level)
  the two profiles are of different devices: /device:TPU:27 before, /device:TPU:64 now
where the time goes in v14:
time: 94 us; the launch traced here: 93.6 us
  starting transfers between devices  41.5 us (44%)
  waiting for transfers between devices  40.7 us (43%)
  Pallas kernels  9.68 us (10%)
  local copies, waits for them, and re-layouts  1.45 us (2%)
    all_to_all x2, starting transfers between devices, exchange(): return lax.all_to_all(x, axes, 0, 0, tiled=True)  14.1 us
    ppermute x2, waiting for transfers between devices, convolve(): side = lax.ppermute(side, ('core', 'zh'), sides(-1))  14.1 us
    all_to_all x2, waiting for transfers between devices, exchange(): return lax.all_to_all(x, axes, 0, 0, tiled=True)  13.2 us
    ppermute x2, waiting for transfers between devices, convolve(): far = lax.ppermute(far, ('core', 'zh'), sides(-1))  11.3 us
    pallas_call x11, Pallas kernels, call(): pl.pallas_call(kernel, out_shape=outs, in_specs=specs, out_specs=jax.tree...  9.68 us
    ppermute x6, starting transfers between devices, near(): lax.ppermute(x, NEAR, [(i, i ^ k) for i in range(4)])  7.06 us
    ppermute x2, starting transfers between devices, convolve(): other = lax.ppermute(other, ('core', 'zh'), sides(1))  6.69 us
    ppermute x1, starting transfers between devices, local(): far = lax.ppermute(far, 'zh', [(i, (i + 2) % 4) for i in range(4)])  5.39 us
  transfers between devices with their start and end apart: 22, of which 9 were waited for; matrix products, arithmetic and copies ran while one was open for 0% of the time, Pallas kernels for 4%

profile of v14, /device:TPU:64, one launch (start us, length us, event | category | flops | bytes accessed | tf_op | source)
XLA Modules:
  0.0 93.6 jit_solution(9775924073650038711)
XLA Ops:
  0.0 2.3 %shard_map.64 = (bf16[8,16,768]{2,1,0:T(8,128)(2,1)}, bf16[8,16,256]{2,1,0:T(8,128)(2,1)}, f32[64,8,128]{2,1,0:T(8,128)}, bf16[2,3,3,16,192]{4,3,2,1,0:T(8,128)(...) custom-call(bf16[4,8,16,128]{3,2,1,0:T(8,128)(2,1)} %x_ref.1, ...), custom_call_target="tpu_custom_call" | custom-call | bytes 704768 | tf_op jit(solution)/shard_map/pallas_call | solution.py:32
  2.3 1.6 %collective-permute-start = (bf16[8,16,768]{2,1,0:T(8,128)(2,1)}, bf16[8,16,768]{2,1,0:T(8,128)(2,1)S(1)}, u32[]{:S(2)}, u32[]{:S(2)}) collective-permute-start(bf16[8,16,768]{2,1,0:T(8,128)(2,1)} %get-tuple-element.27.a_ref), channel_id=1, source_target_pairs={{0,1},{1,0},{2,3},{3,2},{4,5},{5,4},{6,7},{7,6},{8,9},{9,8},{10,11... | collective-permute-start | bytes 589832 | tf_op jit(solution)/shard_map/ppermute | solution.py:267
  3.9 1.9 %collective-permute-start.1 = (bf16[8,16,768]{2,1,0:T(8,128)(2,1)}, bf16[8,16,768]{2,1,0:T(8,128)(2,1)S(1)}, u32[]{:S(2)}, u32[]{:S(2)}) collective-permute-start(bf16[8,16,768]{2,1,0:T(8,128)(2,1)} %get-tuple-element.27.a_ref), channel_id=1, source_target_pairs={{0,2},{1,3},{2,0},{3,1},{4,6},{5,7},{6,4},{7,5},{8,10},{9,11},{10,... | collective-permute-start | bytes 589832 | tf_op jit(solution)/shard_map/ppermute | solution.py:267
  5.8 0.1 collective-permute-start.2
  5.9 5.4 %collective-permute-start.5 = (bf16[3,3,16,192]{3,2,1,0:T(8,128)(2,1)}, bf16[3,3,16,192]{3,2,1,0:T(8,128)(2,1)S(1)}, u32[]{:S(2)}, u32[]{:S(2)}) collective-permute-start(bf16[3,3,16,192]{3,2,1,0:T(8,128)(2,1)} %get-tuple-element.31), channel_id=1, source_target_pairs={{0,8},{4,12},{8,0},{12,4},{1,9},{5,13},{9,1},{13,5},{2,10},{6,14},... | collective-permute-start | bytes 165896 | tf_op jit(solution)/shard_map/ppermute | solution.py:292
  11.3 8.5 %all-to-all-start = ((f32[64,8,128]{2,1,0:T(8,128)}), f32[64,8,128]{2,1,0:T(8,128)S(1)}, u32[]{:S(2)}, u32[]{:S(2)}) async-start(f32[64,8,128]{2,1,0:T(8,128)} %get-tuple-element.30), calls=%async_computation | async-start | bytes 524288 | tf_op jit(solution)/shard_map/all_to_all | solution.py:271
  19.8 0.1 collective-permute-start.7
  19.9 0.0 collective-permute-done.1.c_ref
  19.9 0.0 collective-permute-done.2.d_ref
  20.0 1.3 %collective-permute-start.3 = (bf16[4,16,768]{2,1,0:T(8,128)(2,1)S(1)}, bf16[4,16,768]{2,1,0:T(8,128)(2,1)S(1)}, u32[]{:S(2)}, u32[]{:S(2)}) collective-permute-start(bf16[4,16,768]{2,1,0:T(8,128)(2,1)S(1)} %get-tuple-element.28), channel_id=1, source_target_pairs={{0,16},{16,0},{32,48},{48,32},{64,80},{80,64},{96,112},{112,96},{1... | collective-permute-start | bytes 294920 | tf_op jit(solution)/shard_map/ppermute | solution.py:260
  21.3 0.8 collective-permute-start.4
  22.1 0.0 collective-permute-done.5.far_ref
  22.1 3.1 %collective-permute-start.6 = (bf16[3,3,16,192]{3,2,1,0:T(8,128)(2,1)S(1)}, bf16[3,3,16,192]{3,2,1,0:T(8,128)(2,1)S(1)}, u32[]{:S(2)}, u32[]{:S(2)}) collective-permute-start(bf16[3,3,16,192]{3,2,1,0:T(8,128)(2,1)S(1)} %collective-permute-done.5.far_ref), channel_id=1, source_target_pairs={{0,16},{16,0},{1,17},{17,1},{2,18},{18,2},{3,19},{19,3},{4,20},{20... | collective-permute-start | bytes 165896 | tf_op jit(solution)/shard_map/ppermute | solution.py:297
  25.2 1.3 %collective-permute-done.7.side_ref = bf16[2,3,3,16,192]{4,3,2,1,0:T(8,128)(2,1)S(1)} collective-permute-done((bf16[2,3,3,16,192]{4,3,2,1,0:T(8,128)(2,1)S(1)}, bf16[2,3,3,16,192]{4,3,2,1,0:T(8,128)(2,1)S(1)}, u32[]{:S(2)}, u32[]{:S(2)}) %collective-permute-start.7) | collective-permute-done | bytes 110624 | tf_op jit(solution)/shard_map/ppermute | solution.py:291
  26.5 0.2 collective-permute-start.8
  26.7 0.0 collective-permute-done.6.far2_ref
  26.7 0.0 collective-permute-done.3.chip_ref
  26.7 0.0 collective-permute-done.4.next_ref
  26.7 4.8 %all-to-all-done.stats_ref = f32[64,8,128]{2,1,0:T(8,128)S(1)} async-done(((f32[64,8,128]{2,1,0:T(8,128)}), f32[64,8,128]{2,1,0:T(8,128)S(1)}, u32[]{:S(2)}, u32[]{:S(2)}) %all-to-all-start) | async-done | bytes 262176 | tf_op jit(solution)/shard_map/all_to_all | solution.py:271
  31.5 1.7 %shard_map.66 = (bf16[8,16,512]{2,1,0:T(8,128)(2,1)S(1)}, bf16[10,4,16,768]{3,2,1,0:T(8,128)(2,1)S(1)}) custom-call(bf16[8,16,768]{2,1,0:T(8,128)(2,1)S(1)} %copy-done.1, bf16[8,16,768]{2,1,0:T(8,128)(2,1)S(1)} %collective-permute-done.b_ref, bf16[8,16,768]{2,1,0:T(8,128)(2,1)S(1)} %collective-permute-done.1.c_ref, ...), custom_call_target="tpu_custom_call" | custom-call | flops 226492416 | bytes 1355776 | tf_op jit(solution)/shard_map/pallas_call | solution.py:32
  33.2 1.8 %collective-permute-start.10 = (bf16[8,16,512]{2,1,0:T(8,128)(2,1)S(1)}, bf16[8,16,512]{2,1,0:T(8,128)(2,1)S(1)}, u32[]{:S(2)}, u32[]{:S(2)}) collective-permute-start(bf16[8,16,512]{2,1,0:T(8,128)(2,1)S(1)} %get-tuple-element.38), channel_id=1, source_target_pairs={{0,12},{4,0},{8,4},{12,8},{16,20},{20,24},{24,28},{28,16},{1,13},{... | collective-permute-start | bytes 393224 | tf_op jit(solution)/shard_map/ppermute | solution.py:236
  35.0 1.2 %shard_map.67 = (bf16[8,16,512]{2,1,0:T(8,128)(2,1)S(1)}, bf16[8,16,512]{2,1,0:T(8,128)(2,1)S(1)}, bf16[8,16,512]{2,1,0:T(8,128)(2,1)S(1)}) custom-call(bf16[10,4,16,768]{3,2,1,0:T(8,128)(2,1)S(1)} %get-tuple-element.32.slab_ref, bf16[2,3,3,16,192]{4,3,2,1,0:T(8,128)(2,1)S(1)} %copy-done.3, bf16[2,3,3,16,192]{4,3,2,1,0:T(8,128)(2,1)S(1)} %collective-permute-done.7.side_ref, ...), custom_call_target="tpu_custom_call" | custom-call | flops 679477248 | bytes 1314816 | tf_op jit(solution)/shard_map/pallas_call | solution.py:32
  36.2 2.5 %collective-permute-start.9 = (bf16[8,16,512]{2,1,0:T(8,128)(2,1)S(1)}, bf16[8,16,512]{2,1,0:T(8,128)(2,1)S(1)}, u32[]{:S(2)}, u32[]{:S(2)}) collective-permute-start(bf16[8,16,512]{2,1,0:T(8,128)(2,1)S(1)} %get-tuple-element.36), channel_id=1, source_target_pairs={{0,4},{4,8},{8,12},{12,0},{16,28},{20,16},{24,20},{28,24},{1,5},{5... | collective-permute-start | bytes 393224 | tf_op jit(solution)/shard_map/ppermute | solution.py:240
  38.7 5.6 %collective-permute-done.10.b_ref = bf16[8,16,512]{2,1,0:T(8,128)(2,1)S(1)} collective-permute-done((bf16[8,16,512]{2,1,0:T(8,128)(2,1)S(1)}, bf16[8,16,512]{2,1,0:T(8,128)(2,1)S(1)}, u32[]{:S(2)}, u32[]{:S(2)}) %collective-permute-start.10) | collective-permute-done | bytes 131104 | tf_op jit(solution)/shard_map/ppermute | solution.py:236
  44.3 0.0 copy-start.4
  44.3 0.1 collective-permute-start.11
  44.4 0.5 copy-done.6
  45.0 0.1 copy-done.4
  45.1 0.7 copy-done.5
  45.8 6.3 %collective-permute-done.11.c_ref = bf16[8,16,512]{2,1,0:T(8,128)(2,1)S(1)} collective-permute-done((bf16[8,16,512]{2,1,0:T(8,128)(2,1)S(1)}, bf16[8,16,512]{2,1,0:T(8,128)(2,1)S(1)}, u32[]{:S(2)}, u32[]{:S(2)}) %collective-permute-start.11) | collective-permute-done | bytes 131104 | tf_op jit(solution)/shard_map/ppermute | solution.py:242
  52.1 0.1 broadcast_in_dim.13.bias_ref
  52.1 0.9 shard_map.69
  53.0 3.5 %collective-permute-start.14 = (bf16[8,16,768]{2,1,0:T(8,128)(2,1)S(1)}, bf16[8,16,768]{2,1,0:T(8,128)(2,1)S(1)}, u32[]{:S(2)}, u32[]{:S(2)}) collective-permute-start(bf16[8,16,768]{2,1,0:T(8,128)(2,1)S(1)} %get-tuple-element.40.a_ref), channel_id=1, source_target_pairs={{0,3},{1,2},{2,1},{3,0},{4,7},{5,6},{6,5},{7,4},{8,11},{9,10},{10,... | collective-permute-start | bytes 589832 | tf_op jit(solution)/shard_map/ppermute | solution.py:267
  56.5 5.6 %all-to-all-start.1 = ((f32[64,8,128]{2,1,0:T(8,128)}), f32[64,8,128]{2,1,0:T(8,128)S(1)}, u32[]{:S(2)}, u32[]{:S(2)}) async-start(f32[64,8,128]{2,1,0:T(8,128)} %get-tuple-element.43), calls=%async_computation.1 | async-start | bytes 524288 | tf_op jit(solution)/shard_map/all_to_all | solution.py:271
  62.1 0.2 collective-permute-done.14.d_ref
  62.3 0.1 collective-permute-start.15
  62.4 0.7 collective-permute-start.16
  63.1 0.6 collective-permute-done.15.chip_ref
  63.7 8.4 %all-to-all-done.1.stats_ref = f32[64,8,128]{2,1,0:T(8,128)S(1)} async-done(((f32[64,8,128]{2,1,0:T(8,128)}), f32[64,8,128]{2,1,0:T(8,128)S(1)}, u32[]{:S(2)}, u32[]{:S(2)}) %all-to-all-start.1) | async-done | bytes 262176 | tf_op jit(solution)/shard_map/all_to_all | solution.py:271
  72.1 1.7 %shard_map.71 = (bf16[8,16,512]{2,1,0:T(8,128)(2,1)S(1)}, bf16[10,4,16,768]{3,2,1,0:T(8,128)(2,1)S(1)}) custom-call(bf16[8,16,768]{2,1,0:T(8,128)(2,1)S(1)} %get-tuple-element.40.a_ref, bf16[8,16,768]{2,1,0:T(8,128)(2,1)S(1)} %collective-permute-done.12.b_ref, bf16[8,16,768]{2,1,0:T(8,128)(2,1)S(1)} %collective-permute-done.13.c_ref, ...), custom_call_target="tpu_custom_call" | custom-call | flops 226492416 | bytes 1355776 | tf_op jit(solution)/shard_map/pallas_call | solution.py:32
  73.7 0.1 collective-permute-start.18
  73.8 1.2 %shard_map.72 = (bf16[8,16,512]{2,1,0:T(8,128)(2,1)S(1)}, bf16[8,16,512]{2,1,0:T(8,128)(2,1)S(1)}, bf16[8,16,512]{2,1,0:T(8,128)(2,1)S(1)}) custom-call(bf16[10,4,16,768]{3,2,1,0:T(8,128)(2,1)S(1)} %get-tuple-element.44.slab_ref, bf16[2,3,3,16,192]{4,3,2,1,0:T(8,128)(2,1)S(1)} %copy-done.3, bf16[2,3,3,16,192]{4,3,2,1,0:T(8,128)(2,1)S(1)} %collective-permute-done.7.side_ref, ...), custom_call_target="tpu_custom_call" | custom-call | flops 679477248 | bytes 1314816 | tf_op jit(solution)/shard_map/pallas_call | solution.py:32
  75.0 4.2 %collective-permute-start.17 = (bf16[8,16,512]{2,1,0:T(8,128)(2,1)S(1)}, bf16[8,16,512]{2,1,0:T(8,128)(2,1)S(1)}, u32[]{:S(2)}, u32[]{:S(2)}) collective-permute-start(bf16[8,16,512]{2,1,0:T(8,128)(2,1)S(1)} %get-tuple-element.46), channel_id=1, source_target_pairs={{0,4},{4,8},{8,12},{12,0},{16,28},{20,16},{24,20},{28,24},{1,5},{5... | collective-permute-start | bytes 393224 | tf_op jit(solution)/shard_map/ppermute | solution.py:240
  79.2 5.7 %collective-permute-done.18.b_ref = bf16[8,16,512]{2,1,0:T(8,128)(2,1)S(1)} collective-permute-done((bf16[8,16,512]{2,1,0:T(8,128)(2,1)S(1)}, bf16[8,16,512]{2,1,0:T(8,128)(2,1)S(1)}, u32[]{:S(2)}, u32[]{:S(2)}) %collective-permute-start.18) | collective-permute-done | bytes 131104 | tf_op jit(solution)/shard_map/ppermute | solution.py:236
  84.9 0.1 collective-permute-start.19
  85.0 7.8 %collective-permute-done.19.c_ref = bf16[8,16,512]{2,1,0:T(8,128)(2,1)S(1)} collective-permute-done((bf16[8,16,512]{2,1,0:T(8,128)(2,1)S(1)}, bf16[8,16,512]{2,1,0:T(8,128)(2,1)S(1)}, u32[]{:S(2)}, u32[]{:S(2)}) %collective-permute-start.19) | collective-permute-done | bytes 131104 | tf_op jit(solution)/shard_map/ppermute | solution.py:242
  92.8 0.1 broadcast_in_dim.15.bias_ref
  92.9 0.7 shard_map.74
  (29 shorter events, 0.2 us)
Async XLA Ops:
  2.3 17.6 %collective-permute-start = (bf16[8,16,768]{2,1,0:T(8,128)(2,1)}, bf16[8,16,768]{2,1,0:T(8,128)(2,1)S(1)}, u32[]{:S(2)}, u32[]{:S(2)}) collective-permute-start(bf16[8,16,768]{2,1,0:T(8,128)(2,1)} %get-tuple-element.27.a_ref), channel_id=1, source_target_pairs={{0,1},{1,0},{2,3},{3,2},{4,5},{5,4},{6,7},{7,6},{8,9},{9,8},{10,11... | collective-permute-start | bytes 589832 | tf_op jit(solution)/shard_map/ppermute | solution.py:267
  3.9 16.0 %collective-permute-start.1 = (bf16[8,16,768]{2,1,0:T(8,128)(2,1)}, bf16[8,16,768]{2,1,0:T(8,128)(2,1)S(1)}, u32[]{:S(2)}, u32[]{:S(2)}) collective-permute-start(bf16[8,16,768]{2,1,0:T(8,128)(2,1)} %get-tuple-element.27.a_ref), channel_id=1, source_target_pairs={{0,2},{1,3},{2,0},{3,1},{4,6},{5,7},{6,4},{7,5},{8,10},{9,11},{10,... | collective-permute-start | bytes 589832 | tf_op jit(solution)/shard_map/ppermute | solution.py:267
  5.8 14.1 %collective-permute-start.2 = (bf16[8,16,768]{2,1,0:T(8,128)(2,1)}, bf16[8,16,768]{2,1,0:T(8,128)(2,1)S(1)}, u32[]{:S(2)}, u32[]{:S(2)}) collective-permute-start(bf16[8,16,768]{2,1,0:T(8,128)(2,1)} %get-tuple-element.27.a_ref), channel_id=1, source_target_pairs={{0,3},{1,2},{2,1},{3,0},{4,7},{5,6},{6,5},{7,4},{8,11},{9,10},{10,... | collective-permute-start | bytes 589832 | tf_op jit(solution)/shard_map/ppermute | solution.py:267
  5.9 16.2 %collective-permute-start.5 = (bf16[3,3,16,192]{3,2,1,0:T(8,128)(2,1)}, bf16[3,3,16,192]{3,2,1,0:T(8,128)(2,1)S(1)}, u32[]{:S(2)}, u32[]{:S(2)}) collective-permute-start(bf16[3,3,16,192]{3,2,1,0:T(8,128)(2,1)} %get-tuple-element.31), channel_id=1, source_target_pairs={{0,8},{4,12},{8,0},{12,4},{1,9},{5,13},{9,1},{13,5},{2,10},{6,14},... | collective-permute-start | bytes 165896 | tf_op jit(solution)/shard_map/ppermute | solution.py:292
  11.3 8.5 %copy-start.7 = (bf16[2,3,3,16,192]{4,3,2,1,0:T(8,128)(2,1)S(1)}, bf16[2,3,3,16,192]{4,3,2,1,0:T(8,128)(2,1)}, u32[]{:S(2)}) copy-start(bf16[2,3,3,16,192]{4,3,2,1,0:T(8,128)(2,1)} %get-tuple-element.34) | copy-start | bytes 331780
  11.3 8.7 %copy-start.1 = (bf16[8,16,768]{2,1,0:T(8,128)(2,1)S(1)}, bf16[8,16,768]{2,1,0:T(8,128)(2,1)}, u32[]{:S(2)}) copy-start(bf16[8,16,768]{2,1,0:T(8,128)(2,1)} %get-tuple-element.27.a_ref) | copy-start | bytes 589828
  11.3 20.2 %all-to-all-start = ((f32[64,8,128]{2,1,0:T(8,128)}), f32[64,8,128]{2,1,0:T(8,128)S(1)}, u32[]{:S(2)}, u32[]{:S(2)}) async-start(f32[64,8,128]{2,1,0:T(8,128)} %get-tuple-element.30), calls=%async_computation | async-start | bytes 524288 | tf_op jit(solution)/shard_map/all_to_all | solution.py:271
  19.8 6.7 %collective-permute-start.7 = (bf16[2,3,3,16,192]{4,3,2,1,0:T(8,128)(2,1)S(1)}, bf16[2,3,3,16,192]{4,3,2,1,0:T(8,128)(2,1)S(1)}, u32[]{:S(2)}, u32[]{:S(2)}) collective-permute-start(bf16[2,3,3,16,192]{4,3,2,1,0:T(8,128)(2,1)S(1)} %copy-done.7), channel_id=1, source_target_pairs={{0,4},{4,8},{8,12},{12,0},{16,28},{20,16},{24,20},{28,24},{1,5},{5... | collective-permute-start | bytes 331784 | tf_op jit(solution)/shard_map/ppermute | solution.py:291
  20.0 6.7 %collective-permute-start.3 = (bf16[4,16,768]{2,1,0:T(8,128)(2,1)S(1)}, bf16[4,16,768]{2,1,0:T(8,128)(2,1)S(1)}, u32[]{:S(2)}, u32[]{:S(2)}) collective-permute-start(bf16[4,16,768]{2,1,0:T(8,128)(2,1)S(1)} %get-tuple-element.28), channel_id=1, source_target_pairs={{0,16},{16,0},{32,48},{48,32},{64,80},{80,64},{96,112},{112,96},{1... | collective-permute-start | bytes 294920 | tf_op jit(solution)/shard_map/ppermute | solution.py:260
  21.3 13.7 %copy-start.3 = (bf16[2,3,3,16,192]{4,3,2,1,0:T(8,128)(2,1)S(1)}, bf16[2,3,3,16,192]{4,3,2,1,0:T(8,128)(2,1)}, u32[]{:S(2)}) copy-start(bf16[2,3,3,16,192]{4,3,2,1,0:T(8,128)(2,1)} %get-tuple-element.33.own_ref) | copy-start | bytes 331780
  21.3 5.4 %collective-permute-start.4 = (bf16[4,16,768]{2,1,0:T(8,128)(2,1)S(1)}, bf16[4,16,768]{2,1,0:T(8,128)(2,1)S(1)}, u32[]{:S(2)}, u32[]{:S(2)}) collective-permute-start(bf16[4,16,768]{2,1,0:T(8,128)(2,1)S(1)} %get-tuple-element.29), channel_id=1, source_target_pairs={{16,32},{48,64},{80,96},{112,128},{144,160},{176,192},{208,224},{3... | collective-permute-start | bytes 294920 | tf_op jit(solution)/shard_map/ppermute | solution.py:262
  22.1 4.6 %collective-permute-start.6 = (bf16[3,3,16,192]{3,2,1,0:T(8,128)(2,1)S(1)}, bf16[3,3,16,192]{3,2,1,0:T(8,128)(2,1)S(1)}, u32[]{:S(2)}, u32[]{:S(2)}) collective-permute-start(bf16[3,3,16,192]{3,2,1,0:T(8,128)(2,1)S(1)} %collective-permute-done.5.far_ref), channel_id=1, source_target_pairs={{0,16},{16,0},{1,17},{17,1},{2,18},{18,2},{3,19},{19,3},{4,20},{20... | collective-permute-start | bytes 165896 | tf_op jit(solution)/shard_map/ppermute | solution.py:297
  26.5 8.5 %collective-permute-start.8 = (bf16[2,3,3,16,192]{4,3,2,1,0:T(8,128)(2,1)S(1)}, bf16[2,3,3,16,192]{4,3,2,1,0:T(8,128)(2,1)S(1)}, u32[]{:S(2)}, u32[]{:S(2)}) collective-permute-start(bf16[2,3,3,16,192]{4,3,2,1,0:T(8,128)(2,1)S(1)} %collective-permute-done.7.side_ref), channel_id=1, source_target_pairs={{0,16},{16,0},{1,17},{17,1},{2,18},{18,2},{3,19},{19,3},{4,20},{20... | collective-permute-start | bytes 331784 | tf_op jit(solution)/shard_map/ppermute | solution.py:297
  33.2 11.1 %collective-permute-start.10 = (bf16[8,16,512]{2,1,0:T(8,128)(2,1)S(1)}, bf16[8,16,512]{2,1,0:T(8,128)(2,1)S(1)}, u32[]{:S(2)}, u32[]{:S(2)}) collective-permute-start(bf16[8,16,512]{2,1,0:T(8,128)(2,1)S(1)} %get-tuple-element.38), channel_id=1, source_target_pairs={{0,12},{4,0},{8,4},{12,8},{16,20},{20,24},{24,28},{28,16},{1,13},{... | collective-permute-start | bytes 393224 | tf_op jit(solution)/shard_map/ppermute | solution.py:236
  36.2 9.6 %collective-permute-start.9 = (bf16[8,16,512]{2,1,0:T(8,128)(2,1)S(1)}, bf16[8,16,512]{2,1,0:T(8,128)(2,1)S(1)}, u32[]{:S(2)}, u32[]{:S(2)}) collective-permute-start(bf16[8,16,512]{2,1,0:T(8,128)(2,1)S(1)} %get-tuple-element.36), channel_id=1, source_target_pairs={{0,4},{4,8},{8,12},{12,0},{16,28},{20,16},{24,20},{28,24},{1,5},{5... | collective-permute-start | bytes 393224 | tf_op jit(solution)/shard_map/ppermute | solution.py:240
  44.3 0.7 copy-start.6
  44.3 7.9 %copy-start.2 = (bf16[8,16,256]{2,1,0:T(8,128)(2,1)S(1)}, bf16[8,16,256]{2,1,0:T(8,128)(2,1)}, u32[]{:S(2)}) copy-start(bf16[8,16,256]{2,1,0:T(8,128)(2,1)} %get-tuple-element.39.later_ref) | copy-start | bytes 196612
  44.3 0.7 copy-start.4
  44.3 7.7 %collective-permute-start.11 = (bf16[8,16,512]{2,1,0:T(8,128)(2,1)S(1)}, bf16[8,16,512]{2,1,0:T(8,128)(2,1)S(1)}, u32[]{:S(2)}, u32[]{:S(2)}) collective-permute-start(bf16[8,16,512]{2,1,0:T(8,128)(2,1)S(1)} %shard_map.68), channel_id=1, source_target_pairs={{0,12},{4,0},{8,4},{12,8},{16,20},{20,24},{24,28},{28,16},{1,13},{... | collective-permute-start | bytes 393224 | tf_op jit(solution)/shard_map/ppermute | solution.py:242
  45.0 0.7 copy-start.5
  53.0 9.1 %collective-permute-start.12 = (bf16[8,16,768]{2,1,0:T(8,128)(2,1)S(1)}, bf16[8,16,768]{2,1,0:T(8,128)(2,1)S(1)}, u32[]{:S(2)}, u32[]{:S(2)}) collective-permute-start(bf16[8,16,768]{2,1,0:T(8,128)(2,1)S(1)} %get-tuple-element.40.a_ref), channel_id=1, source_target_pairs={{0,1},{1,0},{2,3},{3,2},{4,5},{5,4},{6,7},{7,6},{8,9},{9,8},{10,11... | collective-permute-start | bytes 589832 | tf_op jit(solution)/shard_map/ppermute | solution.py:267
  53.0 9.1 %collective-permute-start.13 = (bf16[8,16,768]{2,1,0:T(8,128)(2,1)S(1)}, bf16[8,16,768]{2,1,0:T(8,128)(2,1)S(1)}, u32[]{:S(2)}, u32[]{:S(2)}) collective-permute-start(bf16[8,16,768]{2,1,0:T(8,128)(2,1)S(1)} %get-tuple-element.40.a_ref), channel_id=1, source_target_pairs={{0,2},{1,3},{2,0},{3,1},{4,6},{5,7},{6,4},{7,5},{8,10},{9,11},{10,... | collective-permute-start | bytes 589832 | tf_op jit(solution)/shard_map/ppermute | solution.py:267
  53.0 9.2 %collective-permute-start.14 = (bf16[8,16,768]{2,1,0:T(8,128)(2,1)S(1)}, bf16[8,16,768]{2,1,0:T(8,128)(2,1)S(1)}, u32[]{:S(2)}, u32[]{:S(2)}) collective-permute-start(bf16[8,16,768]{2,1,0:T(8,128)(2,1)S(1)} %get-tuple-element.40.a_ref), channel_id=1, source_target_pairs={{0,3},{1,2},{2,1},{3,0},{4,7},{5,6},{6,5},{7,4},{8,11},{9,10},{10,... | collective-permute-start | bytes 589832 | tf_op jit(solution)/shard_map/ppermute | solution.py:267
  56.5 15.5 %all-to-all-start.1 = ((f32[64,8,128]{2,1,0:T(8,128)}), f32[64,8,128]{2,1,0:T(8,128)S(1)}, u32[]{:S(2)}, u32[]{:S(2)}) async-start(f32[64,8,128]{2,1,0:T(8,128)} %get-tuple-element.43), calls=%async_computation.1 | async-start | bytes 524288 | tf_op jit(solution)/shard_map/all_to_all | solution.py:271
  62.3 1.4 %collective-permute-start.15 = (bf16[4,16,768]{2,1,0:T(8,128)(2,1)S(1)}, bf16[4,16,768]{2,1,0:T(8,128)(2,1)S(1)}, u32[]{:S(2)}, u32[]{:S(2)}) collective-permute-start(bf16[4,16,768]{2,1,0:T(8,128)(2,1)S(1)} %get-tuple-element.41), channel_id=1, source_target_pairs={{0,16},{16,0},{32,48},{48,32},{64,80},{80,64},{96,112},{112,96},{1... | collective-permute-start | bytes 294920 | tf_op jit(solution)/shard_map/ppermute | solution.py:260
  62.4 1.3 %collective-permute-start.16 = (bf16[4,16,768]{2,1,0:T(8,128)(2,1)S(1)}, bf16[4,16,768]{2,1,0:T(8,128)(2,1)S(1)}, u32[]{:S(2)}, u32[]{:S(2)}) collective-permute-start(bf16[4,16,768]{2,1,0:T(8,128)(2,1)S(1)} %get-tuple-element.42), channel_id=1, source_target_pairs={{16,32},{48,64},{80,96},{112,128},{144,160},{176,192},{208,224},{3... | collective-permute-start | bytes 294920 | tf_op jit(solution)/shard_map/ppermute | solution.py:262
  73.7 11.2 %collective-permute-start.18 = (bf16[8,16,512]{2,1,0:T(8,128)(2,1)S(1)}, bf16[8,16,512]{2,1,0:T(8,128)(2,1)S(1)}, u32[]{:S(2)}, u32[]{:S(2)}) collective-permute-start(bf16[8,16,512]{2,1,0:T(8,128)(2,1)S(1)} %get-tuple-element.48), channel_id=1, source_target_pairs={{0,12},{4,0},{8,4},{12,8},{16,20},{20,24},{24,28},{28,16},{1,13},{... | collective-permute-start | bytes 393224 | tf_op jit(solution)/shard_map/ppermute | solution.py:236
  75.0 10.0 %collective-permute-start.17 = (bf16[8,16,512]{2,1,0:T(8,128)(2,1)S(1)}, bf16[8,16,512]{2,1,0:T(8,128)(2,1)S(1)}, u32[]{:S(2)}, u32[]{:S(2)}) collective-permute-start(bf16[8,16,512]{2,1,0:T(8,128)(2,1)S(1)} %get-tuple-element.46), channel_id=1, source_target_pairs={{0,4},{4,8},{8,12},{12,0},{16,28},{20,16},{24,20},{28,24},{1,5},{5... | collective-permute-start | bytes 393224 | tf_op jit(solution)/shard_map/ppermute | solution.py:240
  84.9 8.0 %copy-start = (bf16[4,8,16,128]{3,2,1,0:T(8,128)(2,1)S(1)}, bf16[4,8,16,128]{3,2,1,0:T(8,128)(2,1)}, u32[]{:S(2)}) copy-start(bf16[4,8,16,128]{3,2,1,0:T(8,128)(2,1)} %x_ref.1) | copy-start | bytes 393220
  84.9 7.9 %collective-permute-start.19 = (bf16[8,16,512]{2,1,0:T(8,128)(2,1)S(1)}, bf16[8,16,512]{2,1,0:T(8,128)(2,1)S(1)}, u32[]{:S(2)}, u32[]{:S(2)}) collective-permute-start(bf16[8,16,512]{2,1,0:T(8,128)(2,1)S(1)} %shard_map.73), channel_id=1, source_target_pairs={{0,12},{4,0},{8,4},{12,8},{16,20},{20,24},{24,28},{28,16},{1,13},{... | collective-permute-start | bytes 393224 | tf_op jit(solution)/shard_map/ppermute | solution.py:242

commit v15 on v11

--- a/solution.py
+++ b/solution.py
@@ -44,16 +44,13 @@
     return lax.axis_index(ROW), lax.axis_index("zh"), lax.axis_index(NEAR)
 
 
-def put_stats(rows_ref, note_ref, stats_ref):
+def put_stats(rows_ref, note_ref):
     slabs = [rows_ref[:, :, 256 + 128 * t : 384 + 128 * t].astype(F32) for t in range(4)]
     x = jnp.concatenate(slabs, axis=0).reshape(32, 2, GROUP, 128)
-    number = x.shape[0] * GROUP
-    mean = jnp.sum(x, axis=(0, 2), keepdims=True) / number
+    mean = jnp.sum(x, axis=(0, 2), keepdims=True) / (32 * GROUP)
     off = x - mean
-    square = jnp.sum(off * off, axis=(0, 2))
     note_ref[0:2] = mean.reshape(2, 128)
-    note_ref[2:4] = square
-    stats_ref[...] = jnp.broadcast_to(note_ref[...][None], stats_ref.shape)
+    note_ref[2:4] = jnp.sum(off * off, axis=(0, 2))
 
 
 def fetch(pairs, sems):
@@ -98,9 +95,11 @@
     side_ref[...] = pieces_ref[1 + 2 * core]
     far_ref[...] = pieces_ref[2, core]
     note_ref[...] = jnp.zeros((8, 128), F32)
-    note_ref[4:5, 0:16] = gain_ref[0:1, :]
-    note_ref[5:6, 0:16] = shift_ref[0:1, :]
-    put_stats(raw_ref, note_ref, stats_ref)
+    for layer in range(2):
+        note_ref[4 + layer : 5 + layer, 0:16] = gain_ref[layer : layer + 1, :]
+        note_ref[6 + layer : 7 + layer, 0:16] = shift_ref[layer : layer + 1, :]
+    put_stats(raw_ref, note_ref)
+    stats_ref[...] = jnp.broadcast_to(note_ref[...][None], stats_ref.shape)
 
 
 def shift_columns(left, centre, right):
@@ -111,8 +110,9 @@
     return left + centre + right
 
 
-def get_affine(stats_ref, affine_ref):
-    stats = stats_ref[...].reshape(16, 4, 8, 128)
+def get_affine(layer, stats_ref, notes_ref, affine_ref):
+    stats = stats_ref[...]
+    stats = stats.reshape(16, 4, stats.shape[1], 128)
     number = 32 * GROUP
     means = stats[:, :, 0:2]
     mean = jnp.mean(means, axis=(0, 3), keepdims=True)
@@ -123,8 +123,8 @@
     inverse = jnp.broadcast_to(inverse.reshape(4, 2, 1, 1), (4, 2, GROUP, 128)).reshape(4, 16, 128)
     shape = (4, 16, 128)
     same = lax.broadcasted_iota(jnp.int32, shape, 1) == lax.broadcasted_iota(jnp.int32, shape, 2)
-    gain = jnp.sum(jnp.where(same, stats[0, :, 4:5], 0.0), axis=2, keepdims=True)
-    shift = jnp.sum(jnp.where(same, stats[0, :, 5:6], 0.0), axis=2, keepdims=True)
+    gain = jnp.sum(jnp.where(same, notes_ref[0:4, 4 + layer : 5 + layer], 0.0), axis=2, keepdims=True)
+    shift = jnp.sum(jnp.where(same, notes_ref[0:4, 6 + layer : 7 + layer], 0.0), axis=2, keepdims=True)
     affine_ref[0] = mean
     affine_ref[1] = inverse * gain
     affine_ref[2] = jnp.broadcast_to(shift, shape)
@@ -152,11 +152,11 @@
 
 
 def conv_kernel(
-    layer, a_ref, b_ref, c_ref, d_ref, chip_ref, next_ref, stats_ref, other_ref, far_ref, far2_ref,
+    layer, a_ref, b_ref, c_ref, d_ref, chip_ref, next_ref, stats_ref, notes_ref, other_ref, far_ref, far2_ref,
     o2_ref, o3_ref, slab_ref, affine_ref, held_ref,
 ):
     row, _, here = place()
-    get_affine(stats_ref, affine_ref)
+    get_affine(layer, stats_ref, notes_ref, affine_ref)
     upper = lax.rem(row, 2) == 0
     not_top = (row > 0).astype(F32)
     not_bottom = (row < 15).astype(F32)
@@ -197,14 +197,14 @@
     products(layer, w_refs, (o2_ref, o3_ref), slab_ref)
 
 
-def merge_kernel(a_ref, b_ref, c_ref, bias_ref, later_ref, note1_ref, mid_ref, stats_ref, note_ref):
+def merge_kernel(a_ref, b_ref, c_ref, bias_ref, later_ref, mid_ref, stats_ref, note_ref):
     bias = jnp.concatenate([bias_ref[...]] * 4, axis=1)
     for r in range(8):
         summed = a_ref[r].astype(F32) + b_ref[r].astype(F32) + c_ref[r].astype(F32)
         mid_ref[r, :, 0:256] = later_ref[r]
         mid_ref[r, :, 256:768] = (summed + bias).astype(BF16)
-    note_ref[...] = note1_ref[...]
-    put_stats(mid_ref, note_ref, stats_ref)
+    put_stats(mid_ref, note_ref)
+    stats_ref[...] = jnp.broadcast_to(note_ref[...][None], stats_ref.shape)
 
 
 def last_kernel(x_ref, a_ref, b_ref, c_ref, bias_ref, o_ref):
@@ -296,16 +296,16 @@
     swap = [(0, 1), (1, 0)]
     weights = [own, side, far, lax.ppermute(side, "core", swap), lax.ppermute(far, "core", swap)]
     bias = jnp.broadcast_to(conv_bias[:, :, None], (2, 16, 128))
-    note1 = jnp.pad(jnp.stack([norm_gain[1], norm_shift[1]]), ((4, 2), (0, 112)))
-    partial = convolve(0, [*raw, stats], *weights)
+    notes = stats
+    partial = convolve(0, [*raw, stats, notes], *weights)
     middle, stats = call(
-        merge_kernel, (struct((8, 16, 768)), struct((64, 8, 128), F32)), *partial, bias[0], later, note1,
-        scratch=(note,),
+        merge_kernel, (struct((8, 16, 768)), struct((64, 4, 128), F32)), *partial, bias[0], later,
+        scratch=(pltpu.VMEM((4, 128), F32),),
     )
     middle = near(middle)
     stats = exchange(stats, ROW + NEAR)
     middle = middle + rows_beside(middle)
-    partial = convolve(1, [*middle, stats], *weights)
+    partial = convolve(1, [*middle, stats, notes], *weights)
     return call(last_kernel, struct((4, 8, 16, 128)), frames, *partial, bias[1])
 
 

time: 93.6 us -> 93.5 us (level)
    all_to_all x2, waiting for transfers between devices: 0.01 us -> 1.21 us  [exchange(): return lax.all_to_all(x, axes, 0, 0, tiled=True)]
    ppermute x2, waiting for transfers between devices: 9.84 us -> 8.64 us  [rows_beside(): beyond = lax.ppermute(beyond, ROW, pairs)]
  transfers between devices with their start and end apart: 22 -> 22, of which waited for: 7 -> 8; matrix products, arithmetic and copies ran while one was open for 0% -> 0% of each run, Pallas kernels for 2% -> 2%
where the time goes in v15:
time: 93.5 us; the launch traced here: 92.7 us
  starting transfers between devices  48.8 us (52%)
  waiting for transfers between devices  34.2 us (37%)
  Pallas kernels  8.77 us (9%)
    all_to_all x2, starting transfers between devices, exchange(): return lax.all_to_all(x, axes, 0, 0, tiled=True)  18.2 us
    ppermute x2, waiting for transfers between devices, convolve(): side = lax.ppermute(side, ('core', 'zh'), sides(-1))  12.9 us
    ppermute x2, waiting for transfers between devices, convolve(): far = lax.ppermute(far, ('core', 'zh'), sides(-1))  10.1 us
    pallas_call x11, Pallas kernels, call(): pl.pallas_call(kernel, out_shape=outs, in_specs=specs, out_specs=jax.tree...  8.77 us
    ppermute x2, waiting for transfers between devices, rows_beside(): beyond = lax.ppermute(beyond, ROW, pairs)  8.64 us
    ppermute x2, starting transfers between devices, rows_beside(): beyond = lax.ppermute(beyond, ROW, pairs)  7.98 us
    ppermute x6, starting transfers between devices, near(): lax.ppermute(x, NEAR, [(i, i ^ k) for i in range(4)])  6.59 us
    ppermute x2, starting transfers between devices, convolve(): other = lax.ppermute(other, ('core', 'zh'), sides(1))  6.07 us
  transfers between devices with their start and end apart: 22, of which 8 were waited for; matrix products, arithmetic and copies ran while one was open for 0% of the time, Pallas kernels for 2%

profile of v15, /device:TPU:27, one launch (start us, length us, event | category | flops | bytes accessed | tf_op | source)
XLA Modules:
  0.0 92.7 jit_solution(11684155567420433576)
XLA Ops:
  0.0 2.3 %shard_map.64 = (bf16[8,16,768]{2,1,0:T(8,128)(2,1)}, bf16[8,16,256]{2,1,0:T(8,128)(2,1)}, f32[64,8,128]{2,1,0:T(8,128)}, bf16[2,3,3,16,192]{4,3,2,1,0:T(8,128)(...) custom-call(bf16[4,8,16,128]{3,2,1,0:T(8,128)(2,1)} %x_ref.1, ...), custom_call_target="tpu_custom_call" | custom-call | bytes 704768 | tf_op jit(solution)/shard_map/pallas_call | solution.py:32
  2.3 0.3 collective-permute-start
  2.6 1.6 %collective-permute-start.1 = (bf16[8,16,768]{2,1,0:T(8,128)(2,1)}, bf16[8,16,768]{2,1,0:T(8,128)(2,1)S(1)}, u32[]{:S(2)}, u32[]{:S(2)}) collective-permute-start(bf16[8,16,768]{2,1,0:T(8,128)(2,1)} %get-tuple-element.27.a_ref), channel_id=1, source_target_pairs={{0,2},{1,3},{2,0},{3,1},{4,6},{5,7},{6,4},{7,5},{8,10},{9,11},{10,... | collective-permute-start | bytes 589832 | tf_op jit(solution)/shard_map/ppermute | solution.py:267
  4.3 0.9 %collective-permute-start.2 = (bf16[8,16,768]{2,1,0:T(8,128)(2,1)}, bf16[8,16,768]{2,1,0:T(8,128)(2,1)S(1)}, u32[]{:S(2)}, u32[]{:S(2)}) collective-permute-start(bf16[8,16,768]{2,1,0:T(8,128)(2,1)} %get-tuple-element.27.a_ref), channel_id=1, source_target_pairs={{0,3},{1,2},{2,1},{3,0},{4,7},{5,6},{6,5},{7,4},{8,11},{9,10},{10,... | collective-permute-start | bytes 589832 | tf_op jit(solution)/shard_map/ppermute | solution.py:267
  5.2 5.8 %collective-permute-start.5 = (bf16[2,3,3,16,192]{4,3,2,1,0:T(8,128)(2,1)}, bf16[2,3,3,16,192]{4,3,2,1,0:T(8,128)(2,1)S(1)}, u32[]{:S(2)}, u32[]{:S(2)}) collective-permute-start(bf16[2,3,3,16,192]{4,3,2,1,0:T(8,128)(2,1)} %get-tuple-element.31), channel_id=1, source_target_pairs={{0,4},{4,8},{8,12},{12,0},{16,28},{20,16},{24,20},{28,24},{1,5},{5... | collective-permute-start | bytes 331784 | tf_op jit(solution)/shard_map/ppermute | solution.py:291
  11.1 0.9 collective-permute-start.7
  11.9 11.2 %all-to-all-start = ((f32[64,8,128]{2,1,0:T(8,128)}), f32[64,8,128]{2,1,0:T(8,128)S(1)}, u32[]{:S(2)}, u32[]{:S(2)}) async-start(f32[64,8,128]{2,1,0:T(8,128)} %get-tuple-element.30), calls=%async_computation | async-start | bytes 524288 | tf_op jit(solution)/shard_map/all_to_all | solution.py:271
  23.2 0.0 collective-permute-done.5.side_ref
  23.2 1.2 %collective-permute-start.6 = (bf16[2,3,3,16,192]{4,3,2,1,0:T(8,128)(2,1)S(1)}, bf16[2,3,3,16,192]{4,3,2,1,0:T(8,128)(2,1)S(1)}, u32[]{:S(2)}, u32[]{:S(2)}) collective-permute-start(bf16[2,3,3,16,192]{4,3,2,1,0:T(8,128)(2,1)S(1)} %collective-permute-done.5.side_ref), channel_id=1, source_target_pairs={{0,16},{16,0},{1,17},{17,1},{2,18},{18,2},{3,19},{19,3},{4,20},{20... | collective-permute-start | bytes 331784 | tf_op jit(solution)/shard_map/ppermute | solution.py:297
  24.4 0.0 collective-permute-done.b_ref
  24.4 0.0 collective-permute-done.1.c_ref
  24.4 0.0 collective-permute-done.2.d_ref
  24.5 0.1 collective-permute-start.3
  24.6 4.2 %collective-permute-start.4 = (bf16[4,16,768]{2,1,0:T(8,128)(2,1)S(1)}, bf16[4,16,768]{2,1,0:T(8,128)(2,1)S(1)}, u32[]{:S(2)}, u32[]{:S(2)}) collective-permute-start(bf16[4,16,768]{2,1,0:T(8,128)(2,1)S(1)} %get-tuple-element.29), channel_id=1, source_target_pairs={{16,32},{48,64},{80,96},{112,128},{144,160},{176,192},{208,224},{3... | collective-permute-start | bytes 294920 | tf_op jit(solution)/shard_map/ppermute | solution.py:262
  28.8 0.0 collective-permute-done.7.far_ref
  28.8 0.1 collective-permute-start.8
  28.9 1.3 %collective-permute-done.8.far2_ref = bf16[3,3,16,192]{3,2,1,0:T(8,128)(2,1)S(1)} collective-permute-done((bf16[3,3,16,192]{3,2,1,0:T(8,128)(2,1)S(1)}, bf16[3,3,16,192]{3,2,1,0:T(8,128)(2,1)S(1)}, u32[]{:S(2)}, u32[]{:S(2)}) %collective-permute-start.8) | collective-permute-done | bytes 55328 | tf_op jit(solution)/shard_map/ppermute | solution.py:297
  30.2 4.1 %collective-permute-done.4.next_ref = bf16[4,16,768]{2,1,0:T(8,128)(2,1)S(1)} collective-permute-done((bf16[4,16,768]{2,1,0:T(8,128)(2,1)S(1)}, bf16[4,16,768]{2,1,0:T(8,128)(2,1)S(1)}, u32[]{:S(2)}, u32[]{:S(2)}) %collective-permute-start.4) | collective-permute-done | bytes 98336 | tf_op jit(solution)/shard_map/ppermute | solution.py:262
  34.3 0.0 all-to-all-done.stats_ref.notes_ref
  34.3 1.5 %shard_map.66 = (bf16[8,16,512]{2,1,0:T(8,128)(2,1)S(1)}, bf16[8,16,512]{2,1,0:T(8,128)(2,1)S(1)}, bf16[10,4,16,768]{3,2,1,0:T(8,128)(2,1)S(1)}) custom-call(bf16[8,16,768]{2,1,0:T(8,128)(2,1)S(1)} %copy-done.1, bf16[8,16,768]{2,1,0:T(8,128)(2,1)S(1)} %collective-permute-done.b_ref, bf16[8,16,768]{2,1,0:T(8,128)(2,1)S(1)} %collective-permute-done.1.c_ref, ...), custom_call_target="tpu_custom_call" | custom-call | flops 452984832 | bytes 1728512 | tf_op jit(solution)/shard_map/pallas_call | solution.py:32
  35.8 0.1 collective-permute-start.10
  35.9 3.6 %collective-permute-start.9 = (bf16[8,16,512]{2,1,0:T(8,128)(2,1)S(1)}, bf16[8,16,512]{2,1,0:T(8,128)(2,1)S(1)}, u32[]{:S(2)}, u32[]{:S(2)}) collective-permute-start(bf16[8,16,512]{2,1,0:T(8,128)(2,1)S(1)} %get-tuple-element.36), channel_id=1, source_target_pairs={{0,4},{4,8},{8,12},{12,0},{16,28},{20,16},{24,20},{28,24},{1,5},{5... | collective-permute-start | bytes 393224 | tf_op jit(solution)/shard_map/ppermute | solution.py:237
  39.5 0.9 shard_map.67
  40.3 4.4 %collective-permute-done.10.b_ref = bf16[8,16,512]{2,1,0:T(8,128)(2,1)S(1)} collective-permute-done((bf16[8,16,512]{2,1,0:T(8,128)(2,1)S(1)}, bf16[8,16,512]{2,1,0:T(8,128)(2,1)S(1)}, u32[]{:S(2)}, u32[]{:S(2)}) %collective-permute-start.10) | collective-permute-done | bytes 131104 | tf_op jit(solution)/shard_map/ppermute | solution.py:236
  44.8 0.1 collective-permute-start.11
  44.9 0.5 copy-done.4
  45.5 0.0 collective-permute-done.9.b_ref
  45.5 6.3 %collective-permute-done.11.c_ref = bf16[8,16,512]{2,1,0:T(8,128)(2,1)S(1)} collective-permute-done((bf16[8,16,512]{2,1,0:T(8,128)(2,1)S(1)}, bf16[8,16,512]{2,1,0:T(8,128)(2,1)S(1)}, u32[]{:S(2)}, u32[]{:S(2)}) %collective-permute-start.11) | collective-permute-done | bytes 131104 | tf_op jit(solution)/shard_map/ppermute | solution.py:242
  51.8 0.1 broadcast_in_dim.13.bias_ref
  51.9 0.8 shard_map.69
  52.7 0.8 collective-permute-start.12
  53.5 1.7 %collective-permute-start.13 = (bf16[8,16,768]{2,1,0:T(8,128)(2,1)S(1)}, bf16[8,16,768]{2,1,0:T(8,128)(2,1)S(1)}, u32[]{:S(2)}, u32[]{:S(2)}) collective-permute-start(bf16[8,16,768]{2,1,0:T(8,128)(2,1)S(1)} %get-tuple-element.40.a_ref), channel_id=1, source_target_pairs={{0,2},{1,3},{2,0},{3,1},{4,6},{5,7},{6,4},{7,5},{8,10},{9,11},{10,... | collective-permute-start | bytes 589832 | tf_op jit(solution)/shard_map/ppermute | solution.py:267
  55.2 1.2 %collective-permute-start.14 = (bf16[8,16,768]{2,1,0:T(8,128)(2,1)S(1)}, bf16[8,16,768]{2,1,0:T(8,128)(2,1)S(1)}, u32[]{:S(2)}, u32[]{:S(2)}) collective-permute-start(bf16[8,16,768]{2,1,0:T(8,128)(2,1)S(1)} %get-tuple-element.40.a_ref), channel_id=1, source_target_pairs={{0,3},{1,2},{2,1},{3,0},{4,7},{5,6},{6,5},{7,4},{8,11},{9,10},{10,... | collective-permute-start | bytes 589832 | tf_op jit(solution)/shard_map/ppermute | solution.py:267
  56.4 7.0 %all-to-all-start.1 = ((f32[64,4,128]{2,1,0:T(4,128)}), f32[64,4,128]{2,1,0:T(4,128)S(1)}, u32[]{:S(2)}, u32[]{:S(2)}) async-start(f32[64,4,128]{2,1,0:T(4,128)} %get-tuple-element.43), calls=%async_computation.1 | async-start | bytes 262144 | tf_op jit(solution)/shard_map/all_to_all | solution.py:271
  63.4 0.0 collective-permute-done.13.c_ref
  63.4 0.4 collective-permute-start.15
  63.9 3.8 %collective-permute-start.16 = (bf16[4,16,768]{2,1,0:T(8,128)(2,1)S(1)}, bf16[4,16,768]{2,1,0:T(8,128)(2,1)S(1)}, u32[]{:S(2)}, u32[]{:S(2)}) collective-permute-start(bf16[4,16,768]{2,1,0:T(8,128)(2,1)S(1)} %get-tuple-element.42), channel_id=1, source_target_pairs={{16,32},{48,64},{80,96},{112,128},{144,160},{176,192},{208,224},{3... | collective-permute-start | bytes 294920 | tf_op jit(solution)/shard_map/ppermute | solution.py:262
  67.6 1.2 %all-to-all-done.1.stats_ref = f32[64,4,128]{2,1,0:T(4,128)S(1)} async-done(((f32[64,4,128]{2,1,0:T(4,128)}), f32[64,4,128]{2,1,0:T(4,128)S(1)}, u32[]{:S(2)}, u32[]{:S(2)}) %all-to-all-start.1) | async-done | bytes 131104 | tf_op jit(solution)/shard_map/all_to_all | solution.py:271
  68.9 4.5 %collective-permute-done.16.next_ref = bf16[4,16,768]{2,1,0:T(8,128)(2,1)S(1)} collective-permute-done((bf16[4,16,768]{2,1,0:T(8,128)(2,1)S(1)}, bf16[4,16,768]{2,1,0:T(8,128)(2,1)S(1)}, u32[]{:S(2)}, u32[]{:S(2)}) %collective-permute-start.16) | collective-permute-done | bytes 98336 | tf_op jit(solution)/shard_map/ppermute | solution.py:262
  73.4 1.5 %shard_map.71 = (bf16[8,16,512]{2,1,0:T(8,128)(2,1)S(1)}, bf16[8,16,512]{2,1,0:T(8,128)(2,1)S(1)}, bf16[10,4,16,768]{3,2,1,0:T(8,128)(2,1)S(1)}) custom-call(bf16[8,16,768]{2,1,0:T(8,128)(2,1)S(1)} %get-tuple-element.40.a_ref, bf16[8,16,768]{2,1,0:T(8,128)(2,1)S(1)} %collective-permute-done.12.b_ref, bf16[8,16,768]{2,1,0:T(8,128)(2,1)S(1)} %collective-permute-done.13.c_ref, ...), custom_call_target="tpu_custom_call" | custom-call | flops 452984832 | bytes 1597440 | tf_op jit(solution)/shard_map/pallas_call | solution.py:32
  74.9 1.1 %collective-permute-start.18 = (bf16[8,16,512]{2,1,0:T(8,128)(2,1)S(1)}, bf16[8,16,512]{2,1,0:T(8,128)(2,1)S(1)}, u32[]{:S(2)}, u32[]{:S(2)}) collective-permute-start(bf16[8,16,512]{2,1,0:T(8,128)(2,1)S(1)} %get-tuple-element.48), channel_id=1, source_target_pairs={{0,12},{4,0},{8,4},{12,8},{16,20},{20,24},{24,28},{28,16},{1,13},{... | collective-permute-start | bytes 393224 | tf_op jit(solution)/shard_map/ppermute | solution.py:236
  76.1 2.5 %collective-permute-start.17 = (bf16[8,16,512]{2,1,0:T(8,128)(2,1)S(1)}, bf16[8,16,512]{2,1,0:T(8,128)(2,1)S(1)}, u32[]{:S(2)}, u32[]{:S(2)}) collective-permute-start(bf16[8,16,512]{2,1,0:T(8,128)(2,1)S(1)} %get-tuple-element.46), channel_id=1, source_target_pairs={{0,4},{4,8},{8,12},{12,0},{16,28},{20,16},{24,20},{28,24},{1,5},{5... | collective-permute-start | bytes 393224 | tf_op jit(solution)/shard_map/ppermute | solution.py:237
  78.6 0.9 shard_map.72
  79.5 5.7 %collective-permute-done.18.b_ref = bf16[8,16,512]{2,1,0:T(8,128)(2,1)S(1)} collective-permute-done((bf16[8,16,512]{2,1,0:T(8,128)(2,1)S(1)}, bf16[8,16,512]{2,1,0:T(8,128)(2,1)S(1)}, u32[]{:S(2)}, u32[]{:S(2)}) %collective-permute-start.18) | collective-permute-done | bytes 131104 | tf_op jit(solution)/shard_map/ppermute | solution.py:236
  85.2 0.1 collective-permute-start.19
  85.3 6.6 %collective-permute-done.19.c_ref = bf16[8,16,512]{2,1,0:T(8,128)(2,1)S(1)} collective-permute-done((bf16[8,16,512]{2,1,0:T(8,128)(2,1)S(1)}, bf16[8,16,512]{2,1,0:T(8,128)(2,1)S(1)}, u32[]{:S(2)}, u32[]{:S(2)}) %collective-permute-start.19) | collective-permute-done | bytes 131104 | tf_op jit(solution)/shard_map/ppermute | solution.py:242
  91.9 0.1 broadcast_in_dim.15.bias_ref
  91.9 0.7 shard_map.74
  (20 shorter events, 0.2 us)
Async XLA Ops:
  2.3 22.1 %collective-permute-start = (bf16[8,16,768]{2,1,0:T(8,128)(2,1)}, bf16[8,16,768]{2,1,0:T(8,128)(2,1)S(1)}, u32[]{:S(2)}, u32[]{:S(2)}) collective-permute-start(bf16[8,16,768]{2,1,0:T(8,128)(2,1)} %get-tuple-element.27.a_ref), channel_id=1, source_target_pairs={{0,1},{1,0},{2,3},{3,2},{4,5},{5,4},{6,7},{7,6},{8,9},{9,8},{10,11... | collective-permute-start | bytes 589832 | tf_op jit(solution)/shard_map/ppermute | solution.py:267
  2.6 21.8 %collective-permute-start.1 = (bf16[8,16,768]{2,1,0:T(8,128)(2,1)}, bf16[8,16,768]{2,1,0:T(8,128)(2,1)S(1)}, u32[]{:S(2)}, u32[]{:S(2)}) collective-permute-start(bf16[8,16,768]{2,1,0:T(8,128)(2,1)} %get-tuple-element.27.a_ref), channel_id=1, source_target_pairs={{0,2},{1,3},{2,0},{3,1},{4,6},{5,7},{6,4},{7,5},{8,10},{9,11},{10,... | collective-permute-start | bytes 589832 | tf_op jit(solution)/shard_map/ppermute | solution.py:267
  4.3 20.1 %collective-permute-start.2 = (bf16[8,16,768]{2,1,0:T(8,128)(2,1)}, bf16[8,16,768]{2,1,0:T(8,128)(2,1)S(1)}, u32[]{:S(2)}, u32[]{:S(2)}) collective-permute-start(bf16[8,16,768]{2,1,0:T(8,128)(2,1)} %get-tuple-element.27.a_ref), channel_id=1, source_target_pairs={{0,3},{1,2},{2,1},{3,0},{4,7},{5,6},{6,5},{7,4},{8,11},{9,10},{10,... | collective-permute-start | bytes 589832 | tf_op jit(solution)/shard_map/ppermute | solution.py:267
  5.2 18.0 %collective-permute-start.5 = (bf16[2,3,3,16,192]{4,3,2,1,0:T(8,128)(2,1)}, bf16[2,3,3,16,192]{4,3,2,1,0:T(8,128)(2,1)S(1)}, u32[]{:S(2)}, u32[]{:S(2)}) collective-permute-start(bf16[2,3,3,16,192]{4,3,2,1,0:T(8,128)(2,1)} %get-tuple-element.31), channel_id=1, source_target_pairs={{0,4},{4,8},{8,12},{12,0},{16,28},{20,16},{24,20},{28,24},{1,5},{5... | collective-permute-start | bytes 331784 | tf_op jit(solution)/shard_map/ppermute | solution.py:291
  11.1 17.7 %collective-permute-start.7 = (bf16[3,3,16,192]{3,2,1,0:T(8,128)(2,1)}, bf16[3,3,16,192]{3,2,1,0:T(8,128)(2,1)S(1)}, u32[]{:S(2)}, u32[]{:S(2)}) collective-permute-start(bf16[3,3,16,192]{3,2,1,0:T(8,128)(2,1)} %get-tuple-element.32), channel_id=1, source_target_pairs={{0,8},{4,12},{8,0},{12,4},{1,9},{5,13},{9,1},{13,5},{2,10},{6,14},... | collective-permute-start | bytes 165896 | tf_op jit(solution)/shard_map/ppermute | solution.py:292
  11.9 12.5 %copy-start.1 = (bf16[8,16,768]{2,1,0:T(8,128)(2,1)S(1)}, bf16[8,16,768]{2,1,0:T(8,128)(2,1)}, u32[]{:S(2)}) copy-start(bf16[8,16,768]{2,1,0:T(8,128)(2,1)} %get-tuple-element.27.a_ref) | copy-start | bytes 589828
  11.9 22.3 %all-to-all-start = ((f32[64,8,128]{2,1,0:T(8,128)}), f32[64,8,128]{2,1,0:T(8,128)S(1)}, u32[]{:S(2)}, u32[]{:S(2)}) async-start(f32[64,8,128]{2,1,0:T(8,128)} %get-tuple-element.30), calls=%async_computation | async-start | bytes 524288 | tf_op jit(solution)/shard_map/all_to_all | solution.py:271
  23.2 7.0 %collective-permute-start.6 = (bf16[2,3,3,16,192]{4,3,2,1,0:T(8,128)(2,1)S(1)}, bf16[2,3,3,16,192]{4,3,2,1,0:T(8,128)(2,1)S(1)}, u32[]{:S(2)}, u32[]{:S(2)}) collective-permute-start(bf16[2,3,3,16,192]{4,3,2,1,0:T(8,128)(2,1)S(1)} %collective-permute-done.5.side_ref), channel_id=1, source_target_pairs={{0,16},{16,0},{1,17},{17,1},{2,18},{18,2},{3,19},{19,3},{4,20},{20... | collective-permute-start | bytes 331784 | tf_op jit(solution)/shard_map/ppermute | solution.py:297
  24.5 5.7 %collective-permute-start.3 = (bf16[4,16,768]{2,1,0:T(8,128)(2,1)S(1)}, bf16[4,16,768]{2,1,0:T(8,128)(2,1)S(1)}, u32[]{:S(2)}, u32[]{:S(2)}) collective-permute-start(bf16[4,16,768]{2,1,0:T(8,128)(2,1)S(1)} %get-tuple-element.28), channel_id=1, source_target_pairs={{0,16},{16,0},{32,48},{48,32},{64,80},{80,64},{96,112},{112,96},{1... | collective-permute-start | bytes 294920 | tf_op jit(solution)/shard_map/ppermute | solution.py:260
  24.6 14.9 %copy-start.3 = (bf16[2,3,3,16,192]{4,3,2,1,0:T(8,128)(2,1)S(1)}, bf16[2,3,3,16,192]{4,3,2,1,0:T(8,128)(2,1)}, u32[]{:S(2)}) copy-start(bf16[2,3,3,16,192]{4,3,2,1,0:T(8,128)(2,1)} %get-tuple-element.34.own_ref) | copy-start | bytes 331780
  24.6 9.7 %collective-permute-start.4 = (bf16[4,16,768]{2,1,0:T(8,128)(2,1)S(1)}, bf16[4,16,768]{2,1,0:T(8,128)(2,1)S(1)}, u32[]{:S(2)}, u32[]{:S(2)}) collective-permute-start(bf16[4,16,768]{2,1,0:T(8,128)(2,1)S(1)} %get-tuple-element.29), channel_id=1, source_target_pairs={{16,32},{48,64},{80,96},{112,128},{144,160},{176,192},{208,224},{3... | collective-permute-start | bytes 294920 | tf_op jit(solution)/shard_map/ppermute | solution.py:262
  28.8 1.4 %collective-permute-start.8 = (bf16[3,3,16,192]{3,2,1,0:T(8,128)(2,1)S(1)}, bf16[3,3,16,192]{3,2,1,0:T(8,128)(2,1)S(1)}, u32[]{:S(2)}, u32[]{:S(2)}) collective-permute-start(bf16[3,3,16,192]{3,2,1,0:T(8,128)(2,1)S(1)} %collective-permute-done.7.far_ref), channel_id=1, source_target_pairs={{0,16},{16,0},{1,17},{17,1},{2,18},{18,2},{3,19},{19,3},{4,20},{20... | collective-permute-start | bytes 165896 | tf_op jit(solution)/shard_map/ppermute | solution.py:297
  35.8 9.0 %collective-permute-start.10 = (bf16[8,16,512]{2,1,0:T(8,128)(2,1)S(1)}, bf16[8,16,512]{2,1,0:T(8,128)(2,1)S(1)}, u32[]{:S(2)}, u32[]{:S(2)}) collective-permute-start(bf16[8,16,512]{2,1,0:T(8,128)(2,1)S(1)} %get-tuple-element.38), channel_id=1, source_target_pairs={{0,12},{4,0},{8,4},{12,8},{16,20},{20,24},{24,28},{28,16},{1,13},{... | collective-permute-start | bytes 393224 | tf_op jit(solution)/shard_map/ppermute | solution.py:236
  35.9 9.6 %collective-permute-start.9 = (bf16[8,16,512]{2,1,0:T(8,128)(2,1)S(1)}, bf16[8,16,512]{2,1,0:T(8,128)(2,1)S(1)}, u32[]{:S(2)}, u32[]{:S(2)}) collective-permute-start(bf16[8,16,512]{2,1,0:T(8,128)(2,1)S(1)} %get-tuple-element.36), channel_id=1, source_target_pairs={{0,4},{4,8},{8,12},{12,0},{16,28},{20,16},{24,20},{28,24},{1,5},{5... | collective-permute-start | bytes 393224 | tf_op jit(solution)/shard_map/ppermute | solution.py:237
  44.8 0.7 copy-start.4
  44.8 7.1 %copy-start.2 = (bf16[8,16,256]{2,1,0:T(8,128)(2,1)S(1)}, bf16[8,16,256]{2,1,0:T(8,128)(2,1)}, u32[]{:S(2)}) copy-start(bf16[8,16,256]{2,1,0:T(8,128)(2,1)} %get-tuple-element.39.later_ref) | copy-start | bytes 196612
  44.8 7.0 %collective-permute-start.11 = (bf16[8,16,512]{2,1,0:T(8,128)(2,1)S(1)}, bf16[8,16,512]{2,1,0:T(8,128)(2,1)S(1)}, u32[]{:S(2)}, u32[]{:S(2)}) collective-permute-start(bf16[8,16,512]{2,1,0:T(8,128)(2,1)S(1)} %shard_map.68), channel_id=1, source_target_pairs={{0,12},{4,0},{8,4},{12,8},{16,20},{20,24},{24,28},{28,16},{1,13},{... | collective-permute-start | bytes 393224 | tf_op jit(solution)/shard_map/ppermute | solution.py:242
  52.7 10.7 %collective-permute-start.12 = (bf16[8,16,768]{2,1,0:T(8,128)(2,1)S(1)}, bf16[8,16,768]{2,1,0:T(8,128)(2,1)S(1)}, u32[]{:S(2)}, u32[]{:S(2)}) collective-permute-start(bf16[8,16,768]{2,1,0:T(8,128)(2,1)S(1)} %get-tuple-element.40.a_ref), channel_id=1, source_target_pairs={{0,1},{1,0},{2,3},{3,2},{4,5},{5,4},{6,7},{7,6},{8,9},{9,8},{10,11... | collective-permute-start | bytes 589832 | tf_op jit(solution)/shard_map/ppermute | solution.py:267
  53.5 9.9 %collective-permute-start.13 = (bf16[8,16,768]{2,1,0:T(8,128)(2,1)S(1)}, bf16[8,16,768]{2,1,0:T(8,128)(2,1)S(1)}, u32[]{:S(2)}, u32[]{:S(2)}) collective-permute-start(bf16[8,16,768]{2,1,0:T(8,128)(2,1)S(1)} %get-tuple-element.40.a_ref), channel_id=1, source_target_pairs={{0,2},{1,3},{2,0},{3,1},{4,6},{5,7},{6,4},{7,5},{8,10},{9,11},{10,... | collective-permute-start | bytes 589832 | tf_op jit(solution)/shard_map/ppermute | solution.py:267
  55.2 8.2 %collective-permute-start.14 = (bf16[8,16,768]{2,1,0:T(8,128)(2,1)S(1)}, bf16[8,16,768]{2,1,0:T(8,128)(2,1)S(1)}, u32[]{:S(2)}, u32[]{:S(2)}) collective-permute-start(bf16[8,16,768]{2,1,0:T(8,128)(2,1)S(1)} %get-tuple-element.40.a_ref), channel_id=1, source_target_pairs={{0,3},{1,2},{2,1},{3,0},{4,7},{5,6},{6,5},{7,4},{8,11},{9,10},{10,... | collective-permute-start | bytes 589832 | tf_op jit(solution)/shard_map/ppermute | solution.py:267
  56.4 12.5 %all-to-all-start.1 = ((f32[64,4,128]{2,1,0:T(4,128)}), f32[64,4,128]{2,1,0:T(4,128)S(1)}, u32[]{:S(2)}, u32[]{:S(2)}) async-start(f32[64,4,128]{2,1,0:T(4,128)} %get-tuple-element.43), calls=%async_computation.1 | async-start | bytes 262144 | tf_op jit(solution)/shard_map/all_to_all | solution.py:271
  63.4 5.4 %collective-permute-start.15 = (bf16[4,16,768]{2,1,0:T(8,128)(2,1)S(1)}, bf16[4,16,768]{2,1,0:T(8,128)(2,1)S(1)}, u32[]{:S(2)}, u32[]{:S(2)}) collective-permute-start(bf16[4,16,768]{2,1,0:T(8,128)(2,1)S(1)} %get-tuple-element.41), channel_id=1, source_target_pairs={{0,16},{16,0},{32,48},{48,32},{64,80},{80,64},{96,112},{112,96},{1... | collective-permute-start | bytes 294920 | tf_op jit(solution)/shard_map/ppermute | solution.py:260
  63.9 9.5 %collective-permute-start.16 = (bf16[4,16,768]{2,1,0:T(8,128)(2,1)S(1)}, bf16[4,16,768]{2,1,0:T(8,128)(2,1)S(1)}, u32[]{:S(2)}, u32[]{:S(2)}) collective-permute-start(bf16[4,16,768]{2,1,0:T(8,128)(2,1)S(1)} %get-tuple-element.42), channel_id=1, source_target_pairs={{16,32},{48,64},{80,96},{112,128},{144,160},{176,192},{208,224},{3... | collective-permute-start | bytes 294920 | tf_op jit(solution)/shard_map/ppermute | solution.py:262
  74.9 10.2 %collective-permute-start.18 = (bf16[8,16,512]{2,1,0:T(8,128)(2,1)S(1)}, bf16[8,16,512]{2,1,0:T(8,128)(2,1)S(1)}, u32[]{:S(2)}, u32[]{:S(2)}) collective-permute-start(bf16[8,16,512]{2,1,0:T(8,128)(2,1)S(1)} %get-tuple-element.48), channel_id=1, source_target_pairs={{0,12},{4,0},{8,4},{12,8},{16,20},{20,24},{24,28},{28,16},{1,13},{... | collective-permute-start | bytes 393224 | tf_op jit(solution)/shard_map/ppermute | solution.py:236
  76.1 9.2 %collective-permute-start.17 = (bf16[8,16,512]{2,1,0:T(8,128)(2,1)S(1)}, bf16[8,16,512]{2,1,0:T(8,128)(2,1)S(1)}, u32[]{:S(2)}, u32[]{:S(2)}) collective-permute-start(bf16[8,16,512]{2,1,0:T(8,128)(2,1)S(1)} %get-tuple-element.46), channel_id=1, source_target_pairs={{0,4},{4,8},{8,12},{12,0},{16,28},{20,16},{24,20},{28,24},{1,5},{5... | collective-permute-start | bytes 393224 | tf_op jit(solution)/shard_map/ppermute | solution.py:237
  85.1 6.8 %copy-start = (bf16[4,8,16,128]{3,2,1,0:T(8,128)(2,1)S(1)}, bf16[4,8,16,128]{3,2,1,0:T(8,128)(2,1)}, u32[]{:S(2)}) copy-start(bf16[4,8,16,128]{3,2,1,0:T(8,128)(2,1)} %x_ref.1) | copy-start | bytes 393220
  85.2 6.7 %collective-permute-start.19 = (bf16[8,16,512]{2,1,0:T(8,128)(2,1)S(1)}, bf16[8,16,512]{2,1,0:T(8,128)(2,1)S(1)}, u32[]{:S(2)}, u32[]{:S(2)}) collective-permute-start(bf16[8,16,512]{2,1,0:T(8,128)(2,1)S(1)} %shard_map.73), channel_id=1, source_target_pairs={{0,12},{4,0},{8,4},{12,8},{16,20},{20,24},{24,28},{28,16},{1,13},{... | collective-permute-start | bytes 393224 | tf_op jit(solution)/shard_map/ppermute | solution.py:242

commit v16 on v15

--- a/solution.py
+++ b/solution.py
@@ -152,7 +152,7 @@
 
 
 def conv_kernel(
-    layer, a_ref, b_ref, c_ref, d_ref, chip_ref, next_ref, stats_ref, notes_ref, other_ref, far_ref, far2_ref,
+    layer, a_ref, b_ref, c_ref, d_ref, next_ref, chip_ref, stats_ref, notes_ref, other_ref, far_ref, far2_ref,
     o2_ref, o3_ref, slab_ref, affine_ref, held_ref,
 ):
     row, _, here = place()
@@ -257,10 +257,10 @@
 
 def rows_beside(blocks):
     chip, beyond = call(edge_kernel, (struct((4, 16, 768)), struct((4, 16, 768))), *blocks, flops=2 * 10**10)
-    chip = lax.ppermute(chip, ROW, [(i, i ^ 1) for i in range(16)])
     pairs = [(i, i + 1) for i in range(1, 15, 2)] + [(i + 1, i) for i in range(1, 15, 2)]
     beyond = lax.ppermute(beyond, ROW, pairs)
-    return [chip, beyond]
+    chip = lax.ppermute(chip, ROW, [(i, i ^ 1) for i in range(16)])
+    return [beyond, chip]
 
 
 def near(x):

time: 93.5 us -> 92.3 us (0.987)
  waiting for transfers between devices: 34.2 us -> 32.9 us
    ppermute x2, starting transfers between devices: 1.23 us -> 2.31 us  [convolve(): far = lax.ppermute(far, ('core', 'zh'), sides(-1))]
    ppermute x2, starting transfers between devices: 6.07 us -> 4.98 us  [convolve(): other = lax.ppermute(other, ('core', 'zh'), sides(1))]
where the time goes in v16:
time: 92.3 us; the launch traced here: 91.1 us
  starting transfers between devices  48.6 us (53%)
  waiting for transfers between devices  32.9 us (36%)
  Pallas kernels  8.78 us (10%)
    all_to_all x2, starting transfers between devices, exchange(): return lax.all_to_all(x, axes, 0, 0, tiled=True)  18.2 us
    ppermute x2, waiting for transfers between devices, convolve(): side = lax.ppermute(side, ('core', 'zh'), sides(-1))  12.4 us
    ppermute x2, waiting for transfers between devices, convolve(): far = lax.ppermute(far, ('core', 'zh'), sides(-1))  9.64 us
    pallas_call x11, Pallas kernels, call(): pl.pallas_call(kernel, out_shape=outs, in_specs=specs, out_specs=jax.tree...  8.78 us
    ppermute x2, waiting for transfers between devices, rows_beside(): beyond = lax.ppermute(beyond, ROW, pairs)  8.52 us
    ppermute x2, starting transfers between devices, rows_beside(): beyond = lax.ppermute(beyond, ROW, pairs)  7.59 us
    ppermute x6, starting transfers between devices, near(): lax.ppermute(x, NEAR, [(i, i ^ k) for i in range(4)])  6.69 us
    ppermute x1, starting transfers between devices, local(): side = lax.ppermute(side, ('core', 'zh'), sides(1))  5.85 us
  transfers between devices with their start and end apart: 22, of which 8 were waited for; matrix products, arithmetic and copies ran while one was open for 0% of the time, Pallas kernels for 2%

profile of v16, /device:TPU:27, one launch (start us, length us, event | category | flops | bytes accessed | tf_op | source)
XLA Modules:
  0.0 91.1 jit_solution(3935904551909523274)
XLA Ops:
  0.0 2.3 %shard_map.64 = (bf16[8,16,768]{2,1,0:T(8,128)(2,1)}, bf16[8,16,256]{2,1,0:T(8,128)(2,1)}, f32[64,8,128]{2,1,0:T(8,128)}, bf16[2,3,3,16,192]{4,3,2,1,0:T(8,128)(...) custom-call(bf16[4,8,16,128]{3,2,1,0:T(8,128)(2,1)} %x_ref.1, ...), custom_call_target="tpu_custom_call" | custom-call | bytes 704768 | tf_op jit(solution)/shard_map/pallas_call | solution.py:32
  2.3 0.3 collective-permute-start
  2.6 1.6 %collective-permute-start.1 = (bf16[8,16,768]{2,1,0:T(8,128)(2,1)}, bf16[8,16,768]{2,1,0:T(8,128)(2,1)S(1)}, u32[]{:S(2)}, u32[]{:S(2)}) collective-permute-start(bf16[8,16,768]{2,1,0:T(8,128)(2,1)} %get-tuple-element.27.a_ref), channel_id=1, source_target_pairs={{0,2},{1,3},{2,0},{3,1},{4,6},{5,7},{6,4},{7,5},{8,10},{9,11},{10,... | collective-permute-start | bytes 589832 | tf_op jit(solution)/shard_map/ppermute | solution.py:267
  4.3 0.9 %collective-permute-start.2 = (bf16[8,16,768]{2,1,0:T(8,128)(2,1)}, bf16[8,16,768]{2,1,0:T(8,128)(2,1)S(1)}, u32[]{:S(2)}, u32[]{:S(2)}) collective-permute-start(bf16[8,16,768]{2,1,0:T(8,128)(2,1)} %get-tuple-element.27.a_ref), channel_id=1, source_target_pairs={{0,3},{1,2},{2,1},{3,0},{4,7},{5,6},{6,5},{7,4},{8,11},{9,10},{10,... | collective-permute-start | bytes 589832 | tf_op jit(solution)/shard_map/ppermute | solution.py:267
  5.2 5.8 %collective-permute-start.5 = (bf16[2,3,3,16,192]{4,3,2,1,0:T(8,128)(2,1)}, bf16[2,3,3,16,192]{4,3,2,1,0:T(8,128)(2,1)S(1)}, u32[]{:S(2)}, u32[]{:S(2)}) collective-permute-start(bf16[2,3,3,16,192]{4,3,2,1,0:T(8,128)(2,1)} %get-tuple-element.31), channel_id=1, source_target_pairs={{0,4},{4,8},{8,12},{12,0},{16,28},{20,16},{24,20},{28,24},{1,5},{5... | collective-permute-start | bytes 331784 | tf_op jit(solution)/shard_map/ppermute | solution.py:291
  11.1 0.9 collective-permute-start.7
  11.9 11.2 %all-to-all-start = ((f32[64,8,128]{2,1,0:T(8,128)}), f32[64,8,128]{2,1,0:T(8,128)S(1)}, u32[]{:S(2)}, u32[]{:S(2)}) async-start(f32[64,8,128]{2,1,0:T(8,128)} %get-tuple-element.30), calls=%async_computation | async-start | bytes 524288 | tf_op jit(solution)/shard_map/all_to_all | solution.py:271
  23.2 1.2 %collective-permute-start.6 = (bf16[2,3,3,16,192]{4,3,2,1,0:T(8,128)(2,1)S(1)}, bf16[2,3,3,16,192]{4,3,2,1,0:T(8,128)(2,1)S(1)}, u32[]{:S(2)}, u32[]{:S(2)}) collective-permute-start(bf16[2,3,3,16,192]{4,3,2,1,0:T(8,128)(2,1)S(1)} %collective-permute-done.5.side_ref), channel_id=1, source_target_pairs={{0,16},{16,0},{1,17},{17,1},{2,18},{18,2},{3,19},{19,3},{4,20},{20... | collective-permute-start | bytes 331784 | tf_op jit(solution)/shard_map/ppermute | solution.py:297
  24.5 3.6 %collective-permute-start.3 = (bf16[4,16,768]{2,1,0:T(8,128)(2,1)S(1)}, bf16[4,16,768]{2,1,0:T(8,128)(2,1)S(1)}, u32[]{:S(2)}, u32[]{:S(2)}) collective-permute-start(bf16[4,16,768]{2,1,0:T(8,128)(2,1)S(1)} %get-tuple-element.28), channel_id=1, source_target_pairs={{16,32},{48,64},{80,96},{112,128},{144,160},{176,192},{208,224},{3... | collective-permute-start | bytes 294920 | tf_op jit(solution)/shard_map/ppermute | solution.py:261
  28.1 0.1 collective-permute-start.4
  28.2 0.0 collective-permute-done.7.far_ref
  28.2 0.5 collective-permute-start.8
  28.7 0.9 %collective-permute-done.8.far2_ref = bf16[3,3,16,192]{3,2,1,0:T(8,128)(2,1)S(1)} collective-permute-done((bf16[3,3,16,192]{3,2,1,0:T(8,128)(2,1)S(1)}, bf16[3,3,16,192]{3,2,1,0:T(8,128)(2,1)S(1)}, u32[]{:S(2)}, u32[]{:S(2)}) %collective-permute-start.8) | collective-permute-done | bytes 55328 | tf_op jit(solution)/shard_map/ppermute | solution.py:297
  29.6 4.4 %collective-permute-done.3.next_ref = bf16[4,16,768]{2,1,0:T(8,128)(2,1)S(1)} collective-permute-done((bf16[4,16,768]{2,1,0:T(8,128)(2,1)S(1)}, bf16[4,16,768]{2,1,0:T(8,128)(2,1)S(1)}, u32[]{:S(2)}, u32[]{:S(2)}) %collective-permute-start.3) | collective-permute-done | bytes 98336 | tf_op jit(solution)/shard_map/ppermute | solution.py:261
  34.0 0.0 collective-permute-done.4.chip_ref
  34.0 0.0 all-to-all-done.stats_ref.notes_ref
  34.0 1.5 %shard_map.66 = (bf16[8,16,512]{2,1,0:T(8,128)(2,1)S(1)}, bf16[8,16,512]{2,1,0:T(8,128)(2,1)S(1)}, bf16[10,4,16,768]{3,2,1,0:T(8,128)(2,1)S(1)}) custom-call(bf16[8,16,768]{2,1,0:T(8,128)(2,1)S(1)} %copy-done.1, bf16[8,16,768]{2,1,0:T(8,128)(2,1)S(1)} %collective-permute-done.b_ref, bf16[8,16,768]{2,1,0:T(8,128)(2,1)S(1)} %collective-permute-done.1.c_ref, ...), custom_call_target="tpu_custom_call" | custom-call | flops 452984832 | bytes 1728512 | tf_op jit(solution)/shard_map/pallas_call | solution.py:32
  35.6 0.1 collective-permute-start.10
  35.7 3.6 %collective-permute-start.9 = (bf16[8,16,512]{2,1,0:T(8,128)(2,1)S(1)}, bf16[8,16,512]{2,1,0:T(8,128)(2,1)S(1)}, u32[]{:S(2)}, u32[]{:S(2)}) collective-permute-start(bf16[8,16,512]{2,1,0:T(8,128)(2,1)S(1)} %get-tuple-element.36), channel_id=1, source_target_pairs={{0,4},{4,8},{8,12},{12,0},{16,28},{20,16},{24,20},{28,24},{1,5},{5... | collective-permute-start | bytes 393224 | tf_op jit(solution)/shard_map/ppermute | solution.py:237
  39.2 0.9 shard_map.67
  40.1 4.2 %collective-permute-done.10.b_ref = bf16[8,16,512]{2,1,0:T(8,128)(2,1)S(1)} collective-permute-done((bf16[8,16,512]{2,1,0:T(8,128)(2,1)S(1)}, bf16[8,16,512]{2,1,0:T(8,128)(2,1)S(1)}, u32[]{:S(2)}, u32[]{:S(2)}) %collective-permute-start.10) | collective-permute-done | bytes 131104 | tf_op jit(solution)/shard_map/ppermute | solution.py:236
  44.3 0.1 collective-permute-start.11
  44.4 0.5 copy-done.4
  45.0 0.0 collective-permute-done.9.b_ref
  45.0 6.3 %collective-permute-done.11.c_ref = bf16[8,16,512]{2,1,0:T(8,128)(2,1)S(1)} collective-permute-done((bf16[8,16,512]{2,1,0:T(8,128)(2,1)S(1)}, bf16[8,16,512]{2,1,0:T(8,128)(2,1)S(1)}, u32[]{:S(2)}, u32[]{:S(2)}) %collective-permute-start.11) | collective-permute-done | bytes 131104 | tf_op jit(solution)/shard_map/ppermute | solution.py:242
  51.3 0.1 broadcast_in_dim.13.bias_ref
  51.4 0.8 shard_map.69
  52.2 1.4 %collective-permute-start.12 = (bf16[8,16,768]{2,1,0:T(8,128)(2,1)S(1)}, bf16[8,16,768]{2,1,0:T(8,128)(2,1)S(1)}, u32[]{:S(2)}, u32[]{:S(2)}) collective-permute-start(bf16[8,16,768]{2,1,0:T(8,128)(2,1)S(1)} %get-tuple-element.40.a_ref), channel_id=1, source_target_pairs={{0,1},{1,0},{2,3},{3,2},{4,5},{5,4},{6,7},{7,6},{8,9},{9,8},{10,11... | collective-permute-start | bytes 589832 | tf_op jit(solution)/shard_map/ppermute | solution.py:267
  53.6 1.2 %collective-permute-start.13 = (bf16[8,16,768]{2,1,0:T(8,128)(2,1)S(1)}, bf16[8,16,768]{2,1,0:T(8,128)(2,1)S(1)}, u32[]{:S(2)}, u32[]{:S(2)}) collective-permute-start(bf16[8,16,768]{2,1,0:T(8,128)(2,1)S(1)} %get-tuple-element.40.a_ref), channel_id=1, source_target_pairs={{0,2},{1,3},{2,0},{3,1},{4,6},{5,7},{6,4},{7,5},{8,10},{9,11},{10,... | collective-permute-start | bytes 589832 | tf_op jit(solution)/shard_map/ppermute | solution.py:267
  54.8 1.2 %collective-permute-start.14 = (bf16[8,16,768]{2,1,0:T(8,128)(2,1)S(1)}, bf16[8,16,768]{2,1,0:T(8,128)(2,1)S(1)}, u32[]{:S(2)}, u32[]{:S(2)}) collective-permute-start(bf16[8,16,768]{2,1,0:T(8,128)(2,1)S(1)} %get-tuple-element.40.a_ref), channel_id=1, source_target_pairs={{0,3},{1,2},{2,1},{3,0},{4,7},{5,6},{6,5},{7,4},{8,11},{9,10},{10,... | collective-permute-start | bytes 589832 | tf_op jit(solution)/shard_map/ppermute | solution.py:267
  56.0 7.0 %all-to-all-start.1 = ((f32[64,4,128]{2,1,0:T(4,128)}), f32[64,4,128]{2,1,0:T(4,128)S(1)}, u32[]{:S(2)}, u32[]{:S(2)}) async-start(f32[64,4,128]{2,1,0:T(4,128)} %get-tuple-element.43), calls=%async_computation.1 | async-start | bytes 262144 | tf_op jit(solution)/shard_map/all_to_all | solution.py:271
  62.9 0.0 collective-permute-done.12.b_ref
  63.0 0.0 collective-permute-done.14.d_ref
  63.0 4.0 %collective-permute-start.15 = (bf16[4,16,768]{2,1,0:T(8,128)(2,1)S(1)}, bf16[4,16,768]{2,1,0:T(8,128)(2,1)S(1)}, u32[]{:S(2)}, u32[]{:S(2)}) collective-permute-start(bf16[4,16,768]{2,1,0:T(8,128)(2,1)S(1)} %get-tuple-element.41), channel_id=1, source_target_pairs={{16,32},{48,64},{80,96},{112,128},{144,160},{176,192},{208,224},{3... | collective-permute-start | bytes 294920 | tf_op jit(solution)/shard_map/ppermute | solution.py:261
  67.0 0.1 collective-permute-start.16
  67.1 1.3 %all-to-all-done.1.stats_ref = f32[64,4,128]{2,1,0:T(4,128)S(1)} async-done(((f32[64,4,128]{2,1,0:T(4,128)}), f32[64,4,128]{2,1,0:T(4,128)S(1)}, u32[]{:S(2)}, u32[]{:S(2)}) %all-to-all-start.1) | async-done | bytes 131104 | tf_op jit(solution)/shard_map/all_to_all | solution.py:271
  68.5 4.1 %collective-permute-done.15.next_ref = bf16[4,16,768]{2,1,0:T(8,128)(2,1)S(1)} collective-permute-done((bf16[4,16,768]{2,1,0:T(8,128)(2,1)S(1)}, bf16[4,16,768]{2,1,0:T(8,128)(2,1)S(1)}, u32[]{:S(2)}, u32[]{:S(2)}) %collective-permute-start.15) | collective-permute-done | bytes 98336 | tf_op jit(solution)/shard_map/ppermute | solution.py:261
  72.6 0.0 collective-permute-done.16.chip_ref
  72.6 1.5 %shard_map.71 = (bf16[8,16,512]{2,1,0:T(8,128)(2,1)S(1)}, bf16[8,16,512]{2,1,0:T(8,128)(2,1)S(1)}, bf16[10,4,16,768]{3,2,1,0:T(8,128)(2,1)S(1)}) custom-call(bf16[8,16,768]{2,1,0:T(8,128)(2,1)S(1)} %get-tuple-element.40.a_ref, bf16[8,16,768]{2,1,0:T(8,128)(2,1)S(1)} %collective-permute-done.12.b_ref, bf16[8,16,768]{2,1,0:T(8,128)(2,1)S(1)} %collective-permute-done.13.c_ref, ...), custom_call_target="tpu_custom_call" | custom-call | flops 452984832 | bytes 1597440 | tf_op jit(solution)/shard_map/pallas_call | solution.py:32
  74.1 2.2 %collective-permute-start.18 = (bf16[8,16,512]{2,1,0:T(8,128)(2,1)S(1)}, bf16[8,16,512]{2,1,0:T(8,128)(2,1)S(1)}, u32[]{:S(2)}, u32[]{:S(2)}) collective-permute-start(bf16[8,16,512]{2,1,0:T(8,128)(2,1)S(1)} %get-tuple-element.48), channel_id=1, source_target_pairs={{0,12},{4,0},{8,4},{12,8},{16,20},{20,24},{24,28},{28,16},{1,13},{... | collective-permute-start | bytes 393224 | tf_op jit(solution)/shard_map/ppermute | solution.py:236
  76.3 1.4 %collective-permute-start.17 = (bf16[8,16,512]{2,1,0:T(8,128)(2,1)S(1)}, bf16[8,16,512]{2,1,0:T(8,128)(2,1)S(1)}, u32[]{:S(2)}, u32[]{:S(2)}) collective-permute-start(bf16[8,16,512]{2,1,0:T(8,128)(2,1)S(1)} %get-tuple-element.46), channel_id=1, source_target_pairs={{0,4},{4,8},{8,12},{12,0},{16,28},{20,16},{24,20},{28,24},{1,5},{5... | collective-permute-start | bytes 393224 | tf_op jit(solution)/shard_map/ppermute | solution.py:237
  77.8 0.9 shard_map.72
  78.6 5.5 %collective-permute-done.18.b_ref = bf16[8,16,512]{2,1,0:T(8,128)(2,1)S(1)} collective-permute-done((bf16[8,16,512]{2,1,0:T(8,128)(2,1)S(1)}, bf16[8,16,512]{2,1,0:T(8,128)(2,1)S(1)}, u32[]{:S(2)}, u32[]{:S(2)}) %collective-permute-start.18) | collective-permute-done | bytes 131104 | tf_op jit(solution)/shard_map/ppermute | solution.py:236
  84.1 0.1 collective-permute-start.19
  84.2 0.0 collective-permute-done.17.b_ref
  84.2 6.1 %collective-permute-done.19.c_ref = bf16[8,16,512]{2,1,0:T(8,128)(2,1)S(1)} collective-permute-done((bf16[8,16,512]{2,1,0:T(8,128)(2,1)S(1)}, bf16[8,16,512]{2,1,0:T(8,128)(2,1)S(1)}, u32[]{:S(2)}, u32[]{:S(2)}) %collective-permute-start.19) | collective-permute-done | bytes 131104 | tf_op jit(solution)/shard_map/ppermute | solution.py:242
  90.3 0.1 broadcast_in_dim.15.bias_ref
  90.4 0.7 shard_map.74
  (20 shorter events, 0.2 us)
Async XLA Ops:
  2.3 22.1 %collective-permute-start = (bf16[8,16,768]{2,1,0:T(8,128)(2,1)}, bf16[8,16,768]{2,1,0:T(8,128)(2,1)S(1)}, u32[]{:S(2)}, u32[]{:S(2)}) collective-permute-start(bf16[8,16,768]{2,1,0:T(8,128)(2,1)} %get-tuple-element.27.a_ref), channel_id=1, source_target_pairs={{0,1},{1,0},{2,3},{3,2},{4,5},{5,4},{6,7},{7,6},{8,9},{9,8},{10,11... | collective-permute-start | bytes 589832 | tf_op jit(solution)/shard_map/ppermute | solution.py:267
  2.6 21.8 %collective-permute-start.1 = (bf16[8,16,768]{2,1,0:T(8,128)(2,1)}, bf16[8,16,768]{2,1,0:T(8,128)(2,1)S(1)}, u32[]{:S(2)}, u32[]{:S(2)}) collective-permute-start(bf16[8,16,768]{2,1,0:T(8,128)(2,1)} %get-tuple-element.27.a_ref), channel_id=1, source_target_pairs={{0,2},{1,3},{2,0},{3,1},{4,6},{5,7},{6,4},{7,5},{8,10},{9,11},{10,... | collective-permute-start | bytes 589832 | tf_op jit(solution)/shard_map/ppermute | solution.py:267
  4.3 20.1 %collective-permute-start.2 = (bf16[8,16,768]{2,1,0:T(8,128)(2,1)}, bf16[8,16,768]{2,1,0:T(8,128)(2,1)S(1)}, u32[]{:S(2)}, u32[]{:S(2)}) collective-permute-start(bf16[8,16,768]{2,1,0:T(8,128)(2,1)} %get-tuple-element.27.a_ref), channel_id=1, source_target_pairs={{0,3},{1,2},{2,1},{3,0},{4,7},{5,6},{6,5},{7,4},{8,11},{9,10},{10,... | collective-permute-start | bytes 589832 | tf_op jit(solution)/shard_map/ppermute | solution.py:267
  5.2 18.0 %collective-permute-start.5 = (bf16[2,3,3,16,192]{4,3,2,1,0:T(8,128)(2,1)}, bf16[2,3,3,16,192]{4,3,2,1,0:T(8,128)(2,1)S(1)}, u32[]{:S(2)}, u32[]{:S(2)}) collective-permute-start(bf16[2,3,3,16,192]{4,3,2,1,0:T(8,128)(2,1)} %get-tuple-element.31), channel_id=1, source_target_pairs={{0,4},{4,8},{8,12},{12,0},{16,28},{20,16},{24,20},{28,24},{1,5},{5... | collective-permute-start | bytes 331784 | tf_op jit(solution)/shard_map/ppermute | solution.py:291
  11.1 17.1 %collective-permute-start.7 = (bf16[3,3,16,192]{3,2,1,0:T(8,128)(2,1)}, bf16[3,3,16,192]{3,2,1,0:T(8,128)(2,1)S(1)}, u32[]{:S(2)}, u32[]{:S(2)}) collective-permute-start(bf16[3,3,16,192]{3,2,1,0:T(8,128)(2,1)} %get-tuple-element.32), channel_id=1, source_target_pairs={{0,8},{4,12},{8,0},{12,4},{1,9},{5,13},{9,1},{13,5},{2,10},{6,14},... | collective-permute-start | bytes 165896 | tf_op jit(solution)/shard_map/ppermute | solution.py:292
  11.9 12.5 %copy-start.1 = (bf16[8,16,768]{2,1,0:T(8,128)(2,1)S(1)}, bf16[8,16,768]{2,1,0:T(8,128)(2,1)}, u32[]{:S(2)}) copy-start(bf16[8,16,768]{2,1,0:T(8,128)(2,1)} %get-tuple-element.27.a_ref) | copy-start | bytes 589828
  11.9 22.1 %all-to-all-start = ((f32[64,8,128]{2,1,0:T(8,128)}), f32[64,8,128]{2,1,0:T(8,128)S(1)}, u32[]{:S(2)}, u32[]{:S(2)}) async-start(f32[64,8,128]{2,1,0:T(8,128)} %get-tuple-element.30), calls=%async_computation | async-start | bytes 524288 | tf_op jit(solution)/shard_map/all_to_all | solution.py:271
  23.2 6.4 %collective-permute-start.6 = (bf16[2,3,3,16,192]{4,3,2,1,0:T(8,128)(2,1)S(1)}, bf16[2,3,3,16,192]{4,3,2,1,0:T(8,128)(2,1)S(1)}, u32[]{:S(2)}, u32[]{:S(2)}) collective-permute-start(bf16[2,3,3,16,192]{4,3,2,1,0:T(8,128)(2,1)S(1)} %collective-permute-done.5.side_ref), channel_id=1, source_target_pairs={{0,16},{16,0},{1,17},{17,1},{2,18},{18,2},{3,19},{19,3},{4,20},{20... | collective-permute-start | bytes 331784 | tf_op jit(solution)/shard_map/ppermute | solution.py:297
  24.5 9.5 %collective-permute-start.3 = (bf16[4,16,768]{2,1,0:T(8,128)(2,1)S(1)}, bf16[4,16,768]{2,1,0:T(8,128)(2,1)S(1)}, u32[]{:S(2)}, u32[]{:S(2)}) collective-permute-start(bf16[4,16,768]{2,1,0:T(8,128)(2,1)S(1)} %get-tuple-element.28), channel_id=1, source_target_pairs={{16,32},{48,64},{80,96},{112,128},{144,160},{176,192},{208,224},{3... | collective-permute-start | bytes 294920 | tf_op jit(solution)/shard_map/ppermute | solution.py:261
  28.1 11.1 %copy-start.3 = (bf16[2,3,3,16,192]{4,3,2,1,0:T(8,128)(2,1)S(1)}, bf16[2,3,3,16,192]{4,3,2,1,0:T(8,128)(2,1)}, u32[]{:S(2)}) copy-start(bf16[2,3,3,16,192]{4,3,2,1,0:T(8,128)(2,1)} %get-tuple-element.34.own_ref) | copy-start | bytes 331780
  28.1 5.9 %collective-permute-start.4 = (bf16[4,16,768]{2,1,0:T(8,128)(2,1)S(1)}, bf16[4,16,768]{2,1,0:T(8,128)(2,1)S(1)}, u32[]{:S(2)}, u32[]{:S(2)}) collective-permute-start(bf16[4,16,768]{2,1,0:T(8,128)(2,1)S(1)} %get-tuple-element.29), channel_id=1, source_target_pairs={{0,16},{16,0},{32,48},{48,32},{64,80},{80,64},{96,112},{112,96},{1... | collective-permute-start | bytes 294920 | tf_op jit(solution)/shard_map/ppermute | solution.py:262
  28.2 1.4 %collective-permute-start.8 = (bf16[3,3,16,192]{3,2,1,0:T(8,128)(2,1)S(1)}, bf16[3,3,16,192]{3,2,1,0:T(8,128)(2,1)S(1)}, u32[]{:S(2)}, u32[]{:S(2)}) collective-permute-start(bf16[3,3,16,192]{3,2,1,0:T(8,128)(2,1)S(1)} %collective-permute-done.7.far_ref), channel_id=1, source_target_pairs={{0,16},{16,0},{1,17},{17,1},{2,18},{18,2},{3,19},{19,3},{4,20},{20... | collective-permute-start | bytes 165896 | tf_op jit(solution)/shard_map/ppermute | solution.py:297
  35.6 8.7 %collective-permute-start.10 = (bf16[8,16,512]{2,1,0:T(8,128)(2,1)S(1)}, bf16[8,16,512]{2,1,0:T(8,128)(2,1)S(1)}, u32[]{:S(2)}, u32[]{:S(2)}) collective-permute-start(bf16[8,16,512]{2,1,0:T(8,128)(2,1)S(1)} %get-tuple-element.38), channel_id=1, source_target_pairs={{0,12},{4,0},{8,4},{12,8},{16,20},{20,24},{24,28},{28,16},{1,13},{... | collective-permute-start | bytes 393224 | tf_op jit(solution)/shard_map/ppermute | solution.py:236
  35.7 9.3 %collective-permute-start.9 = (bf16[8,16,512]{2,1,0:T(8,128)(2,1)S(1)}, bf16[8,16,512]{2,1,0:T(8,128)(2,1)S(1)}, u32[]{:S(2)}, u32[]{:S(2)}) collective-permute-start(bf16[8,16,512]{2,1,0:T(8,128)(2,1)S(1)} %get-tuple-element.36), channel_id=1, source_target_pairs={{0,4},{4,8},{8,12},{12,0},{16,28},{20,16},{24,20},{28,24},{1,5},{5... | collective-permute-start | bytes 393224 | tf_op jit(solution)/shard_map/ppermute | solution.py:237
  44.3 0.7 copy-start.4
  44.3 7.1 %copy-start.2 = (bf16[8,16,256]{2,1,0:T(8,128)(2,1)S(1)}, bf16[8,16,256]{2,1,0:T(8,128)(2,1)}, u32[]{:S(2)}) copy-start(bf16[8,16,256]{2,1,0:T(8,128)(2,1)} %get-tuple-element.39.later_ref) | copy-start | bytes 196612
  44.3 7.0 %collective-permute-start.11 = (bf16[8,16,512]{2,1,0:T(8,128)(2,1)S(1)}, bf16[8,16,512]{2,1,0:T(8,128)(2,1)S(1)}, u32[]{:S(2)}, u32[]{:S(2)}) collective-permute-start(bf16[8,16,512]{2,1,0:T(8,128)(2,1)S(1)} %shard_map.68), channel_id=1, source_target_pairs={{0,12},{4,0},{8,4},{12,8},{16,20},{20,24},{24,28},{28,16},{1,13},{... | collective-permute-start | bytes 393224 | tf_op jit(solution)/shard_map/ppermute | solution.py:242
  52.2 10.7 %collective-permute-start.12 = (bf16[8,16,768]{2,1,0:T(8,128)(2,1)S(1)}, bf16[8,16,768]{2,1,0:T(8,128)(2,1)S(1)}, u32[]{:S(2)}, u32[]{:S(2)}) collective-permute-start(bf16[8,16,768]{2,1,0:T(8,128)(2,1)S(1)} %get-tuple-element.40.a_ref), channel_id=1, source_target_pairs={{0,1},{1,0},{2,3},{3,2},{4,5},{5,4},{6,7},{7,6},{8,9},{9,8},{10,11... | collective-permute-start | bytes 589832 | tf_op jit(solution)/shard_map/ppermute | solution.py:267
  53.6 9.4 %collective-permute-start.13 = (bf16[8,16,768]{2,1,0:T(8,128)(2,1)S(1)}, bf16[8,16,768]{2,1,0:T(8,128)(2,1)S(1)}, u32[]{:S(2)}, u32[]{:S(2)}) collective-permute-start(bf16[8,16,768]{2,1,0:T(8,128)(2,1)S(1)} %get-tuple-element.40.a_ref), channel_id=1, source_target_pairs={{0,2},{1,3},{2,0},{3,1},{4,6},{5,7},{6,4},{7,5},{8,10},{9,11},{10,... | collective-permute-start | bytes 589832 | tf_op jit(solution)/shard_map/ppermute | solution.py:267
  54.8 8.2 %collective-permute-start.14 = (bf16[8,16,768]{2,1,0:T(8,128)(2,1)S(1)}, bf16[8,16,768]{2,1,0:T(8,128)(2,1)S(1)}, u32[]{:S(2)}, u32[]{:S(2)}) collective-permute-start(bf16[8,16,768]{2,1,0:T(8,128)(2,1)S(1)} %get-tuple-element.40.a_ref), channel_id=1, source_target_pairs={{0,3},{1,2},{2,1},{3,0},{4,7},{5,6},{6,5},{7,4},{8,11},{9,10},{10,... | collective-permute-start | bytes 589832 | tf_op jit(solution)/shard_map/ppermute | solution.py:267
  56.0 12.5 %all-to-all-start.1 = ((f32[64,4,128]{2,1,0:T(4,128)}), f32[64,4,128]{2,1,0:T(4,128)S(1)}, u32[]{:S(2)}, u32[]{:S(2)}) async-start(f32[64,4,128]{2,1,0:T(4,128)} %get-tuple-element.43), calls=%async_computation.1 | async-start | bytes 262144 | tf_op jit(solution)/shard_map/all_to_all | solution.py:271
  63.0 9.5 %collective-permute-start.15 = (bf16[4,16,768]{2,1,0:T(8,128)(2,1)S(1)}, bf16[4,16,768]{2,1,0:T(8,128)(2,1)S(1)}, u32[]{:S(2)}, u32[]{:S(2)}) collective-permute-start(bf16[4,16,768]{2,1,0:T(8,128)(2,1)S(1)} %get-tuple-element.41), channel_id=1, source_target_pairs={{16,32},{48,64},{80,96},{112,128},{144,160},{176,192},{208,224},{3... | collective-permute-start | bytes 294920 | tf_op jit(solution)/shard_map/ppermute | solution.py:261
  67.0 5.6 %collective-permute-start.16 = (bf16[4,16,768]{2,1,0:T(8,128)(2,1)S(1)}, bf16[4,16,768]{2,1,0:T(8,128)(2,1)S(1)}, u32[]{:S(2)}, u32[]{:S(2)}) collective-permute-start(bf16[4,16,768]{2,1,0:T(8,128)(2,1)S(1)} %get-tuple-element.42), channel_id=1, source_target_pairs={{0,16},{16,0},{32,48},{48,32},{64,80},{80,64},{96,112},{112,96},{1... | collective-permute-start | bytes 294920 | tf_op jit(solution)/shard_map/ppermute | solution.py:262
  74.1 10.0 %collective-permute-start.18 = (bf16[8,16,512]{2,1,0:T(8,128)(2,1)S(1)}, bf16[8,16,512]{2,1,0:T(8,128)(2,1)S(1)}, u32[]{:S(2)}, u32[]{:S(2)}) collective-permute-start(bf16[8,16,512]{2,1,0:T(8,128)(2,1)S(1)} %get-tuple-element.48), channel_id=1, source_target_pairs={{0,12},{4,0},{8,4},{12,8},{16,20},{20,24},{24,28},{28,16},{1,13},{... | collective-permute-start | bytes 393224 | tf_op jit(solution)/shard_map/ppermute | solution.py:236
  76.3 7.9 %collective-permute-start.17 = (bf16[8,16,512]{2,1,0:T(8,128)(2,1)S(1)}, bf16[8,16,512]{2,1,0:T(8,128)(2,1)S(1)}, u32[]{:S(2)}, u32[]{:S(2)}) collective-permute-start(bf16[8,16,512]{2,1,0:T(8,128)(2,1)S(1)} %get-tuple-element.46), channel_id=1, source_target_pairs={{0,4},{4,8},{8,12},{12,0},{16,28},{20,16},{24,20},{28,24},{1,5},{5... | collective-permute-start | bytes 393224 | tf_op jit(solution)/shard_map/ppermute | solution.py:237
  84.1 6.3 %copy-start = (bf16[4,8,16,128]{3,2,1,0:T(8,128)(2,1)S(1)}, bf16[4,8,16,128]{3,2,1,0:T(8,128)(2,1)}, u32[]{:S(2)}) copy-start(bf16[4,8,16,128]{3,2,1,0:T(8,128)(2,1)} %x_ref.1) | copy-start | bytes 393220
  84.1 6.2 %collective-permute-start.19 = (bf16[8,16,512]{2,1,0:T(8,128)(2,1)S(1)}, bf16[8,16,512]{2,1,0:T(8,128)(2,1)S(1)}, u32[]{:S(2)}, u32[]{:S(2)}) collective-permute-start(bf16[8,16,512]{2,1,0:T(8,128)(2,1)S(1)} %shard_map.73), channel_id=1, source_target_pairs={{0,12},{4,0},{8,4},{12,8},{16,20},{20,24},{24,28},{28,16},{1,13},{... | collective-permute-start | bytes 393224 | tf_op jit(solution)/shard_map/ppermute | solution.py:242

commit v17 on v16

--- a/solution.py
+++ b/solution.py
@@ -57,8 +57,7 @@
     copies = [pltpu.make_async_copy(src, dst, sems.at[i]) for i, (src, dst) in enumerate(pairs)]
     for copy in copies:
         copy.start()
-    for copy in copies:
-        copy.wait()
+    return copies
 
 
 def begin_kernel(
@@ -66,13 +65,15 @@
     raw_ref, later_ref, stats_ref, own_ref, side_ref, far_ref,
     x_ref, cache_ref, gain_ref, shift_ref, w_ref, note_ref, pieces_ref, sems,
 ):
-    fetch(
+    copies = fetch(
         (
             (x_hbm, x_ref), (cache_hbm, cache_ref), (gain_hbm, gain_ref), (shift_hbm, shift_ref),
             (w_hbm, w_ref),
         ),
         sems,
     )
+    copies[0].wait()
+    copies[1].wait()
     for r in range(8):
         for t in range(2):
             lanes = slice(128 * t, 128 * (t + 1))
@@ -80,6 +81,8 @@
             later_ref[r, :, lanes] = cache_ref[1, t, r]
         for t in range(4):
             raw_ref[r, :, 256 + 128 * t : 384 + 128 * t] = x_ref[t, r]
+    for copy in copies[2:]:
+        copy.wait()
     row, me, _ = place()
     core = lax.rem(row, 2)
     for q in range(4):

time: 92.3 us -> 92.3 us (level)
  no operation moved by 1% of the time
where the time goes in v17:
time: 92.3 us; the launch traced here: 91.1 us
  starting transfers between devices  48.6 us (53%)
  waiting for transfers between devices  32.9 us (36%)
  Pallas kernels  8.76 us (9%)
    all_to_all x2, starting transfers between devices, exchange(): return lax.all_to_all(x, axes, 0, 0, tiled=True)  18.2 us
    ppermute x2, waiting for transfers between devices, convolve(): side = lax.ppermute(side, ('core', 'zh'), sides(-1))  12.4 us
    ppermute x2, waiting for transfers between devices, convolve(): far = lax.ppermute(far, ('core', 'zh'), sides(-1))  9.64 us
    pallas_call x11, Pallas kernels, call(): pl.pallas_call(kernel, out_shape=outs, in_specs=specs, out_specs=jax.tree...  8.76 us
    ppermute x2, waiting for transfers between devices, rows_beside(): beyond = lax.ppermute(beyond, ROW, pairs)  8.52 us
    ppermute x2, starting transfers between devices, rows_beside(): beyond = lax.ppermute(beyond, ROW, pairs)  7.59 us
    ppermute x6, starting transfers between devices, near(): lax.ppermute(x, NEAR, [(i, i ^ k) for i in range(4)])  6.69 us
    ppermute x1, starting transfers between devices, local(): side = lax.ppermute(side, ('core', 'zh'), sides(1))  5.85 us
  transfers between devices with their start and end apart: 22, of which 8 were waited for; matrix products, arithmetic and copies ran while one was open for 0% of the time, Pallas kernels for 2%

profile of v17, /device:TPU:27, one launch (start us, length us, event | category | flops | bytes accessed | tf_op | source)
XLA Modules:
  0.0 91.1 jit_solution(8472958630667943832)
XLA Ops:
  0.0 2.3 %shard_map.64 = (bf16[8,16,768]{2,1,0:T(8,128)(2,1)}, bf16[8,16,256]{2,1,0:T(8,128)(2,1)}, f32[64,8,128]{2,1,0:T(8,128)}, bf16[2,3,3,16,192]{4,3,2,1,0:T(8,128)(...) custom-call(bf16[4,8,16,128]{3,2,1,0:T(8,128)(2,1)} %x_ref.1, ...), custom_call_target="tpu_custom_call" | custom-call | bytes 704768 | tf_op jit(solution)/shard_map/pallas_call | solution.py:32
  2.3 0.3 collective-permute-start
  2.6 1.6 %collective-permute-start.1 = (bf16[8,16,768]{2,1,0:T(8,128)(2,1)}, bf16[8,16,768]{2,1,0:T(8,128)(2,1)S(1)}, u32[]{:S(2)}, u32[]{:S(2)}) collective-permute-start(bf16[8,16,768]{2,1,0:T(8,128)(2,1)} %get-tuple-element.27.a_ref), channel_id=1, source_target_pairs={{0,2},{1,3},{2,0},{3,1},{4,6},{5,7},{6,4},{7,5},{8,10},{9,11},{10,... | collective-permute-start | bytes 589832 | tf_op jit(solution)/shard_map/ppermute | solution.py:270
  4.3 0.9 %collective-permute-start.2 = (bf16[8,16,768]{2,1,0:T(8,128)(2,1)}, bf16[8,16,768]{2,1,0:T(8,128)(2,1)S(1)}, u32[]{:S(2)}, u32[]{:S(2)}) collective-permute-start(bf16[8,16,768]{2,1,0:T(8,128)(2,1)} %get-tuple-element.27.a_ref), channel_id=1, source_target_pairs={{0,3},{1,2},{2,1},{3,0},{4,7},{5,6},{6,5},{7,4},{8,11},{9,10},{10,... | collective-permute-start | bytes 589832 | tf_op jit(solution)/shard_map/ppermute | solution.py:270
  5.2 5.8 %collective-permute-start.5 = (bf16[2,3,3,16,192]{4,3,2,1,0:T(8,128)(2,1)}, bf16[2,3,3,16,192]{4,3,2,1,0:T(8,128)(2,1)S(1)}, u32[]{:S(2)}, u32[]{:S(2)}) collective-permute-start(bf16[2,3,3,16,192]{4,3,2,1,0:T(8,128)(2,1)} %get-tuple-element.31), channel_id=1, source_target_pairs={{0,4},{4,8},{8,12},{12,0},{16,28},{20,16},{24,20},{28,24},{1,5},{5... | collective-permute-start | bytes 331784 | tf_op jit(solution)/shard_map/ppermute | solution.py:294
  11.0 0.9 collective-permute-start.7
  11.9 11.2 %all-to-all-start = ((f32[64,8,128]{2,1,0:T(8,128)}), f32[64,8,128]{2,1,0:T(8,128)S(1)}, u32[]{:S(2)}, u32[]{:S(2)}) async-start(f32[64,8,128]{2,1,0:T(8,128)} %get-tuple-element.30), calls=%async_computation | async-start | bytes 524288 | tf_op jit(solution)/shard_map/all_to_all | solution.py:274
  23.2 1.2 %collective-permute-start.6 = (bf16[2,3,3,16,192]{4,3,2,1,0:T(8,128)(2,1)S(1)}, bf16[2,3,3,16,192]{4,3,2,1,0:T(8,128)(2,1)S(1)}, u32[]{:S(2)}, u32[]{:S(2)}) collective-permute-start(bf16[2,3,3,16,192]{4,3,2,1,0:T(8,128)(2,1)S(1)} %collective-permute-done.5.side_ref), channel_id=1, source_target_pairs={{0,16},{16,0},{1,17},{17,1},{2,18},{18,2},{3,19},{19,3},{4,20},{20... | collective-permute-start | bytes 331784 | tf_op jit(solution)/shard_map/ppermute | solution.py:300
  24.5 3.6 %collective-permute-start.3 = (bf16[4,16,768]{2,1,0:T(8,128)(2,1)S(1)}, bf16[4,16,768]{2,1,0:T(8,128)(2,1)S(1)}, u32[]{:S(2)}, u32[]{:S(2)}) collective-permute-start(bf16[4,16,768]{2,1,0:T(8,128)(2,1)S(1)} %get-tuple-element.28), channel_id=1, source_target_pairs={{16,32},{48,64},{80,96},{112,128},{144,160},{176,192},{208,224},{3... | collective-permute-start | bytes 294920 | tf_op jit(solution)/shard_map/ppermute | solution.py:264
  28.1 0.1 collective-permute-start.4
  28.2 0.0 collective-permute-done.7.far_ref
  28.2 0.5 collective-permute-start.8
  28.7 0.9 %collective-permute-done.8.far2_ref = bf16[3,3,16,192]{3,2,1,0:T(8,128)(2,1)S(1)} collective-permute-done((bf16[3,3,16,192]{3,2,1,0:T(8,128)(2,1)S(1)}, bf16[3,3,16,192]{3,2,1,0:T(8,128)(2,1)S(1)}, u32[]{:S(2)}, u32[]{:S(2)}) %collective-permute-start.8) | collective-permute-done | bytes 55328 | tf_op jit(solution)/shard_map/ppermute | solution.py:300
  29.6 0.0 collective-permute-done.6.other_ref
  29.6 4.4 %collective-permute-done.3.next_ref = bf16[4,16,768]{2,1,0:T(8,128)(2,1)S(1)} collective-permute-done((bf16[4,16,768]{2,1,0:T(8,128)(2,1)S(1)}, bf16[4,16,768]{2,1,0:T(8,128)(2,1)S(1)}, u32[]{:S(2)}, u32[]{:S(2)}) %collective-permute-start.3) | collective-permute-done | bytes 98336 | tf_op jit(solution)/shard_map/ppermute | solution.py:264
  34.0 0.0 collective-permute-done.4.chip_ref
  34.0 0.0 all-to-all-done.stats_ref.notes_ref
  34.0 1.5 %shard_map.66 = (bf16[8,16,512]{2,1,0:T(8,128)(2,1)S(1)}, bf16[8,16,512]{2,1,0:T(8,128)(2,1)S(1)}, bf16[10,4,16,768]{3,2,1,0:T(8,128)(2,1)S(1)}) custom-call(bf16[8,16,768]{2,1,0:T(8,128)(2,1)S(1)} %copy-done.1, bf16[8,16,768]{2,1,0:T(8,128)(2,1)S(1)} %collective-permute-done.b_ref, bf16[8,16,768]{2,1,0:T(8,128)(2,1)S(1)} %collective-permute-done.1.c_ref, ...), custom_call_target="tpu_custom_call" | custom-call | flops 452984832 | bytes 1728512 | tf_op jit(solution)/shard_map/pallas_call | solution.py:32
  35.6 0.1 collective-permute-start.10
  35.7 3.6 %collective-permute-start.9 = (bf16[8,16,512]{2,1,0:T(8,128)(2,1)S(1)}, bf16[8,16,512]{2,1,0:T(8,128)(2,1)S(1)}, u32[]{:S(2)}, u32[]{:S(2)}) collective-permute-start(bf16[8,16,512]{2,1,0:T(8,128)(2,1)S(1)} %get-tuple-element.36), channel_id=1, source_target_pairs={{0,4},{4,8},{8,12},{12,0},{16,28},{20,16},{24,20},{28,24},{1,5},{5... | collective-permute-start | bytes 393224 | tf_op jit(solution)/shard_map/ppermute | solution.py:240
  39.2 0.9 shard_map.67
  40.1 4.2 %collective-permute-done.10.b_ref = bf16[8,16,512]{2,1,0:T(8,128)(2,1)S(1)} collective-permute-done((bf16[8,16,512]{2,1,0:T(8,128)(2,1)S(1)}, bf16[8,16,512]{2,1,0:T(8,128)(2,1)S(1)}, u32[]{:S(2)}, u32[]{:S(2)}) %collective-permute-start.10) | collective-permute-done | bytes 131104 | tf_op jit(solution)/shard_map/ppermute | solution.py:239
  44.3 0.1 collective-permute-start.11
  44.4 0.5 copy-done.4
  45.0 0.0 collective-permute-done.9.b_ref
  45.0 6.3 %collective-permute-done.11.c_ref = bf16[8,16,512]{2,1,0:T(8,128)(2,1)S(1)} collective-permute-done((bf16[8,16,512]{2,1,0:T(8,128)(2,1)S(1)}, bf16[8,16,512]{2,1,0:T(8,128)(2,1)S(1)}, u32[]{:S(2)}, u32[]{:S(2)}) %collective-permute-start.11) | collective-permute-done | bytes 131104 | tf_op jit(solution)/shard_map/ppermute | solution.py:245
  51.3 0.1 broadcast_in_dim.13.bias_ref
  51.4 0.8 shard_map.69
  52.2 1.4 %collective-permute-start.12 = (bf16[8,16,768]{2,1,0:T(8,128)(2,1)S(1)}, bf16[8,16,768]{2,1,0:T(8,128)(2,1)S(1)}, u32[]{:S(2)}, u32[]{:S(2)}) collective-permute-start(bf16[8,16,768]{2,1,0:T(8,128)(2,1)S(1)} %get-tuple-element.40.a_ref), channel_id=1, source_target_pairs={{0,1},{1,0},{2,3},{3,2},{4,5},{5,4},{6,7},{7,6},{8,9},{9,8},{10,11... | collective-permute-start | bytes 589832 | tf_op jit(solution)/shard_map/ppermute | solution.py:270
  53.6 1.2 %collective-permute-start.13 = (bf16[8,16,768]{2,1,0:T(8,128)(2,1)S(1)}, bf16[8,16,768]{2,1,0:T(8,128)(2,1)S(1)}, u32[]{:S(2)}, u32[]{:S(2)}) collective-permute-start(bf16[8,16,768]{2,1,0:T(8,128)(2,1)S(1)} %get-tuple-element.40.a_ref), channel_id=1, source_target_pairs={{0,2},{1,3},{2,0},{3,1},{4,6},{5,7},{6,4},{7,5},{8,10},{9,11},{10,... | collective-permute-start | bytes 589832 | tf_op jit(solution)/shard_map/ppermute | solution.py:270
  54.8 1.2 %collective-permute-start.14 = (bf16[8,16,768]{2,1,0:T(8,128)(2,1)S(1)}, bf16[8,16,768]{2,1,0:T(8,128)(2,1)S(1)}, u32[]{:S(2)}, u32[]{:S(2)}) collective-permute-start(bf16[8,16,768]{2,1,0:T(8,128)(2,1)S(1)} %get-tuple-element.40.a_ref), channel_id=1, source_target_pairs={{0,3},{1,2},{2,1},{3,0},{4,7},{5,6},{6,5},{7,4},{8,11},{9,10},{10,... | collective-permute-start | bytes 589832 | tf_op jit(solution)/shard_map/ppermute | solution.py:270
  56.0 7.0 %all-to-all-start.1 = ((f32[64,4,128]{2,1,0:T(4,128)}), f32[64,4,128]{2,1,0:T(4,128)S(1)}, u32[]{:S(2)}, u32[]{:S(2)}) async-start(f32[64,4,128]{2,1,0:T(4,128)} %get-tuple-element.43), calls=%async_computation.1 | async-start | bytes 262144 | tf_op jit(solution)/shard_map/all_to_all | solution.py:274
  62.9 0.0 collective-permute-done.12.b_ref
  63.0 4.0 %collective-permute-start.15 = (bf16[4,16,768]{2,1,0:T(8,128)(2,1)S(1)}, bf16[4,16,768]{2,1,0:T(8,128)(2,1)S(1)}, u32[]{:S(2)}, u32[]{:S(2)}) collective-permute-start(bf16[4,16,768]{2,1,0:T(8,128)(2,1)S(1)} %get-tuple-element.41), channel_id=1, source_target_pairs={{16,32},{48,64},{80,96},{112,128},{144,160},{176,192},{208,224},{3... | collective-permute-start | bytes 294920 | tf_op jit(solution)/shard_map/ppermute | solution.py:264
  67.0 0.1 collective-permute-start.16
  67.1 1.3 %all-to-all-done.1.stats_ref = f32[64,4,128]{2,1,0:T(4,128)S(1)} async-done(((f32[64,4,128]{2,1,0:T(4,128)}), f32[64,4,128]{2,1,0:T(4,128)S(1)}, u32[]{:S(2)}, u32[]{:S(2)}) %all-to-all-start.1) | async-done | bytes 131104 | tf_op jit(solution)/shard_map/all_to_all | solution.py:274
  68.4 4.1 %collective-permute-done.15.next_ref = bf16[4,16,768]{2,1,0:T(8,128)(2,1)S(1)} collective-permute-done((bf16[4,16,768]{2,1,0:T(8,128)(2,1)S(1)}, bf16[4,16,768]{2,1,0:T(8,128)(2,1)S(1)}, u32[]{:S(2)}, u32[]{:S(2)}) %collective-permute-start.15) | collective-permute-done | bytes 98336 | tf_op jit(solution)/shard_map/ppermute | solution.py:264
  72.5 0.0 collective-permute-done.16.chip_ref
  72.6 1.5 %shard_map.71 = (bf16[8,16,512]{2,1,0:T(8,128)(2,1)S(1)}, bf16[8,16,512]{2,1,0:T(8,128)(2,1)S(1)}, bf16[10,4,16,768]{3,2,1,0:T(8,128)(2,1)S(1)}) custom-call(bf16[8,16,768]{2,1,0:T(8,128)(2,1)S(1)} %get-tuple-element.40.a_ref, bf16[8,16,768]{2,1,0:T(8,128)(2,1)S(1)} %collective-permute-done.12.b_ref, bf16[8,16,768]{2,1,0:T(8,128)(2,1)S(1)} %collective-permute-done.13.c_ref, ...), custom_call_target="tpu_custom_call" | custom-call | flops 452984832 | bytes 1597440 | tf_op jit(solution)/shard_map/pallas_call | solution.py:32
  74.1 2.2 %collective-permute-start.18 = (bf16[8,16,512]{2,1,0:T(8,128)(2,1)S(1)}, bf16[8,16,512]{2,1,0:T(8,128)(2,1)S(1)}, u32[]{:S(2)}, u32[]{:S(2)}) collective-permute-start(bf16[8,16,512]{2,1,0:T(8,128)(2,1)S(1)} %get-tuple-element.48), channel_id=1, source_target_pairs={{0,12},{4,0},{8,4},{12,8},{16,20},{20,24},{24,28},{28,16},{1,13},{... | collective-permute-start | bytes 393224 | tf_op jit(solution)/shard_map/ppermute | solution.py:239
  76.3 1.4 %collective-permute-start.17 = (bf16[8,16,512]{2,1,0:T(8,128)(2,1)S(1)}, bf16[8,16,512]{2,1,0:T(8,128)(2,1)S(1)}, u32[]{:S(2)}, u32[]{:S(2)}) collective-permute-start(bf16[8,16,512]{2,1,0:T(8,128)(2,1)S(1)} %get-tuple-element.46), channel_id=1, source_target_pairs={{0,4},{4,8},{8,12},{12,0},{16,28},{20,16},{24,20},{28,24},{1,5},{5... | collective-permute-start | bytes 393224 | tf_op jit(solution)/shard_map/ppermute | solution.py:240
  77.7 0.9 shard_map.72
  78.6 5.5 %collective-permute-done.18.b_ref = bf16[8,16,512]{2,1,0:T(8,128)(2,1)S(1)} collective-permute-done((bf16[8,16,512]{2,1,0:T(8,128)(2,1)S(1)}, bf16[8,16,512]{2,1,0:T(8,128)(2,1)S(1)}, u32[]{:S(2)}, u32[]{:S(2)}) %collective-permute-start.18) | collective-permute-done | bytes 131104 | tf_op jit(solution)/shard_map/ppermute | solution.py:239
  84.1 0.1 collective-permute-start.19
  84.2 0.0 collective-permute-done.17.b_ref
  84.2 6.1 %collective-permute-done.19.c_ref = bf16[8,16,512]{2,1,0:T(8,128)(2,1)S(1)} collective-permute-done((bf16[8,16,512]{2,1,0:T(8,128)(2,1)S(1)}, bf16[8,16,512]{2,1,0:T(8,128)(2,1)S(1)}, u32[]{:S(2)}, u32[]{:S(2)}) %collective-permute-start.19) | collective-permute-done | bytes 131104 | tf_op jit(solution)/shard_map/ppermute | solution.py:245
  90.3 0.1 broadcast_in_dim.15.bias_ref
  90.4 0.7 shard_map.74
  (20 shorter events, 0.2 us)
Async XLA Ops:
  2.3 22.1 %collective-permute-start = (bf16[8,16,768]{2,1,0:T(8,128)(2,1)}, bf16[8,16,768]{2,1,0:T(8,128)(2,1)S(1)}, u32[]{:S(2)}, u32[]{:S(2)}) collective-permute-start(bf16[8,16,768]{2,1,0:T(8,128)(2,1)} %get-tuple-element.27.a_ref), channel_id=1, source_target_pairs={{0,1},{1,0},{2,3},{3,2},{4,5},{5,4},{6,7},{7,6},{8,9},{9,8},{10,11... | collective-permute-start | bytes 589832 | tf_op jit(solution)/shard_map/ppermute | solution.py:270
  2.6 21.8 %collective-permute-start.1 = (bf16[8,16,768]{2,1,0:T(8,128)(2,1)}, bf16[8,16,768]{2,1,0:T(8,128)(2,1)S(1)}, u32[]{:S(2)}, u32[]{:S(2)}) collective-permute-start(bf16[8,16,768]{2,1,0:T(8,128)(2,1)} %get-tuple-element.27.a_ref), channel_id=1, source_target_pairs={{0,2},{1,3},{2,0},{3,1},{4,6},{5,7},{6,4},{7,5},{8,10},{9,11},{10,... | collective-permute-start | bytes 589832 | tf_op jit(solution)/shard_map/ppermute | solution.py:270
  4.3 20.1 %collective-permute-start.2 = (bf16[8,16,768]{2,1,0:T(8,128)(2,1)}, bf16[8,16,768]{2,1,0:T(8,128)(2,1)S(1)}, u32[]{:S(2)}, u32[]{:S(2)}) collective-permute-start(bf16[8,16,768]{2,1,0:T(8,128)(2,1)} %get-tuple-element.27.a_ref), channel_id=1, source_target_pairs={{0,3},{1,2},{2,1},{3,0},{4,7},{5,6},{6,5},{7,4},{8,11},{9,10},{10,... | collective-permute-start | bytes 589832 | tf_op jit(solution)/shard_map/ppermute | solution.py:270
  5.2 18.0 %collective-permute-start.5 = (bf16[2,3,3,16,192]{4,3,2,1,0:T(8,128)(2,1)}, bf16[2,3,3,16,192]{4,3,2,1,0:T(8,128)(2,1)S(1)}, u32[]{:S(2)}, u32[]{:S(2)}) collective-permute-start(bf16[2,3,3,16,192]{4,3,2,1,0:T(8,128)(2,1)} %get-tuple-element.31), channel_id=1, source_target_pairs={{0,4},{4,8},{8,12},{12,0},{16,28},{20,16},{24,20},{28,24},{1,5},{5... | collective-permute-start | bytes 331784 | tf_op jit(solution)/shard_map/ppermute | solution.py:294
  11.0 17.1 %collective-permute-start.7 = (bf16[3,3,16,192]{3,2,1,0:T(8,128)(2,1)}, bf16[3,3,16,192]{3,2,1,0:T(8,128)(2,1)S(1)}, u32[]{:S(2)}, u32[]{:S(2)}) collective-permute-start(bf16[3,3,16,192]{3,2,1,0:T(8,128)(2,1)} %get-tuple-element.32), channel_id=1, source_target_pairs={{0,8},{4,12},{8,0},{12,4},{1,9},{5,13},{9,1},{13,5},{2,10},{6,14},... | collective-permute-start | bytes 165896 | tf_op jit(solution)/shard_map/ppermute | solution.py:295
  11.9 12.5 %copy-start.1 = (bf16[8,16,768]{2,1,0:T(8,128)(2,1)S(1)}, bf16[8,16,768]{2,1,0:T(8,128)(2,1)}, u32[]{:S(2)}) copy-start(bf16[8,16,768]{2,1,0:T(8,128)(2,1)} %get-tuple-element.27.a_ref) | copy-start | bytes 589828
  11.9 22.1 %all-to-all-start = ((f32[64,8,128]{2,1,0:T(8,128)}), f32[64,8,128]{2,1,0:T(8,128)S(1)}, u32[]{:S(2)}, u32[]{:S(2)}) async-start(f32[64,8,128]{2,1,0:T(8,128)} %get-tuple-element.30), calls=%async_computation | async-start | bytes 524288 | tf_op jit(solution)/shard_map/all_to_all | solution.py:274
  23.2 6.4 %collective-permute-start.6 = (bf16[2,3,3,16,192]{4,3,2,1,0:T(8,128)(2,1)S(1)}, bf16[2,3,3,16,192]{4,3,2,1,0:T(8,128)(2,1)S(1)}, u32[]{:S(2)}, u32[]{:S(2)}) collective-permute-start(bf16[2,3,3,16,192]{4,3,2,1,0:T(8,128)(2,1)S(1)} %collective-permute-done.5.side_ref), channel_id=1, source_target_pairs={{0,16},{16,0},{1,17},{17,1},{2,18},{18,2},{3,19},{19,3},{4,20},{20... | collective-permute-start | bytes 331784 | tf_op jit(solution)/shard_map/ppermute | solution.py:300
  24.5 9.5 %collective-permute-start.3 = (bf16[4,16,768]{2,1,0:T(8,128)(2,1)S(1)}, bf16[4,16,768]{2,1,0:T(8,128)(2,1)S(1)}, u32[]{:S(2)}, u32[]{:S(2)}) collective-permute-start(bf16[4,16,768]{2,1,0:T(8,128)(2,1)S(1)} %get-tuple-element.28), channel_id=1, source_target_pairs={{16,32},{48,64},{80,96},{112,128},{144,160},{176,192},{208,224},{3... | collective-permute-start | bytes 294920 | tf_op jit(solution)/shard_map/ppermute | solution.py:264
  28.1 11.1 %copy-start.3 = (bf16[2,3,3,16,192]{4,3,2,1,0:T(8,128)(2,1)S(1)}, bf16[2,3,3,16,192]{4,3,2,1,0:T(8,128)(2,1)}, u32[]{:S(2)}) copy-start(bf16[2,3,3,16,192]{4,3,2,1,0:T(8,128)(2,1)} %get-tuple-element.34.own_ref) | copy-start | bytes 331780
  28.1 5.9 %collective-permute-start.4 = (bf16[4,16,768]{2,1,0:T(8,128)(2,1)S(1)}, bf16[4,16,768]{2,1,0:T(8,128)(2,1)S(1)}, u32[]{:S(2)}, u32[]{:S(2)}) collective-permute-start(bf16[4,16,768]{2,1,0:T(8,128)(2,1)S(1)} %get-tuple-element.29), channel_id=1, source_target_pairs={{0,16},{16,0},{32,48},{48,32},{64,80},{80,64},{96,112},{112,96},{1... | collective-permute-start | bytes 294920 | tf_op jit(solution)/shard_map/ppermute | solution.py:265
  28.2 1.4 %collective-permute-start.8 = (bf16[3,3,16,192]{3,2,1,0:T(8,128)(2,1)S(1)}, bf16[3,3,16,192]{3,2,1,0:T(8,128)(2,1)S(1)}, u32[]{:S(2)}, u32[]{:S(2)}) collective-permute-start(bf16[3,3,16,192]{3,2,1,0:T(8,128)(2,1)S(1)} %collective-permute-done.7.far_ref), channel_id=1, source_target_pairs={{0,16},{16,0},{1,17},{17,1},{2,18},{18,2},{3,19},{19,3},{4,20},{20... | collective-permute-start | bytes 165896 | tf_op jit(solution)/shard_map/ppermute | solution.py:300
  35.6 8.7 %collective-permute-start.10 = (bf16[8,16,512]{2,1,0:T(8,128)(2,1)S(1)}, bf16[8,16,512]{2,1,0:T(8,128)(2,1)S(1)}, u32[]{:S(2)}, u32[]{:S(2)}) collective-permute-start(bf16[8,16,512]{2,1,0:T(8,128)(2,1)S(1)} %get-tuple-element.38), channel_id=1, source_target_pairs={{0,12},{4,0},{8,4},{12,8},{16,20},{20,24},{24,28},{28,16},{1,13},{... | collective-permute-start | bytes 393224 | tf_op jit(solution)/shard_map/ppermute | solution.py:239
  35.7 9.3 %collective-permute-start.9 = (bf16[8,16,512]{2,1,0:T(8,128)(2,1)S(1)}, bf16[8,16,512]{2,1,0:T(8,128)(2,1)S(1)}, u32[]{:S(2)}, u32[]{:S(2)}) collective-permute-start(bf16[8,16,512]{2,1,0:T(8,128)(2,1)S(1)} %get-tuple-element.36), channel_id=1, source_target_pairs={{0,4},{4,8},{8,12},{12,0},{16,28},{20,16},{24,20},{28,24},{1,5},{5... | collective-permute-start | bytes 393224 | tf_op jit(solution)/shard_map/ppermute | solution.py:240
  44.3 0.7 copy-start.4
  44.3 7.1 %copy-start.2 = (bf16[8,16,256]{2,1,0:T(8,128)(2,1)S(1)}, bf16[8,16,256]{2,1,0:T(8,128)(2,1)}, u32[]{:S(2)}) copy-start(bf16[8,16,256]{2,1,0:T(8,128)(2,1)} %get-tuple-element.39.later_ref) | copy-start | bytes 196612
  44.3 7.0 %collective-permute-start.11 = (bf16[8,16,512]{2,1,0:T(8,128)(2,1)S(1)}, bf16[8,16,512]{2,1,0:T(8,128)(2,1)S(1)}, u32[]{:S(2)}, u32[]{:S(2)}) collective-permute-start(bf16[8,16,512]{2,1,0:T(8,128)(2,1)S(1)} %shard_map.68), channel_id=1, source_target_pairs={{0,12},{4,0},{8,4},{12,8},{16,20},{20,24},{24,28},{28,16},{1,13},{... | collective-permute-start | bytes 393224 | tf_op jit(solution)/shard_map/ppermute | solution.py:245
  52.2 10.7 %collective-permute-start.12 = (bf16[8,16,768]{2,1,0:T(8,128)(2,1)S(1)}, bf16[8,16,768]{2,1,0:T(8,128)(2,1)S(1)}, u32[]{:S(2)}, u32[]{:S(2)}) collective-permute-start(bf16[8,16,768]{2,1,0:T(8,128)(2,1)S(1)} %get-tuple-element.40.a_ref), channel_id=1, source_target_pairs={{0,1},{1,0},{2,3},{3,2},{4,5},{5,4},{6,7},{7,6},{8,9},{9,8},{10,11... | collective-permute-start | bytes 589832 | tf_op jit(solution)/shard_map/ppermute | solution.py:270
  53.6 9.4 %collective-permute-start.13 = (bf16[8,16,768]{2,1,0:T(8,128)(2,1)S(1)}, bf16[8,16,768]{2,1,0:T(8,128)(2,1)S(1)}, u32[]{:S(2)}, u32[]{:S(2)}) collective-permute-start(bf16[8,16,768]{2,1,0:T(8,128)(2,1)S(1)} %get-tuple-element.40.a_ref), channel_id=1, source_target_pairs={{0,2},{1,3},{2,0},{3,1},{4,6},{5,7},{6,4},{7,5},{8,10},{9,11},{10,... | collective-permute-start | bytes 589832 | tf_op jit(solution)/shard_map/ppermute | solution.py:270
  54.8 8.2 %collective-permute-start.14 = (bf16[8,16,768]{2,1,0:T(8,128)(2,1)S(1)}, bf16[8,16,768]{2,1,0:T(8,128)(2,1)S(1)}, u32[]{:S(2)}, u32[]{:S(2)}) collective-permute-start(bf16[8,16,768]{2,1,0:T(8,128)(2,1)S(1)} %get-tuple-element.40.a_ref), channel_id=1, source_target_pairs={{0,3},{1,2},{2,1},{3,0},{4,7},{5,6},{6,5},{7,4},{8,11},{9,10},{10,... | collective-permute-start | bytes 589832 | tf_op jit(solution)/shard_map/ppermute | solution.py:270
  56.0 12.5 %all-to-all-start.1 = ((f32[64,4,128]{2,1,0:T(4,128)}), f32[64,4,128]{2,1,0:T(4,128)S(1)}, u32[]{:S(2)}, u32[]{:S(2)}) async-start(f32[64,4,128]{2,1,0:T(4,128)} %get-tuple-element.43), calls=%async_computation.1 | async-start | bytes 262144 | tf_op jit(solution)/shard_map/all_to_all | solution.py:274
  63.0 9.5 %collective-permute-start.15 = (bf16[4,16,768]{2,1,0:T(8,128)(2,1)S(1)}, bf16[4,16,768]{2,1,0:T(8,128)(2,1)S(1)}, u32[]{:S(2)}, u32[]{:S(2)}) collective-permute-start(bf16[4,16,768]{2,1,0:T(8,128)(2,1)S(1)} %get-tuple-element.41), channel_id=1, source_target_pairs={{16,32},{48,64},{80,96},{112,128},{144,160},{176,192},{208,224},{3... | collective-permute-start | bytes 294920 | tf_op jit(solution)/shard_map/ppermute | solution.py:264
  67.0 5.6 %collective-permute-start.16 = (bf16[4,16,768]{2,1,0:T(8,128)(2,1)S(1)}, bf16[4,16,768]{2,1,0:T(8,128)(2,1)S(1)}, u32[]{:S(2)}, u32[]{:S(2)}) collective-permute-start(bf16[4,16,768]{2,1,0:T(8,128)(2,1)S(1)} %get-tuple-element.42), channel_id=1, source_target_pairs={{0,16},{16,0},{32,48},{48,32},{64,80},{80,64},{96,112},{112,96},{1... | collective-permute-start | bytes 294920 | tf_op jit(solution)/shard_map/ppermute | solution.py:265
  74.1 10.0 %collective-permute-start.18 = (bf16[8,16,512]{2,1,0:T(8,128)(2,1)S(1)}, bf16[8,16,512]{2,1,0:T(8,128)(2,1)S(1)}, u32[]{:S(2)}, u32[]{:S(2)}) collective-permute-start(bf16[8,16,512]{2,1,0:T(8,128)(2,1)S(1)} %get-tuple-element.48), channel_id=1, source_target_pairs={{0,12},{4,0},{8,4},{12,8},{16,20},{20,24},{24,28},{28,16},{1,13},{... | collective-permute-start | bytes 393224 | tf_op jit(solution)/shard_map/ppermute | solution.py:239
  76.3 7.9 %collective-permute-start.17 = (bf16[8,16,512]{2,1,0:T(8,128)(2,1)S(1)}, bf16[8,16,512]{2,1,0:T(8,128)(2,1)S(1)}, u32[]{:S(2)}, u32[]{:S(2)}) collective-permute-start(bf16[8,16,512]{2,1,0:T(8,128)(2,1)S(1)} %get-tuple-element.46), channel_id=1, source_target_pairs={{0,4},{4,8},{8,12},{12,0},{16,28},{20,16},{24,20},{28,24},{1,5},{5... | collective-permute-start | bytes 393224 | tf_op jit(solution)/shard_map/ppermute | solution.py:240
  84.1 6.3 %copy-start = (bf16[4,8,16,128]{3,2,1,0:T(8,128)(2,1)S(1)}, bf16[4,8,16,128]{3,2,1,0:T(8,128)(2,1)}, u32[]{:S(2)}) copy-start(bf16[4,8,16,128]{3,2,1,0:T(8,128)(2,1)} %x_ref.1) | copy-start | bytes 393220
  84.1 6.2 %collective-permute-start.19 = (bf16[8,16,512]{2,1,0:T(8,128)(2,1)S(1)}, bf16[8,16,512]{2,1,0:T(8,128)(2,1)S(1)}, u32[]{:S(2)}, u32[]{:S(2)}) collective-permute-start(bf16[8,16,512]{2,1,0:T(8,128)(2,1)S(1)} %shard_map.73), channel_id=1, source_target_pairs={{0,12},{4,0},{8,4},{12,8},{16,20},{20,24},{24,28},{28,16},{1,13},{... | collective-permute-start | bytes 393224 | tf_op jit(solution)/shard_map/ppermute | solution.py:245
